TPU v7x, 32 devices: a whole 2x2x4 slice. The times are simulated.
32 devices in a mesh: groups: 2 (over y), ctx: 4 (over z), head: 4 (over x, core).
Axes of the slice: x: 2, y: 2, z: 4, core: 2. Of those that a mesh axis runs over, the one named last changes fastest.
Arguments:
- queries: bfloat16 [4096, 4096], P(('groups', 'ctx'), 'head'), parts along dimension 0, may hold values from -6 to 6
- keys: bfloat16 [4096, 2, 4096], P(('groups', 'ctx'), None, 'head'), parts along dimension 0, may hold values from -6 to 6
- values: bfloat16 [4096, 2, 4096], P(('groups', 'ctx'), None, 'head'), parts along dimension 0, may hold values from -6 to 6
- beta: float32 [2, 32, 4096], P(None, 'head', ('groups', 'ctx')), parts along dimension 2, may hold values from 0 to 2, as said below
- gain: float32 [4096], P('head'), may hold values from 0.5 to 1.5
- w_out: bfloat16 [4096, 4096], P('head', 'ctx'), may hold values from -0.09375 to 0.09375
Outputs:
- mixed: bfloat16 [4096, 4096], P(('groups', 'ctx'), 'head'), parts along dimension 0
There are 2 independent parts, one for each index of `groups`. A program takes and returns all parts, laid end to end along the dimension named above; an argument that names none is the same for every part. Nothing has to cross between parts.
Inputs may be any that keep to these rules, and one draw needn't show every extreme that they name: `beta`: every strength lies in the closed range shown; each head either keeps strengths just under 2 at all tokens or spreads them well inside the range.
All inputs are finite; a program needn't handle non-finite values.
Results may differ from a plain program's by a relative error of at most 0.014.
Values may be sent and summed in bfloat16 or wider, within the bound.
No kernel may reach another device: no remote copies, remote signals or barrier semaphores. Data moves between devices by JAX's collectives and lax.ppermute only.
A program may use at most 128 MiB of HBM per device.

v0:
```python
import jax
import jax.numpy as jnp
from jax import lax
from jax.sharding import PartitionSpec as P

DK = 128


def shifted(value, axis, steps):
    count = lax.axis_size(axis)
    initial, last = (max(0, -steps), min(count, count - steps))
    return lax.ppermute(value, axis, [(source, source + steps) for source in range(initial, last)])


def unit_rows(matrix):
    return matrix * lax.rsqrt(jnp.sum(matrix * matrix, axis=-1, keepdims=True) + 1e-06)


def lower_solve(lower_tri, right_side):
    return lax.linalg.triangular_solve(
        lower_tri, right_side, left_side=True, lower=True, transpose_a=False, unit_diagonal=True
    )


def per_device(queries, keys, values, beta, gain, w_out):
    highest = lax.Precision.HIGHEST
    tokens_dev = queries.shape[0]
    head_count = queries.shape[1] // DK
    block_size = 64
    block_count = tokens_dev // block_size
    refl_count = 2 * block_size
    query_unit = unit_rows(queries.reshape(tokens_dev, head_count, DK).astype(jnp.float32))
    key_unit = unit_rows(keys.reshape(tokens_dev, 2, head_count, DK).astype(jnp.float32))
    value_full = values.reshape(tokens_dev, 2, head_count, DK).astype(jnp.float32)
    key_block = key_unit.reshape(block_count, refl_count, head_count, DK).transpose(0, 2, 1, 3)
    value_block = value_full.reshape(block_count, refl_count, head_count, DK).transpose(0, 2, 1, 3)
    query_block = query_unit.reshape(block_count, block_size, head_count, DK).transpose(0, 2, 1, 3)
    beta_block = (
        jnp.transpose(beta, (2, 0, 1))
        .reshape(block_count, refl_count, head_count)
        .transpose(0, 2, 1)
    )
    key_gram = jnp.einsum("nhid,nhjd->nhij", key_block, key_block, precision=highest)
    row_index = jnp.arange(refl_count)
    strict_below = row_index[:, None] > row_index[None, :]
    identity_refl = jnp.eye(refl_count, dtype=jnp.float32)
    lower_tri = identity_refl + jnp.where(strict_below, beta_block[..., None] * key_gram, 0.0)
    w_factor = lower_solve(lower_tri, beta_block[..., None] * key_block)
    u_factor = lower_solve(lower_tri, beta_block[..., None] * value_block)
    reach_mask = 2 * jnp.arange(block_size)[:, None] + 1 >= row_index[None, :]
    key_scores = jnp.where(
        reach_mask, jnp.einsum("nhtd,nhjd->nhtj", query_block, key_block, precision=highest), 0.0
    )
    query_eff = query_block - jnp.einsum("nhtj,nhjd->nhtd", key_scores, w_factor, precision=highest)
    direct = jnp.einsum("nhtj,nhjd->nhtd", key_scores, u_factor, precision=highest)
    identity_head = jnp.broadcast_to(jnp.eye(DK, dtype=jnp.float32), (head_count, DK, DK))
    transition = identity_head - jnp.einsum(
        "nhjd,nhje->nhde", key_block, w_factor, precision=highest
    )
    writes = jnp.einsum("nhjd,nhje->nhde", key_block, u_factor, precision=highest)

    def advance(carried, inputs):
        memory, product = carried
        query_now, direct_now, transition_now, writes_now = inputs
        local_out = direct_now + jnp.einsum("htd,hde->hte", query_now, memory, precision=highest)
        exposure = jnp.einsum("htd,hde->hte", query_now, product, precision=highest)
        memory = jnp.einsum("hde,hef->hdf", transition_now, memory, precision=highest) + writes_now
        product = jnp.einsum("hde,hef->hdf", transition_now, product, precision=highest)
        return ((memory, product), (local_out, exposure))

    zero_state = jnp.zeros((head_count, DK, DK), jnp.float32)
    (state_end, total_end), (local_out, exposure) = lax.scan(
        advance, (zero_state, identity_head), (query_eff, direct, transition, writes)
    )

    def relay(round_index, incoming):
        outgoing = jnp.einsum("hde,hef->hdf", total_end, incoming, precision=highest) + state_end
        return shifted(outgoing.astype(jnp.bfloat16), "ctx", 1).astype(outgoing.dtype)

    incoming = lax.fori_loop(0, lax.axis_size("ctx") - 1, relay, zero_state)
    carried_out = jnp.einsum("nhtd,hde->nhte", exposure, incoming, precision=highest)
    readout = (local_out + carried_out).transpose(0, 2, 1, 3).reshape(tokens_dev, head_count, DK)
    normed = (
        readout
        * lax.rsqrt(jnp.mean(readout * readout, axis=-1, keepdims=True) + 1e-06)
        * gain.reshape(head_count, DK)
    )
    flat = normed.reshape(tokens_dev, head_count * DK).astype(jnp.bfloat16)
    partial_value = jnp.dot(
        flat, lax.all_gather(w_out, "ctx", axis=1, tiled=True), preferred_element_type=jnp.float32
    )
    return lax.psum_scatter(
        partial_value.astype(jnp.bfloat16), "head", scatter_dimension=1, tiled=True
    )


def solution(mesh):
    in_specs = (
        P(("groups", "ctx"), "head"),
        P(("groups", "ctx"), None, "head"),
        P(("groups", "ctx"), None, "head"),
        P(None, "head", ("groups", "ctx")),
        P("head"),
        P("head", "ctx"),
    )
    out_specs = P(("groups", "ctx"), "head")
    return jax.shard_map(
        per_device, mesh=mesh, in_specs=in_specs, out_specs=out_specs, check_vma=False
    )
```

profile of v0, /device:TPU:16, one launch (start us, length us, event | category | flops | bytes accessed | tf_op | source)
XLA Modules:
  0.0 910.2 jit_solution(3411522780533467639)
XLA Ops:
  6.5 0.7 all-gather.2.cloned.1.call-update
  7.3 3.0 fusion.45
  10.3 1.6 convert_bitcast_fusion
  11.9 3.0 reshape.100
  14.9 2.5 convert_multiply_fusion.1
  17.4 6.7 mul.86
  24.1 3.6 reduce_sum.27
  28.7 15.6 %add_bitcast_fusion = f32[8,8,1,128,128]{4,3,2,1,0:T(8,128)} fusion(f32[128,128]{1,0:T(8,128)S(1)} %get-tuple-element.159, f32[8,8,128]{2,1,0:T(8,128)S(1)} %copy.49, f32[128,128]{1,0:T(8,128)S(1)} %get-tuple-element.158, pred[128,128]{1,0:T(8,128)(4,1)S(1)} %get-tuple-element.156, pred[128,128]{1,0:T(8,128)(4,1)S(1)} %get-tuple-element.157, ...), kind=kOutput, calls=%fused_computation.50 | convolution fusion | flops 1616904192 | bytes 8617984 | tf_op jit(solution)/shard_map/nhid,nhjd->nhij/dot_general | solution.py:43
  44.3 630.2 %custom-call.6 = f32[8,8,1,128,128]{3,4,2,1,0:T(8,128)} custom-call(f32[8,8,1,128,128]{4,3,2,1,0:T(8,128)} %add_bitcast_fusion), custom_call_target="InvertDiagBlocksLowerTriangular" | custom-call | tf_op jit(solution)/shard_map/triangular_solve/custom-call.1 | solution.py:20
  674.5 2.1 copy.77
  677.4 2.1 copy.76
  679.5 5.0 reshape.102
  684.5 10.7 %fusion.33 = f32[8,8,64,128]{3,2,1,0:T(8,128)S(1)} fusion(f32[8,128,8,128]{3,2,1,0:T(8,128)} %reshape.100, f32[8,128,8]{1,2,0:T(8,128)S(1)} %copy.46, f32[8,64,8,128]{3,2,1,0:T(8,128)S(1)} %bitcast.133, f32[8,64,8]{1,2,0:T(8,128)S(1)} %copy.57), kind=kOutput, calls=%fused_computation.39 | convolution fusion | flops 806879232 | bytes 8437760 | tf_op jit(solution)/shard_map/nhtd,nhjd->nhtj/dot_general | solution.py:52
  695.3 7.9 fusion.29
  703.2 5.4 fusion.59
  708.6 9.6 %fusion.31 = f32[8,8,128,128]{3,2,1,0:T(8,128)S(1)} fusion(f32[8,8,1,128,128]{3,4,2,1,0:T(8,128)S(1)} %copy-done.1, f32[8,128,8,128]{3,2,1,0:T(8,128)S(1)} %copy-done, f32[8,8,128]{2,1,0:T(8,128)S(1)} %copy.49, f32[8,128,8]{1,2,0:T(8,128)S(1)} %copy.46), kind=kOutput, calls=%fused_computation.37 | convolution fusion | flops 1612709888 | bytes 12648448 | tf_op jit(solution)/shard_map/triangular_solve/dot.1 | solution.py:20
  718.2 5.3 bitcast_subtract_fusion
  723.5 9.6 %fusion.35 = f32[8,8,128,128]{3,2,1,0:T(8,128)} fusion(f32[8,8,128,128]{3,2,1,0:T(8,128)S(1)} %fusion.29, f32[8,128,8,128]{3,2,1,0:T(8,128)S(1)} %copy-done, f32[8,128,8]{1,2,0:T(8,128)S(1)} %copy.46), kind=kOutput, calls=%fused_computation.41 | convolution fusion | flops 1611661312 | bytes 12615680 | tf_op jit(solution)/shard_map/nhjd,nhje->nhde/dot_general | solution.py:60
  733.1 9.8 %fusion.42 = f32[8,8,128,128]{3,2,1,0:T(8,128)} fusion(f32[8,8,128,128]{3,2,1,0:T(8,128)S(1)} %fusion.31, f32[8,128,8,128]{3,2,1,0:T(8,128)S(1)} %copy-done, f32[8,128,8]{1,2,0:T(8,128)S(1)} %copy.46, f32[128,128]{1,0:T(8,128)S(1)} %get-tuple-element.158), kind=kOutput, calls=%fused_computation.53 | convolution fusion | flops 1612709888 | bytes 12681216 | tf_op jit(solution)/shard_map/nhjd,nhje->nhde/dot_general | solution.py:57
  743.0 66.1 %while.28 = (s32[]{:T(128)}, f32[8,128,128]{2,1,0:T(8,128)S(1)}, f32[8,128,128]{2,1,0:T(8,128)S(1)}, f32[8,8,64,128]{3,2,0,1:T(8,128)}, f32[8,8,64,128]{3,2,0,1:...) while((s32[]{:T(128)}, f32[8,128,128]{2,1,0:T(8,128)S(1)}, ...), condition=%wide.region_3.5_spmd.clone, body=%wide.region_2.4_spmd.clone.sunk | while | flops 604438528 | bytes 8130168 | solution.py:72
  743.0 2.3 fusion.109
  745.4 1.8 convolution_add_fusion.4
  747.3 2.3 fusion.110
  749.5 1.7 fusion.108
  751.3 2.3 fusion.109
  753.6 1.8 convolution_add_fusion.4
  755.5 2.3 fusion.110
  757.8 1.7 fusion.108
  759.6 2.3 fusion.109
  761.9 1.8 convolution_add_fusion.4
  763.8 2.3 fusion.110
  766.1 1.7 fusion.108
  767.9 2.3 fusion.109
  770.2 1.8 convolution_add_fusion.4
  772.1 2.3 fusion.110
  774.4 1.7 fusion.108
  776.1 2.3 fusion.109
  778.5 1.8 convolution_add_fusion.4
  780.4 2.3 fusion.110
  782.6 1.7 fusion.108
  784.4 2.3 fusion.109
  786.7 1.8 convolution_add_fusion.4
  788.6 2.3 fusion.110
  790.9 1.7 fusion.108
  792.7 2.3 fusion.109
  795.0 1.8 convolution_add_fusion.4
  796.9 2.3 fusion.110
  799.1 1.7 fusion.108
  800.9 2.3 fusion.109
  803.2 1.8 convolution_add_fusion.4
  805.1 2.3 fusion.110
  807.4 1.7 fusion.108
  809.1 29.6 %while.29 = (s32[]{:T(128)}, f32[8,128,128]{2,1,0:T(8,128)S(1)}, f32[8,128,128]{2,1,0:T(8,128)S(1)}, f32[8,128,128]{2,1,0:T(8,128)S(1)}, s32[]{:T(128)}, /*index=5*/s32[]{:T(128)}) while((s32[]{:T(128)}, f32[8,128,128]{2,1,0:T(8,128)S(1)}, f32[8,128,128]{2,1,0:T(8,128)S(1)}, f32[8,128,128]{2,1,0:T(8,128)S(1)}, s32[]{:T(128)}, ...), condition=%wide.region_5.7_spmd.clone, body=%wide.region_4.6_spmd.clone.sunk | while | flops 201850880 | bytes 3670135 | solution.py:80
  809.8 3.5 collective-permute-start
  813.3 6.4 collective-permute-done
  820.4 3.5 collective-permute-start
  823.9 5.5 collective-permute-done
  829.5 0.6 fusion.113
  830.1 3.5 collective-permute-start
  833.6 4.8 collective-permute-done
  838.7 4.5 multiply_reduce_fusion
  843.3 2.5 copy.61
  846.5 10.7 %convolution_convert_fusion = bf16[512,4096]{1,0:T(8,128)(2,1)} fusion(bf16[1024,4096]{1,0:T(8,128)(2,1)} %all-gather.2.cloned.1.call-done, f32[64,8,8,128]{3,2,1,0:T(8,128)S(1)} %bitcast.138, f32[64,8,8,128]{3,2,1,0:T(8,128)} %bitcast.139, f32[1024]{0:T(1024)S(1)} %copy-done.6), kind=kOutput, calls=%fused_computation.33 | convolution fusion | flops 4298637312 | bytes 16781312 | tf_op jit(solution)/shard_map/dot_general | solution.py:89
  857.2 45.8 %reduce-scatter.2.cloned.1.call-done = bf16[512,1024]{1,0:T(8,128)(2,1)} async-done(((bf16[512,4096]{1,0:T(8,128)(2,1)}), bf16[512,1024]{1,0:T(8,128)(2,1)}) %reduce-scatter.2.cloned.1.call-update) | async-done | bytes 1048592 | tf_op jit(solution)/shard_map/reduce_scatter | solution.py:92
  (61 shorter events, 4.7 us)
Async XLA Ops:
  6.5 3.8 copy-start.4
  6.5 5.4 copy-start.3
  6.5 839.3 %all-gather.2.cloned.1.call-start = ((), (), s32[]{:S(2)}) async-start(), calls=%async_computation.1 | async-start | bytes 10485760 | tf_op jit(solution)/shard_map/all_gather | solution.py:90
  7.3 895.7 %reduce-scatter.2.cloned.1.call-start = ((), (), s32[]{:S(2)}) async-start(), calls=%async_computation.2 | async-start | bytes 5242880 | tf_op jit(solution)/shard_map/reduce_scatter | solution.py:92
  24.1 4.1 copy-start.5
  684.5 10.8 %copy-start.1 = (f32[8,8,1,128,128]{3,4,2,1,0:T(8,128)S(1)}, f32[8,8,1,128,128]{3,4,2,1,0:T(8,128)}, u32[]{:S(2)}) copy-start(f32[8,8,1,128,128]{3,4,2,1,0:T(8,128)} %custom-call.6) | copy-start | bytes 12582916
  684.5 10.8 %copy-start.2 = (f32[8,128,8,128]{3,2,1,0:T(8,128)S(1)}, f32[8,128,8,128]{3,2,1,0:T(8,128)}, u32[]{:S(2)}) copy-start(f32[8,128,8,128]{3,2,1,0:T(8,128)} %reshape.102) | copy-start | bytes 12582916
  703.2 5.4 copy-start
  809.8 9.9 %collective-permute-start = (bf16[8,128,128]{2,1,0:T(8,128)(2,1)S(1)}, bf16[8,128,128]{2,1,0:T(8,128)(2,1)S(1)}, u32[]{:S(2)}, u32[]{:S(2)}) collective-permute-start(bf16[8,128,128]{2,1,0:T(8,128)(2,1)S(1)} %fusion.113), channel_id=1, source_target_pairs={{0,4},{4,8},{8,12},{1,5},{5,9},{9,13},{2,6},{6,10},{10,14},{3,7},{... | collective-permute-start | bytes 786440 | tf_op jit(solution)/shard_map/while/body/eval_jaxpr/ppermute | solution.py:12
  820.4 9.0 collective-permute-start
  830.1 8.3 collective-permute-start
  843.2 3.3 copy-start.6
Sparse Core Ops, SparseCore 0:
  8.9 148.9 all-gather.1
  857.3 45.5 reduce-scatter.1
where the time goes:
time: 922 us; the launch traced here: 910 us
  other arithmetic  642 us (70%)
  matrix products  156 us (17%)
  waiting for transfers between devices  63.2 us (7%)
  local copies, waits for them, and re-layouts  23.4 us (3%)
  between operations  14 us (2%)
  starting transfers between devices  10.5 us (1%)
    another operation x3, other arithmetic, lower_solve(): lax.linalg.triangular_solve(lower_tri, right_side, left_side=True, lower=...  630 us
    reduce_scatter x1, waiting for transfers between devices, per_device(): lax.psum_scatter(partial_value.astype(jnp.bfloat16), 'head', scatter_dime...  45.8 us
    dot_general x8, matrix products, advance(): jnp.einsum('htd,hde->hte', query_now, memory, precision=highest)  18.6 us
  transfers between devices with their start and end apart: 5, of which 4 were waited for; matrix products, arithmetic and copies ran while one was open for 89% of the time, Pallas kernels for 0%

commit v1 on v0

v1 whole, which is shorter than its diff:
```python
import functools

import jax
import jax.numpy as jnp
from jax import lax
from jax.experimental import pallas as pl
from jax.experimental.pallas import tpu as pltpu
from jax.sharding import PartitionSpec as P

DK = 128
REFL = 2
TINY = 1e-06
CHUNK = 128
BASE = 8
F32 = jnp.float32
BF16 = jnp.bfloat16


def shifted(value, axis, steps):
    count = lax.axis_size(axis)
    return lax.ppermute(value, axis, [(source, source + steps) for source in range(count - steps)])


def mxu(left, right):
    return jnp.dot(left, right, preferred_element_type=F32)


def mxu_nt(left, right):
    return lax.dot_general(left, right, (((1,), (1,)), ((), ())), preferred_element_type=F32)


def split(value):
    high = value.astype(BF16)
    return high, (value - high.astype(F32)).astype(BF16)


def mxu3(left, right):
    (left_high, left_low), (right_high, right_low) = left, right
    wide = jnp.concatenate([left_high, left_high], axis=1)
    tall = jnp.concatenate([right_high, right_low], axis=0)
    return mxu(wide, tall) + mxu(left_low, right_high)


def unit_lower_inverse(lower):
    size = lower.shape[0]
    lane = lax.broadcasted_iota(jnp.int32, (BASE, size), 1)
    sub = lax.broadcasted_iota(jnp.int32, (BASE, size), 0)
    block_of = lane // BASE
    compact = jnp.zeros((BASE, size), F32)
    for block in range(size // BASE):
        rows = lower[block * BASE : (block + 1) * BASE, :]
        compact = jnp.where(block_of == block, rows, compact)
    inverse = jnp.where(lane % BASE == sub, 1.0, 0.0).astype(F32)
    for step in range(BASE - 1):
        factor = jnp.take_along_axis(compact, block_of * BASE + step, axis=1)
        inverse = inverse - factor * inverse[step : step + 1, :]
    rows = [jnp.where(block_of == block, inverse, 0.0) for block in range(size // BASE)]
    width = BASE
    while width < size:
        pairs = size // (2 * width)
        per = width // BASE
        whole = jnp.concatenate(rows, axis=0)
        halves = split(whole)
        lane_w = lax.broadcasted_iota(jnp.int32, (width, size), 1) // width
        picked = jnp.concatenate(
            [
                jnp.where(lane_w == 2 * p, lower[(2 * p + 1) * width : (2 * p + 2) * width, :], 0.0)
                for p in range(pairs)
            ],
            axis=0,
        )
        inner = mxu3(split(picked), halves)
        empty = jnp.zeros((width, size), F32)
        spread = jnp.concatenate(
            [x for p in range(pairs) for x in (empty, inner[p * width : (p + 1) * width, :])], axis=0
        )
        below = jnp.concatenate(
            [rows[(2 * p + 1) * per + i] for p in range(pairs) for i in range(per)], axis=0
        )
        joined = below - mxu3(split(below), split(spread))
        for p in range(pairs):
            for i in range(per):
                at = (p * per + i) * BASE
                rows[(2 * p + 1) * per + i] = joined[at : at + BASE, :]
        width *= 2
    return split(jnp.concatenate(rows, axis=0))


def chunk_kernel(group, q_ref, k_ref, v_ref, b_ref, o_ref, e_ref, s_ref, p_ref, state):
    chunk = pl.program_id(1)
    tokens = CHUNK // REFL

    @pl.when(chunk == 0)
    def _():
        lane = lax.broadcasted_iota(jnp.int32, (DK, 2 * DK), 1)
        sub = lax.broadcasted_iota(jnp.int32, (DK, 2 * DK), 0)
        start = jnp.where(lane == sub + DK, 1.0, 0.0).astype(F32)
        for head in range(group):
            state[head] = start

    below = lax.broadcasted_iota(jnp.int32, (CHUNK, CHUNK), 0) > lax.broadcasted_iota(
        jnp.int32, (CHUNK, CHUNK), 1
    )
    reach = REFL * lax.broadcasted_iota(jnp.int32, (tokens, CHUNK), 0) + (
        REFL - 1
    ) >= lax.broadcasted_iota(jnp.int32, (tokens, CHUNK), 1)
    for head in range(group):
        cols = slice(head * DK, (head + 1) * DK)
        k = k_ref[:, cols]
        q = q_ref[:, cols]
        kf = k.astype(F32)
        qf = q.astype(F32)
        k_scale = lax.rsqrt(jnp.sum(kf * kf, axis=-1, keepdims=True) + TINY)
        q_scale = lax.rsqrt(jnp.sum(qf * qf, axis=-1, keepdims=True) + TINY)
        rate = b_ref[0, :, head : head + 1] * k_scale
        rate2 = rate * k_scale
        kq = jnp.concatenate([k, q], axis=0)
        gram = mxu_nt(kq, k)
        inv_high, inv_low = unit_lower_inverse(jnp.where(below, rate2 * gram[:CHUNK], 0.0))
        scores = jnp.where(reach, gram[CHUNK:], 0.0).astype(BF16)
        now = state[head]
        seen = mxu(jnp.concatenate([kq, kq], axis=1), jnp.concatenate(split(now), axis=0))
        scaled = rate2 * seen[:CHUNK]
        right = jnp.concatenate(
            [rate * v_ref[:, cols].astype(F32) - scaled[:, :DK], -scaled[:, DK:]], axis=1
        )
        delta = mxu3((inv_high, inv_low), split(right))
        delta_high, delta_low = split(delta)
        k_t = kf.T.astype(BF16)
        state[head] = now + mxu(
            jnp.concatenate([k_t, k_t], axis=1), jnp.concatenate([delta_high, delta_low], axis=0)
        )
        out = q_scale * (seen[CHUNK:] + mxu(scores, delta_high))
        o_ref[:, cols] = out[:, :DK]
        e_ref[:, cols] = out[:, DK:].astype(BF16)

    @pl.when(chunk == pl.num_programs(1) - 1)
    def _():
        for head in range(group):
            s_ref[head] = state[head, :, :DK]
            p_ref[head] = state[head, :, DK:].astype(BF16)


def local_pass(queries, keys, values, beta, group):
    tokens, width = queries.shape
    heads = width // DK
    tile = CHUNK // REFL
    refl = pl.BlockSpec((CHUNK, group * DK), lambda g, c: (c, g))
    token = pl.BlockSpec((tile, group * DK), lambda g, c: (c, g))
    per_head = pl.BlockSpec((group, DK, DK), lambda g, c: (g, 0, 0))
    return pl.pallas_call(
        functools.partial(chunk_kernel, group),
        grid=(heads // group, tokens // tile),
        in_specs=[
            token,
            refl,
            refl,
            pl.BlockSpec((1, CHUNK, group), lambda g, c: (g, c, 0)),
        ],
        out_specs=[token, token, per_head, per_head],
        out_shape=[
            jax.ShapeDtypeStruct((tokens, width), F32),
            jax.ShapeDtypeStruct((tokens, width), BF16),
            jax.ShapeDtypeStruct((heads, DK, DK), F32),
            jax.ShapeDtypeStruct((heads, DK, DK), BF16),
        ],
        scratch_shapes=[pltpu.VMEM((group, DK, 2 * DK), F32)],
        compiler_params=pltpu.CompilerParams(vmem_limit_bytes=32 * 1024 * 1024),
        name="local_pass",
    )(queries, keys, values, beta)


def norm_kernel(o_ref, e_ref, s_ref, g_ref, out_ref):
    for head in range(s_ref.shape[0]):
        cols = slice(head * DK, (head + 1) * DK)
        readout = o_ref[:, cols] + mxu(e_ref[:, cols], s_ref[head])
        mean = jnp.mean(readout * readout, axis=-1, keepdims=True)
        out_ref[:, cols] = (readout * lax.rsqrt(mean + TINY) * g_ref[:, cols]).astype(BF16)


def normed_rows(local, exposure, incoming, gain):
    tokens, width = local.shape
    tile = 128
    rows = pl.BlockSpec((tile, width), lambda i: (i, 0))
    return pl.pallas_call(
        norm_kernel,
        grid=(tokens // tile,),
        in_specs=[
            rows,
            rows,
            pl.BlockSpec(incoming.shape, lambda i: (0, 0, 0)),
            pl.BlockSpec((1, width), lambda i: (0, 0)),
        ],
        out_specs=rows,
        out_shape=jax.ShapeDtypeStruct((tokens, width), BF16),
        name="normed_rows",
    )(local, exposure, incoming, gain.reshape(1, width))


def per_device(queries, keys, values, beta, gain, w_out):
    tokens, width = queries.shape
    heads = width // DK
    group = min(4, heads)
    keys2 = keys.reshape(tokens * REFL, width)
    values2 = values.reshape(tokens * REFL, width)
    beta_rows = (
        beta.transpose(2, 0, 1)
        .reshape(tokens * REFL, heads // group, group)
        .transpose(1, 0, 2)
    )
    w_full = lax.all_gather(w_out, "ctx", axis=1, tiled=True)
    local, exposure, state_end, total_end = local_pass(queries, keys2, values2, beta_rows, group)

    incoming = jnp.zeros((heads, DK, DK), BF16)
    for _ in range(lax.axis_size("ctx") - 1):
        outgoing = (
            jnp.einsum("hde,hef->hdf", total_end, incoming, preferred_element_type=F32) + state_end
        )
        incoming = shifted(outgoing.astype(BF16), "ctx", 1)
    flat = normed_rows(local, exposure, incoming, gain)
    partial_value = jnp.dot(flat, w_full, preferred_element_type=F32)
    return lax.psum_scatter(
        partial_value.astype(BF16), "head", scatter_dimension=1, tiled=True
    )


def solution(mesh):
    in_specs = (
        P(("groups", "ctx"), "head"),
        P(("groups", "ctx"), None, "head"),
        P(("groups", "ctx"), None, "head"),
        P(None, "head", ("groups", "ctx")),
        P("head"),
        P("head", "ctx"),
    )
    out_specs = P(("groups", "ctx"), "head")
    return jax.shard_map(
        per_device, mesh=mesh, in_specs=in_specs, out_specs=out_specs, check_vma=False
    )
```

time: 922 us -> 246 us (0.27); the launches traced: 910 us -> 244 us
  other arithmetic: 642 us -> 0 us
  matrix products: 156 us -> 10.8 us
  Pallas kernels: 0 us -> 109 us
  waiting for transfers between devices: 63.2 us -> 82.2 us
  local copies, waits for them, and re-layouts: 23.4 us -> 12.9 us
    another operation x5 -> x0, other arithmetic: 630 us -> none  [the longest x3 630 us: lower_solve(): lax.linalg.triangular_solve(lower_tri, right_side, left_side=True, lower=...]
    dot_general x43 -> x4, matrix products: 139 us -> 10.8 us  [the longest x1 10.2 us: per_device(): partial_value = jnp.dot(flat, w_full, preferred_element_type=F32)]
    pallas_call x0 -> x2, Pallas kernels: none -> 109 us  [the longest x1 105 us: local_pass(): pl.pallas_call(functools.partial(chunk_kernel, group), grid=(heads // gro...]
    ppermute x3, waiting for transfers between devices: 16.7 us -> 37.1 us  [shifted(): lax.ppermute(value, axis, [(source, source + steps) for source in range(c...]
    another operation x2 -> x0, matrix products: 17.5 us -> none  [lower_solve(): lax.linalg.triangular_solve(lower_tri, right_side, left_side=True, lower=...]
  transfers between devices with their start and end apart: 5 -> 5, of which waited for: 4 -> 4; matrix products, arithmetic and copies ran while one was open for 89% -> 4% of each run, Pallas kernels for 0% -> 45%
where the time goes in v1:
time: 246 us; the launch traced here: 244 us
  Pallas kernels  109 us (44%)
  waiting for transfers between devices  82.2 us (33%)
  starting transfers between devices  14.8 us (6%)
  between operations  13.5 us (5%)
  local copies, waits for them, and re-layouts  12.9 us (5%)
  matrix products  10.8 us (4%)
    pallas_call x1, Pallas kernels, local_pass(): pl.pallas_call(functools.partial(chunk_kernel, group), grid=(heads // gro...  105 us
    reduce_scatter x1, waiting for transfers between devices, per_device(): lax.psum_scatter(partial_value.astype(BF16), 'head', scatter_dimension=1,...  44.4 us
    ppermute x3, waiting for transfers between devices, shifted(): lax.ppermute(value, axis, [(source, source + steps) for source in range(c...  37.1 us
    ppermute x3, starting transfers between devices, shifted(): lax.ppermute(value, axis, [(source, source + steps) for source in range(c...  14.8 us
    dot_general x1, matrix products, per_device(): partial_value = jnp.dot(flat, w_full, preferred_element_type=F32)  10.2 us
  transfers between devices with their start and end apart: 5, of which 4 were waited for; matrix products, arithmetic and copies ran while one was open for 4% of the time, Pallas kernels for 45%

profile of v1, /device:TPU:16, one launch (start us, length us, event | category | flops | bytes accessed | tf_op | source)
XLA Modules:
  0.0 243.7 jit_solution(4129370908933148375)
XLA Ops:
  6.5 0.0 all-gather.2.cloned.1.call-start
  6.5 0.7 all-gather.2.cloned.1.call-update
  7.3 0.0 reduce-scatter.2.cloned.1.call-start
  7.3 1.0 copy.7
  8.3 0.9 reshape.14
  9.2 0.1 copy.10
  9.3 2.8 %reshape.12.k_ref = bf16[1024,1024]{1,0:T(8,128)(2,1)S(1)} reshape(bf16[512,2,1024]{2,1,0:T(2,128)(2,1)} %param.7) | data formatting | bytes 4194304 | tf_op jit(solution)/shard_map/reshape | solution.py:204
  12.1 4.2 %reshape.13.v_ref = bf16[1024,1024]{1,0:T(8,128)(2,1)} reshape(bf16[512,2,1024]{2,1,0:T(2,128)(2,1)} %param.8) | data formatting | bytes 4194304 | tf_op jit(solution)/shard_map/reshape | solution.py:205
  16.2 0.0 copy-start
  16.2 1.9 copy-done
  18.1 0.0 copy-start.3
  18.1 1.4 copy-done.3
  19.5 104.9 %local_pass.1 = (f32[512,1024]{1,0:T(8,128)S(1)}, bf16[512,1024]{1,0:T(8,128)(2,1)S(1)}, f32[8,128,128]{2,1,0:T(8,128)S(1)}, bf16[8,128,128]{2,1,0:T(8,128)(2,1)S(1)}) custom-call(bf16[512,1024]{1,0:T(8,128)(2,1)S(1)} %copy-done.3, bf16[1024,1024]{1,0:T(8,128)(2,1)S(1)} %reshape.12.k_ref, bf16[1024,1024]{1,0:T(8,128)(2,1)S(1)} %copy-done, ...), custom_call_target="tpu_custom_call" | custom-call | tf_op jit(solution)/shard_map/local_pass/pallas_call | solution.py:151
  124.4 0.0 copy-start.1
  124.4 0.0 copy-start.2
  124.4 0.2 fusion
  124.6 3.5 %collective-permute-start = (bf16[8,128,128]{2,1,0:T(8,128)(2,1)S(1)}, bf16[8,128,128]{2,1,0:T(8,128)(2,1)S(1)}, u32[]{:S(2)}, u32[]{:S(2)}) collective-permute-start(bf16[8,128,128]{2,1,0:T(8,128)(2,1)S(1)} %fusion), channel_id=1, source_target_pairs={{0,4},{4,8},{8,12},{1,5},{5,9},{9,13},{2,6},{6,10},{10,14},{3,7},{... | collective-permute-start | bytes 786440 | tf_op jit(solution)/shard_map/ppermute | solution.py:21
  128.1 18.4 %collective-permute-done = bf16[8,128,128]{2,1,0:T(8,128)(2,1)S(1)} collective-permute-done((bf16[8,128,128]{2,1,0:T(8,128)(2,1)S(1)}, bf16[8,128,128]{2,1,0:T(8,128)(2,1)S(1)}, u32[]{:S(2)}, u32[]{:S(2)}) %collective-permute-start) | collective-permute-done | bytes 262176 | tf_op jit(solution)/shard_map/ppermute | solution.py:21
  146.5 0.2 fusion.1
  146.8 8.0 %collective-permute-start.1 = (bf16[8,128,128]{2,1,0:T(8,128)(2,1)S(1)}, bf16[8,128,128]{2,1,0:T(8,128)(2,1)S(1)}, u32[]{:S(2)}, u32[]{:S(2)}) collective-permute-start(bf16[8,128,128]{2,1,0:T(8,128)(2,1)S(1)} %fusion.1), channel_id=1, source_target_pairs={{0,4},{4,8},{8,12},{1,5},{5,9},{9,13},{2,6},{6,10},{10,14},{3,7},{... | collective-permute-start | bytes 786440 | tf_op jit(solution)/shard_map/ppermute | solution.py:21
  154.8 12.6 %collective-permute-done.1 = bf16[8,128,128]{2,1,0:T(8,128)(2,1)S(1)} collective-permute-done((bf16[8,128,128]{2,1,0:T(8,128)(2,1)S(1)}, bf16[8,128,128]{2,1,0:T(8,128)(2,1)S(1)}, u32[]{:S(2)}, u32[]{:S(2)}) %collective-permute-start.1) | collective-permute-done | bytes 262176 | tf_op jit(solution)/shard_map/ppermute | solution.py:21
  167.4 0.2 fusion.2
  167.7 0.0 copy-done.1
  167.7 3.3 %collective-permute-start.2 = (bf16[8,128,128]{2,1,0:T(8,128)(2,1)S(1)}, bf16[8,128,128]{2,1,0:T(8,128)(2,1)S(1)}, u32[]{:S(2)}, u32[]{:S(2)}) collective-permute-start(bf16[8,128,128]{2,1,0:T(8,128)(2,1)S(1)} %fusion.2), channel_id=1, source_target_pairs={{0,4},{4,8},{8,12},{1,5},{5,9},{9,13},{2,6},{6,10},{10,14},{3,7},{... | collective-permute-start | bytes 786440 | tf_op jit(solution)/shard_map/ppermute | solution.py:21
  170.9 0.0 copy-done.2
  171.0 6.1 %collective-permute-done.2.s_ref = bf16[8,128,128]{2,1,0:T(8,128)(2,1)S(1)} collective-permute-done((bf16[8,128,128]{2,1,0:T(8,128)(2,1)S(1)}, bf16[8,128,128]{2,1,0:T(8,128)(2,1)S(1)}, u32[]{:S(2)}, u32[]{:S(2)}) %collective-permute-start.2) | collective-permute-done | bytes 262176 | tf_op jit(solution)/shard_map/ppermute | solution.py:21
  177.0 0.0 copy-start.4
  177.0 0.7 copy-done.4
  177.7 4.5 %normed_rows.1 = bf16[512,1024]{1,0:T(8,128)(2,1)} custom-call(f32[512,1024]{1,0:T(8,128)} %copy-done.1, bf16[512,1024]{1,0:T(8,128)(2,1)} %copy-done.2, bf16[8,128,128]{2,1,0:T(8,128)(2,1)} %copy-done.4, f32[1,1024]{1,0:T(1,128)} %bitcast.14), custom_call_target="tpu_custom_call" | custom-call | tf_op jit(solution)/shard_map/normed_rows/pallas_call | solution.py:185
  182.2 0.0 all-gather.2.cloned.1.call-done
  182.2 10.2 %convolution_convert_fusion = bf16[512,4096]{1,0:T(8,128)(2,1)} fusion(bf16[512,1024]{1,0:T(8,128)(2,1)} %normed_rows.1, bf16[1024,4096]{1,0:T(8,128)(2,1)} %all-gather.2.cloned.1.call-done), kind=kOutput, calls=%fused_computation | convolution fusion | flops 4297064448 | bytes 13631488 | tf_op jit(solution)/shard_map/dot_general | solution.py:221
  192.4 0.0 reduce-scatter.2.cloned.1.call-update
  192.4 44.4 %reduce-scatter.2.cloned.1.call-done = bf16[512,1024]{1,0:T(8,128)(2,1)} async-done(((bf16[512,4096]{1,0:T(8,128)(2,1)}), bf16[512,1024]{1,0:T(8,128)(2,1)}) %reduce-scatter.2.cloned.1.call-update) | async-done | bytes 1048592 | tf_op jit(solution)/shard_map/reduce_scatter | solution.py:222
Async XLA Ops:
  6.5 175.7 %all-gather.2.cloned.1.call-start = ((), (), s32[]{:S(2)}) async-start(), calls=%async_computation.1 | async-start | bytes 10485760 | tf_op jit(solution)/shard_map/all_gather | solution.py:211
  7.3 229.6 %reduce-scatter.2.cloned.1.call-start = ((), (), s32[]{:S(2)}) async-start(), calls=%async_computation.2 | async-start | bytes 5242880 | tf_op jit(solution)/shard_map/reduce_scatter | solution.py:222
  16.2 1.9 copy-start
  18.1 1.4 copy-start.3
  124.4 43.3 %copy-start.1 = (f32[512,1024]{1,0:T(8,128)}, f32[512,1024]{1,0:T(8,128)S(1)}, u32[]{:S(2)}) copy-start(f32[512,1024]{1,0:T(8,128)S(1)} %get-tuple-element.9.o_ref) | copy-start | bytes 6291460
  124.4 46.5 %copy-start.2 = (bf16[512,1024]{1,0:T(8,128)(2,1)}, bf16[512,1024]{1,0:T(8,128)(2,1)S(1)}, u32[]{:S(2)}) copy-start(bf16[512,1024]{1,0:T(8,128)(2,1)S(1)} %get-tuple-element.10.e_ref) | copy-start | bytes 3145732
  124.6 21.9 %collective-permute-start = (bf16[8,128,128]{2,1,0:T(8,128)(2,1)S(1)}, bf16[8,128,128]{2,1,0:T(8,128)(2,1)S(1)}, u32[]{:S(2)}, u32[]{:S(2)}) collective-permute-start(bf16[8,128,128]{2,1,0:T(8,128)(2,1)S(1)} %fusion), channel_id=1, source_target_pairs={{0,4},{4,8},{8,12},{1,5},{5,9},{9,13},{2,6},{6,10},{10,14},{3,7},{... | collective-permute-start | bytes 786440 | tf_op jit(solution)/shard_map/ppermute | solution.py:21
  146.8 20.7 %collective-permute-start.1 = (bf16[8,128,128]{2,1,0:T(8,128)(2,1)S(1)}, bf16[8,128,128]{2,1,0:T(8,128)(2,1)S(1)}, u32[]{:S(2)}, u32[]{:S(2)}) collective-permute-start(bf16[8,128,128]{2,1,0:T(8,128)(2,1)S(1)} %fusion.1), channel_id=1, source_target_pairs={{0,4},{4,8},{8,12},{1,5},{5,9},{9,13},{2,6},{6,10},{10,14},{3,7},{... | collective-permute-start | bytes 786440 | tf_op jit(solution)/shard_map/ppermute | solution.py:21
  167.7 9.3 %collective-permute-start.2 = (bf16[8,128,128]{2,1,0:T(8,128)(2,1)S(1)}, bf16[8,128,128]{2,1,0:T(8,128)(2,1)S(1)}, u32[]{:S(2)}, u32[]{:S(2)}) collective-permute-start(bf16[8,128,128]{2,1,0:T(8,128)(2,1)S(1)} %fusion.2), channel_id=1, source_target_pairs={{0,4},{4,8},{8,12},{1,5},{5,9},{9,13},{2,6},{6,10},{10,14},{3,7},{... | collective-permute-start | bytes 786440 | tf_op jit(solution)/shard_map/ppermute | solution.py:21
  177.0 0.7 copy-start.4
Sparse Core Ops, SparseCore 0:
  8.9 154.1 all-gather.1
  192.6 44.2 reduce-scatter.1

commit v2 on v1

--- a/solution.py
+++ b/solution.py
@@ -41,49 +41,79 @@
     return mxu(wide, tall) + mxu(left_low, right_high)
 
 
-def unit_lower_inverse(lower):
-    size = lower.shape[0]
+def each(function, *columns):
+    return [function(*row) for row in zip(*columns)]
+
+
+def unit_lower_inverse(lowers):
+    size = lowers[0].shape[0]
     lane = lax.broadcasted_iota(jnp.int32, (BASE, size), 1)
     sub = lax.broadcasted_iota(jnp.int32, (BASE, size), 0)
     block_of = lane // BASE
-    compact = jnp.zeros((BASE, size), F32)
-    for block in range(size // BASE):
-        rows = lower[block * BASE : (block + 1) * BASE, :]
-        compact = jnp.where(block_of == block, rows, compact)
-    inverse = jnp.where(lane % BASE == sub, 1.0, 0.0).astype(F32)
+    blocks = range(size // BASE)
+
+    def compacted(lower):
+        compact = jnp.zeros((BASE, size), F32)
+        for block in blocks:
+            rows = lower[block * BASE : (block + 1) * BASE, :]
+            compact = jnp.where(block_of == block, rows, compact)
+        return compact
+
+    compacts = each(compacted, lowers)
+    inverses = [jnp.where(lane % BASE == sub, 1.0, 0.0).astype(F32) for _ in lowers]
     for step in range(BASE - 1):
-        factor = jnp.take_along_axis(compact, block_of * BASE + step, axis=1)
-        inverse = inverse - factor * inverse[step : step + 1, :]
-    rows = [jnp.where(block_of == block, inverse, 0.0) for block in range(size // BASE)]
+        factors = each(
+            lambda compact: jnp.take_along_axis(compact, block_of * BASE + step, axis=1), compacts
+        )
+        inverses = each(lambda inv, factor: inv - factor * inv[step : step + 1, :], inverses, factors)
+    rows_of = each(lambda inv: [jnp.where(block_of == block, inv, 0.0) for block in blocks], inverses)
     width = BASE
     while width < size:
-        pairs = size // (2 * width)
+        pairs = range(size // (2 * width))
         per = width // BASE
-        whole = jnp.concatenate(rows, axis=0)
-        halves = split(whole)
         lane_w = lax.broadcasted_iota(jnp.int32, (width, size), 1) // width
-        picked = jnp.concatenate(
-            [
-                jnp.where(lane_w == 2 * p, lower[(2 * p + 1) * width : (2 * p + 2) * width, :], 0.0)
-                for p in range(pairs)
-            ],
-            axis=0,
-        )
-        inner = mxu3(split(picked), halves)
         empty = jnp.zeros((width, size), F32)
-        spread = jnp.concatenate(
-            [x for p in range(pairs) for x in (empty, inner[p * width : (p + 1) * width, :])], axis=0
-        )
-        below = jnp.concatenate(
-            [rows[(2 * p + 1) * per + i] for p in range(pairs) for i in range(per)], axis=0
-        )
-        joined = below - mxu3(split(below), split(spread))
-        for p in range(pairs):
-            for i in range(per):
-                at = (p * per + i) * BASE
-                rows[(2 * p + 1) * per + i] = joined[at : at + BASE, :]
+
+        def picked(lower):
+            return jnp.concatenate(
+                [
+                    jnp.where(
+                        lane_w == 2 * p, lower[(2 * p + 1) * width : (2 * p + 2) * width, :], 0.0
+                    )
+                    for p in pairs
+                ],
+                axis=0,
+            )
+
+        def spread(inner):
+            return jnp.concatenate(
+                [x for p in pairs for x in (empty, inner[p * width : (p + 1) * width, :])], axis=0
+            )
+
+        halves = each(lambda rows: split(jnp.concatenate(rows, axis=0)), rows_of)
+        picks = each(lambda lower: split(picked(lower)), lowers)
+        inners = each(mxu3, picks, halves)
+        belows = each(
+            lambda rows: jnp.concatenate(
+                [rows[(2 * p + 1) * per + i] for p in pairs for i in range(per)], axis=0
+            ),
+            rows_of,
+        )
+        joins = each(
+            lambda below, inner: below - mxu3(split(below), split(spread(inner))), belows, inners
+        )
+
+        def placed(rows, joined):
+            rows = list(rows)
+            for p in pairs:
+                for i in range(per):
+                    at = (p * per + i) * BASE
+                    rows[(2 * p + 1) * per + i] = joined[at : at + BASE, :]
+            return rows
+
+        rows_of = each(placed, rows_of, joins)
         width *= 2
-    return split(jnp.concatenate(rows, axis=0))
+    return each(lambda rows: split(jnp.concatenate(rows, axis=0)), rows_of)
 
 
 def chunk_kernel(group, q_ref, k_ref, v_ref, b_ref, o_ref, e_ref, s_ref, p_ref, state):
@@ -104,41 +134,63 @@
     reach = REFL * lax.broadcasted_iota(jnp.int32, (tokens, CHUNK), 0) + (
         REFL - 1
     ) >= lax.broadcasted_iota(jnp.int32, (tokens, CHUNK), 1)
-    for head in range(group):
-        cols = slice(head * DK, (head + 1) * DK)
-        k = k_ref[:, cols]
-        q = q_ref[:, cols]
-        kf = k.astype(F32)
-        qf = q.astype(F32)
-        k_scale = lax.rsqrt(jnp.sum(kf * kf, axis=-1, keepdims=True) + TINY)
-        q_scale = lax.rsqrt(jnp.sum(qf * qf, axis=-1, keepdims=True) + TINY)
-        rate = b_ref[0, :, head : head + 1] * k_scale
-        rate2 = rate * k_scale
-        kq = jnp.concatenate([k, q], axis=0)
-        gram = mxu_nt(kq, k)
-        inv_high, inv_low = unit_lower_inverse(jnp.where(below, rate2 * gram[:CHUNK], 0.0))
-        scores = jnp.where(reach, gram[CHUNK:], 0.0).astype(BF16)
-        now = state[head]
-        seen = mxu(jnp.concatenate([kq, kq], axis=1), jnp.concatenate(split(now), axis=0))
-        scaled = rate2 * seen[:CHUNK]
-        right = jnp.concatenate(
-            [rate * v_ref[:, cols].astype(F32) - scaled[:, :DK], -scaled[:, DK:]], axis=1
-        )
-        delta = mxu3((inv_high, inv_low), split(right))
-        delta_high, delta_low = split(delta)
-        k_t = kf.T.astype(BF16)
-        state[head] = now + mxu(
-            jnp.concatenate([k_t, k_t], axis=1), jnp.concatenate([delta_high, delta_low], axis=0)
-        )
-        out = q_scale * (seen[CHUNK:] + mxu(scores, delta_high))
-        o_ref[:, cols] = out[:, :DK]
-        e_ref[:, cols] = out[:, DK:].astype(BF16)
+    heads = range(group)
+    cols = [slice(head * DK, (head + 1) * DK) for head in heads]
+    ks = [k_ref[:, c] for c in cols]
+    qs = [q_ref[:, c] for c in cols]
+
+    def inverse_norm(rows):
+        rows = rows.astype(F32)
+        return lax.rsqrt(jnp.sum(rows * rows, axis=-1, keepdims=True) + TINY)
+
+    k_scales = each(inverse_norm, ks)
+    q_scales = each(inverse_norm, qs)
+    rates = [b_ref[0, :, head : head + 1] * k_scales[head] for head in heads]
+    rates2 = each(lambda rate, scale: rate * scale, rates, k_scales)
+    kqs = each(lambda k, q: jnp.concatenate([k, q], axis=0), ks, qs)
+    grams = each(mxu_nt, kqs, ks)
+    lowers = each(lambda rate, gram: jnp.where(below, rate * gram[:CHUNK], 0.0), rates2, grams)
+    scores = each(lambda gram: jnp.where(reach, gram[CHUNK:], 0.0).astype(BF16), grams)
+    inverses = unit_lower_inverse(lowers)
+    nows = [state[head] for head in heads]
+    seens = each(
+        lambda kq, now: mxu(
+            jnp.concatenate([kq, kq], axis=1), jnp.concatenate(split(now), axis=0)
+        ),
+        kqs,
+        nows,
+    )
+
+    def right_side(head):
+        scaled = rates2[head] * seens[head][:CHUNK]
+        own = rates[head] * v_ref[:, cols[head]].astype(F32)
+        return split(jnp.concatenate([own - scaled[:, :DK], -scaled[:, DK:]], axis=1))
+
+    rights = each(right_side, heads)
+    deltas = each(lambda inverse, right: split(mxu3(inverse, right)), inverses, rights)
+
+    def stepped(k, now, delta):
+        k_t = k.astype(F32).T.astype(BF16)
+        return now + mxu(jnp.concatenate([k_t, k_t], axis=1), jnp.concatenate(delta, axis=0))
+
+    nexts = each(stepped, ks, nows, deltas)
+    outs = each(
+        lambda scale, seen, score, delta: scale * (seen[CHUNK:] + mxu(score, delta[0])),
+        q_scales,
+        seens,
+        scores,
+        deltas,
+    )
+    for head in heads:
+        state[head] = nexts[head]
+        o_ref[:, cols[head]] = outs[head][:, :DK]
+        e_ref[:, cols[head]] = outs[head][:, DK:].astype(BF16)
 
     @pl.when(chunk == pl.num_programs(1) - 1)
     def _():
-        for head in range(group):
-            s_ref[head] = state[head, :, :DK]
-            p_ref[head] = state[head, :, DK:].astype(BF16)
+        for head in heads:
+            s_ref[head] = nexts[head][:, :DK]
+            p_ref[head] = nexts[head][:, DK:].astype(BF16)
 
 
 def local_pass(queries, keys, values, beta, group):
@@ -200,7 +252,7 @@
 def per_device(queries, keys, values, beta, gain, w_out):
     tokens, width = queries.shape
     heads = width // DK
-    group = min(4, heads)
+    group = min(8, heads)
     keys2 = keys.reshape(tokens * REFL, width)
     values2 = values.reshape(tokens * REFL, width)
     beta_rows = (

time: 246 us -> 238 us (0.967)
  Pallas kernels: 109 us -> 28.2 us
  waiting for transfers between devices: 82.2 us -> 162 us
  starting transfers between devices: 14.8 us -> 10.5 us
    pallas_call x1, Pallas kernels: 105 us -> 23.6 us  [local_pass(): pl.pallas_call(functools.partial(chunk_kernel, group), grid=(heads // gro...]
    all_gather x1, waiting for transfers between devices: 0.01 us -> 49.3 us  [per_device(): w_full = lax.all_gather(w_out, 'ctx', axis=1, tiled=True)]
    ppermute x3, waiting for transfers between devices: 37.1 us -> 61.2 us  [shifted(): lax.ppermute(value, axis, [(source, source + steps) for source in range(c...]
    reduce_scatter x1, waiting for transfers between devices: 44.4 us -> 51.1 us  [per_device(): lax.psum_scatter(partial_value.astype(BF16), 'head', scatter_dimension=1,...]
    ppermute x3, starting transfers between devices: 14.8 us -> 10.4 us  [shifted(): lax.ppermute(value, axis, [(source, source + steps) for source in range(c...]
  transfers between devices with their start and end apart: 5 -> 5, of which waited for: 4 -> 5; matrix products, arithmetic and copies ran while one was open for 4% -> 3% of each run, Pallas kernels for 45% -> 12%
where the time goes in v2:
time: 238 us; the launch traced here: 236 us
  waiting for transfers between devices  162 us (68%)
  Pallas kernels  28.2 us (12%)
  between operations  13.5 us (6%)
  matrix products  10.9 us (5%)
  local copies, waits for them, and re-layouts  10.8 us (5%)
  starting transfers between devices  10.5 us (4%)
    ppermute x3, waiting for transfers between devices, shifted(): lax.ppermute(value, axis, [(source, source + steps) for source in range(c...  61.2 us
    reduce_scatter x1, waiting for transfers between devices, per_device(): lax.psum_scatter(partial_value.astype(BF16), 'head', scatter_dimension=1,...  51.1 us
    all_gather x1, waiting for transfers between devices, per_device(): w_full = lax.all_gather(w_out, 'ctx', axis=1, tiled=True)  49.3 us
    pallas_call x1, Pallas kernels, local_pass(): pl.pallas_call(functools.partial(chunk_kernel, group), grid=(heads // gro...  23.6 us
    ppermute x3, starting transfers between devices, shifted(): lax.ppermute(value, axis, [(source, source + steps) for source in range(c...  10.4 us
    dot_general x1, matrix products, per_device(): partial_value = jnp.dot(flat, w_full, preferred_element_type=F32)  10.2 us
  transfers between devices with their start and end apart: 5, of which 5 were waited for; matrix products, arithmetic and copies ran while one was open for 3% of the time, Pallas kernels for 12%

profile of v2, /device:TPU:16, one launch (start us, length us, event | category | flops | bytes accessed | tf_op | source)
XLA Modules:
  0.0 236.1 jit_solution(11672847755229051316)
XLA Ops:
  6.5 0.0 all-gather.2.cloned.1.call-start
  6.5 0.7 all-gather.2.cloned.1.call-update
  7.3 0.0 copy-start.5
  7.3 0.0 reduce-scatter.2.cloned.1.call-start
  7.3 2.8 %reshape.10.v_ref = bf16[1024,1024]{1,0:T(8,128)(2,1)S(1)} reshape(bf16[512,2,1024]{2,1,0:T(2,128)(2,1)} %param.8) | data formatting | bytes 4194304 | tf_op jit(solution)/shard_map/reshape | solution.py:257
  10.1 4.2 %reshape.9.k_ref = bf16[1024,1024]{1,0:T(8,128)(2,1)} reshape(bf16[512,2,1024]{2,1,0:T(2,128)(2,1)} %param.7) | data formatting | bytes 4194304 | tf_op jit(solution)/shard_map/reshape | solution.py:256
  14.2 0.0 copy-done.5
  14.2 0.2 copy.7
  14.5 0.0 copy-start
  14.5 1.6 copy-done
  16.1 0.0 copy-start.3
  16.1 1.4 copy-done.3
  17.4 23.6 %local_pass.1 = (f32[512,1024]{1,0:T(8,128)S(1)}, bf16[512,1024]{1,0:T(8,128)(2,1)S(1)}, f32[8,128,128]{2,1,0:T(8,128)S(1)}, bf16[8,128,128]{2,1,0:T(8,128)(2,1)S(1)}) custom-call(bf16[512,1024]{1,0:T(8,128)(2,1)S(1)} %copy-done.3, bf16[1024,1024]{1,0:T(8,128)(2,1)S(1)} %copy-done, bf16[1024,1024]{1,0:T(8,128)(2,1)S(1)} %reshape.10.v_ref, ...), custom_call_target="tpu_custom_call" | custom-call | tf_op jit(solution)/shard_map/local_pass/pallas_call | solution.py:203
  41.1 0.0 copy-start.1
  41.1 0.0 copy-start.2
  41.1 0.2 fusion
  41.3 3.5 %collective-permute-start = (bf16[8,128,128]{2,1,0:T(8,128)(2,1)S(1)}, bf16[8,128,128]{2,1,0:T(8,128)(2,1)S(1)}, u32[]{:S(2)}, u32[]{:S(2)}) collective-permute-start(bf16[8,128,128]{2,1,0:T(8,128)(2,1)S(1)} %fusion), channel_id=1, source_target_pairs={{0,4},{4,8},{8,12},{1,5},{5,9},{9,13},{2,6},{6,10},{10,14},{3,7},{... | collective-permute-start | bytes 786440 | tf_op jit(solution)/shard_map/ppermute | solution.py:21
  44.8 20.0 %collective-permute-done = bf16[8,128,128]{2,1,0:T(8,128)(2,1)S(1)} collective-permute-done((bf16[8,128,128]{2,1,0:T(8,128)(2,1)S(1)}, bf16[8,128,128]{2,1,0:T(8,128)(2,1)S(1)}, u32[]{:S(2)}, u32[]{:S(2)}) %collective-permute-start) | collective-permute-done | bytes 262176 | tf_op jit(solution)/shard_map/ppermute | solution.py:21
  64.8 0.2 fusion.1
  65.1 1.9 collective-permute-start.1
  67.0 20.9 %collective-permute-done.1 = bf16[8,128,128]{2,1,0:T(8,128)(2,1)S(1)} collective-permute-done((bf16[8,128,128]{2,1,0:T(8,128)(2,1)S(1)}, bf16[8,128,128]{2,1,0:T(8,128)(2,1)S(1)}, u32[]{:S(2)}, u32[]{:S(2)}) %collective-permute-start.1) | collective-permute-done | bytes 262176 | tf_op jit(solution)/shard_map/ppermute | solution.py:21
  87.9 0.2 fusion.2
  88.2 0.0 copy-done.1
  88.2 5.0 %collective-permute-start.2 = (bf16[8,128,128]{2,1,0:T(8,128)(2,1)S(1)}, bf16[8,128,128]{2,1,0:T(8,128)(2,1)S(1)}, u32[]{:S(2)}, u32[]{:S(2)}) collective-permute-start(bf16[8,128,128]{2,1,0:T(8,128)(2,1)S(1)} %fusion.2), channel_id=1, source_target_pairs={{0,4},{4,8},{8,12},{1,5},{5,9},{9,13},{2,6},{6,10},{10,14},{3,7},{... | collective-permute-start | bytes 786440 | tf_op jit(solution)/shard_map/ppermute | solution.py:21
  93.2 0.0 copy-done.2
  93.2 20.2 %collective-permute-done.2.s_ref = bf16[8,128,128]{2,1,0:T(8,128)(2,1)S(1)} collective-permute-done((bf16[8,128,128]{2,1,0:T(8,128)(2,1)S(1)}, bf16[8,128,128]{2,1,0:T(8,128)(2,1)S(1)}, u32[]{:S(2)}, u32[]{:S(2)}) %collective-permute-start.2) | collective-permute-done | bytes 262176 | tf_op jit(solution)/shard_map/ppermute | solution.py:21
  113.4 0.0 copy-start.4
  113.4 0.7 copy-done.4
  114.1 4.5 %normed_rows.1 = bf16[512,1024]{1,0:T(8,128)(2,1)} custom-call(f32[512,1024]{1,0:T(8,128)} %copy-done.1, bf16[512,1024]{1,0:T(8,128)(2,1)} %copy-done.2, bf16[8,128,128]{2,1,0:T(8,128)(2,1)} %copy-done.4, f32[1,1024]{1,0:T(1,128)} %bitcast.12), custom_call_target="tpu_custom_call" | custom-call | tf_op jit(solution)/shard_map/normed_rows/pallas_call | solution.py:237
  118.7 49.3 %all-gather.2.cloned.1.call-done = bf16[1024,4096]{1,0:T(8,128)(2,1)} async-done(((bf16[1024,1024]{1,0:T(8,128)(2,1)}), bf16[1024,4096]{1,0:T(8,128)(2,1)}) %all-gather.2.cloned.1.call-update) | async-done | bytes 8388624 | tf_op jit(solution)/shard_map/all_gather | solution.py:263
  167.9 10.2 %convolution_convert_fusion = bf16[512,4096]{1,0:T(8,128)(2,1)} fusion(bf16[512,1024]{1,0:T(8,128)(2,1)} %normed_rows.1, bf16[1024,4096]{1,0:T(8,128)(2,1)} %all-gather.2.cloned.1.call-done), kind=kOutput, calls=%fused_computation | convolution fusion | flops 4297064448 | bytes 13631488 | tf_op jit(solution)/shard_map/dot_general | solution.py:273
  178.1 0.0 reduce-scatter.2.cloned.1.call-update
  178.2 51.1 %reduce-scatter.2.cloned.1.call-done = bf16[512,1024]{1,0:T(8,128)(2,1)} async-done(((bf16[512,4096]{1,0:T(8,128)(2,1)}), bf16[512,1024]{1,0:T(8,128)(2,1)}) %reduce-scatter.2.cloned.1.call-update) | async-done | bytes 1048592 | tf_op jit(solution)/shard_map/reduce_scatter | solution.py:274
Async XLA Ops:
  6.5 161.4 %all-gather.2.cloned.1.call-start = ((), (), s32[]{:S(2)}) async-start(), calls=%async_computation.1 | async-start | bytes 10485760 | tf_op jit(solution)/shard_map/all_gather | solution.py:263
  7.3 7.0 %copy-start.5 = (f32[2,8,512]{2,1,0:T(8,128)S(1)}, f32[2,8,512]{2,1,0:T(8,128)}, u32[]{:S(2)}) copy-start(f32[2,8,512]{2,1,0:T(8,128)} %param.9) | copy-start | bytes 98308
  7.3 222.0 %reduce-scatter.2.cloned.1.call-start = ((), (), s32[]{:S(2)}) async-start(), calls=%async_computation.2 | async-start | bytes 5242880 | tf_op jit(solution)/shard_map/reduce_scatter | solution.py:274
  14.5 1.6 copy-start
  16.1 1.4 copy-start.3
  41.1 47.1 %copy-start.1 = (f32[512,1024]{1,0:T(8,128)}, f32[512,1024]{1,0:T(8,128)S(1)}, u32[]{:S(2)}) copy-start(f32[512,1024]{1,0:T(8,128)S(1)} %get-tuple-element.9.o_ref) | copy-start | bytes 6291460
  41.1 52.1 %copy-start.2 = (bf16[512,1024]{1,0:T(8,128)(2,1)}, bf16[512,1024]{1,0:T(8,128)(2,1)S(1)}, u32[]{:S(2)}) copy-start(bf16[512,1024]{1,0:T(8,128)(2,1)S(1)} %get-tuple-element.10.e_ref) | copy-start | bytes 3145732
  41.3 23.5 %collective-permute-start = (bf16[8,128,128]{2,1,0:T(8,128)(2,1)S(1)}, bf16[8,128,128]{2,1,0:T(8,128)(2,1)S(1)}, u32[]{:S(2)}, u32[]{:S(2)}) collective-permute-start(bf16[8,128,128]{2,1,0:T(8,128)(2,1)S(1)} %fusion), channel_id=1, source_target_pairs={{0,4},{4,8},{8,12},{1,5},{5,9},{9,13},{2,6},{6,10},{10,14},{3,7},{... | collective-permute-start | bytes 786440 | tf_op jit(solution)/shard_map/ppermute | solution.py:21
  65.1 22.9 %collective-permute-start.1 = (bf16[8,128,128]{2,1,0:T(8,128)(2,1)S(1)}, bf16[8,128,128]{2,1,0:T(8,128)(2,1)S(1)}, u32[]{:S(2)}, u32[]{:S(2)}) collective-permute-start(bf16[8,128,128]{2,1,0:T(8,128)(2,1)S(1)} %fusion.1), channel_id=1, source_target_pairs={{0,4},{4,8},{8,12},{1,5},{5,9},{9,13},{2,6},{6,10},{10,14},{3,7},{... | collective-permute-start | bytes 786440 | tf_op jit(solution)/shard_map/ppermute | solution.py:21
  88.2 25.3 %collective-permute-start.2 = (bf16[8,128,128]{2,1,0:T(8,128)(2,1)S(1)}, bf16[8,128,128]{2,1,0:T(8,128)(2,1)S(1)}, u32[]{:S(2)}, u32[]{:S(2)}) collective-permute-start(bf16[8,128,128]{2,1,0:T(8,128)(2,1)S(1)} %fusion.2), channel_id=1, source_target_pairs={{0,4},{4,8},{8,12},{1,5},{5,9},{9,13},{2,6},{6,10},{10,14},{3,7},{... | collective-permute-start | bytes 786440 | tf_op jit(solution)/shard_map/ppermute | solution.py:21
  113.4 0.7 copy-start.4
Sparse Core Ops, SparseCore 0:
  8.9 158.9 all-gather.1
  178.3 50.9 reduce-scatter.1

commit v3 on v2

--- a/solution.py
+++ b/solution.py
@@ -14,11 +14,6 @@
 BASE = 8
 F32 = jnp.float32
 BF16 = jnp.bfloat16
-
-
-def shifted(value, axis, steps):
-    count = lax.axis_size(axis)
-    return lax.ppermute(value, axis, [(source, source + steps) for source in range(count - steps)])
 
 
 def mxu(left, right):
@@ -223,11 +218,14 @@
 
 
 def norm_kernel(o_ref, e_ref, s_ref, g_ref, out_ref):
-    for head in range(s_ref.shape[0]):
-        cols = slice(head * DK, (head + 1) * DK)
-        readout = o_ref[:, cols] + mxu(e_ref[:, cols], s_ref[head])
-        mean = jnp.mean(readout * readout, axis=-1, keepdims=True)
-        out_ref[:, cols] = (readout * lax.rsqrt(mean + TINY) * g_ref[:, cols]).astype(BF16)
+    heads = range(s_ref.shape[0])
+    cols = [slice(head * DK, (head + 1) * DK) for head in heads]
+    readouts = [o_ref[:, cols[head]] + mxu(e_ref[:, cols[head]], s_ref[head]) for head in heads]
+    scales = each(
+        lambda rows: lax.rsqrt(jnp.mean(rows * rows, axis=-1, keepdims=True) + TINY), readouts
+    )
+    for head in heads:
+        out_ref[:, cols[head]] = (readouts[head] * scales[head] * g_ref[:, cols[head]]).astype(BF16)
 
 
 def normed_rows(local, exposure, incoming, gain):
@@ -249,6 +247,70 @@
     )(local, exposure, incoming, gain.reshape(1, width))
 
 
+def project_kernel(order_ref, a_ref, w_ref, give_ref, keep_ref):
+    step = pl.program_id(0)
+    half = pl.num_programs(0) // 2
+    product = mxu(a_ref[...], w_ref[...]).astype(BF16)
+
+    @pl.when(step < half)
+    def _():
+        give_ref[...] = product
+
+    @pl.when(step >= half)
+    def _():
+        keep_ref[...] = product
+
+
+def project(order, rows, weights):
+    tokens, depth = rows.shape
+    count = order.shape[0]
+    half = count // 2
+    block = weights.shape[1] // count
+    shape = jax.ShapeDtypeStruct((tokens, half * block), BF16)
+    return pl.pallas_call(
+        project_kernel,
+        grid_spec=pltpu.PrefetchScalarGridSpec(
+            num_scalar_prefetch=1,
+            grid=(count,),
+            in_specs=[
+                pl.BlockSpec((tokens, depth), lambda i, order: (0, 0)),
+                pl.BlockSpec((depth, block), lambda i, order: (0, order[i])),
+            ],
+            out_specs=[
+                pl.BlockSpec((tokens, block), lambda i, order: (0, jnp.minimum(i, half - 1))),
+                pl.BlockSpec((tokens, block), lambda i, order: (0, jnp.maximum(i - half, 0))),
+            ],
+        ),
+        out_shape=[shape, shape],
+        compiler_params=pltpu.CompilerParams(vmem_limit_bytes=32 * 1024 * 1024),
+        name="project",
+    )(order, rows, weights)
+
+
+def halving_order(count):
+    order = [0]
+    bit = count // 2
+    while bit >= 1:
+        order = [m | bit for m in order] + order
+        bit //= 2
+    return order
+
+
+def head_sum(give, keep):
+    count = lax.axis_size("head")
+    bit = 1
+    while bit < count:
+        pairs = [(i, i ^ bit) for i in range(count)]
+        got = lax.ppermute(give, "head", pairs)
+        total = keep.astype(F32) + got.astype(F32)
+        bit *= 2
+        half = total.shape[1] // 2
+        give, keep = total[:, :half].astype(BF16), total[:, half:]
+        if bit >= count:
+            return total.astype(BF16)
+    return keep
+
+
 def per_device(queries, keys, values, beta, gain, w_out):
     tokens, width = queries.shape
     heads = width // DK
@@ -260,20 +322,36 @@
         .reshape(tokens * REFL, heads // group, group)
         .transpose(1, 0, 2)
     )
-    w_full = lax.all_gather(w_out, "ctx", axis=1, tiled=True)
+    side = lax.axis_index("groups")
+    half_cols = w_out.shape[1] // 2
+    w_half = lax.dynamic_slice_in_dim(w_out, side * half_cols, half_cols, 1)
+    w_mine = lax.all_gather(w_half, "ctx", axis=1, tiled=True)
     local, exposure, state_end, total_end = local_pass(queries, keys2, values2, beta_rows, group)
 
     incoming = jnp.zeros((heads, DK, DK), BF16)
-    for _ in range(lax.axis_size("ctx") - 1):
+    outgoing = state_end.astype(BF16)
+    for hop in range(lax.axis_size("ctx") - 1):
+        incoming = incoming + lax.ppermute(outgoing, "ctx", [(hop, hop + 1)])
         outgoing = (
             jnp.einsum("hde,hef->hdf", total_end, incoming, preferred_element_type=F32) + state_end
-        )
-        incoming = shifted(outgoing.astype(BF16), "ctx", 1)
-    flat = normed_rows(local, exposure, incoming, gain)
-    partial_value = jnp.dot(flat, w_full, preferred_element_type=F32)
-    return lax.psum_scatter(
-        partial_value.astype(BF16), "head", scatter_dimension=1, tiled=True
-    )
+        ).astype(BF16)
+    mine = normed_rows(local, exposure, incoming, gain)
+    swap = [(0, 1), (1, 0)]
+    other = lax.ppermute(mine, "groups", swap)
+    head_count = lax.axis_size("head")
+    order = lax.axis_index("head") ^ jnp.asarray(halving_order(head_count), jnp.int32)
+    mine_sum = head_sum(*project(order, mine, w_mine))
+    other_sum = head_sum(*project(order, other, w_mine))
+    back = lax.ppermute(other_sum, "groups", swap)
+    blocks = mine_sum.shape[1] // half_cols
+    mine_sum = mine_sum.reshape(tokens, blocks, 1, half_cols)
+    back = back.reshape(tokens, blocks, 1, half_cols)
+    mixed = jnp.where(
+        side == 0,
+        jnp.concatenate([mine_sum, back], axis=2),
+        jnp.concatenate([back, mine_sum], axis=2),
+    )
+    return mixed.reshape(tokens, blocks * 2 * half_cols)
 
 
 def solution(mesh):

time: 238 us -> 180 us (0.76)
  waiting for transfers between devices: 162 us -> 88.6 us
  local copies, waits for them, and re-layouts: 10.8 us -> 24.2 us
  matrix products: 10.9 us -> 0.47 us
  Pallas kernels: 28.2 us -> 36.6 us
  other arithmetic: 0 us -> 5.57 us
    reduce_scatter x1 -> x0, waiting for transfers between devices: 51.1 us -> none  [per_device(): lax.psum_scatter(partial_value.astype(BF16), 'head', scatter_dimension=1,...]
    all_gather x1, waiting for transfers between devices: 49.3 us -> 0.01 us  [per_device(): w_mine = lax.all_gather(w_half, 'ctx', axis=1, tiled=True)]
    ppermute x3 -> x9, waiting for transfers between devices: 61.2 us -> 88.6 us  [the longest x3 46.3 us: per_device(): incoming = incoming + lax.ppermute(outgoing, 'ctx', [(hop, hop + 1)])]
    dot_general x1 -> x0, matrix products: 10.2 us -> none  [per_device(): partial_value = jnp.dot(flat, w_full, preferred_element_type=F32)]
    pallas_call x0 -> x2, Pallas kernels: none -> 8.41 us  [project(): pl.pallas_call(project_kernel, grid_spec=pltpu.PrefetchScalarGridSpec(num...]
    unnamed x12 -> x24, local copies, waits for them, and re-layouts: 3.67 us -> 10.8 us
    select_n x0 -> x2, local copies, waits for them, and re-layouts: none -> 3.6 us  [per_device(): jnp.where(side == 0, jnp.concatenate([mine_sum, back], axis=2), jnp.conca...]
    ppermute x3 -> x9, starting transfers between devices: 10.4 us -> 9.15 us  [the longest x3 3.28 us: per_device(): incoming = incoming + lax.ppermute(outgoing, 'ctx', [(hop, hop + 1)])]
  transfers between devices with their start and end apart: 5 -> 10, of which waited for: 5 -> 7; matrix products, arithmetic and copies ran while one was open for 3% -> 8% of each run, Pallas kernels for 12% -> 18%
where the time goes in v3:
time: 180 us; the launch traced here: 178 us
  waiting for transfers between devices  88.6 us (49%)
  Pallas kernels  36.6 us (20%)
  local copies, waits for them, and re-layouts  24.2 us (13%)
  between operations  13.6 us (8%)
  starting transfers between devices  9.15 us (5%)
  other arithmetic  5.57 us (3%)
    ppermute x3, waiting for transfers between devices, per_device(): incoming = incoming + lax.ppermute(outgoing, 'ctx', [(hop, hop + 1)])  46.3 us
    pallas_call x1, Pallas kernels, local_pass(): pl.pallas_call(functools.partial(chunk_kernel, group), grid=(heads // gro...  23.6 us
    ppermute x1, waiting for transfers between devices, per_device(): other = lax.ppermute(mine, 'groups', swap)  22.3 us
    ppermute x4, waiting for transfers between devices, head_sum(): got = lax.ppermute(give, 'head', pairs)  18.7 us
    unnamed x24, local copies, waits for them, and re-layouts  10.8 us
    pallas_call x2, Pallas kernels, project(): pl.pallas_call(project_kernel, grid_spec=pltpu.PrefetchScalarGridSpec(num...  8.41 us
    pallas_call x1, Pallas kernels, normed_rows(): pl.pallas_call(norm_kernel, grid=(tokens // tile,), in_specs=[rows, rows,...  4.52 us
    reshape x1, local copies, waits for them, and re-layouts, per_device(): values2 = values.reshape(tokens * REFL, width)  4.19 us
  transfers between devices with their start and end apart: 10, of which 7 were waited for; matrix products, arithmetic and copies ran while one was open for 8% of the time, Pallas kernels for 18%

profile of v3, /device:TPU:16, one launch (start us, length us, event | category | flops | bytes accessed | tf_op | source)
XLA Modules:
  0.0 178.2 jit_solution(2177390505041150357)
XLA Ops:
  6.5 0.0 copy-start
  6.5 0.0 all-gather.2.cloned.1.call-start
  6.5 1.6 copy-done
  8.1 1.2 constant_dynamic-slice_fusion
  9.3 0.0 all-gather.2.cloned.1.call-update
  9.3 4.1 %reshape.33.k_ref = bf16[1024,1024]{1,0:T(8,128)(2,1)} reshape(bf16[512,2,1024]{2,1,0:T(2,128)(2,1)} %param.8) | data formatting | bytes 4194304 | tf_op jit(solution)/shard_map/reshape | solution.py:318
  13.5 0.0 copy-start.10
  13.5 4.2 %reshape.34.v_ref = bf16[1024,1024]{1,0:T(8,128)(2,1)} reshape(bf16[512,2,1024]{2,1,0:T(2,128)(2,1)} %param.9) | data formatting | bytes 4194304 | tf_op jit(solution)/shard_map/reshape | solution.py:319
  17.7 0.0 copy-done.10
  17.7 0.2 copy.9
  17.9 0.0 copy-start.2
  17.9 1.8 %copy-done.2 = bf16[1024,1024]{1,0:T(8,128)(2,1)S(1)} copy-done((bf16[1024,1024]{1,0:T(8,128)(2,1)S(1)}, bf16[1024,1024]{1,0:T(8,128)(2,1)}, u32[]{:S(2)}) %copy-start.2) | copy-done | bytes 2097176
  19.7 0.0 copy-start.3
  19.7 1.8 %copy-done.3 = bf16[1024,1024]{1,0:T(8,128)(2,1)S(1)} copy-done((bf16[1024,1024]{1,0:T(8,128)(2,1)S(1)}, bf16[1024,1024]{1,0:T(8,128)(2,1)}, u32[]{:S(2)}) %copy-start.3) | copy-done | bytes 2097176
  21.5 0.0 copy-start.7
  21.5 1.2 copy-done.7
  22.8 23.6 %local_pass.1 = (f32[512,1024]{1,0:T(8,128)S(1)}, bf16[512,1024]{1,0:T(8,128)(2,1)S(1)}, f32[8,128,128]{2,1,0:T(8,128)S(1)}, bf16[8,128,128]{2,1,0:T(8,128)(2,1)S(1)}) custom-call(bf16[512,1024]{1,0:T(8,128)(2,1)S(1)} %copy-done.7, bf16[1024,1024]{1,0:T(8,128)(2,1)S(1)} %copy-done.2, bf16[1024,1024]{1,0:T(8,128)(2,1)S(1)} %copy-done.3, ...), custom_call_target="tpu_custom_call" | custom-call | tf_op jit(solution)/shard_map/local_pass/pallas_call | solution.py:198
  46.4 0.0 copy-start.5
  46.4 0.0 copy-start.6
  46.5 0.7 collective-permute-start
  47.2 0.0 collective-permute-done
  47.2 0.2 fusion
  47.4 1.3 collective-permute-start.1
  48.7 38.9 %collective-permute-done.1 = bf16[8,128,128]{2,1,0:T(8,128)(2,1)S(1)} collective-permute-done((bf16[8,128,128]{2,1,0:T(8,128)(2,1)S(1)}, bf16[8,128,128]{2,1,0:T(8,128)(2,1)S(1)}, u32[]{:S(2)}, u32[]{:S(2)}) %collective-permute-start.1) | collective-permute-done | bytes 262176 | tf_op jit(solution)/shard_map/ppermute | solution.py:334
  87.7 0.1 add.28
  87.7 0.2 fusion.1
  88.0 0.0 copy-done.5
  88.0 0.0 copy-done.6
  88.0 1.3 collective-permute-start.2
  89.3 7.4 %collective-permute-done.2 = bf16[8,128,128]{2,1,0:T(8,128)(2,1)S(1)} collective-permute-done((bf16[8,128,128]{2,1,0:T(8,128)(2,1)S(1)}, bf16[8,128,128]{2,1,0:T(8,128)(2,1)S(1)}, u32[]{:S(2)}, u32[]{:S(2)}) %collective-permute-start.2) | collective-permute-done | bytes 262176 | tf_op jit(solution)/shard_map/ppermute | solution.py:334
  96.7 0.8 add.30.s_ref
  97.5 0.0 copy-start.11
  97.5 4.5 %normed_rows.1.a_ref = bf16[512,1024]{1,0:T(8,128)(2,1)} custom-call(f32[512,1024]{1,0:T(8,128)} %copy-done.5, bf16[512,1024]{1,0:T(8,128)(2,1)} %copy-done.6, bf16[8,128,128]{2,1,0:T(8,128)(2,1)} %add.30.s_ref, f32[1,1024]{1,0:T(1,128)} %bitcast.15), custom_call_target="tpu_custom_call" | custom-call | tf_op jit(solution)/shard_map/normed_rows/pallas_call | solution.py:235
  102.0 1.4 collective-permute-start.5
  103.4 0.0 copy-done.11
  103.4 22.3 %collective-permute-done.5.a_ref = bf16[512,1024]{1,0:T(8,128)(2,1)S(1)} collective-permute-done((bf16[512,1024]{1,0:T(8,128)(2,1)}, bf16[512,1024]{1,0:T(8,128)(2,1)S(1)}, u32[]{:S(2)}, u32[]{:S(2)}) %collective-permute-start.5) | collective-permute-done | bytes 1048608 | tf_op jit(solution)/shard_map/ppermute | solution.py:340
  125.7 0.0 all-gather.2.cloned.1.call-done.w_ref
  125.7 0.0 copy-start.1
  125.7 2.2 %copy-done.1 = bf16[1024,2048]{1,0:T(8,128)(2,1)S(1)} copy-done((bf16[1024,2048]{1,0:T(8,128)(2,1)S(1)}, bf16[1024,2048]{1,0:T(8,128)(2,1)}, u32[]{:S(2)}) %copy-start.1) | copy-done | bytes 4194328
  127.9 4.2 %project.3 = (bf16[512,1024]{1,0:T(8,128)(2,1)S(1)}, bf16[512,1024]{1,0:T(8,128)(2,1)S(1)}) custom-call(s32[4]{0:T(128)S(1)} %broadcast_xor_fusion.order_ref, bf16[512,1024]{1,0:T(8,128)(2,1)S(1)} %collective-permute-done.5.a_ref, bf16[1024,2048]{1,0:T(8,128)(2,1)S(1)} %copy-done.1), custom_call_target="tpu_custom_call" | custom-call | tf_op jit(solution)/shard_map/project/pallas_call | solution.py:270
  132.1 0.1 collective-permute-start.6
  132.2 0.0 copy-done.4
  132.2 4.2 %project.2 = (bf16[512,1024]{1,0:T(8,128)(2,1)S(1)}, bf16[512,1024]{1,0:T(8,128)(2,1)S(1)}) custom-call(s32[4]{0:T(128)S(1)} %broadcast_xor_fusion.order_ref, bf16[512,1024]{1,0:T(8,128)(2,1)S(1)} %copy-done.4, bf16[1024,2048]{1,0:T(8,128)(2,1)S(1)} %copy-done.1), custom_call_target="tpu_custom_call" | custom-call | tf_op jit(solution)/shard_map/project/pallas_call | solution.py:270
  136.4 0.6 collective-permute-start.3
  137.0 0.0 collective-permute-done.6
  137.0 0.4 convert_add_fusion
  137.4 0.1 slice.32
  137.5 1.3 collective-permute-start.7
  138.7 0.5 collective-permute-done.3
  139.3 0.4 convert_add_fusion.1
  139.6 0.0 copy-start.8
  139.7 1.3 copy-done.8
  141.0 0.1 slice.33
  141.1 1.3 collective-permute-start.4
  142.4 9.9 %collective-permute-done.7 = bf16[512,512]{1,0:T(8,128)(2,1)S(1)} collective-permute-done((bf16[512,512]{1,0:T(8,128)(2,1)S(1)}, bf16[512,512]{1,0:T(8,128)(2,1)S(1)}, u32[]{:S(2)}, u32[]{:S(2)}) %collective-permute-start.7) | collective-permute-done | bytes 524320 | tf_op jit(solution)/shard_map/ppermute | solution.py:304
  152.3 1.0 fusion.2
  153.3 1.2 collective-permute-start.8
  154.5 8.2 %collective-permute-done.4 = bf16[512,512]{1,0:T(8,128)(2,1)} collective-permute-done((bf16[512,512]{1,0:T(8,128)(2,1)S(1)}, bf16[512,512]{1,0:T(8,128)(2,1)}, u32[]{:S(2)}, u32[]{:S(2)}) %collective-permute-start.4) | collective-permute-done | bytes 524320 | tf_op jit(solution)/shard_map/ppermute | solution.py:304
  162.7 1.6 fusion.4
  164.3 1.3 collective-permute-done.8
  165.6 0.8 copy-done.9
  166.4 1.4 maximum_select_fusion
  167.7 1.3 copy.10
  169.1 2.3 %copy.11 = bf16[512,1024]{1,0:T(8,128)(2,1)} copy(bf16[512,1024]{0,1:T(8,128)(2,1)} %bitcast.12) | data formatting | bytes 2097152 | tf_op jit(solution)/shard_map/jit(_where)/select_n | solution.py:349
  (4 shorter events, 0.0 us)
Async XLA Ops:
  6.5 1.6 copy-start
  6.5 119.2 %all-gather.2.cloned.1.call-start = ((), (), s32[]{:S(2)}) async-start(), calls=%async_computation | async-start | bytes 5242880 | tf_op jit(solution)/shard_map/all_gather | solution.py:328
  13.5 4.2 %copy-start.10 = (f32[2,8,512]{2,1,0:T(8,128)S(1)}, f32[2,8,512]{2,1,0:T(8,128)}, u32[]{:S(2)}) copy-start(f32[2,8,512]{2,1,0:T(8,128)} %param.10) | copy-start | bytes 98308
  17.9 1.8 %copy-start.2 = (bf16[1024,1024]{1,0:T(8,128)(2,1)S(1)}, bf16[1024,1024]{1,0:T(8,128)(2,1)}, u32[]{:S(2)}) copy-start(bf16[1024,1024]{1,0:T(8,128)(2,1)} %reshape.33.k_ref) | copy-start | bytes 6291460
  19.7 1.8 %copy-start.3 = (bf16[1024,1024]{1,0:T(8,128)(2,1)S(1)}, bf16[1024,1024]{1,0:T(8,128)(2,1)}, u32[]{:S(2)}) copy-start(bf16[1024,1024]{1,0:T(8,128)(2,1)} %reshape.34.v_ref) | copy-start | bytes 6291460
  21.5 1.2 copy-start.7
  46.4 41.6 %copy-start.5 = (f32[512,1024]{1,0:T(8,128)}, f32[512,1024]{1,0:T(8,128)S(1)}, u32[]{:S(2)}) copy-start(f32[512,1024]{1,0:T(8,128)S(1)} %get-tuple-element.13.o_ref) | copy-start | bytes 6291460
  46.4 41.6 %copy-start.6 = (bf16[512,1024]{1,0:T(8,128)(2,1)}, bf16[512,1024]{1,0:T(8,128)(2,1)S(1)}, u32[]{:S(2)}) copy-start(bf16[512,1024]{1,0:T(8,128)(2,1)S(1)} %get-tuple-element.14.e_ref) | copy-start | bytes 3145732
  46.5 0.7 collective-permute-start
  47.4 40.2 %collective-permute-start.1 = (bf16[8,128,128]{2,1,0:T(8,128)(2,1)S(1)}, bf16[8,128,128]{2,1,0:T(8,128)(2,1)S(1)}, u32[]{:S(2)}, u32[]{:S(2)}) collective-permute-start(bf16[8,128,128]{2,1,0:T(8,128)(2,1)S(1)} %fusion), channel_id=1, source_target_pairs={{4,8},{5,9},{6,10},{7,11},{20,24},{21,25},{22,26},{23,27}} | collective-permute-start | bytes 786440 | tf_op jit(solution)/shard_map/ppermute | solution.py:334
  88.0 8.7 %collective-permute-start.2 = (bf16[8,128,128]{2,1,0:T(8,128)(2,1)S(1)}, bf16[8,128,128]{2,1,0:T(8,128)(2,1)S(1)}, u32[]{:S(2)}, u32[]{:S(2)}) collective-permute-start(bf16[8,128,128]{2,1,0:T(8,128)(2,1)S(1)} %fusion.1), channel_id=1, source_target_pairs={{8,12},{9,13},{10,14},{11,15},{24,28},{25,29},{26,30},{27,31}} | collective-permute-start | bytes 786440 | tf_op jit(solution)/shard_map/ppermute | solution.py:334
  97.5 6.0 %copy-start.11 = (s32[4]{0:T(128)S(1)}, s32[4]{0:T(128)}, u32[]{:S(2)}) copy-start(s32[4]{0:T(128)} %constant.18.clone) | copy-start | bytes 52
  102.0 23.7 %collective-permute-start.5 = (bf16[512,1024]{1,0:T(8,128)(2,1)}, bf16[512,1024]{1,0:T(8,128)(2,1)S(1)}, u32[]{:S(2)}, u32[]{:S(2)}) collective-permute-start(bf16[512,1024]{1,0:T(8,128)(2,1)} %normed_rows.1.a_ref), channel_id=1, source_target_pairs={{0,16},{16,0},{1,17},{17,1},{2,18},{18,2},{3,19},{19,3},{4,20},{20... | collective-permute-start | bytes 3145736 | tf_op jit(solution)/shard_map/ppermute | solution.py:340
  125.7 2.2 %copy-start.1 = (bf16[1024,2048]{1,0:T(8,128)(2,1)S(1)}, bf16[1024,2048]{1,0:T(8,128)(2,1)}, u32[]{:S(2)}) copy-start(bf16[1024,2048]{1,0:T(8,128)(2,1)} %all-gather.2.cloned.1.call-done.w_ref) | copy-start | bytes 12582916
  127.9 4.3 %copy-start.4 = (bf16[512,1024]{1,0:T(8,128)(2,1)S(1)}, bf16[512,1024]{1,0:T(8,128)(2,1)}, u32[]{:S(2)}) copy-start(bf16[512,1024]{1,0:T(8,128)(2,1)} %normed_rows.1.a_ref) | copy-start | bytes 3145732
  132.1 4.9 %collective-permute-start.6 = (bf16[512,1024]{1,0:T(8,128)(2,1)S(1)}, bf16[512,1024]{1,0:T(8,128)(2,1)S(1)}, u32[]{:S(2)}, u32[]{:S(2)}) collective-permute-start(bf16[512,1024]{1,0:T(8,128)(2,1)S(1)} %get-tuple-element.20), channel_id=1, source_target_pairs={{0,1},{1,0},{2,3},{3,2},{4,5},{5,4},{6,7},{7,6},{8,9},{9,8},{10,11... | collective-permute-start | bytes 3145736 | tf_op jit(solution)/shard_map/ppermute | solution.py:304
  136.4 2.8 %collective-permute-start.3 = (bf16[512,1024]{1,0:T(8,128)(2,1)S(1)}, bf16[512,1024]{1,0:T(8,128)(2,1)S(1)}, u32[]{:S(2)}, u32[]{:S(2)}) collective-permute-start(bf16[512,1024]{1,0:T(8,128)(2,1)S(1)} %get-tuple-element.18), channel_id=1, source_target_pairs={{0,1},{1,0},{2,3},{3,2},{4,5},{5,4},{6,7},{7,6},{8,9},{9,8},{10,11... | collective-permute-start | bytes 3145736 | tf_op jit(solution)/shard_map/ppermute | solution.py:304
  137.5 14.8 %collective-permute-start.7 = (bf16[512,512]{1,0:T(8,128)(2,1)S(1)}, bf16[512,512]{1,0:T(8,128)(2,1)S(1)}, u32[]{:S(2)}, u32[]{:S(2)}) collective-permute-start(bf16[512,512]{1,0:T(8,128)(2,1)S(1)} %slice.32), channel_id=1, source_target_pairs={{0,2},{1,3},{2,0},{3,1},{4,6},{5,7},{6,4},{7,5},{8,10},{9,11},{10,... | collective-permute-start | bytes 1572872 | tf_op jit(solution)/shard_map/ppermute | solution.py:304
  139.6 1.3 copy-start.8
  141.1 21.7 %collective-permute-start.4 = (bf16[512,512]{1,0:T(8,128)(2,1)S(1)}, bf16[512,512]{1,0:T(8,128)(2,1)}, u32[]{:S(2)}, u32[]{:S(2)}) collective-permute-start(bf16[512,512]{1,0:T(8,128)(2,1)S(1)} %slice.33), channel_id=1, source_target_pairs={{0,2},{1,3},{2,0},{3,1},{4,6},{5,7},{6,4},{7,5},{8,10},{9,11},{10,... | collective-permute-start | bytes 1572872 | tf_op jit(solution)/shard_map/ppermute | solution.py:304
  153.3 12.3 %collective-permute-start.8 = (bf16[512,512]{1,0:T(8,128)(2,1)}, bf16[512,512]{1,0:T(8,128)(2,1)S(1)}, u32[]{:S(2)}, u32[]{:S(2)}) collective-permute-start(bf16[512,512]{1,0:T(8,128)(2,1)} %fusion.2), channel_id=1, source_target_pairs={{0,16},{16,0},{1,17},{17,1},{2,18},{18,2},{3,19},{19,3},{4,20},{20... | collective-permute-start | bytes 1572872 | tf_op jit(solution)/shard_map/ppermute | solution.py:345
  165.6 0.8 copy-start.9
Sparse Core Ops, SparseCore 0:
  9.4 81.9 all-gather.1

commit v4 on v3

--- a/solution.py
+++ b/solution.py
@@ -131,7 +131,7 @@
     ) >= lax.broadcasted_iota(jnp.int32, (tokens, CHUNK), 1)
     heads = range(group)
     cols = [slice(head * DK, (head + 1) * DK) for head in heads]
-    ks = [k_ref[:, c] for c in cols]
+    ks = [k_ref[:, :, c].reshape(CHUNK, DK) for c in cols]
     qs = [q_ref[:, c] for c in cols]
 
     def inverse_norm(rows):
@@ -158,7 +158,7 @@
 
     def right_side(head):
         scaled = rates2[head] * seens[head][:CHUNK]
-        own = rates[head] * v_ref[:, cols[head]].astype(F32)
+        own = rates[head] * v_ref[:, :, cols[head]].reshape(CHUNK, DK).astype(F32)
         return split(jnp.concatenate([own - scaled[:, :DK], -scaled[:, DK:]], axis=1))
 
     rights = each(right_side, heads)
@@ -192,7 +192,7 @@
     tokens, width = queries.shape
     heads = width // DK
     tile = CHUNK // REFL
-    refl = pl.BlockSpec((CHUNK, group * DK), lambda g, c: (c, g))
+    refl = pl.BlockSpec((tile, REFL, group * DK), lambda g, c: (c, 0, g))
     token = pl.BlockSpec((tile, group * DK), lambda g, c: (c, g))
     per_head = pl.BlockSpec((group, DK, DK), lambda g, c: (g, 0, 0))
     return pl.pallas_call(
@@ -213,6 +213,9 @@
         ],
         scratch_shapes=[pltpu.VMEM((group, DK, 2 * DK), F32)],
         compiler_params=pltpu.CompilerParams(vmem_limit_bytes=32 * 1024 * 1024),
+        cost_estimate=pl.CostEstimate(
+            flops=80 * tokens * width * DK, bytes_accessed=16 * tokens * width, transcendentals=0
+        ),
         name="local_pass",
     )(queries, keys, values, beta)
 
@@ -247,44 +250,47 @@
     )(local, exposure, incoming, gain.reshape(1, width))
 
 
-def project_kernel(order_ref, a_ref, w_ref, give_ref, keep_ref):
-    step = pl.program_id(0)
-    half = pl.num_programs(0) // 2
-    product = mxu(a_ref[...], w_ref[...]).astype(BF16)
-
-    @pl.when(step < half)
-    def _():
-        give_ref[...] = product
-
-    @pl.when(step >= half)
-    def _():
-        keep_ref[...] = product
-
-
-def project(order, rows, weights):
+def project_kernel(place_ref, a_ref, *refs):
+    weights, (give_ref, keep_ref) = refs[:-2], refs[-2:]
+    half, block = len(weights) // 2, weights[0].shape[1]
+    for slot, weight in enumerate(weights):
+        product = mxu(a_ref[...], weight[...]).astype(BF16)
+        place = place_ref[slot]
+
+        @pl.when(place < half)
+        def _():
+            give_ref[:, pl.ds(pl.multiple_of(place * block, block), block)] = product
+
+        @pl.when(place >= half)
+        def _():
+            keep_ref[:, pl.ds(pl.multiple_of((place - half) * block, block), block)] = product
+
+
+def project(places, rows, weights):
     tokens, depth = rows.shape
-    count = order.shape[0]
-    half = count // 2
-    block = weights.shape[1] // count
-    shape = jax.ShapeDtypeStruct((tokens, half * block), BF16)
+    count = len(weights)
+    block = weights[0].shape[1]
+    tile = 128
+    half = pl.BlockSpec((tile, count // 2 * block), lambda i, places: (i, 0))
+    shape = jax.ShapeDtypeStruct((tokens, count // 2 * block), BF16)
     return pl.pallas_call(
         project_kernel,
         grid_spec=pltpu.PrefetchScalarGridSpec(
             num_scalar_prefetch=1,
-            grid=(count,),
-            in_specs=[
-                pl.BlockSpec((tokens, depth), lambda i, order: (0, 0)),
-                pl.BlockSpec((depth, block), lambda i, order: (0, order[i])),
-            ],
-            out_specs=[
-                pl.BlockSpec((tokens, block), lambda i, order: (0, jnp.minimum(i, half - 1))),
-                pl.BlockSpec((tokens, block), lambda i, order: (0, jnp.maximum(i - half, 0))),
-            ],
+            grid=(tokens // tile,),
+            in_specs=[pl.BlockSpec((tile, depth), lambda i, places: (i, 0))]
+            + [pl.BlockSpec((depth, block), lambda i, places: (0, 0))] * count,
+            out_specs=[half, half],
         ),
         out_shape=[shape, shape],
         compiler_params=pltpu.CompilerParams(vmem_limit_bytes=32 * 1024 * 1024),
+        cost_estimate=pl.CostEstimate(
+            flops=2 * tokens * depth * block * count,
+            bytes_accessed=2 * (tokens * depth + (tokens + depth) * block * count),
+            transcendentals=0,
+        ),
         name="project",
-    )(order, rows, weights)
+    )(places, rows, *weights)
 
 
 def halving_order(count):
@@ -311,12 +317,30 @@
     return keep
 
 
+def ring_slots(own, axis):
+    count = lax.axis_size(axis)
+    up, down = {0: own}, {0: own}
+    for step in range(1, count):
+        up[step] = lax.ppermute(up[step - 1], axis, [(i, i + 1) for i in range(step - 1, count - 1)])
+        down[step] = lax.ppermute(
+            down[step - 1], axis, [(i + 1, i) for i in range(count - step)]
+        )
+    return [own] + [up[k] + down[count - k] for k in range(1, count)]
+
+
+def slots_by_head(w_half):
+    ctx, head = lax.axis_size("ctx"), lax.axis_size("head")
+    if ctx == head:
+        slots = ring_slots(w_half, "ctx")
+        return slots, lax.rem(lax.axis_index("ctx") + ctx - jnp.arange(ctx), ctx)
+    whole = lax.all_gather(w_half, "ctx", axis=1, tiled=True)
+    return jnp.split(whole, head, axis=1), jnp.arange(head)
+
+
 def per_device(queries, keys, values, beta, gain, w_out):
     tokens, width = queries.shape
     heads = width // DK
     group = min(8, heads)
-    keys2 = keys.reshape(tokens * REFL, width)
-    values2 = values.reshape(tokens * REFL, width)
     beta_rows = (
         beta.transpose(2, 0, 1)
         .reshape(tokens * REFL, heads // group, group)
@@ -325,8 +349,8 @@
     side = lax.axis_index("groups")
     half_cols = w_out.shape[1] // 2
     w_half = lax.dynamic_slice_in_dim(w_out, side * half_cols, half_cols, 1)
-    w_mine = lax.all_gather(w_half, "ctx", axis=1, tiled=True)
-    local, exposure, state_end, total_end = local_pass(queries, keys2, values2, beta_rows, group)
+    weights, targets = slots_by_head(w_half)
+    local, exposure, state_end, total_end = local_pass(queries, keys, values, beta_rows, group)
 
     incoming = jnp.zeros((heads, DK, DK), BF16)
     outgoing = state_end.astype(BF16)
@@ -338,10 +362,11 @@
     mine = normed_rows(local, exposure, incoming, gain)
     swap = [(0, 1), (1, 0)]
     other = lax.ppermute(mine, "groups", swap)
-    head_count = lax.axis_size("head")
-    order = lax.axis_index("head") ^ jnp.asarray(halving_order(head_count), jnp.int32)
-    mine_sum = head_sum(*project(order, mine, w_mine))
-    other_sum = head_sum(*project(order, other, w_mine))
+    distance = targets ^ lax.axis_index("head")
+    order = jnp.asarray(halving_order(lax.axis_size("head")), jnp.int32)
+    places = jnp.argmax(distance[:, None] == order[None, :], axis=1).astype(jnp.int32)
+    mine_sum = head_sum(*project(places, mine, weights))
+    other_sum = head_sum(*project(places, other, weights))
     back = lax.ppermute(other_sum, "groups", swap)
     blocks = mine_sum.shape[1] // half_cols
     mine_sum = mine_sum.reshape(tokens, blocks, 1, half_cols)

time: 180 us -> 164 us (0.911)
  waiting for transfers between devices: 88.6 us -> 66.7 us
  starting transfers between devices: 9.15 us -> 28.9 us
  between operations: 13.6 us -> 0.26 us
  local copies, waits for them, and re-layouts: 24.2 us -> 13.2 us
  Pallas kernels: 36.6 us -> 42.6 us
  other arithmetic: 5.57 us -> 11.5 us
    ppermute x0 -> x6, starting transfers between devices: none -> 18.8 us  [the longest x3 11.7 us: ring_slots(): lax.ppermute(up[step - 1], axis, [(i, i + 1) for i in range(step - 1, cou...]
    ppermute x1, waiting for transfers between devices: 22.3 us -> 5.9 us  [per_device(): other = lax.ppermute(mine, 'groups', swap)]
    ppermute x3, waiting for transfers between devices: 46.3 us -> 32.4 us  [per_device(): incoming = incoming + lax.ppermute(outgoing, 'ctx', [(hop, hop + 1)])]
    ppermute x0 -> x6, waiting for transfers between devices: none -> 8.91 us  [the longest x3 8.9 us: ring_slots(): lax.ppermute(up[step - 1], axis, [(i, i + 1) for i in range(step - 1, cou...]
    reshape x2 -> x0, local copies, waits for them, and re-layouts: 8.33 us -> none  [the longest x1 4.19 us: per_device(): values2 = values.reshape(tokens * REFL, width)]
    add x0 -> x3, other arithmetic: none -> 5.47 us  [ring_slots(): return [own] + [up[k] + down[count - k] for k in range(1, count)]]
    pallas_call x2, Pallas kernels: 8.41 us -> 12.7 us  [project(): pl.pallas_call(project_kernel, grid_spec=pltpu.PrefetchScalarGridSpec(num...]
    unnamed x24 -> x22, local copies, waits for them, and re-layouts: 10.8 us -> 8.39 us
  transfers between devices with their start and end apart: 10 -> 15, of which waited for: 7 -> 8; matrix products, arithmetic and copies ran while one was open for 8% -> 7% of each run, Pallas kernels for 18% -> 22%
where the time goes in v4:
time: 164 us
  waiting for transfers between devices  66.7 us (41%)
  Pallas kernels  42.6 us (26%)
  starting transfers between devices  28.9 us (18%)
  local copies, waits for them, and re-layouts  13.2 us (8%)
  other arithmetic  11.5 us (7%)
    ppermute x3, waiting for transfers between devices, per_device(): incoming = incoming + lax.ppermute(outgoing, 'ctx', [(hop, hop + 1)])  32.4 us
    pallas_call x1, Pallas kernels, local_pass(): pl.pallas_call(functools.partial(chunk_kernel, group), grid=(heads // gro...  25.3 us
    ppermute x4, waiting for transfers between devices, head_sum(): got = lax.ppermute(give, 'head', pairs)  17.8 us
    pallas_call x2, Pallas kernels, project(): pl.pallas_call(project_kernel, grid_spec=pltpu.PrefetchScalarGridSpec(num...  12.7 us
    ppermute x3, starting transfers between devices, ring_slots(): lax.ppermute(up[step - 1], axis, [(i, i + 1) for i in range(step - 1, cou...  11.7 us
    ppermute x3, waiting for transfers between devices, ring_slots(): lax.ppermute(up[step - 1], axis, [(i, i + 1) for i in range(step - 1, cou...  8.9 us
    unnamed x22, local copies, waits for them, and re-layouts  8.39 us
    ppermute x3, starting transfers between devices, ring_slots(): lax.ppermute(down[step - 1], axis, [(i + 1, i) for i in range(count - ste...  7.12 us
  transfers between devices with their start and end apart: 15, of which 8 were waited for; matrix products, arithmetic and copies ran while one was open for 7% of the time, Pallas kernels for 22%

profile of v4, /device:TPU:16, one launch (start us, length us, event | category | flops | bytes accessed | tf_op | source)
XLA Modules:
  0.0 163.6 jit_solution(13515640301492050566)
XLA Ops:
  0.0 0.0 copy-start
  0.0 1.6 copy-done
  1.6 0.1 constant_dynamic-slice_fusion.refs_0_
  1.7 2.4 %collective-permute-start.4 = (bf16[1024,512]{1,0:T(8,128)(2,1)S(1)}, bf16[1024,512]{1,0:T(8,128)(2,1)}, u32[]{:S(2)}, u32[]{:S(2)}) collective-permute-start(bf16[1024,512]{1,0:T(8,128)(2,1)S(1)} %constant_dynamic-slice_fusion.refs_0_), channel_id=1, source_target_pairs={{4,0},{8,4},{12,8},{5,1},{9,5},{13,9},{6,2},{10,6},{14,10},{7,3},{... | collective-permute-start | bytes 3145736 | tf_op jit(solution)/shard_map/ppermute | solution.py:325
  4.1 4.4 %collective-permute-start.3 = (bf16[1024,512]{1,0:T(8,128)(2,1)S(1)}, bf16[1024,512]{1,0:T(8,128)(2,1)}, u32[]{:S(2)}, u32[]{:S(2)}) collective-permute-start(bf16[1024,512]{1,0:T(8,128)(2,1)S(1)} %constant_dynamic-slice_fusion.refs_0_), channel_id=1, source_target_pairs={{0,4},{4,8},{8,12},{1,5},{5,9},{9,13},{2,6},{6,10},{10,14},{3,7},{... | collective-permute-start | bytes 3145736 | tf_op jit(solution)/shard_map/ppermute | solution.py:324
  8.5 0.0 copy-done.9
  8.5 1.0 copy.12
  9.5 1.0 copy-done.4
  10.6 1.6 copy-done.5
  12.2 1.6 copy-done.6
  13.8 1.2 copy-done.7
  15.0 25.3 %local_pass.1 = (f32[512,1024]{1,0:T(8,128)S(1)}, bf16[512,1024]{1,0:T(8,128)(2,1)S(1)}, f32[8,128,128]{2,1,0:T(8,128)S(1)}, bf16[8,128,128]{2,1,0:T(8,128)(2,1)S(1)}) custom-call(bf16[512,1024]{1,0:T(8,128)(2,1)S(1)} %copy-done.7, bf16[512,2,1024]{2,1,0:T(2,128)(2,1)S(1)} %copy-done.5, bf16[512,2,1024]{2,1,0:T(2,128)(2,1)S(1)} %copy-done.6, ...), custom_call_target="tpu_custom_call" | custom-call | flops 5368709120 | bytes 8388608 | tf_op jit(solution)/shard_map/local_pass/pallas_call | solution.py:198
  40.3 0.0 copy-start.1
  40.3 0.0 copy-start.2
  40.4 0.7 collective-permute-start
  41.1 0.0 collective-permute-done.4
  41.1 3.1 %collective-permute-start.5 = (bf16[1024,512]{1,0:T(8,128)(2,1)}, bf16[1024,512]{1,0:T(8,128)(2,1)}, u32[]{:S(2)}, u32[]{:S(2)}) collective-permute-start(bf16[1024,512]{1,0:T(8,128)(2,1)} %collective-permute-done.4), channel_id=1, source_target_pairs={{4,0},{8,4},{5,1},{9,5},{6,2},{10,6},{7,3},{11,7},{20,16},{24,20},... | collective-permute-start | bytes 3145736 | tf_op jit(solution)/shard_map/ppermute | solution.py:325
  44.1 0.0 collective-permute-done.3
  44.1 1.9 %collective-permute-start.7 = (bf16[1024,512]{1,0:T(8,128)(2,1)}, bf16[1024,512]{1,0:T(8,128)(2,1)}, u32[]{:S(2)}, u32[]{:S(2)}) collective-permute-start(bf16[1024,512]{1,0:T(8,128)(2,1)} %collective-permute-done.3), channel_id=1, source_target_pairs={{4,8},{8,12},{5,9},{9,13},{6,10},{10,14},{7,11},{11,15},{20,24},{2... | collective-permute-start | bytes 3145736 | tf_op jit(solution)/shard_map/ppermute | solution.py:324
  46.1 0.0 collective-permute-done
  46.1 0.2 fusion
  46.3 1.3 collective-permute-start.1
  47.6 28.3 %collective-permute-done.1 = bf16[8,128,128]{2,1,0:T(8,128)(2,1)S(1)} collective-permute-done((bf16[8,128,128]{2,1,0:T(8,128)(2,1)S(1)}, bf16[8,128,128]{2,1,0:T(8,128)(2,1)S(1)}, u32[]{:S(2)}, u32[]{:S(2)}) %collective-permute-start.1) | collective-permute-done | bytes 262176 | tf_op jit(solution)/shard_map/ppermute | solution.py:358
  75.9 0.1 add.41
  76.0 0.2 fusion.1
  76.3 1.3 collective-permute-start.2
  77.6 4.0 %collective-permute-done.2 = bf16[8,128,128]{2,1,0:T(8,128)(2,1)S(1)} collective-permute-done((bf16[8,128,128]{2,1,0:T(8,128)(2,1)S(1)}, bf16[8,128,128]{2,1,0:T(8,128)(2,1)S(1)}, u32[]{:S(2)}, u32[]{:S(2)}) %collective-permute-start.2) | collective-permute-done | bytes 262176 | tf_op jit(solution)/shard_map/ppermute | solution.py:358
  81.6 0.8 add.43.s_ref
  82.4 0.0 collective-permute-done.5
  82.4 1.7 %collective-permute-start.6 = (bf16[1024,512]{1,0:T(8,128)(2,1)}, bf16[1024,512]{1,0:T(8,128)(2,1)}, u32[]{:S(2)}, u32[]{:S(2)}) collective-permute-start(bf16[1024,512]{1,0:T(8,128)(2,1)} %collective-permute-done.5), channel_id=1, source_target_pairs={{4,0},{5,1},{6,2},{7,3},{20,16},{21,17},{22,18},{23,19}} | collective-permute-start | bytes 3145736 | tf_op jit(solution)/shard_map/ppermute | solution.py:325
  84.1 0.0 collective-permute-done.7
  84.1 5.4 %collective-permute-start.8 = (bf16[1024,512]{1,0:T(8,128)(2,1)}, bf16[1024,512]{1,0:T(8,128)(2,1)}, u32[]{:S(2)}, u32[]{:S(2)}) collective-permute-start(bf16[1024,512]{1,0:T(8,128)(2,1)} %collective-permute-done.7), channel_id=1, source_target_pairs={{8,12},{9,13},{10,14},{11,15},{24,28},{25,29},{26,30},{27,31}} | collective-permute-start | bytes 3145736 | tf_op jit(solution)/shard_map/ppermute | solution.py:324
  89.5 4.5 %normed_rows.1.a_ref = bf16[512,1024]{1,0:T(8,128)(2,1)} custom-call(f32[512,1024]{1,0:T(8,128)} %copy-done.1, bf16[512,1024]{1,0:T(8,128)(2,1)} %copy-done.2, bf16[8,128,128]{2,1,0:T(8,128)(2,1)} %add.43.s_ref, f32[1,1024]{1,0:T(1,128)} %bitcast.14), custom_call_target="tpu_custom_call" | custom-call | tf_op jit(solution)/shard_map/normed_rows/pallas_call | solution.py:238
  94.0 1.5 collective-permute-start.11
  95.5 0.7 iota_reduce_fusion
  96.2 1.8 %add.46.refs_2_ = bf16[1024,512]{1,0:T(8,128)(2,1)S(1)} add(bf16[1024,512]{1,0:T(8,128)(2,1)} %collective-permute-done.7, bf16[1024,512]{1,0:T(8,128)(2,1)} %collective-permute-done.5) | non-fusion elementwise | flops 524288 | bytes 3145728 | tf_op jit(solution)/shard_map/add | solution.py:328
  98.1 0.0 collective-permute-done.6
  98.1 1.8 %add.45.refs_1_ = bf16[1024,512]{1,0:T(8,128)(2,1)S(1)} add(bf16[1024,512]{1,0:T(8,128)(2,1)} %collective-permute-done.3, bf16[1024,512]{1,0:T(8,128)(2,1)} %collective-permute-done.6) | non-fusion elementwise | flops 524288 | bytes 3145728 | tf_op jit(solution)/shard_map/add | solution.py:328
  99.9 8.9 %collective-permute-done.8 = bf16[1024,512]{1,0:T(8,128)(2,1)} collective-permute-done((bf16[1024,512]{1,0:T(8,128)(2,1)}, bf16[1024,512]{1,0:T(8,128)(2,1)}, u32[]{:S(2)}, u32[]{:S(2)}) %collective-permute-start.8) | collective-permute-done | bytes 1048608 | tf_op jit(solution)/shard_map/ppermute | solution.py:324
  108.8 1.8 %add.47.refs_3_ = bf16[1024,512]{1,0:T(8,128)(2,1)S(1)} add(bf16[1024,512]{1,0:T(8,128)(2,1)} %collective-permute-done.8, bf16[1024,512]{1,0:T(8,128)(2,1)} %collective-permute-done.4) | non-fusion elementwise | flops 524288 | bytes 3145728 | tf_op jit(solution)/shard_map/add | solution.py:328
  110.6 5.9 %collective-permute-done.11.a_ref = bf16[512,1024]{1,0:T(8,128)(2,1)} collective-permute-done((bf16[512,1024]{1,0:T(8,128)(2,1)}, bf16[512,1024]{1,0:T(8,128)(2,1)}, u32[]{:S(2)}, u32[]{:S(2)}) %collective-permute-start.11) | collective-permute-done | bytes 1048608 | tf_op jit(solution)/shard_map/ppermute | solution.py:364
  116.5 6.8 %project.3 = (bf16[512,1024]{1,0:T(8,128)(2,1)S(1)}, bf16[512,1024]{1,0:T(8,128)(2,1)S(1)}) custom-call(s32[4]{0:T(128)S(1)} %get-tuple-element.14.place_ref, bf16[512,1024]{1,0:T(8,128)(2,1)} %collective-permute-done.11.a_ref, bf16[1024,512]{1,0:T(8,128)(2,1)S(1)} %constant_dynamic-slice_fusion.refs_0_, bf16[1024,512]{1,0:T(8,128)(2,1)S(1)} %add.45.refs_1_, ...), custom_call_target="tpu_custom_call" | custom-call | flops 2147483648 | bytes 7340032 | tf_op jit(solution)/shard_map/project/pallas_call | solution.py:276
  123.4 0.1 collective-permute-start.12
  123.5 5.9 %project.2 = (bf16[512,1024]{1,0:T(8,128)(2,1)S(1)}, bf16[512,1024]{1,0:T(8,128)(2,1)S(1)}) custom-call(s32[4]{0:T(128)S(1)} %get-tuple-element.14.place_ref, bf16[512,1024]{1,0:T(8,128)(2,1)S(1)} %copy-done.3, bf16[1024,512]{1,0:T(8,128)(2,1)S(1)} %constant_dynamic-slice_fusion.refs_0_, bf16[1024,512]{1,0:T(8,128)(2,1)S(1)} %add.45.refs_1_, ...), custom_call_target="tpu_custom_call" | custom-call | flops 2147483648 | bytes 7340032 | tf_op jit(solution)/shard_map/project/pallas_call | solution.py:276
  129.3 0.5 collective-permute-start.9
  129.9 0.0 collective-permute-done.12
  129.9 0.4 convert_add_fusion
  130.2 0.1 slice.32
  130.3 1.5 collective-permute-start.13
  131.9 0.3 collective-permute-done.9
  132.1 0.4 convert_add_fusion.1
  132.5 0.0 copy-start.8
  132.5 1.3 copy-done.8
  133.9 0.1 slice.33
  133.9 1.6 collective-permute-start.10
  135.5 9.7 %collective-permute-done.13 = bf16[512,512]{1,0:T(8,128)(2,1)S(1)} collective-permute-done((bf16[512,512]{1,0:T(8,128)(2,1)S(1)}, bf16[512,512]{1,0:T(8,128)(2,1)S(1)}, u32[]{:S(2)}, u32[]{:S(2)}) %collective-permute-start.13) | collective-permute-done | bytes 524320 | tf_op jit(solution)/shard_map/ppermute | solution.py:310
  145.2 1.0 fusion.2
  146.1 1.5 collective-permute-start.14
  147.7 7.9 %collective-permute-done.10 = bf16[512,512]{1,0:T(8,128)(2,1)S(1)} collective-permute-done((bf16[512,512]{1,0:T(8,128)(2,1)S(1)}, bf16[512,512]{1,0:T(8,128)(2,1)S(1)}, u32[]{:S(2)}, u32[]{:S(2)}) %collective-permute-start.10) | collective-permute-done | bytes 524320 | tf_op jit(solution)/shard_map/ppermute | solution.py:310
  155.5 1.4 fusion.4
  156.9 1.7 %collective-permute-done.14 = bf16[512,512]{1,0:T(8,128)(2,1)} collective-permute-done((bf16[512,512]{1,0:T(8,128)(2,1)}, bf16[512,512]{1,0:T(8,128)(2,1)}, u32[]{:S(2)}, u32[]{:S(2)}) %collective-permute-start.14) | collective-permute-done | bytes 524320 | tf_op jit(solution)/shard_map/ppermute | solution.py:370
  158.6 1.4 maximum_select_fusion
  160.0 1.3 copy.13
  161.3 2.3 %copy.14 = bf16[512,1024]{1,0:T(8,128)(2,1)} copy(bf16[512,1024]{0,1:T(8,128)(2,1)} %bitcast.12) | data formatting | bytes 2097152 | tf_op jit(solution)/shard_map/jit(_where)/select_n | solution.py:374
  (13 shorter events, 0.1 us)
Async XLA Ops:
  0.0 1.6 copy-start
  0.0 8.5 %copy-start.9 = (f32[2,8,512]{2,1,0:T(8,128)S(1)}, f32[2,8,512]{2,1,0:T(8,128)}, u32[]{:S(2)}) copy-start(f32[2,8,512]{2,1,0:T(8,128)} %param.10) | copy-start | bytes 98308
  1.7 39.4 %collective-permute-start.4 = (bf16[1024,512]{1,0:T(8,128)(2,1)S(1)}, bf16[1024,512]{1,0:T(8,128)(2,1)}, u32[]{:S(2)}, u32[]{:S(2)}) collective-permute-start(bf16[1024,512]{1,0:T(8,128)(2,1)S(1)} %constant_dynamic-slice_fusion.refs_0_), channel_id=1, source_target_pairs={{4,0},{8,4},{12,8},{5,1},{9,5},{13,9},{6,2},{10,6},{14,10},{7,3},{... | collective-permute-start | bytes 3145736 | tf_op jit(solution)/shard_map/ppermute | solution.py:325
  4.1 40.1 %collective-permute-start.3 = (bf16[1024,512]{1,0:T(8,128)(2,1)S(1)}, bf16[1024,512]{1,0:T(8,128)(2,1)}, u32[]{:S(2)}, u32[]{:S(2)}) collective-permute-start(bf16[1024,512]{1,0:T(8,128)(2,1)S(1)} %constant_dynamic-slice_fusion.refs_0_), channel_id=1, source_target_pairs={{0,4},{4,8},{8,12},{1,5},{5,9},{9,13},{2,6},{6,10},{10,14},{3,7},{... | collective-permute-start | bytes 3145736 | tf_op jit(solution)/shard_map/ppermute | solution.py:324
  9.5 1.0 copy-start.4
  10.6 1.6 copy-start.5
  12.2 1.6 copy-start.6
  13.8 1.2 copy-start.7
  40.3 35.9 %copy-start.1 = (f32[512,1024]{1,0:T(8,128)}, f32[512,1024]{1,0:T(8,128)S(1)}, u32[]{:S(2)}) copy-start(f32[512,1024]{1,0:T(8,128)S(1)} %get-tuple-element.15.o_ref) | copy-start | bytes 6291460
  40.3 35.9 %copy-start.2 = (bf16[512,1024]{1,0:T(8,128)(2,1)}, bf16[512,1024]{1,0:T(8,128)(2,1)S(1)}, u32[]{:S(2)}) copy-start(bf16[512,1024]{1,0:T(8,128)(2,1)S(1)} %get-tuple-element.16.e_ref) | copy-start | bytes 3145732
  40.4 5.7 %collective-permute-start = (bf16[8,128,128]{2,1,0:T(8,128)(2,1)S(1)}, bf16[8,128,128]{2,1,0:T(8,128)(2,1)S(1)}, u32[]{:S(2)}, u32[]{:S(2)}) collective-permute-start(bf16[8,128,128]{2,1,0:T(8,128)(2,1)S(1)} %convert_element_type.35), channel_id=1, source_target_pairs={{0,4},{1,5},{2,6},{3,7},{16,20},{17,21},{18,22},{19,23}} | collective-permute-start | bytes 786440 | tf_op jit(solution)/shard_map/ppermute | solution.py:358
  41.1 41.3 %collective-permute-start.5 = (bf16[1024,512]{1,0:T(8,128)(2,1)}, bf16[1024,512]{1,0:T(8,128)(2,1)}, u32[]{:S(2)}, u32[]{:S(2)}) collective-permute-start(bf16[1024,512]{1,0:T(8,128)(2,1)} %collective-permute-done.4), channel_id=1, source_target_pairs={{4,0},{8,4},{5,1},{9,5},{6,2},{10,6},{7,3},{11,7},{20,16},{24,20},... | collective-permute-start | bytes 3145736 | tf_op jit(solution)/shard_map/ppermute | solution.py:325
  44.1 40.0 %collective-permute-start.7 = (bf16[1024,512]{1,0:T(8,128)(2,1)}, bf16[1024,512]{1,0:T(8,128)(2,1)}, u32[]{:S(2)}, u32[]{:S(2)}) collective-permute-start(bf16[1024,512]{1,0:T(8,128)(2,1)} %collective-permute-done.3), channel_id=1, source_target_pairs={{4,8},{8,12},{5,9},{9,13},{6,10},{10,14},{7,11},{11,15},{20,24},{2... | collective-permute-start | bytes 3145736 | tf_op jit(solution)/shard_map/ppermute | solution.py:324
  46.3 29.6 %collective-permute-start.1 = (bf16[8,128,128]{2,1,0:T(8,128)(2,1)S(1)}, bf16[8,128,128]{2,1,0:T(8,128)(2,1)S(1)}, u32[]{:S(2)}, u32[]{:S(2)}) collective-permute-start(bf16[8,128,128]{2,1,0:T(8,128)(2,1)S(1)} %fusion), channel_id=1, source_target_pairs={{4,8},{5,9},{6,10},{7,11},{20,24},{21,25},{22,26},{23,27}} | collective-permute-start | bytes 786440 | tf_op jit(solution)/shard_map/ppermute | solution.py:358
  76.3 5.4 %collective-permute-start.2 = (bf16[8,128,128]{2,1,0:T(8,128)(2,1)S(1)}, bf16[8,128,128]{2,1,0:T(8,128)(2,1)S(1)}, u32[]{:S(2)}, u32[]{:S(2)}) collective-permute-start(bf16[8,128,128]{2,1,0:T(8,128)(2,1)S(1)} %fusion.1), channel_id=1, source_target_pairs={{8,12},{9,13},{10,14},{11,15},{24,28},{25,29},{26,30},{27,31}} | collective-permute-start | bytes 786440 | tf_op jit(solution)/shard_map/ppermute | solution.py:358
  82.4 15.7 %collective-permute-start.6 = (bf16[1024,512]{1,0:T(8,128)(2,1)}, bf16[1024,512]{1,0:T(8,128)(2,1)}, u32[]{:S(2)}, u32[]{:S(2)}) collective-permute-start(bf16[1024,512]{1,0:T(8,128)(2,1)} %collective-permute-done.5), channel_id=1, source_target_pairs={{4,0},{5,1},{6,2},{7,3},{20,16},{21,17},{22,18},{23,19}} | collective-permute-start | bytes 3145736 | tf_op jit(solution)/shard_map/ppermute | solution.py:325
  84.1 24.7 %collective-permute-start.8 = (bf16[1024,512]{1,0:T(8,128)(2,1)}, bf16[1024,512]{1,0:T(8,128)(2,1)}, u32[]{:S(2)}, u32[]{:S(2)}) collective-permute-start(bf16[1024,512]{1,0:T(8,128)(2,1)} %collective-permute-done.7), channel_id=1, source_target_pairs={{8,12},{9,13},{10,14},{11,15},{24,28},{25,29},{26,30},{27,31}} | collective-permute-start | bytes 3145736 | tf_op jit(solution)/shard_map/ppermute | solution.py:324
  89.5 6.1 %copy-start.10 = (s32[4]{0:T(128)S(1)}, s32[4]{0:T(128)}, u32[]{:S(2)}) copy-start(s32[4]{0:T(128)} %constant.32.clone) | copy-start | bytes 52
  94.0 22.5 %collective-permute-start.11 = (bf16[512,1024]{1,0:T(8,128)(2,1)}, bf16[512,1024]{1,0:T(8,128)(2,1)}, u32[]{:S(2)}, u32[]{:S(2)}) collective-permute-start(bf16[512,1024]{1,0:T(8,128)(2,1)} %normed_rows.1.a_ref), channel_id=1, source_target_pairs={{0,16},{16,0},{1,17},{17,1},{2,18},{18,2},{3,19},{19,3},{4,20},{20... | collective-permute-start | bytes 3145736 | tf_op jit(solution)/shard_map/ppermute | solution.py:364
  116.5 6.9 %copy-start.3 = (bf16[512,1024]{1,0:T(8,128)(2,1)S(1)}, bf16[512,1024]{1,0:T(8,128)(2,1)}, u32[]{:S(2)}) copy-start(bf16[512,1024]{1,0:T(8,128)(2,1)} %normed_rows.1.a_ref) | copy-start | bytes 3145732
  123.4 6.5 %collective-permute-start.12 = (bf16[512,1024]{1,0:T(8,128)(2,1)S(1)}, bf16[512,1024]{1,0:T(8,128)(2,1)S(1)}, u32[]{:S(2)}, u32[]{:S(2)}) collective-permute-start(bf16[512,1024]{1,0:T(8,128)(2,1)S(1)} %get-tuple-element.22), channel_id=1, source_target_pairs={{0,1},{1,0},{2,3},{3,2},{4,5},{5,4},{6,7},{7,6},{8,9},{9,8},{10,11... | collective-permute-start | bytes 3145736 | tf_op jit(solution)/shard_map/ppermute | solution.py:310
  129.3 2.8 %collective-permute-start.9 = (bf16[512,1024]{1,0:T(8,128)(2,1)S(1)}, bf16[512,1024]{1,0:T(8,128)(2,1)S(1)}, u32[]{:S(2)}, u32[]{:S(2)}) collective-permute-start(bf16[512,1024]{1,0:T(8,128)(2,1)S(1)} %get-tuple-element.20), channel_id=1, source_target_pairs={{0,1},{1,0},{2,3},{3,2},{4,5},{5,4},{6,7},{7,6},{8,9},{9,8},{10,11... | collective-permute-start | bytes 3145736 | tf_op jit(solution)/shard_map/ppermute | solution.py:310
  130.3 14.8 %collective-permute-start.13 = (bf16[512,512]{1,0:T(8,128)(2,1)S(1)}, bf16[512,512]{1,0:T(8,128)(2,1)S(1)}, u32[]{:S(2)}, u32[]{:S(2)}) collective-permute-start(bf16[512,512]{1,0:T(8,128)(2,1)S(1)} %slice.32), channel_id=1, source_target_pairs={{0,2},{1,3},{2,0},{3,1},{4,6},{5,7},{6,4},{7,5},{8,10},{9,11},{10,... | collective-permute-start | bytes 1572872 | tf_op jit(solution)/shard_map/ppermute | solution.py:310
  132.5 1.3 copy-start.8
  133.9 21.6 %collective-permute-start.10 = (bf16[512,512]{1,0:T(8,128)(2,1)S(1)}, bf16[512,512]{1,0:T(8,128)(2,1)S(1)}, u32[]{:S(2)}, u32[]{:S(2)}) collective-permute-start(bf16[512,512]{1,0:T(8,128)(2,1)S(1)} %slice.33), channel_id=1, source_target_pairs={{0,2},{1,3},{2,0},{3,1},{4,6},{5,7},{6,4},{7,5},{8,10},{9,11},{10,... | collective-permute-start | bytes 1572872 | tf_op jit(solution)/shard_map/ppermute | solution.py:310
  146.1 12.5 %collective-permute-start.14 = (bf16[512,512]{1,0:T(8,128)(2,1)}, bf16[512,512]{1,0:T(8,128)(2,1)}, u32[]{:S(2)}, u32[]{:S(2)}) collective-permute-start(bf16[512,512]{1,0:T(8,128)(2,1)} %fusion.2), channel_id=1, source_target_pairs={{0,16},{16,0},{1,17},{17,1},{2,18},{18,2},{3,19},{19,3},{4,20},{20... | collective-permute-start | bytes 1572872 | tf_op jit(solution)/shard_map/ppermute | solution.py:370

commit v5 on v4

--- a/solution.py
+++ b/solution.py
@@ -111,8 +111,12 @@
     return each(lambda rows: split(jnp.concatenate(rows, axis=0)), rows_of)
 
 
-def chunk_kernel(group, q_ref, k_ref, v_ref, b_ref, o_ref, e_ref, s_ref, p_ref, state):
-    chunk = pl.program_id(1)
+def chunk_kernel(group, first, q_ref, k_ref, v_ref, b_ref, *refs):
+    if first:
+        oe_ref, end_ref, state = refs
+    else:
+        start_ref, oe_ref, s_ref, p_ref, state = refs
+    chunk = pl.program_id(0)
     tokens = CHUNK // REFL
 
     @pl.when(chunk == 0)
@@ -121,7 +125,7 @@
         sub = lax.broadcasted_iota(jnp.int32, (DK, 2 * DK), 0)
         start = jnp.where(lane == sub + DK, 1.0, 0.0).astype(F32)
         for head in range(group):
-            state[head] = start
+            state[head] = start if first else start_ref[head]
 
     below = lax.broadcasted_iota(jnp.int32, (CHUNK, CHUNK), 0) > lax.broadcasted_iota(
         jnp.int32, (CHUNK, CHUNK), 1
@@ -140,7 +144,7 @@
 
     k_scales = each(inverse_norm, ks)
     q_scales = each(inverse_norm, qs)
-    rates = [b_ref[0, :, head : head + 1] * k_scales[head] for head in heads]
+    rates = [b_ref[:, head : head + 1] * k_scales[head] for head in heads]
     rates2 = each(lambda rate, scale: rate * scale, rates, k_scales)
     kqs = each(lambda k, q: jnp.concatenate([k, q], axis=0), ks, qs)
     grams = each(mxu_nt, kqs, ks)
@@ -178,83 +182,122 @@
     )
     for head in heads:
         state[head] = nexts[head]
-        o_ref[:, cols[head]] = outs[head][:, :DK]
-        e_ref[:, cols[head]] = outs[head][:, DK:].astype(BF16)
-
-    @pl.when(chunk == pl.num_programs(1) - 1)
+        oe_ref[:, cols[head]] = outs[head][:, :DK].astype(BF16)
+        oe_ref[:, slice((group + head) * DK, (group + head + 1) * DK)] = outs[head][:, DK:].astype(
+            BF16
+        )
+
+    @pl.when(chunk == pl.num_programs(0) - 1)
     def _():
         for head in heads:
-            s_ref[head] = nexts[head][:, :DK]
-            p_ref[head] = nexts[head][:, DK:].astype(BF16)
-
-
-def local_pass(queries, keys, values, beta, group):
+            if first:
+                end_ref[head] = nexts[head]
+            else:
+                s_ref[head] = nexts[head][:, :DK]
+                p_ref[head] = nexts[head][:, DK:].astype(BF16)
+
+
+def local_half(queries, keys, values, beta, start=None):
     tokens, width = queries.shape
-    heads = width // DK
+    group = width // DK
     tile = CHUNK // REFL
-    refl = pl.BlockSpec((tile, REFL, group * DK), lambda g, c: (c, 0, g))
-    token = pl.BlockSpec((tile, group * DK), lambda g, c: (c, g))
-    per_head = pl.BlockSpec((group, DK, DK), lambda g, c: (g, 0, 0))
+    steps = tokens // tile // 2
+    first = start is None
+    skip = 0 if first else steps
+    refl = pl.BlockSpec((tile, REFL, width), lambda c: (c + skip, 0, 0))
+    whole = pl.BlockSpec((group, DK, 2 * DK), lambda c: (0, 0, 0))
+    square = pl.BlockSpec((group, DK, DK), lambda c: (0, 0, 0))
+    rows = jax.ShapeDtypeStruct((steps * tile, 2 * width), BF16)
     return pl.pallas_call(
-        functools.partial(chunk_kernel, group),
-        grid=(heads // group, tokens // tile),
+        functools.partial(chunk_kernel, group, first),
+        grid=(steps,),
         in_specs=[
-            token,
+            pl.BlockSpec((tile, width), lambda c: (c + skip, 0)),
             refl,
             refl,
-            pl.BlockSpec((1, CHUNK, group), lambda g, c: (g, c, 0)),
-        ],
-        out_specs=[token, token, per_head, per_head],
-        out_shape=[
-            jax.ShapeDtypeStruct((tokens, width), F32),
-            jax.ShapeDtypeStruct((tokens, width), BF16),
-            jax.ShapeDtypeStruct((heads, DK, DK), F32),
-            jax.ShapeDtypeStruct((heads, DK, DK), BF16),
-        ],
+            pl.BlockSpec((CHUNK, group), lambda c: (c + skip, 0)),
+        ]
+        + ([] if first else [whole]),
+        out_specs=[pl.BlockSpec((tile, 2 * width), lambda c: (c, 0))]
+        + ([whole] if first else [square, square]),
+        out_shape=[rows]
+        + (
+            [jax.ShapeDtypeStruct((group, DK, 2 * DK), F32)]
+            if first
+            else [
+                jax.ShapeDtypeStruct((group, DK, DK), F32),
+                jax.ShapeDtypeStruct((group, DK, DK), BF16),
+            ]
+        ),
         scratch_shapes=[pltpu.VMEM((group, DK, 2 * DK), F32)],
-        compiler_params=pltpu.CompilerParams(vmem_limit_bytes=32 * 1024 * 1024),
+        compiler_params=pltpu.CompilerParams(vmem_limit_bytes=56 * 1024 * 1024),
         cost_estimate=pl.CostEstimate(
-            flops=80 * tokens * width * DK, bytes_accessed=16 * tokens * width, transcendentals=0
+            flops=200 * tokens * width * DK, bytes_accessed=8 * tokens * width, transcendentals=0
         ),
-        name="local_pass",
-    )(queries, keys, values, beta)
-
-
-def norm_kernel(o_ref, e_ref, s_ref, g_ref, out_ref):
-    heads = range(s_ref.shape[0])
+        name="local_half",
+    )(queries, keys, values, beta, *([] if first else [start]))
+
+
+def norm_kernel(first_ref, second_ref, s_ref, g_ref, out_ref):
+    group = s_ref.shape[0]
+    heads = range(group)
     cols = [slice(head * DK, (head + 1) * DK) for head in heads]
-    readouts = [o_ref[:, cols[head]] + mxu(e_ref[:, cols[head]], s_ref[head]) for head in heads]
-    scales = each(
-        lambda rows: lax.rsqrt(jnp.mean(rows * rows, axis=-1, keepdims=True) + TINY), readouts
-    )
-    for head in heads:
-        out_ref[:, cols[head]] = (readouts[head] * scales[head] * g_ref[:, cols[head]]).astype(BF16)
-
-
-def normed_rows(local, exposure, incoming, gain):
-    tokens, width = local.shape
-    tile = 128
-    rows = pl.BlockSpec((tile, width), lambda i: (i, 0))
+    tile = min(128, first_ref.shape[0])
+    for half, oe_ref in enumerate((first_ref, second_ref)):
+        for at in range(0, oe_ref.shape[0], tile):
+            rows = slice(at, at + tile)
+            to = slice(half * oe_ref.shape[0] + at, half * oe_ref.shape[0] + at + tile)
+            seen = [
+                mxu(oe_ref[rows, (group + head) * DK : (group + head + 1) * DK], s_ref[head])
+                for head in heads
+            ]
+            readouts = [oe_ref[rows, cols[head]].astype(F32) + seen[head] for head in heads]
+            scales = each(
+                lambda x: lax.rsqrt(jnp.mean(x * x, axis=-1, keepdims=True) + TINY), readouts
+            )
+            for head in heads:
+                out_ref[to, cols[head]] = (
+                    readouts[head] * scales[head] * g_ref[:, cols[head]]
+                ).astype(BF16)
+
+
+def normed_rows(first, second, incoming, gain):
+    width = gain.shape[0]
+    tokens = 2 * first.shape[0]
     return pl.pallas_call(
         norm_kernel,
-        grid=(tokens // tile,),
-        in_specs=[
-            rows,
-            rows,
-            pl.BlockSpec(incoming.shape, lambda i: (0, 0, 0)),
-            pl.BlockSpec((1, width), lambda i: (0, 0)),
-        ],
-        out_specs=rows,
+        in_specs=[pl.BlockSpec(memory_space=pltpu.VMEM)] * 4,
+        out_specs=pl.BlockSpec(memory_space=pltpu.VMEM),
         out_shape=jax.ShapeDtypeStruct((tokens, width), BF16),
+        cost_estimate=pl.CostEstimate(
+            flops=2 * tokens * width * DK, bytes_accessed=6 * tokens * width, transcendentals=0
+        ),
         name="normed_rows",
-    )(local, exposure, incoming, gain.reshape(1, width))
-
-
-def project_kernel(place_ref, a_ref, *refs):
-    weights, (give_ref, keep_ref) = refs[:-2], refs[-2:]
-    half, block = len(weights) // 2, weights[0].shape[1]
-    for slot, weight in enumerate(weights):
-        product = mxu(a_ref[...], weight[...]).astype(BF16)
+    )(first, second, incoming, gain.reshape(1, width))
+
+
+def project_kernel(choices, place_ref, first_ref, a_ref, *refs):
+    weights = refs[: sum(choices)]
+    give_ref, keep_ref, held, sems = refs[sum(choices) :]
+    half, block = len(choices) // 2, held.shape[2]
+    at = 0
+    for slot, options in enumerate(choices):
+        here = weights[at : at + options]
+        at += options
+        if options == 1:
+            pltpu.make_async_copy(here[0], held.at[slot], sems.at[slot]).start()
+            continue
+        for option in range(2):
+
+            @pl.when(first_ref[slot] == 1 - option)
+            def _():
+                pltpu.make_async_copy(here[option], held.at[slot], sems.at[slot]).start()
+
+    at = 0
+    for slot, options in enumerate(choices):
+        pltpu.make_async_copy(weights[at], held.at[slot], sems.at[slot]).wait()
+        at += options
+        product = mxu(a_ref[...], held[slot]).astype(BF16)
         place = place_ref[slot]
 
         @pl.when(place < half)
@@ -266,31 +309,32 @@
             keep_ref[:, pl.ds(pl.multiple_of((place - half) * block, block), block)] = product
 
 
-def project(places, rows, weights):
+def project(places, first, rows, weights):
     tokens, depth = rows.shape
     count = len(weights)
-    block = weights[0].shape[1]
-    tile = 128
-    half = pl.BlockSpec((tile, count // 2 * block), lambda i, places: (i, 0))
+    block = weights[0][0].shape[1]
+    choices = tuple(len(options) for options in weights)
+    half = pl.BlockSpec(memory_space=pltpu.VMEM)
     shape = jax.ShapeDtypeStruct((tokens, count // 2 * block), BF16)
     return pl.pallas_call(
-        project_kernel,
-        grid_spec=pltpu.PrefetchScalarGridSpec(
-            num_scalar_prefetch=1,
-            grid=(tokens // tile,),
-            in_specs=[pl.BlockSpec((tile, depth), lambda i, places: (i, 0))]
-            + [pl.BlockSpec((depth, block), lambda i, places: (0, 0))] * count,
-            out_specs=[half, half],
-        ),
+        functools.partial(project_kernel, choices),
+        in_specs=[pl.BlockSpec(memory_space=pltpu.SMEM)] * 2
+        + [half]
+        + [pl.BlockSpec(memory_space=pl.ANY)] * sum(choices),
+        out_specs=[half, half],
         out_shape=[shape, shape],
-        compiler_params=pltpu.CompilerParams(vmem_limit_bytes=32 * 1024 * 1024),
+        scratch_shapes=[
+            pltpu.VMEM((count, depth, block), BF16),
+            pltpu.SemaphoreType.DMA((count,)),
+        ],
+        compiler_params=pltpu.CompilerParams(vmem_limit_bytes=48 * 1024 * 1024),
         cost_estimate=pl.CostEstimate(
             flops=2 * tokens * depth * block * count,
             bytes_accessed=2 * (tokens * depth + (tokens + depth) * block * count),
             transcendentals=0,
         ),
         name="project",
-    )(places, rows, *weights)
+    )(places, first, rows, *[w for options in weights for w in options])
 
 
 def halving_order(count):
@@ -317,58 +361,83 @@
     return keep
 
 
-def ring_slots(own, axis):
-    count = lax.axis_size(axis)
-    up, down = {0: own}, {0: own}
-    for step in range(1, count):
-        up[step] = lax.ppermute(up[step - 1], axis, [(i, i + 1) for i in range(step - 1, count - 1)])
-        down[step] = lax.ppermute(
-            down[step - 1], axis, [(i + 1, i) for i in range(count - step)]
-        )
-    return [own] + [up[k] + down[count - k] for k in range(1, count)]
-
-
-def slots_by_head(w_half):
-    ctx, head = lax.axis_size("ctx"), lax.axis_size("head")
-    if ctx == head:
-        slots = ring_slots(w_half, "ctx")
-        return slots, lax.rem(lax.axis_index("ctx") + ctx - jnp.arange(ctx), ctx)
-    whole = lax.all_gather(w_half, "ctx", axis=1, tiled=True)
-    return jnp.split(whole, head, axis=1), jnp.arange(head)
+def tied(*values):
+    return lax.optimization_barrier(values)
+
+
+def send(value, axis, pairs):
+    return lax.ppermute(value, axis, pairs)
 
 
 def per_device(queries, keys, values, beta, gain, w_out):
     tokens, width = queries.shape
     heads = width // DK
-    group = min(8, heads)
-    beta_rows = (
-        beta.transpose(2, 0, 1)
-        .reshape(tokens * REFL, heads // group, group)
-        .transpose(1, 0, 2)
-    )
-    side = lax.axis_index("groups")
+    ctx, head = lax.axis_size("ctx"), lax.axis_size("head")
+    here, side = lax.axis_index("ctx"), lax.axis_index("groups")
+    beta_rows = beta.transpose(2, 0, 1).reshape(tokens * REFL, heads)
     half_cols = w_out.shape[1] // 2
-    w_half = lax.dynamic_slice_in_dim(w_out, side * half_cols, half_cols, 1)
-    weights, targets = slots_by_head(w_half)
-    local, exposure, state_end, total_end = local_pass(queries, keys, values, beta_rows, group)
+    own = lax.dynamic_slice_in_dim(w_out, side * half_cols, half_cols, 1)
+    ring = ctx == head and ctx >= 4
+    up, down = {0: own}, {0: own}
+
+    def pass_up(step):
+        up[step] = send(up[step - 1], "ctx", [(i, i + 1) for i in range(step - 1, ctx - 1)])
+
+    def pass_down(step):
+        down[step] = send(down[step - 1], "ctx", [(i + 1, i) for i in range(ctx - step)])
+
+    if ring:
+        pass_up(1)
+        pass_down(1)
+    swap = [(0, 1), (1, 0)]
+    near, middle = local_half(queries, keys, values, beta_rows)
+    if ring:
+        up[1], down[1], middle = tied(up[1], down[1], middle)
+        pass_up(2)
+        pass_down(2)
+    near_other = send(near, "groups", swap)
+    far, state_end, total_end = local_half(queries, keys, values, beta_rows, middle)
+    far_other = send(far, "groups", swap)
 
     incoming = jnp.zeros((heads, DK, DK), BF16)
     outgoing = state_end.astype(BF16)
-    for hop in range(lax.axis_size("ctx") - 1):
-        incoming = incoming + lax.ppermute(outgoing, "ctx", [(hop, hop + 1)])
+    for hop in range(ctx - 1):
+        if hop == 1 and ring:
+            up[2], down[2], near_other, outgoing = tied(up[2], down[2], near_other, outgoing)
+        incoming = incoming + send(outgoing, "ctx", [(hop, hop + 1)])
         outgoing = (
             jnp.einsum("hde,hef->hdf", total_end, incoming, preferred_element_type=F32) + state_end
         ).astype(BF16)
-    mine = normed_rows(local, exposure, incoming, gain)
-    swap = [(0, 1), (1, 0)]
-    other = lax.ppermute(mine, "groups", swap)
+    if ring:
+        for step in range(3, ctx):
+            pass_down(step)
+        up[2], incoming = tied(up[2], incoming)
+        for step in range(3, ctx):
+            pass_up(step)
+        weights = [(own,)] + [(up[k], down[ctx - k]) for k in range(1, ctx)]
+        targets = lax.rem(here + ctx - jnp.arange(ctx), ctx)
+        first = (here >= jnp.arange(ctx)).astype(jnp.int32)
+    else:
+        whole = lax.all_gather(own, "ctx", axis=1, tiled=True)
+        weights = [(w,) for w in jnp.split(whole, head, axis=1)]
+        targets = jnp.arange(head)
+        first = jnp.ones((head,), jnp.int32)
+    incoming_other = send(incoming, "groups", swap)
+    mine = normed_rows(near, far, incoming, gain)
+    other = normed_rows(near_other, far_other, incoming_other, gain)
     distance = targets ^ lax.axis_index("head")
-    order = jnp.asarray(halving_order(lax.axis_size("head")), jnp.int32)
+    order = jnp.asarray(halving_order(head), jnp.int32)
     places = jnp.argmax(distance[:, None] == order[None, :], axis=1).astype(jnp.int32)
-    mine_sum = head_sum(*project(places, mine, weights))
-    other_sum = head_sum(*project(places, other, weights))
-    back = lax.ppermute(other_sum, "groups", swap)
+    other_sum = head_sum(*project(places, first, other, weights))
+    mine_sum = head_sum(*project(places, first, mine, weights))
+    back = send(other_sum, "groups", swap)
     blocks = mine_sum.shape[1] // half_cols
+    if blocks == 1:
+        return jnp.where(
+            side == 0,
+            jnp.concatenate([mine_sum, back], axis=1),
+            jnp.concatenate([back, mine_sum], axis=1),
+        )
     mine_sum = mine_sum.reshape(tokens, blocks, 1, half_cols)
     back = back.reshape(tokens, blocks, 1, half_cols)
     mixed = jnp.where(

time: 164 us -> 152 us (0.927)
  waiting for transfers between devices: 66.7 us -> 52.9 us
  local copies, waits for them, and re-layouts: 13.2 us -> 8.32 us
  starting transfers between devices: 28.9 us -> 33.6 us
  Pallas kernels: 42.6 us -> 46.7 us
  other arithmetic: 11.5 us -> 7.75 us
    ppermute x11 -> x13, waiting for transfers between devices: 48.9 us -> 34 us  [send(): return lax.ppermute(value, axis, pairs)]
    add x5 -> x2, other arithmetic: 6.32 us -> 0.14 us  [per_device(): incoming = incoming + send(outgoing, 'ctx', [(hop, hop + 1)])]
    ppermute x11 -> x13, starting transfers between devices: 25.2 us -> 30.9 us  [send(): return lax.ppermute(value, axis, pairs)]
    pallas_call x4 -> x6, Pallas kernels: 42.6 us -> 46.7 us  [the longest x2 30.3 us: local_half(): pl.pallas_call(functools.partial(chunk_kernel, group, first), grid=(steps...]
    select_n x2 -> x0, local copies, waits for them, and re-layouts: 3.6 us -> none  [per_device(): jnp.where(side == 0, jnp.concatenate([mine_sum, back], axis=2), jnp.conca...]
    unnamed x22 -> x26, local copies, waits for them, and re-layouts: 8.39 us -> 7.07 us
  transfers between devices with their start and end apart: 15 -> 17, of which waited for: 8 -> 10; matrix products, arithmetic and copies ran while one was open for 7% -> 6% of each run, Pallas kernels for 22% -> 27%
where the time goes in v5:
time: 152 us; the launch traced here: 151 us
  waiting for transfers between devices  52.9 us (35%)
  Pallas kernels  46.7 us (31%)
  starting transfers between devices  33.6 us (22%)
  local copies, waits for them, and re-layouts  8.32 us (5%)
  other arithmetic  7.75 us (5%)
  matrix products  1.58 us (1%)
    ppermute x13, waiting for transfers between devices, send(): return lax.ppermute(value, axis, pairs)  34 us
    ppermute x13, starting transfers between devices, send(): return lax.ppermute(value, axis, pairs)  30.9 us
    pallas_call x2, Pallas kernels, local_half(): pl.pallas_call(functools.partial(chunk_kernel, group, first), grid=(steps...  30.3 us
    ppermute x4, waiting for transfers between devices, head_sum(): got = lax.ppermute(give, 'head', pairs)  18.9 us
    pallas_call x2, Pallas kernels, project(): pl.pallas_call(functools.partial(project_kernel, choices), in_specs=[pl.B...  9.53 us
    unnamed x26, local copies, waits for them, and re-layouts  7.07 us
    pallas_call x2, Pallas kernels, normed_rows(): pl.pallas_call(norm_kernel, in_specs=[pl.BlockSpec(memory_space=pltpu.VME...  6.84 us
  transfers between devices with their start and end apart: 17, of which 10 were waited for; matrix products, arithmetic and copies ran while one was open for 6% of the time, Pallas kernels for 27%

profile of v5, /device:TPU:16, one launch (start us, length us, event | category | flops | bytes accessed | tf_op | source)
XLA Modules:
  0.0 151.1 jit_solution(7496687483651143461)
XLA Ops:
  0.0 0.0 copy-start
  0.0 1.6 %copy-done = bf16[1024,1024]{1,0:T(8,128)(2,1)S(1)} copy-done((bf16[1024,1024]{1,0:T(8,128)(2,1)S(1)}, bf16[1024,1024]{1,0:T(8,128)(2,1)}, u32[]{:S(2)}) %copy-start) | copy-done | bytes 2097176
  1.6 0.1 constant_dynamic-slice_fusion.refs_0_
  1.7 2.4 %collective-permute-start.1 = (bf16[1024,512]{1,0:T(8,128)(2,1)S(1)}, bf16[1024,512]{1,0:T(8,128)(2,1)}, u32[]{:S(2)}, u32[]{:S(2)}) collective-permute-start(bf16[1024,512]{1,0:T(8,128)(2,1)S(1)} %constant_dynamic-slice_fusion.refs_0_), channel_id=1, source_target_pairs={{4,0},{8,4},{12,8},{5,1},{9,5},{13,9},{6,2},{10,6},{14,10},{7,3},{... | collective-permute-start | bytes 3145736 | tf_op jit(solution)/shard_map/ppermute | solution.py:369
  4.1 4.4 %collective-permute-start = (bf16[1024,512]{1,0:T(8,128)(2,1)S(1)}, bf16[1024,512]{1,0:T(8,128)(2,1)}, u32[]{:S(2)}, u32[]{:S(2)}) collective-permute-start(bf16[1024,512]{1,0:T(8,128)(2,1)S(1)} %constant_dynamic-slice_fusion.refs_0_), channel_id=1, source_target_pairs={{0,4},{4,8},{8,12},{1,5},{5,9},{9,13},{2,6},{6,10},{10,14},{3,7},{... | collective-permute-start | bytes 3145736 | tf_op jit(solution)/shard_map/ppermute | solution.py:369
  8.5 0.0 copy-done.11
  8.5 1.0 copy.9
  9.5 15.0 %local_half.2 = (bf16[256,2048]{1,0:T(8,128)(2,1)}, f32[8,128,256]{2,1,0:T(8,128)}) custom-call(bf16[512,1024]{1,0:T(8,128)(2,1)} %q_ref.3, bf16[512,2,1024]{2,1,0:T(2,128)(2,1)} %k_ref.3, bf16[512,2,1024]{2,1,0:T(2,128)(2,1)} %v_ref.3, f32[1024,8]{1,0:T(8,128)} %bitcast.7), custom_call_target="tpu_custom_call" | custom-call | flops 13421772800 | bytes 4194304 | tf_op jit(solution)/shard_map/local_half/pallas_call | solution.py:211
  24.5 1.5 %collective-permute-start.4 = (bf16[256,2048]{1,0:T(8,128)(2,1)}, bf16[256,2048]{1,0:T(8,128)(2,1)S(1)}, u32[]{:S(2)}, u32[]{:S(2)}) collective-permute-start(bf16[256,2048]{1,0:T(8,128)(2,1)} %get-tuple-element.25.first_ref), channel_id=1, source_target_pairs={{0,16},{16,0},{1,17},{17,1},{2,18},{18,2},{3,19},{19,3},{4,20},{20... | collective-permute-start | bytes 3145736 | tf_op jit(solution)/shard_map/ppermute | solution.py:369
  26.0 2.6 %collective-permute-done.1.refs_6_ = bf16[1024,512]{1,0:T(8,128)(2,1)} collective-permute-done((bf16[1024,512]{1,0:T(8,128)(2,1)S(1)}, bf16[1024,512]{1,0:T(8,128)(2,1)}, u32[]{:S(2)}, u32[]{:S(2)}) %collective-permute-start.1) | collective-permute-done | bytes 1048608 | tf_op jit(solution)/shard_map/ppermute | solution.py:369
  28.6 2.1 %collective-permute-done.refs_1_ = bf16[1024,512]{1,0:T(8,128)(2,1)} collective-permute-done((bf16[1024,512]{1,0:T(8,128)(2,1)S(1)}, bf16[1024,512]{1,0:T(8,128)(2,1)}, u32[]{:S(2)}, u32[]{:S(2)}) %collective-permute-start) | collective-permute-done | bytes 1048608 | tf_op jit(solution)/shard_map/ppermute | solution.py:369
  30.7 4.4 %collective-permute-start.2 = (bf16[1024,512]{1,0:T(8,128)(2,1)}, bf16[1024,512]{1,0:T(8,128)(2,1)}, u32[]{:S(2)}, u32[]{:S(2)}) collective-permute-start(bf16[1024,512]{1,0:T(8,128)(2,1)} %collective-permute-done.refs_1_), channel_id=1, source_target_pairs={{4,8},{8,12},{5,9},{9,13},{6,10},{10,14},{7,11},{11,15},{20,24},{2... | collective-permute-start | bytes 3145736 | tf_op jit(solution)/shard_map/ppermute | solution.py:369
  35.1 3.3 %collective-permute-start.3 = (bf16[1024,512]{1,0:T(8,128)(2,1)}, bf16[1024,512]{1,0:T(8,128)(2,1)}, u32[]{:S(2)}, u32[]{:S(2)}) collective-permute-start(bf16[1024,512]{1,0:T(8,128)(2,1)} %collective-permute-done.1.refs_6_), channel_id=1, source_target_pairs={{4,0},{8,4},{5,1},{9,5},{6,2},{10,6},{7,3},{11,7},{20,16},{24,20},... | collective-permute-start | bytes 3145736 | tf_op jit(solution)/shard_map/ppermute | solution.py:369
  38.5 15.4 %local_half.3 = (bf16[256,2048]{1,0:T(8,128)(2,1)}, f32[8,128,128]{2,1,0:T(8,128)}, bf16[8,128,128]{2,1,0:T(8,128)(2,1)}) custom-call(bf16[512,1024]{1,0:T(8,128)(2,1)} %q_ref.3, bf16[512,2,1024]{2,1,0:T(2,128)(2,1)} %k_ref.3, bf16[512,2,1024]{2,1,0:T(2,128)(2,1)} %v_ref.3, f32[1024,8]{1,0:T(8,128)} %bitcast.8, f32[8,128,256]{2,1,0:T(8,128)} %get-tuple-element.27.refs_0_), custom_call_target="tpu_custom_call" | custom-call | flops 13421772800 | bytes 4194304 | tf_op jit(solution)/shard_map/local_half/pallas_call | solution.py:211
  53.8 1.1 convert_element_type.39
  55.0 0.7 collective-permute-start.5
  55.7 0.0 collective-permute-done.5
  55.7 0.0 copy-start.12
  55.7 1.4 fusion
  57.1 0.0 collective-permute-done.4.first_ref
  57.1 0.0 collective-permute-done.2.refs_3_
  57.1 1.6 %collective-permute-done.3.refs_4_ = bf16[1024,512]{1,0:T(8,128)(2,1)} collective-permute-done((bf16[1024,512]{1,0:T(8,128)(2,1)}, bf16[1024,512]{1,0:T(8,128)(2,1)}, u32[]{:S(2)}, u32[]{:S(2)}) %collective-permute-start.3) | collective-permute-done | bytes 1048608 | tf_op jit(solution)/shard_map/ppermute | solution.py:369
  58.7 1.3 collective-permute-start.6
  60.0 9.6 %collective-permute-done.6 = bf16[8,128,128]{2,1,0:T(8,128)(2,1)S(1)} collective-permute-done((bf16[8,128,128]{2,1,0:T(8,128)(2,1)S(1)}, bf16[8,128,128]{2,1,0:T(8,128)(2,1)S(1)}, u32[]{:S(2)}, u32[]{:S(2)}) %collective-permute-start.6) | collective-permute-done | bytes 262176 | tf_op jit(solution)/shard_map/ppermute | solution.py:369
  69.6 0.1 add.33
  69.7 0.2 fusion.1
  69.9 1.3 collective-permute-start.7
  71.2 1.6 %collective-permute-start.12 = (bf16[256,2048]{1,0:T(8,128)(2,1)}, bf16[256,2048]{1,0:T(8,128)(2,1)}, u32[]{:S(2)}, u32[]{:S(2)}) collective-permute-start(bf16[256,2048]{1,0:T(8,128)(2,1)} %get-tuple-element.28.second_ref), channel_id=1, source_target_pairs={{0,16},{16,0},{1,17},{17,1},{2,18},{18,2},{3,19},{19,3},{4,20},{20... | collective-permute-start | bytes 3145736 | tf_op jit(solution)/shard_map/ppermute | solution.py:369
  72.8 1.6 %collective-permute-start.8 = (bf16[1024,512]{1,0:T(8,128)(2,1)}, bf16[1024,512]{1,0:T(8,128)(2,1)}, u32[]{:S(2)}, u32[]{:S(2)}) collective-permute-start(bf16[1024,512]{1,0:T(8,128)(2,1)} %collective-permute-done.3.refs_4_), channel_id=1, source_target_pairs={{4,0},{5,1},{6,2},{7,3},{20,16},{21,17},{22,18},{23,19}} | collective-permute-start | bytes 3145736 | tf_op jit(solution)/shard_map/ppermute | solution.py:369
  74.4 0.7 collective-permute-done.7
  75.1 0.1 add.35.s_ref
  75.2 5.4 %collective-permute-start.9 = (bf16[1024,512]{1,0:T(8,128)(2,1)}, bf16[1024,512]{1,0:T(8,128)(2,1)}, u32[]{:S(2)}, u32[]{:S(2)}) collective-permute-start(bf16[1024,512]{1,0:T(8,128)(2,1)} %collective-permute-done.2.refs_3_), channel_id=1, source_target_pairs={{8,12},{9,13},{10,14},{11,15},{24,28},{25,29},{26,30},{27,31}} | collective-permute-start | bytes 3145736 | tf_op jit(solution)/shard_map/ppermute | solution.py:369
  80.5 1.5 collective-permute-start.13
  82.0 0.7 iota_reduce_fusion
  82.8 13.4 %collective-permute-done.12.second_ref = bf16[256,2048]{1,0:T(8,128)(2,1)} collective-permute-done((bf16[256,2048]{1,0:T(8,128)(2,1)}, bf16[256,2048]{1,0:T(8,128)(2,1)}, u32[]{:S(2)}, u32[]{:S(2)}) %collective-permute-start.12) | collective-permute-done | bytes 1048608 | tf_op jit(solution)/shard_map/ppermute | solution.py:369
  96.2 2.7 %collective-permute-done.13.s_ref = bf16[8,128,128]{2,1,0:T(8,128)(2,1)S(1)} collective-permute-done((bf16[8,128,128]{2,1,0:T(8,128)(2,1)S(1)}, bf16[8,128,128]{2,1,0:T(8,128)(2,1)S(1)}, u32[]{:S(2)}, u32[]{:S(2)}) %collective-permute-start.13) | collective-permute-done | bytes 262176 | tf_op jit(solution)/shard_map/ppermute | solution.py:369
  98.9 0.7 copy-done.10
  99.6 3.4 %normed_rows.3.a_ref = bf16[512,1024]{1,0:T(8,128)(2,1)} custom-call(bf16[256,2048]{1,0:T(8,128)(2,1)} %copy-done.8, bf16[256,2048]{1,0:T(8,128)(2,1)} %collective-permute-done.12.second_ref, bf16[8,128,128]{2,1,0:T(8,128)(2,1)} %copy-done.10, f32[1,1024]{1,0:T(1,128)} %bitcast.10), custom_call_target="tpu_custom_call" | custom-call | flops 134217728 | bytes 3145728 | tf_op jit(solution)/shard_map/normed_rows/pallas_call | solution.py:267
  103.0 0.0 collective-permute-done.8.refs_2_
  103.0 0.0 collective-permute-done.9.refs_5_
  103.0 1.2 copy-done.2
  104.2 5.4 %project.3 = (bf16[512,1024]{1,0:T(8,128)(2,1)}, bf16[512,1024]{1,0:T(8,128)(2,1)S(1)}) custom-call(s32[4]{0:T(128)S(1)} %get-tuple-element.24.place_ref, s32[4]{0:T(128)S(1)} %compare_convert_fusion.first_ref, bf16[512,1024]{1,0:T(8,128)(2,1)S(1)} %copy-done.2, bf16[1024,512]{1,0:T(8,128)(2,1)S(1)} %constant_dynamic-slice_fusion.refs_0_, ...), custom_call_target="tpu_custom_call" | custom-call | flops 2147483648 | bytes 7340032 | tf_op jit(solution)/shard_map/project/pallas_call | solution.py:319
  109.6 1.0 copy-done.3
  110.6 0.0 collective-permute-start.14
  110.6 3.4 %normed_rows.2.a_ref = bf16[512,1024]{1,0:T(8,128)(2,1)} custom-call(bf16[256,2048]{1,0:T(8,128)(2,1)} %get-tuple-element.25.first_ref, bf16[256,2048]{1,0:T(8,128)(2,1)} %get-tuple-element.28.second_ref, bf16[8,128,128]{2,1,0:T(8,128)(2,1)} %copy-done.9, f32[1,1024]{1,0:T(1,128)} %bitcast.11), custom_call_target="tpu_custom_call" | custom-call | flops 134217728 | bytes 3145728 | tf_op jit(solution)/shard_map/normed_rows/pallas_call | solution.py:267
  114.1 1.2 copy-done.1
  115.3 4.1 %project.2 = (bf16[512,1024]{1,0:T(8,128)(2,1)S(1)}, bf16[512,1024]{1,0:T(8,128)(2,1)S(1)}) custom-call(s32[4]{0:T(128)S(1)} %get-tuple-element.24.place_ref, s32[4]{0:T(128)S(1)} %compare_convert_fusion.first_ref, bf16[512,1024]{1,0:T(8,128)(2,1)S(1)} %copy-done.1, bf16[1024,512]{1,0:T(8,128)(2,1)S(1)} %constant_dynamic-slice_fusion.refs_0_, ...), custom_call_target="tpu_custom_call" | custom-call | flops 2147483648 | bytes 7340032 | tf_op jit(solution)/shard_map/project/pallas_call | solution.py:319
  119.4 0.6 collective-permute-start.10
  120.0 0.0 collective-permute-done.14
  120.0 1.6 %convert_add_fusion = f32[512,1024]{1,0:T(8,128)S(1)} fusion(bf16[512,1024]{1,0:T(8,128)(2,1)} %collective-permute-done.14, bf16[512,1024]{1,0:T(8,128)(2,1)S(1)} %copy-done.4), kind=kLoop, calls=%fused_computation | loop fusion | flops 1572864 | bytes 4194304 | tf_op jit(solution)/shard_map/add | solution.py:355
  121.6 0.1 slice.30
  121.7 1.5 %collective-permute-start.15 = (bf16[512,512]{1,0:T(8,128)(2,1)S(1)}, bf16[512,512]{1,0:T(8,128)(2,1)S(1)}, u32[]{:S(2)}, u32[]{:S(2)}) collective-permute-start(bf16[512,512]{1,0:T(8,128)(2,1)S(1)} %slice.30), channel_id=1, source_target_pairs={{0,2},{1,3},{2,0},{3,1},{4,6},{5,7},{6,4},{7,5},{8,10},{9,11},{10,... | collective-permute-start | bytes 1572872 | tf_op jit(solution)/shard_map/ppermute | solution.py:354
  123.3 0.0 collective-permute-done.10
  123.3 0.4 convert_add_fusion.1
  123.7 1.3 copy-done.5
  125.0 0.1 slice.31
  125.1 0.6 collective-permute-start.11
  125.7 10.9 %collective-permute-done.15 = bf16[512,512]{1,0:T(8,128)(2,1)S(1)} collective-permute-done((bf16[512,512]{1,0:T(8,128)(2,1)S(1)}, bf16[512,512]{1,0:T(8,128)(2,1)S(1)}, u32[]{:S(2)}, u32[]{:S(2)}) %collective-permute-start.15) | collective-permute-done | bytes 524320 | tf_op jit(solution)/shard_map/ppermute | solution.py:354
  136.6 1.0 fusion.2
  137.5 1.5 collective-permute-start.16
  139.0 8.0 %collective-permute-done.11 = bf16[512,512]{1,0:T(8,128)(2,1)} collective-permute-done((bf16[512,512]{1,0:T(8,128)(2,1)S(1)}, bf16[512,512]{1,0:T(8,128)(2,1)}, u32[]{:S(2)}, u32[]{:S(2)}) %collective-permute-start.11) | collective-permute-done | bytes 524320 | tf_op jit(solution)/shard_map/ppermute | solution.py:354
  147.0 1.5 %fusion.3 = bf16[512,512]{1,0:T(8,128)(2,1)S(1)} fusion(f32[512,1024]{1,0:T(8,128)} %copy-done.5, bf16[512,512]{1,0:T(8,128)(2,1)} %collective-permute-done.11), kind=kLoop, calls=%fused_computation.11 | loop fusion | flops 786432 | bytes 2097152 | tf_op jit(solution)/shard_map/convert_element_type | solution.py:360
  148.5 1.3 collective-permute-done.16
  149.8 1.3 maximum_select_fusion
  (19 shorter events, 0.0 us)
Async XLA Ops:
  0.0 1.6 %copy-start = (bf16[1024,1024]{1,0:T(8,128)(2,1)S(1)}, bf16[1024,1024]{1,0:T(8,128)(2,1)}, u32[]{:S(2)}) copy-start(bf16[1024,1024]{1,0:T(8,128)(2,1)} %param.12) | copy-start | bytes 6291460
  0.0 8.5 %copy-start.11 = (f32[2,8,512]{2,1,0:T(8,128)S(1)}, f32[2,8,512]{2,1,0:T(8,128)}, u32[]{:S(2)}) copy-start(f32[2,8,512]{2,1,0:T(8,128)} %param.10) | copy-start | bytes 98308
  1.7 26.9 %collective-permute-start.1 = (bf16[1024,512]{1,0:T(8,128)(2,1)S(1)}, bf16[1024,512]{1,0:T(8,128)(2,1)}, u32[]{:S(2)}, u32[]{:S(2)}) collective-permute-start(bf16[1024,512]{1,0:T(8,128)(2,1)S(1)} %constant_dynamic-slice_fusion.refs_0_), channel_id=1, source_target_pairs={{4,0},{8,4},{12,8},{5,1},{9,5},{13,9},{6,2},{10,6},{14,10},{7,3},{... | collective-permute-start | bytes 3145736 | tf_op jit(solution)/shard_map/ppermute | solution.py:369
  4.1 26.6 %collective-permute-start = (bf16[1024,512]{1,0:T(8,128)(2,1)S(1)}, bf16[1024,512]{1,0:T(8,128)(2,1)}, u32[]{:S(2)}, u32[]{:S(2)}) collective-permute-start(bf16[1024,512]{1,0:T(8,128)(2,1)S(1)} %constant_dynamic-slice_fusion.refs_0_), channel_id=1, source_target_pairs={{0,4},{4,8},{8,12},{1,5},{5,9},{9,13},{2,6},{6,10},{10,14},{3,7},{... | collective-permute-start | bytes 3145736 | tf_op jit(solution)/shard_map/ppermute | solution.py:369
  24.5 32.6 %collective-permute-start.4 = (bf16[256,2048]{1,0:T(8,128)(2,1)}, bf16[256,2048]{1,0:T(8,128)(2,1)S(1)}, u32[]{:S(2)}, u32[]{:S(2)}) collective-permute-start(bf16[256,2048]{1,0:T(8,128)(2,1)} %get-tuple-element.25.first_ref), channel_id=1, source_target_pairs={{0,16},{16,0},{1,17},{17,1},{2,18},{18,2},{3,19},{19,3},{4,20},{20... | collective-permute-start | bytes 3145736 | tf_op jit(solution)/shard_map/ppermute | solution.py:369
  30.7 26.4 %collective-permute-start.2 = (bf16[1024,512]{1,0:T(8,128)(2,1)}, bf16[1024,512]{1,0:T(8,128)(2,1)}, u32[]{:S(2)}, u32[]{:S(2)}) collective-permute-start(bf16[1024,512]{1,0:T(8,128)(2,1)} %collective-permute-done.refs_1_), channel_id=1, source_target_pairs={{4,8},{8,12},{5,9},{9,13},{6,10},{10,14},{7,11},{11,15},{20,24},{2... | collective-permute-start | bytes 3145736 | tf_op jit(solution)/shard_map/ppermute | solution.py:369
  35.1 23.6 %collective-permute-start.3 = (bf16[1024,512]{1,0:T(8,128)(2,1)}, bf16[1024,512]{1,0:T(8,128)(2,1)}, u32[]{:S(2)}, u32[]{:S(2)}) collective-permute-start(bf16[1024,512]{1,0:T(8,128)(2,1)} %collective-permute-done.1.refs_6_), channel_id=1, source_target_pairs={{4,0},{8,4},{5,1},{9,5},{6,2},{10,6},{7,3},{11,7},{20,16},{24,20},... | collective-permute-start | bytes 3145736 | tf_op jit(solution)/shard_map/ppermute | solution.py:369
  53.8 15.8 %copy-start.6 = (f32[8,128,128]{2,1,0:T(8,128)S(1)}, f32[8,128,128]{2,1,0:T(8,128)}, u32[]{:S(2)}) copy-start(f32[8,128,128]{2,1,0:T(8,128)} %get-tuple-element.32) | copy-start | bytes 1572868
  53.8 15.8 %copy-start.7 = (bf16[8,128,128]{2,1,0:T(8,128)(2,1)S(1)}, bf16[8,128,128]{2,1,0:T(8,128)(2,1)}, u32[]{:S(2)}) copy-start(bf16[8,128,128]{2,1,0:T(8,128)(2,1)} %get-tuple-element.31) | copy-start | bytes 786436
  55.0 0.7 collective-permute-start.5
  55.7 26.4 %copy-start.12 = (s32[4]{0:T(128)S(1)}, s32[4]{0:T(128)}, u32[]{:S(2)}) copy-start(s32[4]{0:T(128)} %constant.32.clone) | copy-start | bytes 52
  57.1 18.1 %copy-start.8 = (bf16[256,2048]{1,0:T(8,128)(2,1)}, bf16[256,2048]{1,0:T(8,128)(2,1)S(1)}, u32[]{:S(2)}) copy-start(bf16[256,2048]{1,0:T(8,128)(2,1)S(1)} %collective-permute-done.4.first_ref) | copy-start | bytes 3145732
  58.7 10.9 %collective-permute-start.6 = (bf16[8,128,128]{2,1,0:T(8,128)(2,1)S(1)}, bf16[8,128,128]{2,1,0:T(8,128)(2,1)S(1)}, u32[]{:S(2)}, u32[]{:S(2)}) collective-permute-start(bf16[8,128,128]{2,1,0:T(8,128)(2,1)S(1)} %fusion), channel_id=1, source_target_pairs={{4,8},{5,9},{6,10},{7,11},{20,24},{21,25},{22,26},{23,27}} | collective-permute-start | bytes 786440 | tf_op jit(solution)/shard_map/ppermute | solution.py:369
  69.9 5.2 %collective-permute-start.7 = (bf16[8,128,128]{2,1,0:T(8,128)(2,1)S(1)}, bf16[8,128,128]{2,1,0:T(8,128)(2,1)S(1)}, u32[]{:S(2)}, u32[]{:S(2)}) collective-permute-start(bf16[8,128,128]{2,1,0:T(8,128)(2,1)S(1)} %fusion.1), channel_id=1, source_target_pairs={{8,12},{9,13},{10,14},{11,15},{24,28},{25,29},{26,30},{27,31}} | collective-permute-start | bytes 786440 | tf_op jit(solution)/shard_map/ppermute | solution.py:369
  71.2 25.0 %collective-permute-start.12 = (bf16[256,2048]{1,0:T(8,128)(2,1)}, bf16[256,2048]{1,0:T(8,128)(2,1)}, u32[]{:S(2)}, u32[]{:S(2)}) collective-permute-start(bf16[256,2048]{1,0:T(8,128)(2,1)} %get-tuple-element.28.second_ref), channel_id=1, source_target_pairs={{0,16},{16,0},{1,17},{17,1},{2,18},{18,2},{3,19},{19,3},{4,20},{20... | collective-permute-start | bytes 3145736 | tf_op jit(solution)/shard_map/ppermute | solution.py:369
  72.8 30.2 %collective-permute-start.8 = (bf16[1024,512]{1,0:T(8,128)(2,1)}, bf16[1024,512]{1,0:T(8,128)(2,1)}, u32[]{:S(2)}, u32[]{:S(2)}) collective-permute-start(bf16[1024,512]{1,0:T(8,128)(2,1)} %collective-permute-done.3.refs_4_), channel_id=1, source_target_pairs={{4,0},{5,1},{6,2},{7,3},{20,16},{21,17},{22,18},{23,19}} | collective-permute-start | bytes 3145736 | tf_op jit(solution)/shard_map/ppermute | solution.py:369
  75.2 34.5 %copy-start.9 = (bf16[8,128,128]{2,1,0:T(8,128)(2,1)}, bf16[8,128,128]{2,1,0:T(8,128)(2,1)S(1)}, u32[]{:S(2)}) copy-start(bf16[8,128,128]{2,1,0:T(8,128)(2,1)S(1)} %add.35.s_ref) | copy-start | bytes 786436
  75.2 27.8 %collective-permute-start.9 = (bf16[1024,512]{1,0:T(8,128)(2,1)}, bf16[1024,512]{1,0:T(8,128)(2,1)}, u32[]{:S(2)}, u32[]{:S(2)}) collective-permute-start(bf16[1024,512]{1,0:T(8,128)(2,1)} %collective-permute-done.2.refs_3_), channel_id=1, source_target_pairs={{8,12},{9,13},{10,14},{11,15},{24,28},{25,29},{26,30},{27,31}} | collective-permute-start | bytes 3145736 | tf_op jit(solution)/shard_map/ppermute | solution.py:369
  80.5 18.3 %collective-permute-start.13 = (bf16[8,128,128]{2,1,0:T(8,128)(2,1)S(1)}, bf16[8,128,128]{2,1,0:T(8,128)(2,1)S(1)}, u32[]{:S(2)}, u32[]{:S(2)}) collective-permute-start(bf16[8,128,128]{2,1,0:T(8,128)(2,1)S(1)} %add.35.s_ref), channel_id=1, source_target_pairs={{0,16},{16,0},{1,17},{17,1},{2,18},{18,2},{3,19},{19,3},{4,20},{20... | collective-permute-start | bytes 786440 | tf_op jit(solution)/shard_map/ppermute | solution.py:369
  98.9 0.7 copy-start.10
  103.0 1.2 copy-start.2
  109.6 1.0 copy-start.3
  110.6 9.4 %collective-permute-start.14 = (bf16[512,1024]{1,0:T(8,128)(2,1)}, bf16[512,1024]{1,0:T(8,128)(2,1)}, u32[]{:S(2)}, u32[]{:S(2)}) collective-permute-start(bf16[512,1024]{1,0:T(8,128)(2,1)} %get-tuple-element.42), channel_id=1, source_target_pairs={{0,1},{1,0},{2,3},{3,2},{4,5},{5,4},{6,7},{7,6},{8,9},{9,8},{10,11... | collective-permute-start | bytes 3145736 | tf_op jit(solution)/shard_map/ppermute | solution.py:354
  114.1 1.2 copy-start.1
  115.3 4.7 %copy-start.4 = (bf16[512,1024]{1,0:T(8,128)(2,1)S(1)}, bf16[512,1024]{1,0:T(8,128)(2,1)}, u32[]{:S(2)}) copy-start(bf16[512,1024]{1,0:T(8,128)(2,1)} %copy-done.3) | copy-start | bytes 3145732
  119.4 3.8 %collective-permute-start.10 = (bf16[512,1024]{1,0:T(8,128)(2,1)S(1)}, bf16[512,1024]{1,0:T(8,128)(2,1)S(1)}, u32[]{:S(2)}, u32[]{:S(2)}) collective-permute-start(bf16[512,1024]{1,0:T(8,128)(2,1)S(1)} %get-tuple-element.39), channel_id=1, source_target_pairs={{0,1},{1,0},{2,3},{3,2},{4,5},{5,4},{6,7},{7,6},{8,9},{9,8},{10,11... | collective-permute-start | bytes 3145736 | tf_op jit(solution)/shard_map/ppermute | solution.py:354
  121.7 14.8 %collective-permute-start.15 = (bf16[512,512]{1,0:T(8,128)(2,1)S(1)}, bf16[512,512]{1,0:T(8,128)(2,1)S(1)}, u32[]{:S(2)}, u32[]{:S(2)}) collective-permute-start(bf16[512,512]{1,0:T(8,128)(2,1)S(1)} %slice.30), channel_id=1, source_target_pairs={{0,2},{1,3},{2,0},{3,1},{4,6},{5,7},{6,4},{7,5},{8,10},{9,11},{10,... | collective-permute-start | bytes 1572872 | tf_op jit(solution)/shard_map/ppermute | solution.py:354
  123.7 1.3 copy-start.5
  125.1 21.9 %collective-permute-start.11 = (bf16[512,512]{1,0:T(8,128)(2,1)S(1)}, bf16[512,512]{1,0:T(8,128)(2,1)}, u32[]{:S(2)}, u32[]{:S(2)}) collective-permute-start(bf16[512,512]{1,0:T(8,128)(2,1)S(1)} %slice.31), channel_id=1, source_target_pairs={{0,2},{1,3},{2,0},{3,1},{4,6},{5,7},{6,4},{7,5},{8,10},{9,11},{10,... | collective-permute-start | bytes 1572872 | tf_op jit(solution)/shard_map/ppermute | solution.py:354
  137.5 12.3 %collective-permute-start.16 = (bf16[512,512]{1,0:T(8,128)(2,1)}, bf16[512,512]{1,0:T(8,128)(2,1)S(1)}, u32[]{:S(2)}, u32[]{:S(2)}) collective-permute-start(bf16[512,512]{1,0:T(8,128)(2,1)} %fusion.2), channel_id=1, source_target_pairs={{0,16},{16,0},{1,17},{17,1},{2,18},{18,2},{3,19},{19,3},{4,20},{20... | collective-permute-start | bytes 1572872 | tf_op jit(solution)/shard_map/ppermute | solution.py:369

commit v6 on v5

--- a/solution.py
+++ b/solution.py
@@ -14,6 +14,10 @@
 BASE = 8
 F32 = jnp.float32
 BF16 = jnp.bfloat16
+
+
+def tied(*values):
+    return lax.optimization_barrier(values)
 
 
 def mxu(left, right):
@@ -197,13 +201,11 @@
                 p_ref[head] = nexts[head][:, DK:].astype(BF16)
 
 
-def local_half(queries, keys, values, beta, start=None):
+def local_part(queries, keys, values, beta, skip, steps, start=None):
     tokens, width = queries.shape
     group = width // DK
     tile = CHUNK // REFL
-    steps = tokens // tile // 2
     first = start is None
-    skip = 0 if first else steps
     refl = pl.BlockSpec((tile, REFL, width), lambda c: (c + skip, 0, 0))
     whole = pl.BlockSpec((group, DK, 2 * DK), lambda c: (0, 0, 0))
     square = pl.BlockSpec((group, DK, DK), lambda c: (0, 0, 0))
@@ -232,9 +234,9 @@
         scratch_shapes=[pltpu.VMEM((group, DK, 2 * DK), F32)],
         compiler_params=pltpu.CompilerParams(vmem_limit_bytes=56 * 1024 * 1024),
         cost_estimate=pl.CostEstimate(
-            flops=200 * tokens * width * DK, bytes_accessed=8 * tokens * width, transcendentals=0
+            flops=400 * steps * tile * width * DK, bytes_accessed=16 * steps * tile * width, transcendentals=0
         ),
-        name="local_half",
+        name="local_part",
     )(queries, keys, values, beta, *([] if first else [start]))
 
 
@@ -242,11 +244,11 @@
     group = s_ref.shape[0]
     heads = range(group)
     cols = [slice(head * DK, (head + 1) * DK) for head in heads]
-    tile = min(128, first_ref.shape[0])
+    tile = min(128, second_ref.shape[0])
     for half, oe_ref in enumerate((first_ref, second_ref)):
         for at in range(0, oe_ref.shape[0], tile):
             rows = slice(at, at + tile)
-            to = slice(half * oe_ref.shape[0] + at, half * oe_ref.shape[0] + at + tile)
+            to = slice(half * first_ref.shape[0] + at, half * first_ref.shape[0] + at + tile)
             seen = [
                 mxu(oe_ref[rows, (group + head) * DK : (group + head + 1) * DK], s_ref[head])
                 for head in heads
@@ -263,7 +265,7 @@
 
 def normed_rows(first, second, incoming, gain):
     width = gain.shape[0]
-    tokens = 2 * first.shape[0]
+    tokens = first.shape[0] + second.shape[0]
     return pl.pallas_call(
         norm_kernel,
         in_specs=[pl.BlockSpec(memory_space=pltpu.VMEM)] * 4,
@@ -277,26 +279,28 @@
 
 
 def project_kernel(choices, place_ref, first_ref, a_ref, *refs):
-    weights = refs[: sum(choices)]
-    give_ref, keep_ref, held, sems = refs[sum(choices) :]
+    count = sum(sum(options) for options in choices)
+    weights = list(refs[:count])
+    give_ref, keep_ref, held, sems = refs[count:]
     half, block = len(choices) // 2, held.shape[2]
-    at = 0
+    whole = weights[0]
+
+    def fetch(slot, pieces):
+        row = 0
+        for piece in pieces:
+            rows = pl.ds(row, piece.shape[0])
+            pltpu.make_async_copy(piece, held.at[slot, rows], sems.at[slot]).start()
+            row += piece.shape[0]
+
     for slot, options in enumerate(choices):
-        here = weights[at : at + options]
-        at += options
-        if options == 1:
-            pltpu.make_async_copy(here[0], held.at[slot], sems.at[slot]).start()
-            continue
-        for option in range(2):
-
-            @pl.when(first_ref[slot] == 1 - option)
-            def _():
-                pltpu.make_async_copy(here[option], held.at[slot], sems.at[slot]).start()
-
-    at = 0
-    for slot, options in enumerate(choices):
-        pltpu.make_async_copy(weights[at], held.at[slot], sems.at[slot]).wait()
-        at += options
+        for option, pieces in enumerate(options):
+            taken, weights = weights[:pieces], weights[pieces:]
+            if len(options) == 1:
+                fetch(slot, taken)
+            else:
+                pl.when(first_ref[slot] == 1 - option)(functools.partial(fetch, slot, taken))
+    for slot in range(len(choices)):
+        pltpu.make_async_copy(whole, held.at[slot], sems.at[slot]).wait()
         product = mxu(a_ref[...], held[slot]).astype(BF16)
         place = place_ref[slot]
 
@@ -312,15 +316,16 @@
 def project(places, first, rows, weights):
     tokens, depth = rows.shape
     count = len(weights)
-    block = weights[0][0].shape[1]
-    choices = tuple(len(options) for options in weights)
+    block = weights[0][0][0].shape[1]
+    choices = tuple(tuple(len(pieces) for pieces in options) for options in weights)
+    flat = [piece for options in weights for pieces in options for piece in pieces]
     half = pl.BlockSpec(memory_space=pltpu.VMEM)
     shape = jax.ShapeDtypeStruct((tokens, count // 2 * block), BF16)
     return pl.pallas_call(
         functools.partial(project_kernel, choices),
         in_specs=[pl.BlockSpec(memory_space=pltpu.SMEM)] * 2
         + [half]
-        + [pl.BlockSpec(memory_space=pl.ANY)] * sum(choices),
+        + [pl.BlockSpec(memory_space=pl.ANY)] * len(flat),
         out_specs=[half, half],
         out_shape=[shape, shape],
         scratch_shapes=[
@@ -334,7 +339,7 @@
             transcendentals=0,
         ),
         name="project",
-    )(places, first, rows, *[w for options in weights for w in options])
+    )(places, first, rows, *flat)
 
 
 def halving_order(count):
@@ -346,23 +351,22 @@
     return order
 
 
-def head_sum(give, keep):
+def head_sum(give, keep, pieces):
     count = lax.axis_size("head")
     bit = 1
-    while bit < count:
-        pairs = [(i, i ^ bit) for i in range(count)]
-        got = lax.ppermute(give, "head", pairs)
+    while bit * 2 < count:
+        got = lax.ppermute(give, "head", [(i, i ^ bit) for i in range(count)])
         total = keep.astype(F32) + got.astype(F32)
-        bit *= 2
         half = total.shape[1] // 2
         give, keep = total[:, :half].astype(BF16), total[:, half:]
-        if bit >= count:
-            return total.astype(BF16)
-    return keep
-
-
-def tied(*values):
-    return lax.optimization_barrier(values)
+        bit *= 2
+    result = []
+    for sent, kept in zip(jnp.split(give, pieces), jnp.split(keep, pieces)):
+        got = lax.ppermute(sent, "head", [(i, i ^ bit) for i in range(count)])
+        if result:
+            kept, result[-1] = tied(kept, result[-1])
+        result.append((kept.astype(F32) + got.astype(F32)).astype(BF16))
+    return result
 
 
 def send(value, axis, pairs):
@@ -377,7 +381,7 @@
     beta_rows = beta.transpose(2, 0, 1).reshape(tokens * REFL, heads)
     half_cols = w_out.shape[1] // 2
     own = lax.dynamic_slice_in_dim(w_out, side * half_cols, half_cols, 1)
-    ring = ctx == head and ctx >= 4
+    ring = ctx == head and ctx == 4
     up, down = {0: own}, {0: own}
 
     def pass_up(step):
@@ -390,36 +394,43 @@
         pass_up(1)
         pass_down(1)
     swap = [(0, 1), (1, 0)]
-    near, middle = local_half(queries, keys, values, beta_rows)
+    steps = tokens * REFL // CHUNK
+    early = steps * 3 // 4
+    near, middle = local_part(queries, keys, values, beta_rows, 0, early)
     if ring:
         up[1], down[1], middle = tied(up[1], down[1], middle)
         pass_up(2)
         pass_down(2)
     near_other = send(near, "groups", swap)
-    far, state_end, total_end = local_half(queries, keys, values, beta_rows, middle)
+    far, state_end, total_end = local_part(
+        queries, keys, values, beta_rows, early, steps - early, middle
+    )
     far_other = send(far, "groups", swap)
 
     incoming = jnp.zeros((heads, DK, DK), BF16)
     outgoing = state_end.astype(BF16)
     for hop in range(ctx - 1):
         if hop == 1 and ring:
-            up[2], down[2], near_other, outgoing = tied(up[2], down[2], near_other, outgoing)
+            up[2], down[2], outgoing = tied(up[2], down[2], outgoing)
+            ahead = up[2].shape[0] // 4
+            last = [(i, i + 1) for i in range(2, ctx - 1)]
+            up_first = send(up[2][:ahead], "ctx", last)
+        if hop == 2 and ring:
+            up_first, near_other, outgoing = tied(up_first, near_other, outgoing)
         incoming = incoming + send(outgoing, "ctx", [(hop, hop + 1)])
         outgoing = (
             jnp.einsum("hde,hef->hdf", total_end, incoming, preferred_element_type=F32) + state_end
         ).astype(BF16)
     if ring:
-        for step in range(3, ctx):
-            pass_down(step)
-        up[2], incoming = tied(up[2], incoming)
-        for step in range(3, ctx):
-            pass_up(step)
-        weights = [(own,)] + [(up[k], down[ctx - k]) for k in range(1, ctx)]
+        pass_down(3)
+        up_rest, incoming = tied(up[2][ahead:], incoming)
+        up[3] = [up_first, send(up_rest, "ctx", last)]
+        weights = [([own],), ([up[1]], [down[3]]), ([up[2]], [down[2]]), (up[3], [down[1]])]
         targets = lax.rem(here + ctx - jnp.arange(ctx), ctx)
         first = (here >= jnp.arange(ctx)).astype(jnp.int32)
     else:
         whole = lax.all_gather(own, "ctx", axis=1, tiled=True)
-        weights = [(w,) for w in jnp.split(whole, head, axis=1)]
+        weights = [([w],) for w in jnp.split(whole, head, axis=1)]
         targets = jnp.arange(head)
         first = jnp.ones((head,), jnp.int32)
     incoming_other = send(incoming, "groups", swap)
@@ -428,9 +439,10 @@
     distance = targets ^ lax.axis_index("head")
     order = jnp.asarray(halving_order(head), jnp.int32)
     places = jnp.argmax(distance[:, None] == order[None, :], axis=1).astype(jnp.int32)
-    other_sum = head_sum(*project(places, first, other, weights))
-    mine_sum = head_sum(*project(places, first, mine, weights))
-    back = send(other_sum, "groups", swap)
+    mine, other = tied(mine, other)
+    other_sums = head_sum(*project(places, first, other, weights), 2)
+    (mine_sum,) = head_sum(*project(places, first, mine, weights), 1)
+    back = jnp.concatenate([send(piece, "groups", swap) for piece in other_sums], axis=0)
     blocks = mine_sum.shape[1] // half_cols
     if blocks == 1:
         return jnp.where(

time: 152 us -> 154 us (1.013)
  starting transfers between devices: 33.6 us -> 37.1 us
    unnamed x26 -> x23, local copies, waits for them, and re-layouts: 7.07 us -> 4.15 us
    ppermute x13 -> x15, starting transfers between devices: 30.9 us -> 33.1 us  [send(): return lax.ppermute(value, axis, pairs)]
    another operation x0 -> x1, other arithmetic: none -> 1.8 us
    add x2 -> x1, other arithmetic: 2 us -> 0.39 us  [head_sum(): total = keep.astype(F32) + got.astype(F32)]
    ppermute x4 -> x5, starting transfers between devices: 2.73 us -> 4.04 us  [the longest x3 3.41 us: head_sum(): got = lax.ppermute(sent, 'head', [(i, i ^ bit) for i in range(count)])]
    ppermute x4 -> x5, waiting for transfers between devices: 18.9 us -> 18.7 us  [the longest x3 18.7 us: head_sum(): got = lax.ppermute(sent, 'head', [(i, i ^ bit) for i in range(count)])]
    ppermute x13 -> x15, waiting for transfers between devices: 34 us -> 33.9 us  [send(): return lax.ppermute(value, axis, pairs)]
  transfers between devices with their start and end apart: 17 -> 20, of which waited for: 10 -> 10; matrix products, arithmetic and copies ran while one was open for 6% -> 8% of each run, Pallas kernels for 27% -> 27%
where the time goes in v6:
time: 154 us; the launch traced here: 153 us
  waiting for transfers between devices  52.7 us (34%)
  Pallas kernels  45.6 us (30%)
  starting transfers between devices  37.1 us (24%)
  other arithmetic  8.88 us (6%)
  local copies, waits for them, and re-layouts  7.04 us (5%)
  matrix products  1.56 us (1%)
    ppermute x15, waiting for transfers between devices, send(): return lax.ppermute(value, axis, pairs)  33.9 us
    ppermute x15, starting transfers between devices, send(): return lax.ppermute(value, axis, pairs)  33.1 us
    pallas_call x2, Pallas kernels, local_part(): pl.pallas_call(functools.partial(chunk_kernel, group, first), grid=(steps...  30.2 us
    ppermute x3, waiting for transfers between devices, head_sum(): got = lax.ppermute(sent, 'head', [(i, i ^ bit) for i in range(count)])  18.7 us
    pallas_call x2, Pallas kernels, project(): pl.pallas_call(functools.partial(project_kernel, choices), in_specs=[pl.B...  8.47 us
    pallas_call x2, Pallas kernels, normed_rows(): pl.pallas_call(norm_kernel, in_specs=[pl.BlockSpec(memory_space=pltpu.VME...  6.9 us
    unnamed x23, local copies, waits for them, and re-layouts  4.15 us
    ppermute x3, starting transfers between devices, head_sum(): got = lax.ppermute(sent, 'head', [(i, i ^ bit) for i in range(count)])  3.41 us
  transfers between devices with their start and end apart: 20, of which 10 were waited for; matrix products, arithmetic and copies ran while one was open for 8% of the time, Pallas kernels for 27%

profile of v6, /device:TPU:16, one launch (start us, length us, event | category | flops | bytes accessed | tf_op | source)
XLA Modules:
  0.0 153.1 jit_solution(16712183388755444407)
XLA Ops:
  0.0 1.6 %copy-done = bf16[1024,1024]{1,0:T(8,128)(2,1)S(1)} copy-done((bf16[1024,1024]{1,0:T(8,128)(2,1)S(1)}, bf16[1024,1024]{1,0:T(8,128)(2,1)}, u32[]{:S(2)}) %copy-start) | copy-done | bytes 2097176
  1.6 0.1 constant_dynamic-slice_fusion.refs_0_
  1.7 3.5 %collective-permute-start = (bf16[1024,512]{1,0:T(8,128)(2,1)S(1)}, bf16[1024,512]{1,0:T(8,128)(2,1)}, u32[]{:S(2)}, u32[]{:S(2)}) collective-permute-start(bf16[1024,512]{1,0:T(8,128)(2,1)S(1)} %constant_dynamic-slice_fusion.refs_0_), channel_id=1, source_target_pairs={{0,4},{4,8},{8,12},{1,5},{5,9},{9,13},{2,6},{6,10},{10,14},{3,7},{... | collective-permute-start | bytes 3145736 | tf_op jit(solution)/shard_map/ppermute | solution.py:373
  5.2 2.4 %collective-permute-start.1 = (bf16[1024,512]{1,0:T(8,128)(2,1)S(1)}, bf16[1024,512]{1,0:T(8,128)(2,1)}, u32[]{:S(2)}, u32[]{:S(2)}) collective-permute-start(bf16[1024,512]{1,0:T(8,128)(2,1)S(1)} %constant_dynamic-slice_fusion.refs_0_), channel_id=1, source_target_pairs={{4,0},{8,4},{12,8},{5,1},{9,5},{13,9},{6,2},{10,6},{14,10},{7,3},{... | collective-permute-start | bytes 3145736 | tf_op jit(solution)/shard_map/ppermute | solution.py:373
  7.6 1.0 copy.9
  8.6 21.3 %local_part.2 = (bf16[384,2048]{1,0:T(8,128)(2,1)}, f32[8,128,256]{2,1,0:T(8,128)}) custom-call(bf16[512,1024]{1,0:T(8,128)(2,1)} %q_ref.3, bf16[512,2,1024]{2,1,0:T(2,128)(2,1)} %k_ref.3, bf16[512,2,1024]{2,1,0:T(2,128)(2,1)} %v_ref.3, f32[1024,8]{1,0:T(8,128)} %bitcast.7), custom_call_target="tpu_custom_call" | custom-call | flops 20132659200 | bytes 6291456 | tf_op jit(solution)/shard_map/local_part/pallas_call | solution.py:213
  29.9 1.5 collective-permute-start.7
  31.4 0.0 collective-permute-done.refs_1_
  31.4 0.4 collective-permute-done.1.refs_7_
  31.8 4.0 %collective-permute-start.2 = (bf16[1024,512]{1,0:T(8,128)(2,1)}, bf16[1024,512]{1,0:T(8,128)(2,1)S(1)}, u32[]{:S(2)}, u32[]{:S(2)}) collective-permute-start(bf16[1024,512]{1,0:T(8,128)(2,1)} %collective-permute-done.refs_1_), channel_id=1, source_target_pairs={{4,8},{8,12},{5,9},{9,13},{6,10},{10,14},{7,11},{11,15},{20,24},{2... | collective-permute-start | bytes 3145736 | tf_op jit(solution)/shard_map/ppermute | solution.py:373
  35.9 2.8 %collective-permute-start.3 = (bf16[1024,512]{1,0:T(8,128)(2,1)}, bf16[1024,512]{1,0:T(8,128)(2,1)}, u32[]{:S(2)}, u32[]{:S(2)}) collective-permute-start(bf16[1024,512]{1,0:T(8,128)(2,1)} %collective-permute-done.1.refs_7_), channel_id=1, source_target_pairs={{4,0},{8,4},{5,1},{9,5},{6,2},{10,6},{7,3},{11,7},{20,16},{24,20},... | collective-permute-start | bytes 3145736 | tf_op jit(solution)/shard_map/ppermute | solution.py:373
  38.7 9.0 %local_part.3 = (bf16[128,2048]{1,0:T(8,128)(2,1)}, f32[8,128,128]{2,1,0:T(8,128)}, bf16[8,128,128]{2,1,0:T(8,128)(2,1)}) custom-call(bf16[512,1024]{1,0:T(8,128)(2,1)} %q_ref.3, bf16[512,2,1024]{2,1,0:T(2,128)(2,1)} %k_ref.3, bf16[512,2,1024]{2,1,0:T(2,128)(2,1)} %v_ref.3, f32[1024,8]{1,0:T(8,128)} %bitcast.8, f32[8,128,256]{2,1,0:T(8,128)} %get-tuple-element.33.refs_0_), custom_call_target="tpu_custom_call" | custom-call | flops 6710886400 | bytes 2097152 | tf_op jit(solution)/shard_map/local_part/pallas_call | solution.py:213
  47.7 1.1 convert_element_type.45
  48.8 0.7 collective-permute-start.4
  49.5 0.0 collective-permute-done.4
  49.5 1.3 fusion
  50.9 6.9 %collective-permute-done.2.refs_3_ = bf16[1024,512]{1,0:T(8,128)(2,1)S(1)} collective-permute-done((bf16[1024,512]{1,0:T(8,128)(2,1)}, bf16[1024,512]{1,0:T(8,128)(2,1)S(1)}, u32[]{:S(2)}, u32[]{:S(2)}) %collective-permute-start.2) | collective-permute-done | bytes 1048608 | tf_op jit(solution)/shard_map/ppermute | solution.py:373
  57.8 1.3 collective-permute-done.3.refs_4_
  59.1 1.3 collective-permute-start.5
  60.4 0.0 copy-start.10
  60.4 2.4 %collective-permute-start.6 = (bf16[256,512]{1,0:T(8,128)(2,1)S(1)}, bf16[256,512]{1,0:T(8,128)(2,1)S(1)}, u32[]{:S(2)}, u32[]{:S(2)}) collective-permute-start(bf16[256,512]{1,0:T(8,128)(2,1)S(1)} %slice.21), channel_id=1, source_target_pairs={{8,12},{9,13},{10,14},{11,15},{24,28},{25,29},{26,30},{27,31}} | collective-permute-start | bytes 786440 | tf_op jit(solution)/shard_map/ppermute | solution.py:373
  62.8 4.5 %collective-permute-done.5 = bf16[8,128,128]{2,1,0:T(8,128)(2,1)S(1)} collective-permute-done((bf16[8,128,128]{2,1,0:T(8,128)(2,1)S(1)}, bf16[8,128,128]{2,1,0:T(8,128)(2,1)S(1)}, u32[]{:S(2)}, u32[]{:S(2)}) %collective-permute-start.5) | collective-permute-done | bytes 262176 | tf_op jit(solution)/shard_map/ppermute | solution.py:373
  67.3 0.1 add.36
  67.4 0.2 fusion.1
  67.7 0.0 collective-permute-done.7.first_ref
  67.7 0.0 collective-permute-done.6.refs_5_
  67.7 3.4 %collective-permute-start.8 = (bf16[8,128,128]{2,1,0:T(8,128)(2,1)S(1)}, bf16[8,128,128]{2,1,0:T(8,128)(2,1)S(1)}, u32[]{:S(2)}, u32[]{:S(2)}) collective-permute-start(bf16[8,128,128]{2,1,0:T(8,128)(2,1)S(1)} %fusion.1), channel_id=1, source_target_pairs={{8,12},{9,13},{10,14},{11,15},{24,28},{25,29},{26,30},{27,31}} | collective-permute-start | bytes 786440 | tf_op jit(solution)/shard_map/ppermute | solution.py:373
  71.1 1.7 %collective-permute-start.11 = (bf16[1024,512]{1,0:T(8,128)(2,1)}, bf16[1024,512]{1,0:T(8,128)(2,1)}, u32[]{:S(2)}, u32[]{:S(2)}) collective-permute-start(bf16[1024,512]{1,0:T(8,128)(2,1)} %collective-permute-done.3.refs_4_), channel_id=1, source_target_pairs={{4,0},{5,1},{6,2},{7,3},{20,16},{21,17},{22,18},{23,19}} | collective-permute-start | bytes 3145736 | tf_op jit(solution)/shard_map/ppermute | solution.py:373
  72.8 0.9 slice.20
  73.7 1.2 collective-permute-done.8
  74.9 0.8 add.38.s_ref
  75.7 5.3 %collective-permute-start.12 = (bf16[768,512]{1,0:T(8,128)(2,1)}, bf16[768,512]{1,0:T(8,128)(2,1)}, u32[]{:S(2)}, u32[]{:S(2)}) collective-permute-start(bf16[768,512]{1,0:T(8,128)(2,1)} %slice.20), channel_id=1, source_target_pairs={{8,12},{9,13},{10,14},{11,15},{24,28},{25,29},{26,30},{27,31}} | collective-permute-start | bytes 2359304 | tf_op jit(solution)/shard_map/ppermute | solution.py:373
  80.9 0.9 collective-permute-start.9
  81.8 1.1 collective-permute-start.10
  83.0 0.8 iota_reduce_fusion
  83.8 3.5 %normed_rows.2.a_ref = bf16[512,1024]{1,0:T(8,128)(2,1)} custom-call(bf16[384,2048]{1,0:T(8,128)(2,1)} %get-tuple-element.31.first_ref, bf16[128,2048]{1,0:T(8,128)(2,1)} %get-tuple-element.34.second_ref, bf16[8,128,128]{2,1,0:T(8,128)(2,1)} %add.38.s_ref, f32[1,1024]{1,0:T(1,128)} %bitcast.10), custom_call_target="tpu_custom_call" | custom-call | flops 134217728 | bytes 3145728 | tf_op jit(solution)/shard_map/normed_rows/pallas_call | solution.py:269
  87.3 7.0 %collective-permute-done.9.second_ref = bf16[128,2048]{1,0:T(8,128)(2,1)} collective-permute-done((bf16[128,2048]{1,0:T(8,128)(2,1)}, bf16[128,2048]{1,0:T(8,128)(2,1)}, u32[]{:S(2)}, u32[]{:S(2)}) %collective-permute-start.9) | collective-permute-done | bytes 524320 | tf_op jit(solution)/shard_map/ppermute | solution.py:373
  94.2 2.8 %collective-permute-done.10.s_ref = bf16[8,128,128]{2,1,0:T(8,128)(2,1)} collective-permute-done((bf16[8,128,128]{2,1,0:T(8,128)(2,1)}, bf16[8,128,128]{2,1,0:T(8,128)(2,1)}, u32[]{:S(2)}, u32[]{:S(2)}) %collective-permute-start.10) | collective-permute-done | bytes 262176 | tf_op jit(solution)/shard_map/ppermute | solution.py:373
  97.1 3.4 %normed_rows.3.a_ref = bf16[512,1024]{1,0:T(8,128)(2,1)} custom-call(bf16[384,2048]{1,0:T(8,128)(2,1)} %copy-done.7, bf16[128,2048]{1,0:T(8,128)(2,1)} %collective-permute-done.9.second_ref, bf16[8,128,128]{2,1,0:T(8,128)(2,1)} %collective-permute-done.10.s_ref, f32[1,1024]{1,0:T(1,128)} %bitcast.11), custom_call_target="tpu_custom_call" | custom-call | flops 134217728 | bytes 3145728 | tf_op jit(solution)/shard_map/normed_rows/pallas_call | solution.py:269
  100.5 1.2 copy-done.2
  101.7 4.3 %project.3 = (bf16[512,1024]{1,0:T(8,128)(2,1)S(1)}, bf16[512,1024]{1,0:T(8,128)(2,1)S(1)}) custom-call(s32[4]{0:T(128)S(1)} %get-tuple-element.30.place_ref, s32[4]{0:T(128)S(1)} %compare_convert_fusion.first_ref, bf16[512,1024]{1,0:T(8,128)(2,1)S(1)} %copy-done.2, bf16[1024,512]{1,0:T(8,128)(2,1)S(1)} %constant_dynamic-slice_fusion.refs_0_, ...), custom_call_target="tpu_custom_call" | custom-call | flops 2147483648 | bytes 7340032 | tf_op jit(solution)/shard_map/project/pallas_call | solution.py:324
  106.0 0.1 collective-permute-start.15
  106.1 4.2 %project.2 = (bf16[512,1024]{1,0:T(8,128)(2,1)S(1)}, bf16[512,1024]{1,0:T(8,128)(2,1)S(1)}) custom-call(s32[4]{0:T(128)S(1)} %get-tuple-element.30.place_ref, s32[4]{0:T(128)S(1)} %compare_convert_fusion.first_ref, bf16[512,1024]{1,0:T(8,128)(2,1)S(1)} %copy-done.1, bf16[1024,512]{1,0:T(8,128)(2,1)S(1)} %constant_dynamic-slice_fusion.refs_0_, ...), custom_call_target="tpu_custom_call" | custom-call | flops 2147483648 | bytes 7340032 | tf_op jit(solution)/shard_map/project/pallas_call | solution.py:324
  110.3 0.6 collective-permute-start.13
  110.8 0.0 collective-permute-done.15
  110.8 1.8 %fusion.6 = (bf16[512,1024]{1,0:T(8,128)(2,1)S(1)}, f32[512,1024]{1,0:T(8,128)}) fusion(bf16[512,1024]{1,0:T(8,128)(2,1)S(1)} %collective-permute-done.15, bf16[512,1024]{1,0:T(8,128)(2,1)S(1)} %get-tuple-element.51), kind=kLoop, calls=%fused_computation.22 | loop fusion | flops 2097152 | bytes 5242880 | tf_op jit(solution)/shard_map/convert
  112.6 0.7 fusion.7
  113.4 1.3 collective-permute-start.16
  114.7 0.0 collective-permute-done.13
  114.7 0.4 convert_add_fusion.1
  115.1 1.3 copy-done.4
  116.4 0.1 slice.30
  116.5 0.8 collective-permute-start.14
  117.2 1.3 collective-permute-start.18
  118.5 4.3 %collective-permute-done.16 = bf16[256,512]{1,0:T(8,128)(2,1)} collective-permute-done((bf16[256,512]{1,0:T(8,128)(2,1)}, bf16[256,512]{1,0:T(8,128)(2,1)}, u32[]{:S(2)}, u32[]{:S(2)}) %collective-permute-start.16) | collective-permute-done | bytes 262176 | tf_op jit(solution)/shard_map/ppermute | solution.py:365
  122.8 1.4 fusion.3
  124.2 14.4 %collective-permute-done.18 = bf16[256,512]{1,0:T(8,128)(2,1)S(1)} collective-permute-done((bf16[256,512]{1,0:T(8,128)(2,1)S(1)}, bf16[256,512]{1,0:T(8,128)(2,1)S(1)}, u32[]{:S(2)}, u32[]{:S(2)}) %collective-permute-start.18) | collective-permute-done | bytes 262176 | tf_op jit(solution)/shard_map/ppermute | solution.py:365
  138.7 0.1 add_convert_fusion
  138.7 1.8 %collective-permute-start.19 = (bf16[256,512]{1,0:T(8,128)(2,1)S(1)}, bf16[256,512]{1,0:T(8,128)(2,1)S(1)}, u32[]{:S(2)}, u32[]{:S(2)}) collective-permute-start(bf16[256,512]{1,0:T(8,128)(2,1)S(1)} %add_convert_fusion), channel_id=1, source_target_pairs={{0,16},{16,0},{1,17},{17,1},{2,18},{18,2},{3,19},{19,3},{4,20},{20... | collective-permute-start | bytes 786440 | tf_op jit(solution)/shard_map/ppermute | solution.py:373
  140.5 0.3 collective-permute-start.17
  140.8 0.0 collective-permute-done.14
  140.8 1.2 fusion.2
  142.0 9.8 %collective-permute-done.17 = bf16[256,512]{1,0:T(8,128)(2,1)S(1)} collective-permute-done((bf16[256,512]{1,0:T(8,128)(2,1)S(1)}, bf16[256,512]{1,0:T(8,128)(2,1)S(1)}, u32[]{:S(2)}, u32[]{:S(2)}) %collective-permute-start.17) | collective-permute-done | bytes 262176 | tf_op jit(solution)/shard_map/ppermute | solution.py:373
  151.9 1.3 maximum_select_fusion
  (26 shorter events, 0.1 us)
Async XLA Ops:
  0.0 1.6 %copy-start = (bf16[1024,1024]{1,0:T(8,128)(2,1)S(1)}, bf16[1024,1024]{1,0:T(8,128)(2,1)}, u32[]{:S(2)}) copy-start(bf16[1024,1024]{1,0:T(8,128)(2,1)} %param.12) | copy-start | bytes 6291460
  0.0 7.6 %copy-start.9 = (f32[2,8,512]{2,1,0:T(8,128)S(1)}, f32[2,8,512]{2,1,0:T(8,128)}, u32[]{:S(2)}) copy-start(f32[2,8,512]{2,1,0:T(8,128)} %param.10) | copy-start | bytes 98308
  1.7 29.7 %collective-permute-start = (bf16[1024,512]{1,0:T(8,128)(2,1)S(1)}, bf16[1024,512]{1,0:T(8,128)(2,1)}, u32[]{:S(2)}, u32[]{:S(2)}) collective-permute-start(bf16[1024,512]{1,0:T(8,128)(2,1)S(1)} %constant_dynamic-slice_fusion.refs_0_), channel_id=1, source_target_pairs={{0,4},{4,8},{8,12},{1,5},{5,9},{9,13},{2,6},{6,10},{10,14},{3,7},{... | collective-permute-start | bytes 3145736 | tf_op jit(solution)/shard_map/ppermute | solution.py:373
  5.2 26.6 %collective-permute-start.1 = (bf16[1024,512]{1,0:T(8,128)(2,1)S(1)}, bf16[1024,512]{1,0:T(8,128)(2,1)}, u32[]{:S(2)}, u32[]{:S(2)}) collective-permute-start(bf16[1024,512]{1,0:T(8,128)(2,1)S(1)} %constant_dynamic-slice_fusion.refs_0_), channel_id=1, source_target_pairs={{4,0},{8,4},{12,8},{5,1},{9,5},{13,9},{6,2},{10,6},{14,10},{7,3},{... | collective-permute-start | bytes 3145736 | tf_op jit(solution)/shard_map/ppermute | solution.py:373
  29.9 37.8 %collective-permute-start.7 = (bf16[384,2048]{1,0:T(8,128)(2,1)}, bf16[384,2048]{1,0:T(8,128)(2,1)S(1)}, u32[]{:S(2)}, u32[]{:S(2)}) collective-permute-start(bf16[384,2048]{1,0:T(8,128)(2,1)} %get-tuple-element.31.first_ref), channel_id=1, source_target_pairs={{0,16},{16,0},{1,17},{17,1},{2,18},{18,2},{3,19},{19,3},{4,20},{20... | collective-permute-start | bytes 4718600 | tf_op jit(solution)/shard_map/ppermute | solution.py:373
  31.8 26.0 %collective-permute-start.2 = (bf16[1024,512]{1,0:T(8,128)(2,1)}, bf16[1024,512]{1,0:T(8,128)(2,1)S(1)}, u32[]{:S(2)}, u32[]{:S(2)}) collective-permute-start(bf16[1024,512]{1,0:T(8,128)(2,1)} %collective-permute-done.refs_1_), channel_id=1, source_target_pairs={{4,8},{8,12},{5,9},{9,13},{6,10},{10,14},{7,11},{11,15},{20,24},{2... | collective-permute-start | bytes 3145736 | tf_op jit(solution)/shard_map/ppermute | solution.py:373
  35.9 23.2 %collective-permute-start.3 = (bf16[1024,512]{1,0:T(8,128)(2,1)}, bf16[1024,512]{1,0:T(8,128)(2,1)}, u32[]{:S(2)}, u32[]{:S(2)}) collective-permute-start(bf16[1024,512]{1,0:T(8,128)(2,1)} %collective-permute-done.1.refs_7_), channel_id=1, source_target_pairs={{4,0},{8,4},{5,1},{9,5},{6,2},{10,6},{7,3},{11,7},{20,16},{24,20},... | collective-permute-start | bytes 3145736 | tf_op jit(solution)/shard_map/ppermute | solution.py:373
  47.7 19.8 %copy-start.6 = (f32[8,128,128]{2,1,0:T(8,128)S(1)}, f32[8,128,128]{2,1,0:T(8,128)}, u32[]{:S(2)}) copy-start(f32[8,128,128]{2,1,0:T(8,128)} %get-tuple-element.38) | copy-start | bytes 1572868
  47.7 19.8 %copy-start.8 = (bf16[8,128,128]{2,1,0:T(8,128)(2,1)S(1)}, bf16[8,128,128]{2,1,0:T(8,128)(2,1)}, u32[]{:S(2)}) copy-start(bf16[8,128,128]{2,1,0:T(8,128)(2,1)} %get-tuple-element.37) | copy-start | bytes 786436
  48.8 0.7 collective-permute-start.4
  57.8 16.0 %copy-start.3 = (bf16[1024,512]{1,0:T(8,128)(2,1)}, bf16[1024,512]{1,0:T(8,128)(2,1)S(1)}, u32[]{:S(2)}) copy-start(bf16[1024,512]{1,0:T(8,128)(2,1)S(1)} %collective-permute-done.2.refs_3_) | copy-start | bytes 3145732
  59.1 8.3 %collective-permute-start.5 = (bf16[8,128,128]{2,1,0:T(8,128)(2,1)S(1)}, bf16[8,128,128]{2,1,0:T(8,128)(2,1)S(1)}, u32[]{:S(2)}, u32[]{:S(2)}) collective-permute-start(bf16[8,128,128]{2,1,0:T(8,128)(2,1)S(1)} %fusion), channel_id=1, source_target_pairs={{4,8},{5,9},{6,10},{7,11},{20,24},{21,25},{22,26},{23,27}} | collective-permute-start | bytes 786440 | tf_op jit(solution)/shard_map/ppermute | solution.py:373
  60.4 22.6 %copy-start.10 = (s32[4]{0:T(128)S(1)}, s32[4]{0:T(128)}, u32[]{:S(2)}) copy-start(s32[4]{0:T(128)} %constant.32.clone) | copy-start | bytes 52
  60.4 7.3 %collective-permute-start.6 = (bf16[256,512]{1,0:T(8,128)(2,1)S(1)}, bf16[256,512]{1,0:T(8,128)(2,1)S(1)}, u32[]{:S(2)}, u32[]{:S(2)}) collective-permute-start(bf16[256,512]{1,0:T(8,128)(2,1)S(1)} %slice.21), channel_id=1, source_target_pairs={{8,12},{9,13},{10,14},{11,15},{24,28},{25,29},{26,30},{27,31}} | collective-permute-start | bytes 786440 | tf_op jit(solution)/shard_map/ppermute | solution.py:373
  67.7 8.0 %copy-start.7 = (bf16[384,2048]{1,0:T(8,128)(2,1)}, bf16[384,2048]{1,0:T(8,128)(2,1)S(1)}, u32[]{:S(2)}) copy-start(bf16[384,2048]{1,0:T(8,128)(2,1)S(1)} %collective-permute-done.7.first_ref) | copy-start | bytes 4718596
  67.7 7.2 %collective-permute-start.8 = (bf16[8,128,128]{2,1,0:T(8,128)(2,1)S(1)}, bf16[8,128,128]{2,1,0:T(8,128)(2,1)S(1)}, u32[]{:S(2)}, u32[]{:S(2)}) collective-permute-start(bf16[8,128,128]{2,1,0:T(8,128)(2,1)S(1)} %fusion.1), channel_id=1, source_target_pairs={{8,12},{9,13},{10,14},{11,15},{24,28},{25,29},{26,30},{27,31}} | collective-permute-start | bytes 786440 | tf_op jit(solution)/shard_map/ppermute | solution.py:373
  71.1 29.4 %collective-permute-start.11 = (bf16[1024,512]{1,0:T(8,128)(2,1)}, bf16[1024,512]{1,0:T(8,128)(2,1)}, u32[]{:S(2)}, u32[]{:S(2)}) collective-permute-start(bf16[1024,512]{1,0:T(8,128)(2,1)} %collective-permute-done.3.refs_4_), channel_id=1, source_target_pairs={{4,0},{5,1},{6,2},{7,3},{20,16},{21,17},{22,18},{23,19}} | collective-permute-start | bytes 3145736 | tf_op jit(solution)/shard_map/ppermute | solution.py:373
  75.7 24.8 %collective-permute-start.12 = (bf16[768,512]{1,0:T(8,128)(2,1)}, bf16[768,512]{1,0:T(8,128)(2,1)}, u32[]{:S(2)}, u32[]{:S(2)}) collective-permute-start(bf16[768,512]{1,0:T(8,128)(2,1)} %slice.20), channel_id=1, source_target_pairs={{8,12},{9,13},{10,14},{11,15},{24,28},{25,29},{26,30},{27,31}} | collective-permute-start | bytes 2359304 | tf_op jit(solution)/shard_map/ppermute | solution.py:373
  80.9 13.3 %collective-permute-start.9 = (bf16[128,2048]{1,0:T(8,128)(2,1)}, bf16[128,2048]{1,0:T(8,128)(2,1)}, u32[]{:S(2)}, u32[]{:S(2)}) collective-permute-start(bf16[128,2048]{1,0:T(8,128)(2,1)} %get-tuple-element.34.second_ref), channel_id=1, source_target_pairs={{0,16},{16,0},{1,17},{17,1},{2,18},{18,2},{3,19},{19,3},{4,20},{20... | collective-permute-start | bytes 1572872 | tf_op jit(solution)/shard_map/ppermute | solution.py:373
  81.8 15.2 %collective-permute-start.10 = (bf16[8,128,128]{2,1,0:T(8,128)(2,1)}, bf16[8,128,128]{2,1,0:T(8,128)(2,1)}, u32[]{:S(2)}, u32[]{:S(2)}) collective-permute-start(bf16[8,128,128]{2,1,0:T(8,128)(2,1)} %add.38.s_ref), channel_id=1, source_target_pairs={{0,16},{16,0},{1,17},{17,1},{2,18},{18,2},{3,19},{19,3},{4,20},{20... | collective-permute-start | bytes 786440 | tf_op jit(solution)/shard_map/ppermute | solution.py:373
  100.5 1.2 copy-start.2
  101.7 4.4 %copy-start.1 = (bf16[512,1024]{1,0:T(8,128)(2,1)S(1)}, bf16[512,1024]{1,0:T(8,128)(2,1)}, u32[]{:S(2)}) copy-start(bf16[512,1024]{1,0:T(8,128)(2,1)} %normed_rows.2.a_ref) | copy-start | bytes 3145732
  106.0 4.8 %collective-permute-start.15 = (bf16[512,1024]{1,0:T(8,128)(2,1)S(1)}, bf16[512,1024]{1,0:T(8,128)(2,1)S(1)}, u32[]{:S(2)}, u32[]{:S(2)}) collective-permute-start(bf16[512,1024]{1,0:T(8,128)(2,1)S(1)} %get-tuple-element.52), channel_id=1, source_target_pairs={{0,1},{1,0},{2,3},{3,2},{4,5},{5,4},{6,7},{7,6},{8,9},{9,8},{10,11... | collective-permute-start | bytes 3145736 | tf_op jit(solution)/shard_map/ppermute | solution.py:358
  110.3 4.4 %collective-permute-start.13 = (bf16[512,1024]{1,0:T(8,128)(2,1)S(1)}, bf16[512,1024]{1,0:T(8,128)(2,1)S(1)}, u32[]{:S(2)}, u32[]{:S(2)}) collective-permute-start(bf16[512,1024]{1,0:T(8,128)(2,1)S(1)} %get-tuple-element.49), channel_id=1, source_target_pairs={{0,1},{1,0},{2,3},{3,2},{4,5},{5,4},{6,7},{7,6},{8,9},{9,8},{10,11... | collective-permute-start | bytes 3145736 | tf_op jit(solution)/shard_map/ppermute | solution.py:358
  113.4 9.5 %collective-permute-start.16 = (bf16[256,512]{1,0:T(8,128)(2,1)}, bf16[256,512]{1,0:T(8,128)(2,1)}, u32[]{:S(2)}, u32[]{:S(2)}) collective-permute-start(bf16[256,512]{1,0:T(8,128)(2,1)} %get-tuple-element.60), channel_id=1, source_target_pairs={{0,2},{1,3},{2,0},{3,1},{4,6},{5,7},{6,4},{7,5},{8,10},{9,11},{10,... | collective-permute-start | bytes 786440 | tf_op jit(solution)/shard_map/ppermute | solution.py:365
  115.1 1.3 copy-start.4
  116.5 24.4 %collective-permute-start.14 = (bf16[512,512]{1,0:T(8,128)(2,1)S(1)}, bf16[512,512]{1,0:T(8,128)(2,1)}, u32[]{:S(2)}, u32[]{:S(2)}) collective-permute-start(bf16[512,512]{1,0:T(8,128)(2,1)S(1)} %slice.30), channel_id=1, source_target_pairs={{0,2},{1,3},{2,0},{3,1},{4,6},{5,7},{6,4},{7,5},{8,10},{9,11},{10,... | collective-permute-start | bytes 1572872 | tf_op jit(solution)/shard_map/ppermute | solution.py:365
  117.2 23.6 %copy-start.5 = (f32[512,1024]{1,0:T(8,128)S(1)}, f32[512,1024]{1,0:T(8,128)}, u32[]{:S(2)}) copy-start(f32[512,1024]{1,0:T(8,128)} %copy-done.4) | copy-start | bytes 6291460
  117.2 21.4 %collective-permute-start.18 = (bf16[256,512]{1,0:T(8,128)(2,1)S(1)}, bf16[256,512]{1,0:T(8,128)(2,1)S(1)}, u32[]{:S(2)}, u32[]{:S(2)}) collective-permute-start(bf16[256,512]{1,0:T(8,128)(2,1)S(1)} %get-tuple-element.59), channel_id=1, source_target_pairs={{0,2},{1,3},{2,0},{3,1},{4,6},{5,7},{6,4},{7,5},{8,10},{9,11},{10,... | collective-permute-start | bytes 786440 | tf_op jit(solution)/shard_map/ppermute | solution.py:365
  138.7 13.1 %collective-permute-start.19 = (bf16[256,512]{1,0:T(8,128)(2,1)S(1)}, bf16[256,512]{1,0:T(8,128)(2,1)S(1)}, u32[]{:S(2)}, u32[]{:S(2)}) collective-permute-start(bf16[256,512]{1,0:T(8,128)(2,1)S(1)} %add_convert_fusion), channel_id=1, source_target_pairs={{0,16},{16,0},{1,17},{17,1},{2,18},{18,2},{3,19},{19,3},{4,20},{20... | collective-permute-start | bytes 786440 | tf_op jit(solution)/shard_map/ppermute | solution.py:373
  140.5 11.3 %collective-permute-start.17 = (bf16[256,512]{1,0:T(8,128)(2,1)S(1)}, bf16[256,512]{1,0:T(8,128)(2,1)S(1)}, u32[]{:S(2)}, u32[]{:S(2)}) collective-permute-start(bf16[256,512]{1,0:T(8,128)(2,1)S(1)} %get-tuple-element.53), channel_id=1, source_target_pairs={{0,16},{16,0},{1,17},{17,1},{2,18},{18,2},{3,19},{19,3},{4,20},{20... | collective-permute-start | bytes 786440 | tf_op jit(solution)/shard_map/ppermute | solution.py:373

commit v7 on v6

--- a/solution.py
+++ b/solution.py
@@ -119,7 +119,7 @@
     if first:
         oe_ref, end_ref, state = refs
     else:
-        start_ref, oe_ref, s_ref, p_ref, state = refs
+        start_ref, oe_ref, s_ref, sent_ref, p_ref, state = refs
     chunk = pl.program_id(0)
     tokens = CHUNK // REFL
 
@@ -198,6 +198,7 @@
                 end_ref[head] = nexts[head]
             else:
                 s_ref[head] = nexts[head][:, :DK]
+                sent_ref[head] = nexts[head][:, :DK].astype(BF16)
                 p_ref[head] = nexts[head][:, DK:].astype(BF16)
 
 
@@ -221,13 +222,14 @@
         ]
         + ([] if first else [whole]),
         out_specs=[pl.BlockSpec((tile, 2 * width), lambda c: (c, 0))]
-        + ([whole] if first else [square, square]),
+        + ([whole] if first else [square] * 3),
         out_shape=[rows]
         + (
             [jax.ShapeDtypeStruct((group, DK, 2 * DK), F32)]
             if first
             else [
                 jax.ShapeDtypeStruct((group, DK, DK), F32),
+                jax.ShapeDtypeStruct((group, DK, DK), BF16),
                 jax.ShapeDtypeStruct((group, DK, DK), BF16),
             ]
         ),
@@ -244,8 +246,8 @@
     group = s_ref.shape[0]
     heads = range(group)
     cols = [slice(head * DK, (head + 1) * DK) for head in heads]
-    tile = min(128, second_ref.shape[0])
     for half, oe_ref in enumerate((first_ref, second_ref)):
+        tile = oe_ref.shape[0] // 2
         for at in range(0, oe_ref.shape[0], tile):
             rows = slice(at, at + tile)
             to = slice(half * first_ref.shape[0] + at, half * first_ref.shape[0] + at + tile)
@@ -351,22 +353,23 @@
     return order
 
 
-def head_sum(give, keep, pieces):
-    count = lax.axis_size("head")
+def head_pairs(bit):
+    return [(i, i ^ bit) for i in range(lax.axis_size("head"))]
+
+
+def head_halved(give, keep):
     bit = 1
-    while bit * 2 < count:
-        got = lax.ppermute(give, "head", [(i, i ^ bit) for i in range(count)])
+    while bit * 2 < lax.axis_size("head"):
+        got = lax.ppermute(give, "head", head_pairs(bit))
         total = keep.astype(F32) + got.astype(F32)
         half = total.shape[1] // 2
         give, keep = total[:, :half].astype(BF16), total[:, half:]
         bit *= 2
-    result = []
-    for sent, kept in zip(jnp.split(give, pieces), jnp.split(keep, pieces)):
-        got = lax.ppermute(sent, "head", [(i, i ^ bit) for i in range(count)])
-        if result:
-            kept, result[-1] = tied(kept, result[-1])
-        result.append((kept.astype(F32) + got.astype(F32)).astype(BF16))
-    return result
+    return give, keep
+
+
+def summed(keep, got):
+    return (keep.astype(F32) + got.astype(F32)).astype(BF16)
 
 
 def send(value, axis, pairs):
@@ -395,20 +398,19 @@
         pass_down(1)
     swap = [(0, 1), (1, 0)]
     steps = tokens * REFL // CHUNK
-    early = steps * 3 // 4
+    early = steps * 5 // 8
     near, middle = local_part(queries, keys, values, beta_rows, 0, early)
     if ring:
         up[1], down[1], middle = tied(up[1], down[1], middle)
         pass_up(2)
         pass_down(2)
     near_other = send(near, "groups", swap)
-    far, state_end, total_end = local_part(
+    far, state_end, outgoing, total_end = local_part(
         queries, keys, values, beta_rows, early, steps - early, middle
     )
     far_other = send(far, "groups", swap)
 
     incoming = jnp.zeros((heads, DK, DK), BF16)
-    outgoing = state_end.astype(BF16)
     for hop in range(ctx - 1):
         if hop == 1 and ring:
             up[2], down[2], outgoing = tied(up[2], down[2], outgoing)
@@ -433,6 +435,7 @@
         weights = [([w],) for w in jnp.split(whole, head, axis=1)]
         targets = jnp.arange(head)
         first = jnp.ones((head,), jnp.int32)
+    far_other, incoming = tied(far_other, incoming)
     incoming_other = send(incoming, "groups", swap)
     mine = normed_rows(near, far, incoming, gain)
     other = normed_rows(near_other, far_other, incoming_other, gain)
@@ -440,9 +443,20 @@
     order = jnp.asarray(halving_order(head), jnp.int32)
     places = jnp.argmax(distance[:, None] == order[None, :], axis=1).astype(jnp.int32)
     mine, other = tied(mine, other)
-    other_sums = head_sum(*project(places, first, other, weights), 2)
-    (mine_sum,) = head_sum(*project(places, first, mine, weights), 1)
-    back = jnp.concatenate([send(piece, "groups", swap) for piece in other_sums], axis=0)
+    give, keep = head_halved(*project(places, first, other, weights))
+    own_give, own_keep = head_halved(*project(places, first, mine, weights))
+    last_pairs = head_pairs(head // 2)
+    give_a, give_b = jnp.split(give, 2)
+    keep_a, keep_b = jnp.split(keep, 2)
+    got_a = send(give_a, "head", last_pairs)
+    got_b = send(give_b, "head", last_pairs)
+    got_a, own_give = tied(got_a, own_give)
+    back_a = send(summed(keep_a, got_a), "groups", swap)
+    own_got = send(own_give, "head", last_pairs)
+    back_a, got_b, keep_b = tied(back_a, got_b, keep_b)
+    back_b = send(summed(keep_b, got_b), "groups", swap)
+    mine_sum = summed(own_keep, own_got)
+    back = jnp.concatenate([back_a, back_b], axis=0)
     blocks = mine_sum.shape[1] // half_cols
     if blocks == 1:
         return jnp.where(

time: 154 us -> 137 us (0.89)
  waiting for transfers between devices: 52.7 us -> 33.6 us
  starting transfers between devices: 37.1 us -> 40.3 us
  other arithmetic: 8.88 us -> 7.06 us
    ppermute x5 -> x2, waiting for transfers between devices: 18.7 us -> 0.01 us  [head_halved(): got = lax.ppermute(give, 'head', head_pairs(bit))]
    ppermute x15 -> x18, starting transfers between devices: 33.1 us -> 39.7 us  [send(): return lax.ppermute(value, axis, pairs)]
    ppermute x5 -> x2, starting transfers between devices: 4.04 us -> 0.62 us  [head_halved(): got = lax.ppermute(give, 'head', head_pairs(bit))]
    convert_element_type x4 -> x2, other arithmetic: 3.81 us -> 2.54 us  [summed(): return (keep.astype(F32) + got.astype(F32)).astype(BF16)]
    ppermute x15 -> x18, waiting for transfers between devices: 33.9 us -> 33.6 us  [send(): return lax.ppermute(value, axis, pairs)]
    unnamed x23 -> x21, local copies, waits for them, and re-layouts: 4.15 us -> 4.18 us
  transfers between devices with their start and end apart: 20 -> 20, of which waited for: 10 -> 10; matrix products, arithmetic and copies ran while one was open for 8% -> 7% of each run, Pallas kernels for 27% -> 31%
where the time goes in v7:
time: 137 us; the launch traced here: 136 us
  Pallas kernels  45.7 us (33%)
  starting transfers between devices  40.3 us (29%)
  waiting for transfers between devices  33.6 us (25%)
  local copies, waits for them, and re-layouts  7.06 us (5%)
  other arithmetic  7.06 us (5%)
  matrix products  1.56 us (1%)
    ppermute x18, starting transfers between devices, send(): return lax.ppermute(value, axis, pairs)  39.7 us
    ppermute x18, waiting for transfers between devices, send(): return lax.ppermute(value, axis, pairs)  33.6 us
    pallas_call x2, Pallas kernels, local_part(): pl.pallas_call(functools.partial(chunk_kernel, group, first), grid=(steps...  30.4 us
    pallas_call x2, Pallas kernels, project(): pl.pallas_call(functools.partial(project_kernel, choices), in_specs=[pl.B...  8.47 us
    pallas_call x2, Pallas kernels, normed_rows(): pl.pallas_call(norm_kernel, in_specs=[pl.BlockSpec(memory_space=pltpu.VME...  6.88 us
    unnamed x21, local copies, waits for them, and re-layouts  4.18 us
  transfers between devices with their start and end apart: 20, of which 10 were waited for; matrix products, arithmetic and copies ran while one was open for 7% of the time, Pallas kernels for 31%

profile of v7, /device:TPU:16, one launch (start us, length us, event | category | flops | bytes accessed | tf_op | source)
XLA Modules:
  0.0 135.7 jit_solution(15090402357748153773)
XLA Ops:
  0.0 1.6 %copy-done = bf16[1024,1024]{1,0:T(8,128)(2,1)S(1)} copy-done((bf16[1024,1024]{1,0:T(8,128)(2,1)S(1)}, bf16[1024,1024]{1,0:T(8,128)(2,1)}, u32[]{:S(2)}) %copy-start) | copy-done | bytes 2097176
  1.6 0.1 constant_dynamic-slice_fusion.refs_0_
  1.7 2.4 %collective-permute-start.1 = (bf16[1024,512]{1,0:T(8,128)(2,1)S(1)}, bf16[1024,512]{1,0:T(8,128)(2,1)}, u32[]{:S(2)}, u32[]{:S(2)}) collective-permute-start(bf16[1024,512]{1,0:T(8,128)(2,1)S(1)} %constant_dynamic-slice_fusion.refs_0_), channel_id=1, source_target_pairs={{4,0},{8,4},{12,8},{5,1},{9,5},{13,9},{6,2},{10,6},{14,10},{7,3},{... | collective-permute-start | bytes 3145736 | tf_op jit(solution)/shard_map/ppermute | solution.py:376
  4.1 4.4 %collective-permute-start = (bf16[1024,512]{1,0:T(8,128)(2,1)S(1)}, bf16[1024,512]{1,0:T(8,128)(2,1)}, u32[]{:S(2)}, u32[]{:S(2)}) collective-permute-start(bf16[1024,512]{1,0:T(8,128)(2,1)S(1)} %constant_dynamic-slice_fusion.refs_0_), channel_id=1, source_target_pairs={{0,4},{4,8},{8,12},{1,5},{5,9},{9,13},{2,6},{6,10},{10,14},{3,7},{... | collective-permute-start | bytes 3145736 | tf_op jit(solution)/shard_map/ppermute | solution.py:376
  8.5 1.0 copy.9
  9.5 18.1 %local_part.2 = (bf16[320,2048]{1,0:T(8,128)(2,1)}, f32[8,128,256]{2,1,0:T(8,128)}) custom-call(bf16[512,1024]{1,0:T(8,128)(2,1)} %q_ref.3, bf16[512,2,1024]{2,1,0:T(2,128)(2,1)} %k_ref.3, bf16[512,2,1024]{2,1,0:T(2,128)(2,1)} %v_ref.3, f32[1024,8]{1,0:T(8,128)} %bitcast.7), custom_call_target="tpu_custom_call" | custom-call | flops 16777216000 | bytes 5242880 | tf_op jit(solution)/shard_map/local_part/pallas_call | solution.py:214
  27.6 1.5 %collective-permute-start.8 = (bf16[320,2048]{1,0:T(8,128)(2,1)}, bf16[320,2048]{1,0:T(8,128)(2,1)S(1)}, u32[]{:S(2)}, u32[]{:S(2)}) collective-permute-start(bf16[320,2048]{1,0:T(8,128)(2,1)} %get-tuple-element.37.first_ref), channel_id=1, source_target_pairs={{0,16},{16,0},{1,17},{17,1},{2,18},{18,2},{3,19},{19,3},{4,20},{20... | collective-permute-start | bytes 3932168 | tf_op jit(solution)/shard_map/ppermute | solution.py:376
  29.2 0.0 collective-permute-done.1.refs_7_
  29.2 1.5 %collective-permute-done.refs_1_ = bf16[1024,512]{1,0:T(8,128)(2,1)} collective-permute-done((bf16[1024,512]{1,0:T(8,128)(2,1)S(1)}, bf16[1024,512]{1,0:T(8,128)(2,1)}, u32[]{:S(2)}, u32[]{:S(2)}) %collective-permute-start) | collective-permute-done | bytes 1048608 | tf_op jit(solution)/shard_map/ppermute | solution.py:376
  30.7 4.4 %collective-permute-start.3 = (bf16[1024,512]{1,0:T(8,128)(2,1)}, bf16[1024,512]{1,0:T(8,128)(2,1)S(1)}, u32[]{:S(2)}, u32[]{:S(2)}) collective-permute-start(bf16[1024,512]{1,0:T(8,128)(2,1)} %collective-permute-done.refs_1_), channel_id=1, source_target_pairs={{4,8},{8,12},{5,9},{9,13},{6,10},{10,14},{7,11},{11,15},{20,24},{2... | collective-permute-start | bytes 3145736 | tf_op jit(solution)/shard_map/ppermute | solution.py:376
  35.1 2.5 %collective-permute-start.4 = (bf16[1024,512]{1,0:T(8,128)(2,1)}, bf16[1024,512]{1,0:T(8,128)(2,1)}, u32[]{:S(2)}, u32[]{:S(2)}) collective-permute-start(bf16[1024,512]{1,0:T(8,128)(2,1)} %collective-permute-done.1.refs_7_), channel_id=1, source_target_pairs={{4,0},{8,4},{5,1},{9,5},{6,2},{10,6},{7,3},{11,7},{20,16},{24,20},... | collective-permute-start | bytes 3145736 | tf_op jit(solution)/shard_map/ppermute | solution.py:376
  37.6 12.3 %local_part.3 = (bf16[192,2048]{1,0:T(8,128)(2,1)}, f32[8,128,128]{2,1,0:T(8,128)}, bf16[8,128,128]{2,1,0:T(8,128)(2,1)}, bf16[8,128,128]{2,1,0:T(8,128)(2,1)}) custom-call(bf16[512,1024]{1,0:T(8,128)(2,1)} %q_ref.3, bf16[512,2,1024]{2,1,0:T(2,128)(2,1)} %k_ref.3, bf16[512,2,1024]{2,1,0:T(2,128)(2,1)} %v_ref.3, f32[1024,8]{1,0:T(8,128)} %bitcast.8, ...), custom_call_target="tpu_custom_call" | custom-call | flops 10066329600 | bytes 3145728 | tf_op jit(solution)/shard_map/local_part/pallas_call | solution.py:214
  49.9 0.8 collective-permute-start.5
  50.7 0.0 collective-permute-done.5
  50.7 1.3 fusion
  52.0 4.6 %collective-permute-done.3.refs_3_ = bf16[1024,512]{1,0:T(8,128)(2,1)S(1)} collective-permute-done((bf16[1024,512]{1,0:T(8,128)(2,1)}, bf16[1024,512]{1,0:T(8,128)(2,1)S(1)}, u32[]{:S(2)}, u32[]{:S(2)}) %collective-permute-start.3) | collective-permute-done | bytes 1048608 | tf_op jit(solution)/shard_map/ppermute | solution.py:376
  56.6 1.3 collective-permute-done.4.refs_4_
  57.9 1.3 collective-permute-start.6
  59.3 2.4 %collective-permute-start.7 = (bf16[256,512]{1,0:T(8,128)(2,1)S(1)}, bf16[256,512]{1,0:T(8,128)(2,1)S(1)}, u32[]{:S(2)}, u32[]{:S(2)}) collective-permute-start(bf16[256,512]{1,0:T(8,128)(2,1)S(1)} %slice.21), channel_id=1, source_target_pairs={{8,12},{9,13},{10,14},{11,15},{24,28},{25,29},{26,30},{27,31}} | collective-permute-start | bytes 786440 | tf_op jit(solution)/shard_map/ppermute | solution.py:376
  61.7 0.0 copy-start.9
  61.7 1.6 %collective-permute-start.2 = (bf16[192,2048]{1,0:T(8,128)(2,1)}, bf16[192,2048]{1,0:T(8,128)(2,1)}, u32[]{:S(2)}, u32[]{:S(2)}) collective-permute-start(bf16[192,2048]{1,0:T(8,128)(2,1)} %get-tuple-element.40.second_ref), channel_id=1, source_target_pairs={{0,16},{16,0},{1,17},{17,1},{2,18},{18,2},{3,19},{19,3},{4,20},{20... | collective-permute-start | bytes 2359304 | tf_op jit(solution)/shard_map/ppermute | solution.py:376
  63.3 2.9 %collective-permute-done.6 = bf16[8,128,128]{2,1,0:T(8,128)(2,1)S(1)} collective-permute-done((bf16[8,128,128]{2,1,0:T(8,128)(2,1)S(1)}, bf16[8,128,128]{2,1,0:T(8,128)(2,1)S(1)}, u32[]{:S(2)}, u32[]{:S(2)}) %collective-permute-start.6) | collective-permute-done | bytes 262176 | tf_op jit(solution)/shard_map/ppermute | solution.py:376
  66.2 0.1 add.36
  66.3 0.2 fusion.1
  66.5 0.0 collective-permute-done.8.first_ref
  66.5 0.0 collective-permute-done.7.refs_5_
  66.6 3.3 %collective-permute-start.9 = (bf16[8,128,128]{2,1,0:T(8,128)(2,1)S(1)}, bf16[8,128,128]{2,1,0:T(8,128)(2,1)S(1)}, u32[]{:S(2)}, u32[]{:S(2)}) collective-permute-start(bf16[8,128,128]{2,1,0:T(8,128)(2,1)S(1)} %fusion.1), channel_id=1, source_target_pairs={{8,12},{9,13},{10,14},{11,15},{24,28},{25,29},{26,30},{27,31}} | collective-permute-start | bytes 786440 | tf_op jit(solution)/shard_map/ppermute | solution.py:376
  69.9 1.7 %collective-permute-start.11 = (bf16[1024,512]{1,0:T(8,128)(2,1)}, bf16[1024,512]{1,0:T(8,128)(2,1)}, u32[]{:S(2)}, u32[]{:S(2)}) collective-permute-start(bf16[1024,512]{1,0:T(8,128)(2,1)} %collective-permute-done.4.refs_4_), channel_id=1, source_target_pairs={{4,0},{5,1},{6,2},{7,3},{20,16},{21,17},{22,18},{23,19}} | collective-permute-start | bytes 3145736 | tf_op jit(solution)/shard_map/ppermute | solution.py:376
  71.6 0.9 slice.20
  72.5 1.3 collective-permute-done.9
  73.8 0.8 add.38.s_ref
  74.5 5.3 %collective-permute-start.12 = (bf16[768,512]{1,0:T(8,128)(2,1)}, bf16[768,512]{1,0:T(8,128)(2,1)}, u32[]{:S(2)}, u32[]{:S(2)}) collective-permute-start(bf16[768,512]{1,0:T(8,128)(2,1)} %slice.20), channel_id=1, source_target_pairs={{8,12},{9,13},{10,14},{11,15},{24,28},{25,29},{26,30},{27,31}} | collective-permute-start | bytes 2359304 | tf_op jit(solution)/shard_map/ppermute | solution.py:376
  79.8 0.0 collective-permute-done.2.second_ref
  79.8 1.5 %collective-permute-start.10 = (bf16[8,128,128]{2,1,0:T(8,128)(2,1)}, bf16[8,128,128]{2,1,0:T(8,128)(2,1)}, u32[]{:S(2)}, u32[]{:S(2)}) collective-permute-start(bf16[8,128,128]{2,1,0:T(8,128)(2,1)} %add.38.s_ref), channel_id=1, source_target_pairs={{0,16},{16,0},{1,17},{17,1},{2,18},{18,2},{3,19},{19,3},{4,20},{20... | collective-permute-start | bytes 786440 | tf_op jit(solution)/shard_map/ppermute | solution.py:376
  81.4 0.7 iota_reduce_fusion
  82.1 3.5 %normed_rows.2.a_ref = bf16[512,1024]{1,0:T(8,128)(2,1)} custom-call(bf16[320,2048]{1,0:T(8,128)(2,1)} %get-tuple-element.37.first_ref, bf16[192,2048]{1,0:T(8,128)(2,1)} %get-tuple-element.40.second_ref, bf16[8,128,128]{2,1,0:T(8,128)(2,1)} %add.38.s_ref, f32[1,1024]{1,0:T(1,128)} %bitcast.10), custom_call_target="tpu_custom_call" | custom-call | flops 134217728 | bytes 3145728 | tf_op jit(solution)/shard_map/normed_rows/pallas_call | solution.py:271
  85.6 1.0 collective-permute-done.10.s_ref
  86.5 3.4 %normed_rows.3.a_ref = bf16[512,1024]{1,0:T(8,128)(2,1)} custom-call(bf16[320,2048]{1,0:T(8,128)(2,1)} %copy-done.6, bf16[192,2048]{1,0:T(8,128)(2,1)} %collective-permute-done.2.second_ref, bf16[8,128,128]{2,1,0:T(8,128)(2,1)} %collective-permute-done.10.s_ref, f32[1,1024]{1,0:T(1,128)} %bitcast.11), custom_call_target="tpu_custom_call" | custom-call | flops 134217728 | bytes 3145728 | tf_op jit(solution)/shard_map/normed_rows/pallas_call | solution.py:271
  89.9 0.0 collective-permute-done.11.refs_2_
  89.9 2.1 %collective-permute-done.12.refs_6_ = bf16[768,512]{1,0:T(8,128)(2,1)} collective-permute-done((bf16[768,512]{1,0:T(8,128)(2,1)}, bf16[768,512]{1,0:T(8,128)(2,1)}, u32[]{:S(2)}, u32[]{:S(2)}) %collective-permute-start.12) | collective-permute-done | bytes 786464 | tf_op jit(solution)/shard_map/ppermute | solution.py:376
  92.0 1.2 copy-done.2
  93.2 4.3 %project.3 = (bf16[512,1024]{1,0:T(8,128)(2,1)S(1)}, bf16[512,1024]{1,0:T(8,128)(2,1)S(1)}) custom-call(s32[4]{0:T(128)S(1)} %get-tuple-element.36.place_ref, s32[4]{0:T(128)S(1)} %compare_convert_fusion.first_ref, bf16[512,1024]{1,0:T(8,128)(2,1)S(1)} %copy-done.2, bf16[1024,512]{1,0:T(8,128)(2,1)S(1)} %constant_dynamic-slice_fusion.refs_0_, ...), custom_call_target="tpu_custom_call" | custom-call | flops 2147483648 | bytes 7340032 | tf_op jit(solution)/shard_map/project/pallas_call | solution.py:326
  97.6 0.1 collective-permute-start.14
  97.7 4.2 %project.2 = (bf16[512,1024]{1,0:T(8,128)(2,1)S(1)}, bf16[512,1024]{1,0:T(8,128)(2,1)S(1)}) custom-call(s32[4]{0:T(128)S(1)} %get-tuple-element.36.place_ref, s32[4]{0:T(128)S(1)} %compare_convert_fusion.first_ref, bf16[512,1024]{1,0:T(8,128)(2,1)S(1)} %copy-done.1, bf16[1024,512]{1,0:T(8,128)(2,1)S(1)} %constant_dynamic-slice_fusion.refs_0_, ...), custom_call_target="tpu_custom_call" | custom-call | flops 2147483648 | bytes 7340032 | tf_op jit(solution)/shard_map/project/pallas_call | solution.py:326
  101.8 0.6 collective-permute-start.13
  102.4 0.0 collective-permute-done.14
  102.4 0.5 fusion.6
  102.9 0.7 fusion.8
  103.6 1.5 %collective-permute-start.18 = (bf16[256,512]{1,0:T(8,128)(2,1)}, bf16[256,512]{1,0:T(8,128)(2,1)}, u32[]{:S(2)}, u32[]{:S(2)}) collective-permute-start(bf16[256,512]{1,0:T(8,128)(2,1)} %get-tuple-element.71), channel_id=1, source_target_pairs={{0,2},{1,3},{2,0},{3,1},{4,6},{5,7},{6,4},{7,5},{8,10},{9,11},{10,... | collective-permute-start | bytes 786440 | tf_op jit(solution)/shard_map/ppermute | solution.py:376
  105.1 0.5 collective-permute-start.15
  105.6 0.4 convert_add_fusion.1
  106.0 1.3 copy-done.4
  107.3 0.1 slice.30
  107.4 10.2 %collective-permute-done.15 = bf16[256,512]{1,0:T(8,128)(2,1)S(1)} collective-permute-done((bf16[256,512]{1,0:T(8,128)(2,1)S(1)}, bf16[256,512]{1,0:T(8,128)(2,1)S(1)}, u32[]{:S(2)}, u32[]{:S(2)}) %collective-permute-start.15) | collective-permute-done | bytes 262176 | tf_op jit(solution)/shard_map/ppermute | solution.py:376
  117.7 0.8 fusion.7
  118.5 1.5 %collective-permute-start.17 = (bf16[256,512]{1,0:T(8,128)(2,1)}, bf16[256,512]{1,0:T(8,128)(2,1)S(1)}, u32[]{:S(2)}, u32[]{:S(2)}) collective-permute-start(bf16[256,512]{1,0:T(8,128)(2,1)} %get-tuple-element.68), channel_id=1, source_target_pairs={{0,16},{16,0},{1,17},{17,1},{2,18},{18,2},{3,19},{19,3},{4,20},{20... | collective-permute-start | bytes 786440 | tf_op jit(solution)/shard_map/ppermute | solution.py:376
  120.0 1.5 %collective-permute-start.16 = (bf16[512,512]{1,0:T(8,128)(2,1)S(1)}, bf16[512,512]{1,0:T(8,128)(2,1)}, u32[]{:S(2)}, u32[]{:S(2)}) collective-permute-start(bf16[512,512]{1,0:T(8,128)(2,1)S(1)} %slice.30), channel_id=1, source_target_pairs={{0,2},{1,3},{2,0},{3,1},{4,6},{5,7},{6,4},{7,5},{8,10},{9,11},{10,... | collective-permute-start | bytes 1572872 | tf_op jit(solution)/shard_map/ppermute | solution.py:376
  121.5 0.0 collective-permute-done.18
  121.5 4.6 %collective-permute-done.17 = bf16[256,512]{1,0:T(8,128)(2,1)S(1)} collective-permute-done((bf16[256,512]{1,0:T(8,128)(2,1)}, bf16[256,512]{1,0:T(8,128)(2,1)S(1)}, u32[]{:S(2)}, u32[]{:S(2)}) %collective-permute-start.17) | collective-permute-done | bytes 262176 | tf_op jit(solution)/shard_map/ppermute | solution.py:376
  126.1 1.0 add_convert_fusion
  127.1 1.6 %collective-permute-start.19 = (bf16[256,512]{1,0:T(8,128)(2,1)S(1)}, bf16[256,512]{1,0:T(8,128)(2,1)S(1)}, u32[]{:S(2)}, u32[]{:S(2)}) collective-permute-start(bf16[256,512]{1,0:T(8,128)(2,1)S(1)} %add_convert_fusion), channel_id=1, source_target_pairs={{0,16},{16,0},{1,17},{17,1},{2,18},{18,2},{3,19},{19,3},{4,20},{20... | collective-permute-start | bytes 786440 | tf_op jit(solution)/shard_map/ppermute | solution.py:376
  128.7 4.1 %collective-permute-done.16 = bf16[512,512]{1,0:T(8,128)(2,1)} collective-permute-done((bf16[512,512]{1,0:T(8,128)(2,1)S(1)}, bf16[512,512]{1,0:T(8,128)(2,1)}, u32[]{:S(2)}, u32[]{:S(2)}) %collective-permute-start.16) | collective-permute-done | bytes 524320 | tf_op jit(solution)/shard_map/ppermute | solution.py:376
  132.8 1.5 %fusion.2 = bf16[512,512]{1,0:T(8,128)(2,1)S(1)} fusion(f32[512,1024]{1,0:T(8,128)} %copy-done.4, bf16[512,512]{1,0:T(8,128)(2,1)} %collective-permute-done.16), kind=kLoop, calls=%fused_computation.8 | loop fusion | flops 786432 | bytes 2097152 | tf_op jit(solution)/shard_map/convert_element_type | solution.py:372
  134.4 1.3 maximum_select_fusion
  (23 shorter events, 0.1 us)
Async XLA Ops:
  0.0 1.6 %copy-start = (bf16[1024,1024]{1,0:T(8,128)(2,1)S(1)}, bf16[1024,1024]{1,0:T(8,128)(2,1)}, u32[]{:S(2)}) copy-start(bf16[1024,1024]{1,0:T(8,128)(2,1)} %param.12) | copy-start | bytes 6291460
  0.0 8.5 %copy-start.8 = (f32[2,8,512]{2,1,0:T(8,128)S(1)}, f32[2,8,512]{2,1,0:T(8,128)}, u32[]{:S(2)}) copy-start(f32[2,8,512]{2,1,0:T(8,128)} %param.10) | copy-start | bytes 98308
  1.7 27.5 %collective-permute-start.1 = (bf16[1024,512]{1,0:T(8,128)(2,1)S(1)}, bf16[1024,512]{1,0:T(8,128)(2,1)}, u32[]{:S(2)}, u32[]{:S(2)}) collective-permute-start(bf16[1024,512]{1,0:T(8,128)(2,1)S(1)} %constant_dynamic-slice_fusion.refs_0_), channel_id=1, source_target_pairs={{4,0},{8,4},{12,8},{5,1},{9,5},{13,9},{6,2},{10,6},{14,10},{7,3},{... | collective-permute-start | bytes 3145736 | tf_op jit(solution)/shard_map/ppermute | solution.py:376
  4.1 26.6 %collective-permute-start = (bf16[1024,512]{1,0:T(8,128)(2,1)S(1)}, bf16[1024,512]{1,0:T(8,128)(2,1)}, u32[]{:S(2)}, u32[]{:S(2)}) collective-permute-start(bf16[1024,512]{1,0:T(8,128)(2,1)S(1)} %constant_dynamic-slice_fusion.refs_0_), channel_id=1, source_target_pairs={{0,4},{4,8},{8,12},{1,5},{5,9},{9,13},{2,6},{6,10},{10,14},{3,7},{... | collective-permute-start | bytes 3145736 | tf_op jit(solution)/shard_map/ppermute | solution.py:376
  27.6 38.9 %collective-permute-start.8 = (bf16[320,2048]{1,0:T(8,128)(2,1)}, bf16[320,2048]{1,0:T(8,128)(2,1)S(1)}, u32[]{:S(2)}, u32[]{:S(2)}) collective-permute-start(bf16[320,2048]{1,0:T(8,128)(2,1)} %get-tuple-element.37.first_ref), channel_id=1, source_target_pairs={{0,16},{16,0},{1,17},{17,1},{2,18},{18,2},{3,19},{19,3},{4,20},{20... | collective-permute-start | bytes 3932168 | tf_op jit(solution)/shard_map/ppermute | solution.py:376
  30.7 26.0 %collective-permute-start.3 = (bf16[1024,512]{1,0:T(8,128)(2,1)}, bf16[1024,512]{1,0:T(8,128)(2,1)S(1)}, u32[]{:S(2)}, u32[]{:S(2)}) collective-permute-start(bf16[1024,512]{1,0:T(8,128)(2,1)} %collective-permute-done.refs_1_), channel_id=1, source_target_pairs={{4,8},{8,12},{5,9},{9,13},{6,10},{10,14},{7,11},{11,15},{20,24},{2... | collective-permute-start | bytes 3145736 | tf_op jit(solution)/shard_map/ppermute | solution.py:376
  35.1 22.8 %collective-permute-start.4 = (bf16[1024,512]{1,0:T(8,128)(2,1)}, bf16[1024,512]{1,0:T(8,128)(2,1)}, u32[]{:S(2)}, u32[]{:S(2)}) collective-permute-start(bf16[1024,512]{1,0:T(8,128)(2,1)} %collective-permute-done.1.refs_7_), channel_id=1, source_target_pairs={{4,0},{8,4},{5,1},{9,5},{6,2},{10,6},{7,3},{11,7},{20,16},{24,20},... | collective-permute-start | bytes 3145736 | tf_op jit(solution)/shard_map/ppermute | solution.py:376
  49.9 16.4 %copy-start.5 = (f32[8,128,128]{2,1,0:T(8,128)S(1)}, f32[8,128,128]{2,1,0:T(8,128)}, u32[]{:S(2)}) copy-start(f32[8,128,128]{2,1,0:T(8,128)} %get-tuple-element.45) | copy-start | bytes 1572868
  49.9 16.4 %copy-start.7 = (bf16[8,128,128]{2,1,0:T(8,128)(2,1)S(1)}, bf16[8,128,128]{2,1,0:T(8,128)(2,1)}, u32[]{:S(2)}) copy-start(bf16[8,128,128]{2,1,0:T(8,128)(2,1)} %get-tuple-element.43) | copy-start | bytes 786436
  49.9 0.8 collective-permute-start.5
  56.6 15.9 %copy-start.3 = (bf16[1024,512]{1,0:T(8,128)(2,1)}, bf16[1024,512]{1,0:T(8,128)(2,1)S(1)}, u32[]{:S(2)}) copy-start(bf16[1024,512]{1,0:T(8,128)(2,1)S(1)} %collective-permute-done.3.refs_3_) | copy-start | bytes 3145732
  57.9 8.3 %collective-permute-start.6 = (bf16[8,128,128]{2,1,0:T(8,128)(2,1)S(1)}, bf16[8,128,128]{2,1,0:T(8,128)(2,1)S(1)}, u32[]{:S(2)}, u32[]{:S(2)}) collective-permute-start(bf16[8,128,128]{2,1,0:T(8,128)(2,1)S(1)} %fusion), channel_id=1, source_target_pairs={{4,8},{5,9},{6,10},{7,11},{20,24},{21,25},{22,26},{23,27}} | collective-permute-start | bytes 786440 | tf_op jit(solution)/shard_map/ppermute | solution.py:376
  59.3 7.3 %collective-permute-start.7 = (bf16[256,512]{1,0:T(8,128)(2,1)S(1)}, bf16[256,512]{1,0:T(8,128)(2,1)S(1)}, u32[]{:S(2)}, u32[]{:S(2)}) collective-permute-start(bf16[256,512]{1,0:T(8,128)(2,1)S(1)} %slice.21), channel_id=1, source_target_pairs={{8,12},{9,13},{10,14},{11,15},{24,28},{25,29},{26,30},{27,31}} | collective-permute-start | bytes 786440 | tf_op jit(solution)/shard_map/ppermute | solution.py:376
  61.7 19.7 %copy-start.9 = (s32[4]{0:T(128)S(1)}, s32[4]{0:T(128)}, u32[]{:S(2)}) copy-start(s32[4]{0:T(128)} %constant.32.clone) | copy-start | bytes 52
  61.7 18.2 %collective-permute-start.2 = (bf16[192,2048]{1,0:T(8,128)(2,1)}, bf16[192,2048]{1,0:T(8,128)(2,1)}, u32[]{:S(2)}, u32[]{:S(2)}) collective-permute-start(bf16[192,2048]{1,0:T(8,128)(2,1)} %get-tuple-element.40.second_ref), channel_id=1, source_target_pairs={{0,16},{16,0},{1,17},{17,1},{2,18},{18,2},{3,19},{19,3},{4,20},{20... | collective-permute-start | bytes 2359304 | tf_op jit(solution)/shard_map/ppermute | solution.py:376
  66.5 8.0 %copy-start.6 = (bf16[320,2048]{1,0:T(8,128)(2,1)}, bf16[320,2048]{1,0:T(8,128)(2,1)S(1)}, u32[]{:S(2)}) copy-start(bf16[320,2048]{1,0:T(8,128)(2,1)S(1)} %collective-permute-done.8.first_ref) | copy-start | bytes 3932164
  66.6 7.2 %collective-permute-start.9 = (bf16[8,128,128]{2,1,0:T(8,128)(2,1)S(1)}, bf16[8,128,128]{2,1,0:T(8,128)(2,1)S(1)}, u32[]{:S(2)}, u32[]{:S(2)}) collective-permute-start(bf16[8,128,128]{2,1,0:T(8,128)(2,1)S(1)} %fusion.1), channel_id=1, source_target_pairs={{8,12},{9,13},{10,14},{11,15},{24,28},{25,29},{26,30},{27,31}} | collective-permute-start | bytes 786440 | tf_op jit(solution)/shard_map/ppermute | solution.py:376
  69.9 20.0 %collective-permute-start.11 = (bf16[1024,512]{1,0:T(8,128)(2,1)}, bf16[1024,512]{1,0:T(8,128)(2,1)}, u32[]{:S(2)}, u32[]{:S(2)}) collective-permute-start(bf16[1024,512]{1,0:T(8,128)(2,1)} %collective-permute-done.4.refs_4_), channel_id=1, source_target_pairs={{4,0},{5,1},{6,2},{7,3},{20,16},{21,17},{22,18},{23,19}} | collective-permute-start | bytes 3145736 | tf_op jit(solution)/shard_map/ppermute | solution.py:376
  74.5 17.5 %collective-permute-start.12 = (bf16[768,512]{1,0:T(8,128)(2,1)}, bf16[768,512]{1,0:T(8,128)(2,1)}, u32[]{:S(2)}, u32[]{:S(2)}) collective-permute-start(bf16[768,512]{1,0:T(8,128)(2,1)} %slice.20), channel_id=1, source_target_pairs={{8,12},{9,13},{10,14},{11,15},{24,28},{25,29},{26,30},{27,31}} | collective-permute-start | bytes 2359304 | tf_op jit(solution)/shard_map/ppermute | solution.py:376
  79.8 6.7 %collective-permute-start.10 = (bf16[8,128,128]{2,1,0:T(8,128)(2,1)}, bf16[8,128,128]{2,1,0:T(8,128)(2,1)}, u32[]{:S(2)}, u32[]{:S(2)}) collective-permute-start(bf16[8,128,128]{2,1,0:T(8,128)(2,1)} %add.38.s_ref), channel_id=1, source_target_pairs={{0,16},{16,0},{1,17},{17,1},{2,18},{18,2},{3,19},{19,3},{4,20},{20... | collective-permute-start | bytes 786440 | tf_op jit(solution)/shard_map/ppermute | solution.py:376
  92.0 1.2 copy-start.2
  93.2 4.4 %copy-start.1 = (bf16[512,1024]{1,0:T(8,128)(2,1)S(1)}, bf16[512,1024]{1,0:T(8,128)(2,1)}, u32[]{:S(2)}) copy-start(bf16[512,1024]{1,0:T(8,128)(2,1)} %normed_rows.2.a_ref) | copy-start | bytes 3145732
  97.6 4.8 %collective-permute-start.14 = (bf16[512,1024]{1,0:T(8,128)(2,1)S(1)}, bf16[512,1024]{1,0:T(8,128)(2,1)S(1)}, u32[]{:S(2)}, u32[]{:S(2)}) collective-permute-start(bf16[512,1024]{1,0:T(8,128)(2,1)S(1)} %get-tuple-element.61), channel_id=1, source_target_pairs={{0,1},{1,0},{2,3},{3,2},{4,5},{5,4},{6,7},{7,6},{8,9},{9,8},{10,11... | collective-permute-start | bytes 3145736 | tf_op jit(solution)/shard_map/ppermute | solution.py:363
  101.8 3.8 %collective-permute-start.13 = (bf16[512,1024]{1,0:T(8,128)(2,1)S(1)}, bf16[512,1024]{1,0:T(8,128)(2,1)S(1)}, u32[]{:S(2)}, u32[]{:S(2)}) collective-permute-start(bf16[512,1024]{1,0:T(8,128)(2,1)S(1)} %get-tuple-element.58), channel_id=1, source_target_pairs={{0,1},{1,0},{2,3},{3,2},{4,5},{5,4},{6,7},{7,6},{8,9},{9,8},{10,11... | collective-permute-start | bytes 3145736 | tf_op jit(solution)/shard_map/ppermute | solution.py:363
  103.6 17.9 %collective-permute-start.18 = (bf16[256,512]{1,0:T(8,128)(2,1)}, bf16[256,512]{1,0:T(8,128)(2,1)}, u32[]{:S(2)}, u32[]{:S(2)}) collective-permute-start(bf16[256,512]{1,0:T(8,128)(2,1)} %get-tuple-element.71), channel_id=1, source_target_pairs={{0,2},{1,3},{2,0},{3,1},{4,6},{5,7},{6,4},{7,5},{8,10},{9,11},{10,... | collective-permute-start | bytes 786440 | tf_op jit(solution)/shard_map/ppermute | solution.py:376
  105.1 12.6 %collective-permute-start.15 = (bf16[256,512]{1,0:T(8,128)(2,1)S(1)}, bf16[256,512]{1,0:T(8,128)(2,1)S(1)}, u32[]{:S(2)}, u32[]{:S(2)}) collective-permute-start(bf16[256,512]{1,0:T(8,128)(2,1)S(1)} %get-tuple-element.72), channel_id=1, source_target_pairs={{0,2},{1,3},{2,0},{3,1},{4,6},{5,7},{6,4},{7,5},{8,10},{9,11},{10,... | collective-permute-start | bytes 786440 | tf_op jit(solution)/shard_map/ppermute | solution.py:376
  106.0 1.3 copy-start.4
  118.5 7.6 %collective-permute-start.17 = (bf16[256,512]{1,0:T(8,128)(2,1)}, bf16[256,512]{1,0:T(8,128)(2,1)S(1)}, u32[]{:S(2)}, u32[]{:S(2)}) collective-permute-start(bf16[256,512]{1,0:T(8,128)(2,1)} %get-tuple-element.68), channel_id=1, source_target_pairs={{0,16},{16,0},{1,17},{17,1},{2,18},{18,2},{3,19},{19,3},{4,20},{20... | collective-permute-start | bytes 786440 | tf_op jit(solution)/shard_map/ppermute | solution.py:376
  120.0 12.8 %collective-permute-start.16 = (bf16[512,512]{1,0:T(8,128)(2,1)S(1)}, bf16[512,512]{1,0:T(8,128)(2,1)}, u32[]{:S(2)}, u32[]{:S(2)}) collective-permute-start(bf16[512,512]{1,0:T(8,128)(2,1)S(1)} %slice.30), channel_id=1, source_target_pairs={{0,2},{1,3},{2,0},{3,1},{4,6},{5,7},{6,4},{7,5},{8,10},{9,11},{10,... | collective-permute-start | bytes 1572872 | tf_op jit(solution)/shard_map/ppermute | solution.py:376
  127.1 7.3 %collective-permute-start.19 = (bf16[256,512]{1,0:T(8,128)(2,1)S(1)}, bf16[256,512]{1,0:T(8,128)(2,1)S(1)}, u32[]{:S(2)}, u32[]{:S(2)}) collective-permute-start(bf16[256,512]{1,0:T(8,128)(2,1)S(1)} %add_convert_fusion), channel_id=1, source_target_pairs={{0,16},{16,0},{1,17},{17,1},{2,18},{18,2},{3,19},{19,3},{4,20},{20... | collective-permute-start | bytes 786440 | tf_op jit(solution)/shard_map/ppermute | solution.py:376

commit v8 on v7

--- a/solution.py
+++ b/solution.py
@@ -413,12 +413,11 @@
     incoming = jnp.zeros((heads, DK, DK), BF16)
     for hop in range(ctx - 1):
         if hop == 1 and ring:
-            up[2], down[2], outgoing = tied(up[2], down[2], outgoing)
             ahead = up[2].shape[0] // 4
             last = [(i, i + 1) for i in range(2, ctx - 1)]
             up_first = send(up[2][:ahead], "ctx", last)
         if hop == 2 and ring:
-            up_first, near_other, outgoing = tied(up_first, near_other, outgoing)
+            up_first, down[2], near_other, outgoing = tied(up_first, down[2], near_other, outgoing)
         incoming = incoming + send(outgoing, "ctx", [(hop, hop + 1)])
         outgoing = (
             jnp.einsum("hde,hef->hdf", total_end, incoming, preferred_element_type=F32) + state_end
@@ -449,6 +448,7 @@
     give_a, give_b = jnp.split(give, 2)
     keep_a, keep_b = jnp.split(keep, 2)
     got_a = send(give_a, "head", last_pairs)
+    give_b, own_give = tied(give_b, own_give)
     got_b = send(give_b, "head", last_pairs)
     got_a, own_give = tied(got_a, own_give)
     back_a = send(summed(keep_a, got_a), "groups", swap)

time: 137 us -> 132 us (0.964)
  waiting for transfers between devices: 33.6 us -> 25.6 us
  starting transfers between devices: 40.3 us -> 43.6 us
    ppermute x18, waiting for transfers between devices: 33.6 us -> 25.6 us  [send(): return lax.ppermute(value, axis, pairs)]
    ppermute x18, starting transfers between devices: 39.7 us -> 43 us  [send(): return lax.ppermute(value, axis, pairs)]
  transfers between devices with their start and end apart: 20 -> 20, of which waited for: 10 -> 10; matrix products, arithmetic and copies ran while one was open for 7% -> 8% of each run, Pallas kernels for 31% -> 32%
where the time goes in v8:
time: 132 us; the launch traced here: 131 us
  Pallas kernels  45.7 us (35%)
  starting transfers between devices  43.6 us (33%)
  waiting for transfers between devices  25.6 us (19%)
  local copies, waits for them, and re-layouts  7.06 us (5%)
  other arithmetic  7.06 us (5%)
  matrix products  1.56 us (1%)
    ppermute x18, starting transfers between devices, send(): return lax.ppermute(value, axis, pairs)  43 us
    pallas_call x2, Pallas kernels, local_part(): pl.pallas_call(functools.partial(chunk_kernel, group, first), grid=(steps...  30.4 us
    ppermute x18, waiting for transfers between devices, send(): return lax.ppermute(value, axis, pairs)  25.6 us
    pallas_call x2, Pallas kernels, project(): pl.pallas_call(functools.partial(project_kernel, choices), in_specs=[pl.B...  8.48 us
    pallas_call x2, Pallas kernels, normed_rows(): pl.pallas_call(norm_kernel, in_specs=[pl.BlockSpec(memory_space=pltpu.VME...  6.88 us
    unnamed x21, local copies, waits for them, and re-layouts  4.18 us
  transfers between devices with their start and end apart: 20, of which 10 were waited for; matrix products, arithmetic and copies ran while one was open for 8% of the time, Pallas kernels for 32%

profile of v8, /device:TPU:16, one launch (start us, length us, event | category | flops | bytes accessed | tf_op | source)
XLA Modules:
  0.0 130.9 jit_solution(7647236849500025163)
XLA Ops:
  0.0 1.6 %copy-done = bf16[1024,1024]{1,0:T(8,128)(2,1)S(1)} copy-done((bf16[1024,1024]{1,0:T(8,128)(2,1)S(1)}, bf16[1024,1024]{1,0:T(8,128)(2,1)}, u32[]{:S(2)}) %copy-start) | copy-done | bytes 2097176
  1.6 0.1 constant_dynamic-slice_fusion.refs_0_
  1.7 2.4 %collective-permute-start.1 = (bf16[1024,512]{1,0:T(8,128)(2,1)S(1)}, bf16[1024,512]{1,0:T(8,128)(2,1)}, u32[]{:S(2)}, u32[]{:S(2)}) collective-permute-start(bf16[1024,512]{1,0:T(8,128)(2,1)S(1)} %constant_dynamic-slice_fusion.refs_0_), channel_id=1, source_target_pairs={{4,0},{8,4},{12,8},{5,1},{9,5},{13,9},{6,2},{10,6},{14,10},{7,3},{... | collective-permute-start | bytes 3145736 | tf_op jit(solution)/shard_map/ppermute | solution.py:376
  4.1 4.4 %collective-permute-start = (bf16[1024,512]{1,0:T(8,128)(2,1)S(1)}, bf16[1024,512]{1,0:T(8,128)(2,1)}, u32[]{:S(2)}, u32[]{:S(2)}) collective-permute-start(bf16[1024,512]{1,0:T(8,128)(2,1)S(1)} %constant_dynamic-slice_fusion.refs_0_), channel_id=1, source_target_pairs={{0,4},{4,8},{8,12},{1,5},{5,9},{9,13},{2,6},{6,10},{10,14},{3,7},{... | collective-permute-start | bytes 3145736 | tf_op jit(solution)/shard_map/ppermute | solution.py:376
  8.5 1.0 copy.9
  9.5 18.1 %local_part.2 = (bf16[320,2048]{1,0:T(8,128)(2,1)}, f32[8,128,256]{2,1,0:T(8,128)}) custom-call(bf16[512,1024]{1,0:T(8,128)(2,1)} %q_ref.3, bf16[512,2,1024]{2,1,0:T(2,128)(2,1)} %k_ref.3, bf16[512,2,1024]{2,1,0:T(2,128)(2,1)} %v_ref.3, f32[1024,8]{1,0:T(8,128)} %bitcast.7), custom_call_target="tpu_custom_call" | custom-call | flops 16777216000 | bytes 5242880 | tf_op jit(solution)/shard_map/local_part/pallas_call | solution.py:214
  27.6 1.5 %collective-permute-start.8 = (bf16[320,2048]{1,0:T(8,128)(2,1)}, bf16[320,2048]{1,0:T(8,128)(2,1)S(1)}, u32[]{:S(2)}, u32[]{:S(2)}) collective-permute-start(bf16[320,2048]{1,0:T(8,128)(2,1)} %get-tuple-element.37.first_ref), channel_id=1, source_target_pairs={{0,16},{16,0},{1,17},{17,1},{2,18},{18,2},{3,19},{19,3},{4,20},{20... | collective-permute-start | bytes 3932168 | tf_op jit(solution)/shard_map/ppermute | solution.py:376
  29.2 0.0 collective-permute-done.1.refs_7_
  29.2 1.5 %collective-permute-done.refs_1_ = bf16[1024,512]{1,0:T(8,128)(2,1)} collective-permute-done((bf16[1024,512]{1,0:T(8,128)(2,1)S(1)}, bf16[1024,512]{1,0:T(8,128)(2,1)}, u32[]{:S(2)}, u32[]{:S(2)}) %collective-permute-start) | collective-permute-done | bytes 1048608 | tf_op jit(solution)/shard_map/ppermute | solution.py:376
  30.7 4.4 %collective-permute-start.3 = (bf16[1024,512]{1,0:T(8,128)(2,1)}, bf16[1024,512]{1,0:T(8,128)(2,1)S(1)}, u32[]{:S(2)}, u32[]{:S(2)}) collective-permute-start(bf16[1024,512]{1,0:T(8,128)(2,1)} %collective-permute-done.refs_1_), channel_id=1, source_target_pairs={{4,8},{8,12},{5,9},{9,13},{6,10},{10,14},{7,11},{11,15},{20,24},{2... | collective-permute-start | bytes 3145736 | tf_op jit(solution)/shard_map/ppermute | solution.py:376
  35.1 2.5 %collective-permute-start.7 = (bf16[1024,512]{1,0:T(8,128)(2,1)}, bf16[1024,512]{1,0:T(8,128)(2,1)}, u32[]{:S(2)}, u32[]{:S(2)}) collective-permute-start(bf16[1024,512]{1,0:T(8,128)(2,1)} %collective-permute-done.1.refs_7_), channel_id=1, source_target_pairs={{4,0},{8,4},{5,1},{9,5},{6,2},{10,6},{7,3},{11,7},{20,16},{24,20},... | collective-permute-start | bytes 3145736 | tf_op jit(solution)/shard_map/ppermute | solution.py:376
  37.6 12.3 %local_part.3 = (bf16[192,2048]{1,0:T(8,128)(2,1)}, f32[8,128,128]{2,1,0:T(8,128)}, bf16[8,128,128]{2,1,0:T(8,128)(2,1)}, bf16[8,128,128]{2,1,0:T(8,128)(2,1)}) custom-call(bf16[512,1024]{1,0:T(8,128)(2,1)} %q_ref.3, bf16[512,2,1024]{2,1,0:T(2,128)(2,1)} %k_ref.3, bf16[512,2,1024]{2,1,0:T(2,128)(2,1)} %v_ref.3, f32[1024,8]{1,0:T(8,128)} %bitcast.8, ...), custom_call_target="tpu_custom_call" | custom-call | flops 10066329600 | bytes 3145728 | tf_op jit(solution)/shard_map/local_part/pallas_call | solution.py:214
  49.9 0.8 collective-permute-start.4
  50.7 0.0 collective-permute-done.4
  50.7 1.3 %fusion = bf16[8,128,128]{2,1,0:T(8,128)(2,1)S(1)} fusion(f32[8,128,128]{2,1,0:T(8,128)} %get-tuple-element.44, bf16[8,128,128]{2,1,0:T(8,128)(2,1)} %get-tuple-element.43, bf16[8,128,128]{2,1,0:T(8,128)(2,1)S(1)} %collective-permute-done.4), kind=kOutput, calls=%fused_computation.4 | convolution fusion | flops 33816576 | bytes 1310720 | tf_op jit(solution)/shard_map/hde,hef->hdf/dot_general | solution.py:423
  52.0 1.3 collective-permute-start.5
  53.3 3.3 %collective-permute-done.3.refs_3_ = bf16[1024,512]{1,0:T(8,128)(2,1)S(1)} collective-permute-done((bf16[1024,512]{1,0:T(8,128)(2,1)}, bf16[1024,512]{1,0:T(8,128)(2,1)S(1)}, u32[]{:S(2)}, u32[]{:S(2)}) %collective-permute-start.3) | collective-permute-done | bytes 1048608 | tf_op jit(solution)/shard_map/ppermute | solution.py:376
  56.7 4.3 %collective-permute-start.6 = (bf16[256,512]{1,0:T(8,128)(2,1)S(1)}, bf16[256,512]{1,0:T(8,128)(2,1)S(1)}, u32[]{:S(2)}, u32[]{:S(2)}) collective-permute-start(bf16[256,512]{1,0:T(8,128)(2,1)S(1)} %slice.25), channel_id=1, source_target_pairs={{8,12},{9,13},{10,14},{11,15},{24,28},{25,29},{26,30},{27,31}} | collective-permute-start | bytes 786440 | tf_op jit(solution)/shard_map/ppermute | solution.py:376
  61.0 0.0 copy-start.9
  61.0 1.6 %collective-permute-start.2 = (bf16[192,2048]{1,0:T(8,128)(2,1)}, bf16[192,2048]{1,0:T(8,128)(2,1)}, u32[]{:S(2)}, u32[]{:S(2)}) collective-permute-start(bf16[192,2048]{1,0:T(8,128)(2,1)} %get-tuple-element.40.second_ref), channel_id=1, source_target_pairs={{0,16},{16,0},{1,17},{17,1},{2,18},{18,2},{3,19},{19,3},{4,20},{20... | collective-permute-start | bytes 2359304 | tf_op jit(solution)/shard_map/ppermute | solution.py:376
  62.6 2.2 %collective-permute-done.5 = bf16[8,128,128]{2,1,0:T(8,128)(2,1)S(1)} collective-permute-done((bf16[8,128,128]{2,1,0:T(8,128)(2,1)S(1)}, bf16[8,128,128]{2,1,0:T(8,128)(2,1)S(1)}, u32[]{:S(2)}, u32[]{:S(2)}) %collective-permute-start.5) | collective-permute-done | bytes 262176 | tf_op jit(solution)/shard_map/ppermute | solution.py:376
  64.7 0.1 add.36
  64.8 0.2 fusion.1
  65.0 0.0 collective-permute-done.8.first_ref
  65.1 0.0 collective-permute-done.6.refs_5_
  65.1 4.1 %collective-permute-start.9 = (bf16[8,128,128]{2,1,0:T(8,128)(2,1)S(1)}, bf16[8,128,128]{2,1,0:T(8,128)(2,1)S(1)}, u32[]{:S(2)}, u32[]{:S(2)}) collective-permute-start(bf16[8,128,128]{2,1,0:T(8,128)(2,1)S(1)} %fusion.1), channel_id=1, source_target_pairs={{8,12},{9,13},{10,14},{11,15},{24,28},{25,29},{26,30},{27,31}} | collective-permute-start | bytes 786440 | tf_op jit(solution)/shard_map/ppermute | solution.py:376
  69.2 1.7 %collective-permute-start.11 = (bf16[1024,512]{1,0:T(8,128)(2,1)}, bf16[1024,512]{1,0:T(8,128)(2,1)}, u32[]{:S(2)}, u32[]{:S(2)}) collective-permute-start(bf16[1024,512]{1,0:T(8,128)(2,1)} %collective-permute-done.7.refs_4_), channel_id=1, source_target_pairs={{4,0},{5,1},{6,2},{7,3},{20,16},{21,17},{22,18},{23,19}} | collective-permute-start | bytes 3145736 | tf_op jit(solution)/shard_map/ppermute | solution.py:376
  70.9 0.9 slice.24
  71.8 1.3 collective-permute-done.9
  73.1 0.8 add.38.s_ref
  73.9 5.3 %collective-permute-start.12 = (bf16[768,512]{1,0:T(8,128)(2,1)}, bf16[768,512]{1,0:T(8,128)(2,1)}, u32[]{:S(2)}, u32[]{:S(2)}) collective-permute-start(bf16[768,512]{1,0:T(8,128)(2,1)} %slice.24), channel_id=1, source_target_pairs={{8,12},{9,13},{10,14},{11,15},{24,28},{25,29},{26,30},{27,31}} | collective-permute-start | bytes 2359304 | tf_op jit(solution)/shard_map/ppermute | solution.py:376
  79.1 0.0 collective-permute-done.2.second_ref
  79.1 1.5 %collective-permute-start.10 = (bf16[8,128,128]{2,1,0:T(8,128)(2,1)}, bf16[8,128,128]{2,1,0:T(8,128)(2,1)}, u32[]{:S(2)}, u32[]{:S(2)}) collective-permute-start(bf16[8,128,128]{2,1,0:T(8,128)(2,1)} %add.38.s_ref), channel_id=1, source_target_pairs={{0,16},{16,0},{1,17},{17,1},{2,18},{18,2},{3,19},{19,3},{4,20},{20... | collective-permute-start | bytes 786440 | tf_op jit(solution)/shard_map/ppermute | solution.py:376
  80.7 0.7 iota_reduce_fusion
  81.4 3.5 %normed_rows.2.a_ref = bf16[512,1024]{1,0:T(8,128)(2,1)} custom-call(bf16[320,2048]{1,0:T(8,128)(2,1)} %get-tuple-element.37.first_ref, bf16[192,2048]{1,0:T(8,128)(2,1)} %get-tuple-element.40.second_ref, bf16[8,128,128]{2,1,0:T(8,128)(2,1)} %add.38.s_ref, f32[1,1024]{1,0:T(1,128)} %bitcast.10), custom_call_target="tpu_custom_call" | custom-call | flops 134217728 | bytes 3145728 | tf_op jit(solution)/shard_map/normed_rows/pallas_call | solution.py:271
  84.9 1.0 collective-permute-done.10.s_ref
  85.8 3.4 %normed_rows.3.a_ref = bf16[512,1024]{1,0:T(8,128)(2,1)} custom-call(bf16[320,2048]{1,0:T(8,128)(2,1)} %copy-done.6, bf16[192,2048]{1,0:T(8,128)(2,1)} %collective-permute-done.2.second_ref, bf16[8,128,128]{2,1,0:T(8,128)(2,1)} %collective-permute-done.10.s_ref, f32[1,1024]{1,0:T(1,128)} %bitcast.11), custom_call_target="tpu_custom_call" | custom-call | flops 134217728 | bytes 3145728 | tf_op jit(solution)/shard_map/normed_rows/pallas_call | solution.py:271
  89.2 2.1 %collective-permute-done.12.refs_6_ = bf16[768,512]{1,0:T(8,128)(2,1)} collective-permute-done((bf16[768,512]{1,0:T(8,128)(2,1)}, bf16[768,512]{1,0:T(8,128)(2,1)}, u32[]{:S(2)}, u32[]{:S(2)}) %collective-permute-start.12) | collective-permute-done | bytes 786464 | tf_op jit(solution)/shard_map/ppermute | solution.py:376
  91.3 0.0 collective-permute-done.11.refs_2_
  91.3 1.2 copy-done.2
  92.6 4.3 %project.3 = (bf16[512,1024]{1,0:T(8,128)(2,1)S(1)}, bf16[512,1024]{1,0:T(8,128)(2,1)S(1)}) custom-call(s32[4]{0:T(128)S(1)} %get-tuple-element.36.place_ref, s32[4]{0:T(128)S(1)} %compare_convert_fusion.first_ref, bf16[512,1024]{1,0:T(8,128)(2,1)S(1)} %copy-done.2, bf16[1024,512]{1,0:T(8,128)(2,1)S(1)} %constant_dynamic-slice_fusion.refs_0_, ...), custom_call_target="tpu_custom_call" | custom-call | flops 2147483648 | bytes 7340032 | tf_op jit(solution)/shard_map/project/pallas_call | solution.py:326
  96.9 0.1 collective-permute-start.14
  97.0 4.2 %project.2 = (bf16[512,1024]{1,0:T(8,128)(2,1)S(1)}, bf16[512,1024]{1,0:T(8,128)(2,1)S(1)}) custom-call(s32[4]{0:T(128)S(1)} %get-tuple-element.36.place_ref, s32[4]{0:T(128)S(1)} %compare_convert_fusion.first_ref, bf16[512,1024]{1,0:T(8,128)(2,1)S(1)} %copy-done.1, bf16[1024,512]{1,0:T(8,128)(2,1)S(1)} %constant_dynamic-slice_fusion.refs_0_, ...), custom_call_target="tpu_custom_call" | custom-call | flops 2147483648 | bytes 7340032 | tf_op jit(solution)/shard_map/project/pallas_call | solution.py:326
  101.1 0.6 collective-permute-start.13
  101.7 0.5 fusion.6
  102.2 0.7 fusion.8
  102.9 1.5 %collective-permute-start.15 = (bf16[256,512]{1,0:T(8,128)(2,1)S(1)}, bf16[256,512]{1,0:T(8,128)(2,1)S(1)}, u32[]{:S(2)}, u32[]{:S(2)}) collective-permute-start(bf16[256,512]{1,0:T(8,128)(2,1)S(1)} %get-tuple-element.72), channel_id=1, source_target_pairs={{0,2},{1,3},{2,0},{3,1},{4,6},{5,7},{6,4},{7,5},{8,10},{9,11},{10,... | collective-permute-start | bytes 786440 | tf_op jit(solution)/shard_map/ppermute | solution.py:376
  104.4 0.0 collective-permute-done.13
  104.4 0.4 convert_add_fusion.1
  104.8 1.3 %copy-done.4 = f32[512,1024]{1,0:T(8,128)} copy-done((f32[512,1024]{1,0:T(8,128)}, f32[512,1024]{1,0:T(8,128)S(1)}, u32[]{:S(2)}) %copy-start.4) | copy-done | bytes 2097176
  106.1 0.1 slice.32
  106.2 1.1 collective-permute-start.18
  107.4 4.7 %collective-permute-done.15 = bf16[256,512]{1,0:T(8,128)(2,1)S(1)} collective-permute-done((bf16[256,512]{1,0:T(8,128)(2,1)S(1)}, bf16[256,512]{1,0:T(8,128)(2,1)S(1)}, u32[]{:S(2)}, u32[]{:S(2)}) %collective-permute-start.15) | collective-permute-done | bytes 262176 | tf_op jit(solution)/shard_map/ppermute | solution.py:376
  112.1 0.8 fusion.7
  112.9 1.5 %collective-permute-start.17 = (bf16[256,512]{1,0:T(8,128)(2,1)}, bf16[256,512]{1,0:T(8,128)(2,1)S(1)}, u32[]{:S(2)}, u32[]{:S(2)}) collective-permute-start(bf16[256,512]{1,0:T(8,128)(2,1)} %get-tuple-element.68), channel_id=1, source_target_pairs={{0,16},{16,0},{1,17},{17,1},{2,18},{18,2},{3,19},{19,3},{4,20},{20... | collective-permute-start | bytes 786440 | tf_op jit(solution)/shard_map/ppermute | solution.py:376
  114.4 1.5 %collective-permute-start.16 = (bf16[512,512]{1,0:T(8,128)(2,1)S(1)}, bf16[512,512]{1,0:T(8,128)(2,1)}, u32[]{:S(2)}, u32[]{:S(2)}) collective-permute-start(bf16[512,512]{1,0:T(8,128)(2,1)S(1)} %slice.32), channel_id=1, source_target_pairs={{0,2},{1,3},{2,0},{3,1},{4,6},{5,7},{6,4},{7,5},{8,10},{9,11},{10,... | collective-permute-start | bytes 1572872 | tf_op jit(solution)/shard_map/ppermute | solution.py:376
  115.9 1.9 %collective-permute-done.18 = bf16[256,512]{1,0:T(8,128)(2,1)} collective-permute-done((bf16[256,512]{1,0:T(8,128)(2,1)}, bf16[256,512]{1,0:T(8,128)(2,1)}, u32[]{:S(2)}, u32[]{:S(2)}) %collective-permute-start.18) | collective-permute-done | bytes 262176 | tf_op jit(solution)/shard_map/ppermute | solution.py:376
  117.8 1.8 %collective-permute-done.17 = bf16[256,512]{1,0:T(8,128)(2,1)S(1)} collective-permute-done((bf16[256,512]{1,0:T(8,128)(2,1)}, bf16[256,512]{1,0:T(8,128)(2,1)S(1)}, u32[]{:S(2)}, u32[]{:S(2)}) %collective-permute-start.17) | collective-permute-done | bytes 262176 | tf_op jit(solution)/shard_map/ppermute | solution.py:376
  119.6 1.0 add_convert_fusion
  120.6 1.6 %collective-permute-start.19 = (bf16[256,512]{1,0:T(8,128)(2,1)S(1)}, bf16[256,512]{1,0:T(8,128)(2,1)S(1)}, u32[]{:S(2)}, u32[]{:S(2)}) collective-permute-start(bf16[256,512]{1,0:T(8,128)(2,1)S(1)} %add_convert_fusion), channel_id=1, source_target_pairs={{0,16},{16,0},{1,17},{17,1},{2,18},{18,2},{3,19},{19,3},{4,20},{20... | collective-permute-start | bytes 786440 | tf_op jit(solution)/shard_map/ppermute | solution.py:376
  122.2 5.9 %collective-permute-done.16 = bf16[512,512]{1,0:T(8,128)(2,1)} collective-permute-done((bf16[512,512]{1,0:T(8,128)(2,1)S(1)}, bf16[512,512]{1,0:T(8,128)(2,1)}, u32[]{:S(2)}, u32[]{:S(2)}) %collective-permute-start.16) | collective-permute-done | bytes 524320 | tf_op jit(solution)/shard_map/ppermute | solution.py:376
  128.1 1.5 %fusion.2 = bf16[512,512]{1,0:T(8,128)(2,1)S(1)} fusion(f32[512,1024]{1,0:T(8,128)} %copy-done.4, bf16[512,512]{1,0:T(8,128)(2,1)} %collective-permute-done.16), kind=kLoop, calls=%fused_computation.8 | loop fusion | flops 786432 | bytes 2097152 | tf_op jit(solution)/shard_map/convert_element_type | solution.py:372
  129.6 0.0 collective-permute-done.19
  129.7 1.3 maximum_select_fusion
  (23 shorter events, 0.1 us)
Async XLA Ops:
  0.0 1.6 %copy-start = (bf16[1024,1024]{1,0:T(8,128)(2,1)S(1)}, bf16[1024,1024]{1,0:T(8,128)(2,1)}, u32[]{:S(2)}) copy-start(bf16[1024,1024]{1,0:T(8,128)(2,1)} %param.12) | copy-start | bytes 6291460
  0.0 8.5 %copy-start.8 = (f32[2,8,512]{2,1,0:T(8,128)S(1)}, f32[2,8,512]{2,1,0:T(8,128)}, u32[]{:S(2)}) copy-start(f32[2,8,512]{2,1,0:T(8,128)} %param.10) | copy-start | bytes 98308
  1.7 27.5 %collective-permute-start.1 = (bf16[1024,512]{1,0:T(8,128)(2,1)S(1)}, bf16[1024,512]{1,0:T(8,128)(2,1)}, u32[]{:S(2)}, u32[]{:S(2)}) collective-permute-start(bf16[1024,512]{1,0:T(8,128)(2,1)S(1)} %constant_dynamic-slice_fusion.refs_0_), channel_id=1, source_target_pairs={{4,0},{8,4},{12,8},{5,1},{9,5},{13,9},{6,2},{10,6},{14,10},{7,3},{... | collective-permute-start | bytes 3145736 | tf_op jit(solution)/shard_map/ppermute | solution.py:376
  4.1 26.6 %collective-permute-start = (bf16[1024,512]{1,0:T(8,128)(2,1)S(1)}, bf16[1024,512]{1,0:T(8,128)(2,1)}, u32[]{:S(2)}, u32[]{:S(2)}) collective-permute-start(bf16[1024,512]{1,0:T(8,128)(2,1)S(1)} %constant_dynamic-slice_fusion.refs_0_), channel_id=1, source_target_pairs={{0,4},{4,8},{8,12},{1,5},{5,9},{9,13},{2,6},{6,10},{10,14},{3,7},{... | collective-permute-start | bytes 3145736 | tf_op jit(solution)/shard_map/ppermute | solution.py:376
  27.6 37.4 %collective-permute-start.8 = (bf16[320,2048]{1,0:T(8,128)(2,1)}, bf16[320,2048]{1,0:T(8,128)(2,1)S(1)}, u32[]{:S(2)}, u32[]{:S(2)}) collective-permute-start(bf16[320,2048]{1,0:T(8,128)(2,1)} %get-tuple-element.37.first_ref), channel_id=1, source_target_pairs={{0,16},{16,0},{1,17},{17,1},{2,18},{18,2},{3,19},{19,3},{4,20},{20... | collective-permute-start | bytes 3932168 | tf_op jit(solution)/shard_map/ppermute | solution.py:376
  30.7 26.0 %collective-permute-start.3 = (bf16[1024,512]{1,0:T(8,128)(2,1)}, bf16[1024,512]{1,0:T(8,128)(2,1)S(1)}, u32[]{:S(2)}, u32[]{:S(2)}) collective-permute-start(bf16[1024,512]{1,0:T(8,128)(2,1)} %collective-permute-done.refs_1_), channel_id=1, source_target_pairs={{4,8},{8,12},{5,9},{9,13},{6,10},{10,14},{7,11},{11,15},{20,24},{2... | collective-permute-start | bytes 3145736 | tf_op jit(solution)/shard_map/ppermute | solution.py:376
  35.1 29.9 %collective-permute-start.7 = (bf16[1024,512]{1,0:T(8,128)(2,1)}, bf16[1024,512]{1,0:T(8,128)(2,1)}, u32[]{:S(2)}, u32[]{:S(2)}) collective-permute-start(bf16[1024,512]{1,0:T(8,128)(2,1)} %collective-permute-done.1.refs_7_), channel_id=1, source_target_pairs={{4,0},{8,4},{5,1},{9,5},{6,2},{10,6},{7,3},{11,7},{20,16},{24,20},... | collective-permute-start | bytes 3145736 | tf_op jit(solution)/shard_map/ppermute | solution.py:376
  49.9 14.9 %copy-start.5 = (f32[8,128,128]{2,1,0:T(8,128)S(1)}, f32[8,128,128]{2,1,0:T(8,128)}, u32[]{:S(2)}) copy-start(f32[8,128,128]{2,1,0:T(8,128)} %get-tuple-element.44) | copy-start | bytes 1572868
  49.9 14.9 %copy-start.7 = (bf16[8,128,128]{2,1,0:T(8,128)(2,1)S(1)}, bf16[8,128,128]{2,1,0:T(8,128)(2,1)}, u32[]{:S(2)}) copy-start(bf16[8,128,128]{2,1,0:T(8,128)(2,1)} %get-tuple-element.43) | copy-start | bytes 786436
  49.9 0.8 collective-permute-start.4
  52.0 12.7 %collective-permute-start.5 = (bf16[8,128,128]{2,1,0:T(8,128)(2,1)S(1)}, bf16[8,128,128]{2,1,0:T(8,128)(2,1)S(1)}, u32[]{:S(2)}, u32[]{:S(2)}) collective-permute-start(bf16[8,128,128]{2,1,0:T(8,128)(2,1)S(1)} %fusion), channel_id=1, source_target_pairs={{4,8},{5,9},{6,10},{7,11},{20,24},{21,25},{22,26},{23,27}} | collective-permute-start | bytes 786440 | tf_op jit(solution)/shard_map/ppermute | solution.py:376
  56.6 15.2 %copy-start.3 = (bf16[1024,512]{1,0:T(8,128)(2,1)}, bf16[1024,512]{1,0:T(8,128)(2,1)S(1)}, u32[]{:S(2)}) copy-start(bf16[1024,512]{1,0:T(8,128)(2,1)S(1)} %collective-permute-done.3.refs_3_) | copy-start | bytes 3145732
  56.7 8.4 %collective-permute-start.6 = (bf16[256,512]{1,0:T(8,128)(2,1)S(1)}, bf16[256,512]{1,0:T(8,128)(2,1)S(1)}, u32[]{:S(2)}, u32[]{:S(2)}) collective-permute-start(bf16[256,512]{1,0:T(8,128)(2,1)S(1)} %slice.25), channel_id=1, source_target_pairs={{8,12},{9,13},{10,14},{11,15},{24,28},{25,29},{26,30},{27,31}} | collective-permute-start | bytes 786440 | tf_op jit(solution)/shard_map/ppermute | solution.py:376
  61.0 19.7 %copy-start.9 = (s32[4]{0:T(128)S(1)}, s32[4]{0:T(128)}, u32[]{:S(2)}) copy-start(s32[4]{0:T(128)} %constant.32.clone) | copy-start | bytes 52
  61.0 18.2 %collective-permute-start.2 = (bf16[192,2048]{1,0:T(8,128)(2,1)}, bf16[192,2048]{1,0:T(8,128)(2,1)}, u32[]{:S(2)}, u32[]{:S(2)}) collective-permute-start(bf16[192,2048]{1,0:T(8,128)(2,1)} %get-tuple-element.40.second_ref), channel_id=1, source_target_pairs={{0,16},{16,0},{1,17},{17,1},{2,18},{18,2},{3,19},{19,3},{4,20},{20... | collective-permute-start | bytes 2359304 | tf_op jit(solution)/shard_map/ppermute | solution.py:376
  65.1 8.8 %copy-start.6 = (bf16[320,2048]{1,0:T(8,128)(2,1)}, bf16[320,2048]{1,0:T(8,128)(2,1)S(1)}, u32[]{:S(2)}) copy-start(bf16[320,2048]{1,0:T(8,128)(2,1)S(1)} %collective-permute-done.8.first_ref) | copy-start | bytes 3932164
  65.1 8.0 %collective-permute-start.9 = (bf16[8,128,128]{2,1,0:T(8,128)(2,1)S(1)}, bf16[8,128,128]{2,1,0:T(8,128)(2,1)S(1)}, u32[]{:S(2)}, u32[]{:S(2)}) collective-permute-start(bf16[8,128,128]{2,1,0:T(8,128)(2,1)S(1)} %fusion.1), channel_id=1, source_target_pairs={{8,12},{9,13},{10,14},{11,15},{24,28},{25,29},{26,30},{27,31}} | collective-permute-start | bytes 786440 | tf_op jit(solution)/shard_map/ppermute | solution.py:376
  69.2 22.1 %collective-permute-start.11 = (bf16[1024,512]{1,0:T(8,128)(2,1)}, bf16[1024,512]{1,0:T(8,128)(2,1)}, u32[]{:S(2)}, u32[]{:S(2)}) collective-permute-start(bf16[1024,512]{1,0:T(8,128)(2,1)} %collective-permute-done.7.refs_4_), channel_id=1, source_target_pairs={{4,0},{5,1},{6,2},{7,3},{20,16},{21,17},{22,18},{23,19}} | collective-permute-start | bytes 3145736 | tf_op jit(solution)/shard_map/ppermute | solution.py:376
  73.9 17.5 %collective-permute-start.12 = (bf16[768,512]{1,0:T(8,128)(2,1)}, bf16[768,512]{1,0:T(8,128)(2,1)}, u32[]{:S(2)}, u32[]{:S(2)}) collective-permute-start(bf16[768,512]{1,0:T(8,128)(2,1)} %slice.24), channel_id=1, source_target_pairs={{8,12},{9,13},{10,14},{11,15},{24,28},{25,29},{26,30},{27,31}} | collective-permute-start | bytes 2359304 | tf_op jit(solution)/shard_map/ppermute | solution.py:376
  79.1 6.7 %collective-permute-start.10 = (bf16[8,128,128]{2,1,0:T(8,128)(2,1)}, bf16[8,128,128]{2,1,0:T(8,128)(2,1)}, u32[]{:S(2)}, u32[]{:S(2)}) collective-permute-start(bf16[8,128,128]{2,1,0:T(8,128)(2,1)} %add.38.s_ref), channel_id=1, source_target_pairs={{0,16},{16,0},{1,17},{17,1},{2,18},{18,2},{3,19},{19,3},{4,20},{20... | collective-permute-start | bytes 786440 | tf_op jit(solution)/shard_map/ppermute | solution.py:376
  91.3 1.2 copy-start.2
  92.6 4.4 %copy-start.1 = (bf16[512,1024]{1,0:T(8,128)(2,1)S(1)}, bf16[512,1024]{1,0:T(8,128)(2,1)}, u32[]{:S(2)}) copy-start(bf16[512,1024]{1,0:T(8,128)(2,1)} %normed_rows.2.a_ref) | copy-start | bytes 3145732
  96.9 4.8 %collective-permute-start.14 = (bf16[512,1024]{1,0:T(8,128)(2,1)S(1)}, bf16[512,1024]{1,0:T(8,128)(2,1)S(1)}, u32[]{:S(2)}, u32[]{:S(2)}) collective-permute-start(bf16[512,1024]{1,0:T(8,128)(2,1)S(1)} %get-tuple-element.59), channel_id=1, source_target_pairs={{0,1},{1,0},{2,3},{3,2},{4,5},{5,4},{6,7},{7,6},{8,9},{9,8},{10,11... | collective-permute-start | bytes 3145736 | tf_op jit(solution)/shard_map/ppermute | solution.py:363
  101.1 3.3 %collective-permute-start.13 = (bf16[512,1024]{1,0:T(8,128)(2,1)S(1)}, bf16[512,1024]{1,0:T(8,128)(2,1)S(1)}, u32[]{:S(2)}, u32[]{:S(2)}) collective-permute-start(bf16[512,1024]{1,0:T(8,128)(2,1)S(1)} %get-tuple-element.56), channel_id=1, source_target_pairs={{0,1},{1,0},{2,3},{3,2},{4,5},{5,4},{6,7},{7,6},{8,9},{9,8},{10,11... | collective-permute-start | bytes 3145736 | tf_op jit(solution)/shard_map/ppermute | solution.py:363
  102.9 9.2 %collective-permute-start.15 = (bf16[256,512]{1,0:T(8,128)(2,1)S(1)}, bf16[256,512]{1,0:T(8,128)(2,1)S(1)}, u32[]{:S(2)}, u32[]{:S(2)}) collective-permute-start(bf16[256,512]{1,0:T(8,128)(2,1)S(1)} %get-tuple-element.72), channel_id=1, source_target_pairs={{0,2},{1,3},{2,0},{3,1},{4,6},{5,7},{6,4},{7,5},{8,10},{9,11},{10,... | collective-permute-start | bytes 786440 | tf_op jit(solution)/shard_map/ppermute | solution.py:376
  104.8 1.3 %copy-start.4 = (f32[512,1024]{1,0:T(8,128)}, f32[512,1024]{1,0:T(8,128)S(1)}, u32[]{:S(2)}) copy-start(f32[512,1024]{1,0:T(8,128)S(1)} %convert_add_fusion.1) | copy-start | bytes 6291460
  106.2 11.6 %collective-permute-start.18 = (bf16[256,512]{1,0:T(8,128)(2,1)}, bf16[256,512]{1,0:T(8,128)(2,1)}, u32[]{:S(2)}, u32[]{:S(2)}) collective-permute-start(bf16[256,512]{1,0:T(8,128)(2,1)} %get-tuple-element.63), channel_id=1, source_target_pairs={{0,2},{1,3},{2,0},{3,1},{4,6},{5,7},{6,4},{7,5},{8,10},{9,11},{10,... | collective-permute-start | bytes 786440 | tf_op jit(solution)/shard_map/ppermute | solution.py:376
  112.9 6.7 %collective-permute-start.17 = (bf16[256,512]{1,0:T(8,128)(2,1)}, bf16[256,512]{1,0:T(8,128)(2,1)S(1)}, u32[]{:S(2)}, u32[]{:S(2)}) collective-permute-start(bf16[256,512]{1,0:T(8,128)(2,1)} %get-tuple-element.68), channel_id=1, source_target_pairs={{0,16},{16,0},{1,17},{17,1},{2,18},{18,2},{3,19},{19,3},{4,20},{20... | collective-permute-start | bytes 786440 | tf_op jit(solution)/shard_map/ppermute | solution.py:376
  114.4 13.7 %collective-permute-start.16 = (bf16[512,512]{1,0:T(8,128)(2,1)S(1)}, bf16[512,512]{1,0:T(8,128)(2,1)}, u32[]{:S(2)}, u32[]{:S(2)}) collective-permute-start(bf16[512,512]{1,0:T(8,128)(2,1)S(1)} %slice.32), channel_id=1, source_target_pairs={{0,2},{1,3},{2,0},{3,1},{4,6},{5,7},{6,4},{7,5},{8,10},{9,11},{10,... | collective-permute-start | bytes 1572872 | tf_op jit(solution)/shard_map/ppermute | solution.py:376
  120.6 9.0 %collective-permute-start.19 = (bf16[256,512]{1,0:T(8,128)(2,1)S(1)}, bf16[256,512]{1,0:T(8,128)(2,1)S(1)}, u32[]{:S(2)}, u32[]{:S(2)}) collective-permute-start(bf16[256,512]{1,0:T(8,128)(2,1)S(1)} %add_convert_fusion), channel_id=1, source_target_pairs={{0,16},{16,0},{1,17},{17,1},{2,18},{18,2},{3,19},{19,3},{4,20},{20... | collective-permute-start | bytes 786440 | tf_op jit(solution)/shard_map/ppermute | solution.py:376

commit v9 on v8

--- a/solution.py
+++ b/solution.py
@@ -283,8 +283,10 @@
 def project_kernel(choices, place_ref, first_ref, a_ref, *refs):
     count = sum(sum(options) for options in choices)
     weights = list(refs[:count])
-    give_ref, keep_ref, held, sems = refs[count:]
-    half, block = len(choices) // 2, held.shape[2]
+    *done, give_ref, keep_ref, held, sems = refs[count:]
+    done_ref = done[0] if done else None
+    block = held.shape[2]
+    half = give_ref.shape[1] // block
     whole = weights[0]
 
     def fetch(slot, pieces):
@@ -301,11 +303,7 @@
                 fetch(slot, taken)
             else:
                 pl.when(first_ref[slot] == 1 - option)(functools.partial(fetch, slot, taken))
-    for slot in range(len(choices)):
-        pltpu.make_async_copy(whole, held.at[slot], sems.at[slot]).wait()
-        product = mxu(a_ref[...], held[slot]).astype(BF16)
-        place = place_ref[slot]
-
+    def put(place, product):
         @pl.when(place < half)
         def _():
             give_ref[:, pl.ds(pl.multiple_of(place * block, block), block)] = product
@@ -314,21 +312,51 @@
         def _():
             keep_ref[:, pl.ds(pl.multiple_of((place - half) * block, block), block)] = product
 
-
-def project(places, first, rows, weights):
+    if done_ref is not None:
+        for slot in range(done_ref.shape[1] // block):
+            put(place_ref[len(choices) + slot], done_ref[:, slot * block : (slot + 1) * block])
+    for slot in range(len(choices)):
+        pltpu.make_async_copy(whole, held.at[slot], sems.at[slot]).wait()
+        put(place_ref[slot], mxu(a_ref[...], held[slot]).astype(BF16))
+
+
+def product_kernel(a_ref, *refs):
+    weights, out_ref = refs[:-1], refs[-1]
+    block = weights[0].shape[1]
+    for slot, weight in enumerate(weights):
+        out_ref[:, slot * block : (slot + 1) * block] = mxu(a_ref[...], weight[...]).astype(BF16)
+
+
+def products(rows, weights):
+    tokens, block = rows.shape[0], weights[0].shape[1]
+    vmem = pl.BlockSpec(memory_space=pltpu.VMEM)
+    return pl.pallas_call(
+        product_kernel,
+        in_specs=[vmem] * (1 + len(weights)),
+        out_specs=vmem,
+        out_shape=jax.ShapeDtypeStruct((tokens, block * len(weights)), BF16),
+        compiler_params=pltpu.CompilerParams(vmem_limit_bytes=32 * 1024 * 1024),
+        name="products",
+    )(rows, *weights)
+
+
+def project(places, first, rows, weights, done=None):
     tokens, depth = rows.shape
     count = len(weights)
     block = weights[0][0][0].shape[1]
     choices = tuple(tuple(len(pieces) for pieces in options) for options in weights)
     flat = [piece for options in weights for pieces in options for piece in pieces]
-    half = pl.BlockSpec(memory_space=pltpu.VMEM)
-    shape = jax.ShapeDtypeStruct((tokens, count // 2 * block), BF16)
+    vmem = pl.BlockSpec(memory_space=pltpu.VMEM)
+    extra = [] if done is None else [done]
+    total = count + sum(array.shape[1] // block for array in extra)
+    shape = jax.ShapeDtypeStruct((tokens, total // 2 * block), BF16)
     return pl.pallas_call(
         functools.partial(project_kernel, choices),
         in_specs=[pl.BlockSpec(memory_space=pltpu.SMEM)] * 2
-        + [half]
-        + [pl.BlockSpec(memory_space=pl.ANY)] * len(flat),
-        out_specs=[half, half],
+        + [vmem]
+        + [pl.BlockSpec(memory_space=pl.ANY)] * len(flat)
+        + [vmem] * len(extra),
+        out_specs=[vmem, vmem],
         out_shape=[shape, shape],
         scratch_shapes=[
             pltpu.VMEM((count, depth, block), BF16),
@@ -341,7 +369,7 @@
             transcendentals=0,
         ),
         name="project",
-    )(places, first, rows, *flat)
+    )(places, first, rows, *flat, *extra)
 
 
 def halving_order(count):
@@ -395,25 +423,26 @@
 
     if ring:
         pass_up(1)
+        down[0], beta_rows = tied(own, beta_rows)
         pass_down(1)
     swap = [(0, 1), (1, 0)]
     steps = tokens * REFL // CHUNK
-    early = steps * 5 // 8
-    near, middle = local_part(queries, keys, values, beta_rows, 0, early)
+    cut = steps * 5 // 8
+    near, middle = local_part(queries, keys, values, beta_rows, 0, cut)
     if ring:
         up[1], down[1], middle = tied(up[1], down[1], middle)
         pass_up(2)
         pass_down(2)
     near_other = send(near, "groups", swap)
     far, state_end, outgoing, total_end = local_part(
-        queries, keys, values, beta_rows, early, steps - early, middle
+        queries, keys, values, beta_rows, cut, steps - cut, middle
     )
     far_other = send(far, "groups", swap)
 
     incoming = jnp.zeros((heads, DK, DK), BF16)
     for hop in range(ctx - 1):
         if hop == 1 and ring:
-            ahead = up[2].shape[0] // 4
+            ahead = up[2].shape[0] * 3 // 8
             last = [(i, i + 1) for i in range(2, ctx - 1)]
             up_first = send(up[2][:ahead], "ctx", last)
         if hop == 2 and ring:
@@ -426,14 +455,17 @@
         pass_down(3)
         up_rest, incoming = tied(up[2][ahead:], incoming)
         up[3] = [up_first, send(up_rest, "ctx", last)]
-        weights = [([own],), ([up[1]], [down[3]]), ([up[2]], [down[2]]), (up[3], [down[1]])]
-        targets = lax.rem(here + ctx - jnp.arange(ctx), ctx)
-        first = (here >= jnp.arange(ctx)).astype(jnp.int32)
+        weights = [(up[3], [down[1]]), ([up[1]], [down[3]])]
+        slots = jnp.asarray([3, 1, 0, 2], jnp.int32)
+        targets = lax.rem(here + ctx - slots, ctx)
+        first = (here >= slots).astype(jnp.int32)
+        early = [own, jnp.where(here >= 2, up[2], down[2])]
     else:
         whole = lax.all_gather(own, "ctx", axis=1, tiled=True)
         weights = [([w],) for w in jnp.split(whole, head, axis=1)]
         targets = jnp.arange(head)
         first = jnp.ones((head,), jnp.int32)
+        early = []
     far_other, incoming = tied(far_other, incoming)
     incoming_other = send(incoming, "groups", swap)
     mine = normed_rows(near, far, incoming, gain)
@@ -441,9 +473,12 @@
     distance = targets ^ lax.axis_index("head")
     order = jnp.asarray(halving_order(head), jnp.int32)
     places = jnp.argmax(distance[:, None] == order[None, :], axis=1).astype(jnp.int32)
-    mine, other = tied(mine, other)
-    give, keep = head_halved(*project(places, first, other, weights))
-    own_give, own_keep = head_halved(*project(places, first, mine, weights))
+    done = products(mine, early) if early else None
+    other_done = products(other, early) if early else None
+    if early:
+        done, other_done = tied(done, other_done)
+    give, keep = head_halved(*project(places, first, other, weights, other_done))
+    own_give, own_keep = head_halved(*project(places, first, mine, weights, done))
     last_pairs = head_pairs(head // 2)
     give_a, give_b = jnp.split(give, 2)
     keep_a, keep_b = jnp.split(keep, 2)

time: 132 us -> 143 us (1.083)
  local copies, waits for them, and re-layouts: 7.06 us -> 13.8 us
  starting transfers between devices: 43.6 us -> 38.9 us
  waiting for transfers between devices: 25.6 us -> 29.8 us
  other arithmetic: 7.06 us -> 10.4 us
    unnamed x21 -> x43, local copies, waits for them, and re-layouts: 4.18 us -> 9.84 us
    ppermute x18, starting transfers between devices: 43 us -> 38.3 us  [send(): return lax.ppermute(value, axis, pairs)]
    ppermute x18, waiting for transfers between devices: 25.6 us -> 29.8 us  [send(): return lax.ppermute(value, axis, pairs)]
    pallas_call x0 -> x2, Pallas kernels: none -> 2.49 us  [products(): pl.pallas_call(product_kernel, in_specs=[vmem] * (1 + len(weights)), out_...]
    select_n x0 -> x1, other arithmetic: none -> 2.37 us  [per_device(): early = [own, jnp.where(here >= 2, up[2], down[2])]]
    pallas_call x2, Pallas kernels: 8.48 us -> 6.74 us  [project(): pl.pallas_call(functools.partial(project_kernel, choices), in_specs=[pl.B...]
  transfers between devices with their start and end apart: 20 -> 20, of which waited for: 10 -> 8; matrix products, arithmetic and copies ran while one was open for 8% -> 11% of each run, Pallas kernels for 32% -> 30%
where the time goes in v9:
time: 143 us; the launch traced here: 142 us
  Pallas kernels  46.5 us (33%)
  starting transfers between devices  38.9 us (27%)
  waiting for transfers between devices  29.8 us (21%)
  local copies, waits for them, and re-layouts  13.8 us (10%)
  other arithmetic  10.4 us (7%)
  matrix products  2.27 us (2%)
    ppermute x18, starting transfers between devices, send(): return lax.ppermute(value, axis, pairs)  38.3 us
    pallas_call x2, Pallas kernels, local_part(): pl.pallas_call(functools.partial(chunk_kernel, group, first), grid=(steps...  30.4 us
    ppermute x18, waiting for transfers between devices, send(): return lax.ppermute(value, axis, pairs)  29.8 us
    unnamed x43, local copies, waits for them, and re-layouts  9.84 us
    pallas_call x2, Pallas kernels, normed_rows(): pl.pallas_call(norm_kernel, in_specs=[pl.BlockSpec(memory_space=pltpu.VME...  6.85 us
    pallas_call x2, Pallas kernels, project(): pl.pallas_call(functools.partial(project_kernel, choices), in_specs=[pl.B...  6.74 us
  transfers between devices with their start and end apart: 20, of which 8 were waited for; matrix products, arithmetic and copies ran while one was open for 11% of the time, Pallas kernels for 30%

profile of v9, /device:TPU:16, one launch (start us, length us, event | category | flops | bytes accessed | tf_op | source)
XLA Modules:
  0.0 142.1 jit_solution(9180323076843013226)
XLA Ops:
  0.0 1.6 %copy-done = bf16[1024,1024]{1,0:T(8,128)(2,1)S(1)} copy-done((bf16[1024,1024]{1,0:T(8,128)(2,1)S(1)}, bf16[1024,1024]{1,0:T(8,128)(2,1)}, u32[]{:S(2)}) %copy-start) | copy-done | bytes 2097176
  1.6 0.1 constant_dynamic-slice_fusion.refs_0_
  1.7 3.5 %collective-permute-start = (bf16[1024,512]{1,0:T(8,128)(2,1)S(1)}, bf16[1024,512]{1,0:T(8,128)(2,1)}, u32[]{:S(2)}, u32[]{:S(2)}) collective-permute-start(bf16[1024,512]{1,0:T(8,128)(2,1)S(1)} %constant_dynamic-slice_fusion.refs_0_), channel_id=1, source_target_pairs={{0,4},{4,8},{8,12},{1,5},{5,9},{9,13},{2,6},{6,10},{10,14},{3,7},{... | collective-permute-start | bytes 3145736 | tf_op jit(solution)/shard_map/ppermute | solution.py:404
  5.2 1.0 copy.10
  6.2 2.3 %collective-permute-start.1 = (bf16[1024,512]{1,0:T(8,128)(2,1)S(1)}, bf16[1024,512]{1,0:T(8,128)(2,1)S(1)}, u32[]{:S(2)}, u32[]{:S(2)}) collective-permute-start(bf16[1024,512]{1,0:T(8,128)(2,1)S(1)} %constant_dynamic-slice_fusion.refs_0_), channel_id=1, source_target_pairs={{4,0},{8,4},{12,8},{5,1},{9,5},{13,9},{6,2},{10,6},{14,10},{7,3},{... | collective-permute-start | bytes 3145736 | tf_op jit(solution)/shard_map/ppermute | solution.py:404
  8.6 18.1 %local_part.2 = (bf16[320,2048]{1,0:T(8,128)(2,1)}, f32[8,128,256]{2,1,0:T(8,128)}) custom-call(bf16[512,1024]{1,0:T(8,128)(2,1)} %q_ref.3, bf16[512,2,1024]{2,1,0:T(2,128)(2,1)} %k_ref.3, bf16[512,2,1024]{2,1,0:T(2,128)(2,1)} %v_ref.3, f32[1024,8]{1,0:T(8,128)} %bitcast.7), custom_call_target="tpu_custom_call" | custom-call | flops 16777216000 | bytes 5242880 | tf_op jit(solution)/shard_map/local_part/pallas_call | solution.py:214
  26.7 1.5 %collective-permute-start.8 = (bf16[320,2048]{1,0:T(8,128)(2,1)}, bf16[320,2048]{1,0:T(8,128)(2,1)S(1)}, u32[]{:S(2)}, u32[]{:S(2)}) collective-permute-start(bf16[320,2048]{1,0:T(8,128)(2,1)} %get-tuple-element.40.first_ref), channel_id=1, source_target_pairs={{0,16},{16,0},{1,17},{17,1},{2,18},{18,2},{3,19},{19,3},{4,20},{20... | collective-permute-start | bytes 3932168 | tf_op jit(solution)/shard_map/ppermute | solution.py:404
  28.2 4.5 %collective-permute-done.1.refs_2_ = bf16[1024,512]{1,0:T(8,128)(2,1)S(1)} collective-permute-done((bf16[1024,512]{1,0:T(8,128)(2,1)S(1)}, bf16[1024,512]{1,0:T(8,128)(2,1)S(1)}, u32[]{:S(2)}, u32[]{:S(2)}) %collective-permute-start.1) | collective-permute-done | bytes 1048608 | tf_op jit(solution)/shard_map/ppermute | solution.py:404
  32.7 1.9 %collective-permute-start.3 = (bf16[1024,512]{1,0:T(8,128)(2,1)}, bf16[1024,512]{1,0:T(8,128)(2,1)S(1)}, u32[]{:S(2)}, u32[]{:S(2)}) collective-permute-start(bf16[1024,512]{1,0:T(8,128)(2,1)} %collective-permute-done.refs_3_), channel_id=1, source_target_pairs={{4,8},{8,12},{5,9},{9,13},{6,10},{10,14},{7,11},{11,15},{20,24},{2... | collective-permute-start | bytes 3145736 | tf_op jit(solution)/shard_map/ppermute | solution.py:404
  34.7 5.0 %collective-permute-start.7 = (bf16[1024,512]{1,0:T(8,128)(2,1)S(1)}, bf16[1024,512]{1,0:T(8,128)(2,1)}, u32[]{:S(2)}, u32[]{:S(2)}) collective-permute-start(bf16[1024,512]{1,0:T(8,128)(2,1)S(1)} %collective-permute-done.1.refs_2_), channel_id=1, source_target_pairs={{4,0},{8,4},{5,1},{9,5},{6,2},{10,6},{7,3},{11,7},{20,16},{24,20},... | collective-permute-start | bytes 3145736 | tf_op jit(solution)/shard_map/ppermute | solution.py:404
  39.6 12.3 %local_part.3 = (bf16[192,2048]{1,0:T(8,128)(2,1)}, f32[8,128,128]{2,1,0:T(8,128)}, bf16[8,128,128]{2,1,0:T(8,128)(2,1)}, bf16[8,128,128]{2,1,0:T(8,128)(2,1)}) custom-call(bf16[512,1024]{1,0:T(8,128)(2,1)} %q_ref.3, bf16[512,2,1024]{2,1,0:T(2,128)(2,1)} %k_ref.3, bf16[512,2,1024]{2,1,0:T(2,128)(2,1)} %v_ref.3, f32[1024,8]{1,0:T(8,128)} %bitcast.8, ...), custom_call_target="tpu_custom_call" | custom-call | flops 10066329600 | bytes 3145728 | tf_op jit(solution)/shard_map/local_part/pallas_call | solution.py:214
  52.0 0.8 collective-permute-start.4
  52.8 0.0 copy-start.20
  52.8 1.3 fusion
  54.1 1.3 collective-permute-start.5
  55.4 3.1 %collective-permute-done.3 = bf16[1024,512]{1,0:T(8,128)(2,1)S(1)} collective-permute-done((bf16[1024,512]{1,0:T(8,128)(2,1)}, bf16[1024,512]{1,0:T(8,128)(2,1)S(1)}, u32[]{:S(2)}, u32[]{:S(2)}) %collective-permute-start.3) | collective-permute-done | bytes 1048608 | tf_op jit(solution)/shard_map/ppermute | solution.py:404
  58.6 2.2 %collective-permute-start.6 = (bf16[384,512]{1,0:T(8,128)(2,1)S(1)}, bf16[384,512]{1,0:T(8,128)(2,1)S(1)}, u32[]{:S(2)}, u32[]{:S(2)}) collective-permute-start(bf16[384,512]{1,0:T(8,128)(2,1)S(1)} %slice.25), channel_id=1, source_target_pairs={{8,12},{9,13},{10,14},{11,15},{24,28},{25,29},{26,30},{27,31}} | collective-permute-start | bytes 1179656 | tf_op jit(solution)/shard_map/ppermute | solution.py:404
  60.8 0.0 copy-start.19
  60.8 0.0 copy-start.18
  60.8 1.6 %collective-permute-start.2 = (bf16[192,2048]{1,0:T(8,128)(2,1)}, bf16[192,2048]{1,0:T(8,128)(2,1)}, u32[]{:S(2)}, u32[]{:S(2)}) collective-permute-start(bf16[192,2048]{1,0:T(8,128)(2,1)} %get-tuple-element.44.second_ref), channel_id=1, source_target_pairs={{0,16},{16,0},{1,17},{17,1},{2,18},{18,2},{3,19},{19,3},{4,20},{20... | collective-permute-start | bytes 2359304 | tf_op jit(solution)/shard_map/ppermute | solution.py:404
  62.4 4.4 %collective-permute-done.5 = bf16[8,128,128]{2,1,0:T(8,128)(2,1)S(1)} collective-permute-done((bf16[8,128,128]{2,1,0:T(8,128)(2,1)S(1)}, bf16[8,128,128]{2,1,0:T(8,128)(2,1)S(1)}, u32[]{:S(2)}, u32[]{:S(2)}) %collective-permute-start.5) | collective-permute-done | bytes 262176 | tf_op jit(solution)/shard_map/ppermute | solution.py:404
  66.8 0.1 add.36
  66.9 0.9 fusion.1
  67.9 1.7 %collective-permute-start.11 = (bf16[1024,512]{1,0:T(8,128)(2,1)}, bf16[1024,512]{1,0:T(8,128)(2,1)}, u32[]{:S(2)}, u32[]{:S(2)}) collective-permute-start(bf16[1024,512]{1,0:T(8,128)(2,1)} %collective-permute-done.7), channel_id=1, source_target_pairs={{4,0},{5,1},{6,2},{7,3},{20,16},{21,17},{22,18},{23,19}} | collective-permute-start | bytes 3145736 | tf_op jit(solution)/shard_map/ppermute | solution.py:404
  69.5 4.5 %collective-permute-start.9 = (bf16[8,128,128]{2,1,0:T(8,128)(2,1)}, bf16[8,128,128]{2,1,0:T(8,128)(2,1)}, u32[]{:S(2)}, u32[]{:S(2)}) collective-permute-start(bf16[8,128,128]{2,1,0:T(8,128)(2,1)} %fusion.1), channel_id=1, source_target_pairs={{8,12},{9,13},{10,14},{11,15},{24,28},{25,29},{26,30},{27,31}} | collective-permute-start | bytes 786440 | tf_op jit(solution)/shard_map/ppermute | solution.py:404
  74.0 2.0 %slice.24 = bf16[640,512]{1,0:T(8,128)(2,1)} slice(bf16[1024,512]{1,0:T(8,128)(2,1)} %copy-done.12), slice={[384:1024], [0:512]} | slice | bytes 1310720 | tf_op jit(solution)/shard_map/slice | solution.py:456
  76.0 1.5 %collective-permute-done.9 = bf16[8,128,128]{2,1,0:T(8,128)(2,1)} collective-permute-done((bf16[8,128,128]{2,1,0:T(8,128)(2,1)}, bf16[8,128,128]{2,1,0:T(8,128)(2,1)}, u32[]{:S(2)}, u32[]{:S(2)}) %collective-permute-start.9) | collective-permute-done | bytes 262176 | tf_op jit(solution)/shard_map/ppermute | solution.py:404
  77.5 1.8 %add.38.s_ref = bf16[8,128,128]{2,1,0:T(8,128)(2,1)} add(bf16[8,128,128]{2,1,0:T(8,128)(2,1)} %copy-done.13, bf16[8,128,128]{2,1,0:T(8,128)(2,1)} %collective-permute-done.9) | non-fusion elementwise | flops 131072 | bytes 786432 | tf_op jit(solution)/shard_map/add | solution.py:450
  79.3 5.2 %collective-permute-start.10 = (bf16[640,512]{1,0:T(8,128)(2,1)}, bf16[640,512]{1,0:T(8,128)(2,1)}, u32[]{:S(2)}, u32[]{:S(2)}) collective-permute-start(bf16[640,512]{1,0:T(8,128)(2,1)} %slice.24), channel_id=1, source_target_pairs={{8,12},{9,13},{10,14},{11,15},{24,28},{25,29},{26,30},{27,31}} | collective-permute-start | bytes 1966088 | tf_op jit(solution)/shard_map/ppermute | solution.py:404
  84.6 0.7 iota_reduce_fusion
  85.3 1.5 %collective-permute-start.12 = (bf16[8,128,128]{2,1,0:T(8,128)(2,1)}, bf16[8,128,128]{2,1,0:T(8,128)(2,1)}, u32[]{:S(2)}, u32[]{:S(2)}) collective-permute-start(bf16[8,128,128]{2,1,0:T(8,128)(2,1)} %add.38.s_ref), channel_id=1, source_target_pairs={{0,16},{16,0},{1,17},{17,1},{2,18},{18,2},{3,19},{19,3},{4,20},{20... | collective-permute-start | bytes 786440 | tf_op jit(solution)/shard_map/ppermute | solution.py:404
  86.8 2.4 %broadcast_select_fusion.refs_1_ = bf16[1024,512]{1,0:T(8,128)(2,1)} fusion(bf16[1024,512]{1,0:T(8,128)(2,1)} %copy-done.12, bf16[1024,512]{1,0:T(8,128)(2,1)} %collective-permute-done.7, pred[]{:T(512)S(6)} %ge.11), kind=kLoop, calls=%fused_computation.10 | loop fusion | flops 524288 | bytes 3145729 | tf_op jit(solution)/shard_map/jit(_where)/select_n | solution.py:462
  89.2 3.4 %normed_rows.2.a_ref = bf16[512,1024]{1,0:T(8,128)(2,1)} custom-call(bf16[320,2048]{1,0:T(8,128)(2,1)} %get-tuple-element.40.first_ref, bf16[192,2048]{1,0:T(8,128)(2,1)} %get-tuple-element.44.second_ref, bf16[8,128,128]{2,1,0:T(8,128)(2,1)} %add.38.s_ref, f32[1,1024]{1,0:T(1,128)} %bitcast.10), custom_call_target="tpu_custom_call" | custom-call | flops 134217728 | bytes 3145728 | tf_op jit(solution)/shard_map/normed_rows/pallas_call | solution.py:271
  92.6 1.2 copy-done.1
  93.9 1.2 copy-done.3
  95.1 1.2 products.2.refs_5_
  96.3 1.0 copy-done.9
  97.3 3.4 %normed_rows.3.a_ref = bf16[512,1024]{1,0:T(8,128)(2,1)} custom-call(bf16[320,2048]{1,0:T(8,128)(2,1)} %copy-done.15, bf16[192,2048]{1,0:T(8,128)(2,1)} %collective-permute-done.2.second_ref, bf16[8,128,128]{2,1,0:T(8,128)(2,1)} %collective-permute-done.12.s_ref, f32[1,1024]{1,0:T(1,128)} %bitcast.11), custom_call_target="tpu_custom_call" | custom-call | flops 134217728 | bytes 3145728 | tf_op jit(solution)/shard_map/normed_rows/pallas_call | solution.py:271
  100.7 1.2 copy-done.2
  101.9 1.2 copy-done.5
  103.2 1.2 products.3.refs_5_
  104.4 1.0 copy-done.10
  105.4 3.4 %project.3 = (bf16[512,1024]{1,0:T(8,128)(2,1)S(1)}, bf16[512,1024]{1,0:T(8,128)(2,1)S(1)}) custom-call(s32[4]{0:T(128)S(1)} %get-tuple-element.38.place_ref, s32[4]{0:T(128)S(1)} %compare_convert_fusion.first_ref, bf16[512,1024]{1,0:T(8,128)(2,1)S(1)} %copy-done.6, bf16[384,512]{1,0:T(8,128)(2,1)S(1)} %collective-permute-done.6.refs_0_, ...), custom_call_target="tpu_custom_call" | custom-call | flops 1073741824 | bytes 4194304 | tf_op jit(solution)/shard_map/project/pallas_call | solution.py:353
  108.8 0.1 collective-permute-start.14
  108.9 3.3 %project.2 = (bf16[512,1024]{1,0:T(8,128)(2,1)S(1)}, bf16[512,1024]{1,0:T(8,128)(2,1)S(1)}) custom-call(s32[4]{0:T(128)S(1)} %get-tuple-element.38.place_ref, s32[4]{0:T(128)S(1)} %compare_convert_fusion.first_ref, bf16[512,1024]{1,0:T(8,128)(2,1)S(1)} %copy-done.4, bf16[384,512]{1,0:T(8,128)(2,1)S(1)} %collective-permute-done.6.refs_0_, ...), custom_call_target="tpu_custom_call" | custom-call | flops 1073741824 | bytes 4194304 | tf_op jit(solution)/shard_map/project/pallas_call | solution.py:353
  112.3 0.6 collective-permute-start.13
  112.8 0.5 fusion.6
  113.3 0.7 fusion.8
  114.0 1.5 %collective-permute-start.15 = (bf16[256,512]{1,0:T(8,128)(2,1)S(1)}, bf16[256,512]{1,0:T(8,128)(2,1)S(1)}, u32[]{:S(2)}, u32[]{:S(2)}) collective-permute-start(bf16[256,512]{1,0:T(8,128)(2,1)S(1)} %get-tuple-element.76), channel_id=1, source_target_pairs={{0,2},{1,3},{2,0},{3,1},{4,6},{5,7},{6,4},{7,5},{8,10},{9,11},{10,... | collective-permute-start | bytes 786440 | tf_op jit(solution)/shard_map/ppermute | solution.py:404
  115.5 0.4 convert_add_fusion.1
  115.9 1.3 copy-done.11
  117.3 0.1 slice.32
  117.4 1.1 collective-permute-start.18
  118.5 4.7 %collective-permute-done.15 = bf16[256,512]{1,0:T(8,128)(2,1)S(1)} collective-permute-done((bf16[256,512]{1,0:T(8,128)(2,1)S(1)}, bf16[256,512]{1,0:T(8,128)(2,1)S(1)}, u32[]{:S(2)}, u32[]{:S(2)}) %collective-permute-start.15) | collective-permute-done | bytes 262176 | tf_op jit(solution)/shard_map/ppermute | solution.py:404
  123.2 0.8 fusion.7
  124.0 0.5 collective-permute-start.17
  124.5 1.5 %collective-permute-start.16 = (bf16[512,512]{1,0:T(8,128)(2,1)S(1)}, bf16[512,512]{1,0:T(8,128)(2,1)}, u32[]{:S(2)}, u32[]{:S(2)}) collective-permute-start(bf16[512,512]{1,0:T(8,128)(2,1)S(1)} %slice.32), channel_id=1, source_target_pairs={{0,2},{1,3},{2,0},{3,1},{4,6},{5,7},{6,4},{7,5},{8,10},{9,11},{10,... | collective-permute-start | bytes 1572872 | tf_op jit(solution)/shard_map/ppermute | solution.py:404
  126.0 2.9 %collective-permute-done.18 = bf16[256,512]{1,0:T(8,128)(2,1)} collective-permute-done((bf16[256,512]{1,0:T(8,128)(2,1)}, bf16[256,512]{1,0:T(8,128)(2,1)}, u32[]{:S(2)}, u32[]{:S(2)}) %collective-permute-start.18) | collective-permute-done | bytes 262176 | tf_op jit(solution)/shard_map/ppermute | solution.py:404
  128.9 1.8 %collective-permute-done.17 = bf16[256,512]{1,0:T(8,128)(2,1)S(1)} collective-permute-done((bf16[256,512]{1,0:T(8,128)(2,1)}, bf16[256,512]{1,0:T(8,128)(2,1)S(1)}, u32[]{:S(2)}, u32[]{:S(2)}) %collective-permute-start.17) | collective-permute-done | bytes 262176 | tf_op jit(solution)/shard_map/ppermute | solution.py:404
  130.7 1.0 add_convert_fusion
  131.7 0.6 collective-permute-start.19
  132.3 6.9 %collective-permute-done.16 = bf16[512,512]{1,0:T(8,128)(2,1)} collective-permute-done((bf16[512,512]{1,0:T(8,128)(2,1)S(1)}, bf16[512,512]{1,0:T(8,128)(2,1)}, u32[]{:S(2)}, u32[]{:S(2)}) %collective-permute-start.16) | collective-permute-done | bytes 524320 | tf_op jit(solution)/shard_map/ppermute | solution.py:404
  139.2 1.5 %fusion.2 = bf16[512,512]{1,0:T(8,128)(2,1)S(1)} fusion(f32[512,1024]{1,0:T(8,128)} %copy-done.11, bf16[512,512]{1,0:T(8,128)(2,1)} %collective-permute-done.16), kind=kLoop, calls=%fused_computation.8 | loop fusion | flops 786432 | bytes 2097152 | tf_op jit(solution)/shard_map/convert_element_type | solution.py:400
  140.8 1.3 maximum_select_fusion
  (48 shorter events, 0.2 us)
Async XLA Ops:
  0.0 1.6 %copy-start = (bf16[1024,1024]{1,0:T(8,128)(2,1)S(1)}, bf16[1024,1024]{1,0:T(8,128)(2,1)}, u32[]{:S(2)}) copy-start(bf16[1024,1024]{1,0:T(8,128)(2,1)} %param.13) | copy-start | bytes 6291460
  0.0 5.2 %copy-start.17 = (f32[2,8,512]{2,1,0:T(8,128)S(1)}, f32[2,8,512]{2,1,0:T(8,128)}, u32[]{:S(2)}) copy-start(f32[2,8,512]{2,1,0:T(8,128)} %param.11) | copy-start | bytes 98308
  1.7 31.0 %collective-permute-start = (bf16[1024,512]{1,0:T(8,128)(2,1)S(1)}, bf16[1024,512]{1,0:T(8,128)(2,1)}, u32[]{:S(2)}, u32[]{:S(2)}) collective-permute-start(bf16[1024,512]{1,0:T(8,128)(2,1)S(1)} %constant_dynamic-slice_fusion.refs_0_), channel_id=1, source_target_pairs={{0,4},{4,8},{8,12},{1,5},{5,9},{9,13},{2,6},{6,10},{10,14},{3,7},{... | collective-permute-start | bytes 3145736 | tf_op jit(solution)/shard_map/ppermute | solution.py:404
  6.2 26.5 %collective-permute-start.1 = (bf16[1024,512]{1,0:T(8,128)(2,1)S(1)}, bf16[1024,512]{1,0:T(8,128)(2,1)S(1)}, u32[]{:S(2)}, u32[]{:S(2)}) collective-permute-start(bf16[1024,512]{1,0:T(8,128)(2,1)S(1)} %constant_dynamic-slice_fusion.refs_0_), channel_id=1, source_target_pairs={{4,0},{8,4},{12,8},{5,1},{9,5},{13,9},{6,2},{10,6},{14,10},{7,3},{... | collective-permute-start | bytes 3145736 | tf_op jit(solution)/shard_map/ppermute | solution.py:404
  26.7 41.1 %collective-permute-start.8 = (bf16[320,2048]{1,0:T(8,128)(2,1)}, bf16[320,2048]{1,0:T(8,128)(2,1)S(1)}, u32[]{:S(2)}, u32[]{:S(2)}) collective-permute-start(bf16[320,2048]{1,0:T(8,128)(2,1)} %get-tuple-element.40.first_ref), channel_id=1, source_target_pairs={{0,16},{16,0},{1,17},{17,1},{2,18},{18,2},{3,19},{19,3},{4,20},{20... | collective-permute-start | bytes 3932168 | tf_op jit(solution)/shard_map/ppermute | solution.py:404
  32.7 19.2 %copy-start.7 = (bf16[1024,512]{1,0:T(8,128)(2,1)}, bf16[1024,512]{1,0:T(8,128)(2,1)S(1)}, u32[]{:S(2)}) copy-start(bf16[1024,512]{1,0:T(8,128)(2,1)S(1)} %collective-permute-done.1.refs_2_) | copy-start | bytes 3145732
  32.7 25.8 %collective-permute-start.3 = (bf16[1024,512]{1,0:T(8,128)(2,1)}, bf16[1024,512]{1,0:T(8,128)(2,1)S(1)}, u32[]{:S(2)}, u32[]{:S(2)}) collective-permute-start(bf16[1024,512]{1,0:T(8,128)(2,1)} %collective-permute-done.refs_3_), channel_id=1, source_target_pairs={{4,8},{8,12},{5,9},{9,13},{6,10},{10,14},{7,11},{11,15},{20,24},{2... | collective-permute-start | bytes 3145736 | tf_op jit(solution)/shard_map/ppermute | solution.py:404
  34.7 33.2 %collective-permute-start.7 = (bf16[1024,512]{1,0:T(8,128)(2,1)S(1)}, bf16[1024,512]{1,0:T(8,128)(2,1)}, u32[]{:S(2)}, u32[]{:S(2)}) collective-permute-start(bf16[1024,512]{1,0:T(8,128)(2,1)S(1)} %collective-permute-done.1.refs_2_), channel_id=1, source_target_pairs={{4,0},{8,4},{5,1},{9,5},{6,2},{10,6},{7,3},{11,7},{20,16},{24,20},... | collective-permute-start | bytes 3145736 | tf_op jit(solution)/shard_map/ppermute | solution.py:404
  51.9 15.0 %copy-start.14 = (f32[8,128,128]{2,1,0:T(8,128)S(1)}, f32[8,128,128]{2,1,0:T(8,128)}, u32[]{:S(2)}) copy-start(f32[8,128,128]{2,1,0:T(8,128)} %get-tuple-element.48) | copy-start | bytes 1572868
  51.9 15.0 %copy-start.16 = (bf16[8,128,128]{2,1,0:T(8,128)(2,1)S(1)}, bf16[8,128,128]{2,1,0:T(8,128)(2,1)}, u32[]{:S(2)}) copy-start(bf16[8,128,128]{2,1,0:T(8,128)(2,1)} %get-tuple-element.47) | copy-start | bytes 786436
  52.0 0.8 collective-permute-start.4
  52.8 21.3 %copy-start.20 = (s32[4]{0:T(128)S(1)}, s32[4]{0:T(128)}, u32[]{:S(2)}) copy-start(s32[4]{0:T(128)} %constant.36.clone) | copy-start | bytes 52
  54.1 12.7 %collective-permute-start.5 = (bf16[8,128,128]{2,1,0:T(8,128)(2,1)S(1)}, bf16[8,128,128]{2,1,0:T(8,128)(2,1)S(1)}, u32[]{:S(2)}, u32[]{:S(2)}) collective-permute-start(bf16[8,128,128]{2,1,0:T(8,128)(2,1)S(1)} %fusion), channel_id=1, source_target_pairs={{4,8},{5,9},{6,10},{7,11},{20,24},{21,25},{22,26},{23,27}} | collective-permute-start | bytes 786440 | tf_op jit(solution)/shard_map/ppermute | solution.py:404
  58.5 9.3 %copy-start.12 = (bf16[1024,512]{1,0:T(8,128)(2,1)}, bf16[1024,512]{1,0:T(8,128)(2,1)S(1)}, u32[]{:S(2)}) copy-start(bf16[1024,512]{1,0:T(8,128)(2,1)S(1)} %collective-permute-done.3) | copy-start | bytes 3145732
  58.6 9.3 %collective-permute-start.6 = (bf16[384,512]{1,0:T(8,128)(2,1)S(1)}, bf16[384,512]{1,0:T(8,128)(2,1)S(1)}, u32[]{:S(2)}, u32[]{:S(2)}) collective-permute-start(bf16[384,512]{1,0:T(8,128)(2,1)S(1)} %slice.25), channel_id=1, source_target_pairs={{8,12},{9,13},{10,14},{11,15},{24,28},{25,29},{26,30},{27,31}} | collective-permute-start | bytes 1179656 | tf_op jit(solution)/shard_map/ppermute | solution.py:404
  60.8 23.8 %copy-start.19 = (s32[4]{0:T(128)S(1)}, s32[4]{0:T(128)}, u32[]{:S(2)}) copy-start(s32[4]{0:T(128)} %constant.38) | copy-start | bytes 52
  60.8 23.8 %copy-start.18 = (s32[4]{0:T(128)S(1)}, s32[4]{0:T(128)}, u32[]{:S(2)}) copy-start(s32[4]{0:T(128)} %constant.37.clone) | copy-start | bytes 52
  60.8 24.5 %collective-permute-start.2 = (bf16[192,2048]{1,0:T(8,128)(2,1)}, bf16[192,2048]{1,0:T(8,128)(2,1)}, u32[]{:S(2)}, u32[]{:S(2)}) collective-permute-start(bf16[192,2048]{1,0:T(8,128)(2,1)} %get-tuple-element.44.second_ref), channel_id=1, source_target_pairs={{0,16},{16,0},{1,17},{17,1},{2,18},{18,2},{3,19},{19,3},{4,20},{20... | collective-permute-start | bytes 2359304 | tf_op jit(solution)/shard_map/ppermute | solution.py:404
  66.9 2.6 %copy-start.13 = (bf16[8,128,128]{2,1,0:T(8,128)(2,1)}, bf16[8,128,128]{2,1,0:T(8,128)(2,1)S(1)}, u32[]{:S(2)}) copy-start(bf16[8,128,128]{2,1,0:T(8,128)(2,1)S(1)} %add.36) | copy-start | bytes 786436
  67.8 1.7 %copy-start.15 = (bf16[320,2048]{1,0:T(8,128)(2,1)}, bf16[320,2048]{1,0:T(8,128)(2,1)S(1)}, u32[]{:S(2)}) copy-start(bf16[320,2048]{1,0:T(8,128)(2,1)S(1)} %collective-permute-done.8.first_ref) | copy-start | bytes 3932164
  67.9 37.5 %collective-permute-start.11 = (bf16[1024,512]{1,0:T(8,128)(2,1)}, bf16[1024,512]{1,0:T(8,128)(2,1)}, u32[]{:S(2)}, u32[]{:S(2)}) collective-permute-start(bf16[1024,512]{1,0:T(8,128)(2,1)} %collective-permute-done.7), channel_id=1, source_target_pairs={{4,0},{5,1},{6,2},{7,3},{20,16},{21,17},{22,18},{23,19}} | collective-permute-start | bytes 3145736 | tf_op jit(solution)/shard_map/ppermute | solution.py:404
  69.5 8.0 %collective-permute-start.9 = (bf16[8,128,128]{2,1,0:T(8,128)(2,1)}, bf16[8,128,128]{2,1,0:T(8,128)(2,1)}, u32[]{:S(2)}, u32[]{:S(2)}) collective-permute-start(bf16[8,128,128]{2,1,0:T(8,128)(2,1)} %fusion.1), channel_id=1, source_target_pairs={{8,12},{9,13},{10,14},{11,15},{24,28},{25,29},{26,30},{27,31}} | collective-permute-start | bytes 786440 | tf_op jit(solution)/shard_map/ppermute | solution.py:404
  79.3 26.1 %collective-permute-start.10 = (bf16[640,512]{1,0:T(8,128)(2,1)}, bf16[640,512]{1,0:T(8,128)(2,1)}, u32[]{:S(2)}, u32[]{:S(2)}) collective-permute-start(bf16[640,512]{1,0:T(8,128)(2,1)} %slice.24), channel_id=1, source_target_pairs={{8,12},{9,13},{10,14},{11,15},{24,28},{25,29},{26,30},{27,31}} | collective-permute-start | bytes 1966088 | tf_op jit(solution)/shard_map/ppermute | solution.py:404
  85.3 12.0 %collective-permute-start.12 = (bf16[8,128,128]{2,1,0:T(8,128)(2,1)}, bf16[8,128,128]{2,1,0:T(8,128)(2,1)}, u32[]{:S(2)}, u32[]{:S(2)}) collective-permute-start(bf16[8,128,128]{2,1,0:T(8,128)(2,1)} %add.38.s_ref), channel_id=1, source_target_pairs={{0,16},{16,0},{1,17},{17,1},{2,18},{18,2},{3,19},{19,3},{4,20},{20... | collective-permute-start | bytes 786440 | tf_op jit(solution)/shard_map/ppermute | solution.py:404
  92.6 1.2 copy-start.1
  93.9 1.2 copy-start.3
  96.3 1.0 copy-start.9
  100.7 1.2 copy-start.2
  101.9 1.2 copy-start.5
  103.2 2.2 %copy-start.6 = (bf16[512,1024]{1,0:T(8,128)(2,1)S(1)}, bf16[512,1024]{1,0:T(8,128)(2,1)}, u32[]{:S(2)}) copy-start(bf16[512,1024]{1,0:T(8,128)(2,1)} %normed_rows.3.a_ref) | copy-start | bytes 3145732
  103.2 2.2 %copy-start.8 = (bf16[1024,512]{1,0:T(8,128)(2,1)S(1)}, bf16[1024,512]{1,0:T(8,128)(2,1)}, u32[]{:S(2)}) copy-start(bf16[1024,512]{1,0:T(8,128)(2,1)} %copy-done.7) | copy-start | bytes 3145732
  104.4 1.0 copy-start.10
  105.4 3.5 %copy-start.4 = (bf16[512,1024]{1,0:T(8,128)(2,1)S(1)}, bf16[512,1024]{1,0:T(8,128)(2,1)}, u32[]{:S(2)}) copy-start(bf16[512,1024]{1,0:T(8,128)(2,1)} %normed_rows.2.a_ref) | copy-start | bytes 3145732
  108.8 4.0 %collective-permute-start.14 = (bf16[512,1024]{1,0:T(8,128)(2,1)S(1)}, bf16[512,1024]{1,0:T(8,128)(2,1)S(1)}, u32[]{:S(2)}, u32[]{:S(2)}) collective-permute-start(bf16[512,1024]{1,0:T(8,128)(2,1)S(1)} %get-tuple-element.63), channel_id=1, source_target_pairs={{0,1},{1,0},{2,3},{3,2},{4,5},{5,4},{6,7},{7,6},{8,9},{9,8},{10,11... | collective-permute-start | bytes 3145736 | tf_op jit(solution)/shard_map/ppermute | solution.py:391
  112.3 3.3 %collective-permute-start.13 = (bf16[512,1024]{1,0:T(8,128)(2,1)S(1)}, bf16[512,1024]{1,0:T(8,128)(2,1)S(1)}, u32[]{:S(2)}, u32[]{:S(2)}) collective-permute-start(bf16[512,1024]{1,0:T(8,128)(2,1)S(1)} %get-tuple-element.60), channel_id=1, source_target_pairs={{0,1},{1,0},{2,3},{3,2},{4,5},{5,4},{6,7},{7,6},{8,9},{9,8},{10,11... | collective-permute-start | bytes 3145736 | tf_op jit(solution)/shard_map/ppermute | solution.py:391
  114.0 9.2 %collective-permute-start.15 = (bf16[256,512]{1,0:T(8,128)(2,1)S(1)}, bf16[256,512]{1,0:T(8,128)(2,1)S(1)}, u32[]{:S(2)}, u32[]{:S(2)}) collective-permute-start(bf16[256,512]{1,0:T(8,128)(2,1)S(1)} %get-tuple-element.76), channel_id=1, source_target_pairs={{0,2},{1,3},{2,0},{3,1},{4,6},{5,7},{6,4},{7,5},{8,10},{9,11},{10,... | collective-permute-start | bytes 786440 | tf_op jit(solution)/shard_map/ppermute | solution.py:404
  115.9 1.4 copy-start.11
  117.4 11.6 %collective-permute-start.18 = (bf16[256,512]{1,0:T(8,128)(2,1)}, bf16[256,512]{1,0:T(8,128)(2,1)}, u32[]{:S(2)}, u32[]{:S(2)}) collective-permute-start(bf16[256,512]{1,0:T(8,128)(2,1)} %get-tuple-element.67), channel_id=1, source_target_pairs={{0,2},{1,3},{2,0},{3,1},{4,6},{5,7},{6,4},{7,5},{8,10},{9,11},{10,... | collective-permute-start | bytes 786440 | tf_op jit(solution)/shard_map/ppermute | solution.py:404
  124.0 6.7 %collective-permute-start.17 = (bf16[256,512]{1,0:T(8,128)(2,1)}, bf16[256,512]{1,0:T(8,128)(2,1)S(1)}, u32[]{:S(2)}, u32[]{:S(2)}) collective-permute-start(bf16[256,512]{1,0:T(8,128)(2,1)} %get-tuple-element.72), channel_id=1, source_target_pairs={{0,16},{16,0},{1,17},{17,1},{2,18},{18,2},{3,19},{19,3},{4,20},{20... | collective-permute-start | bytes 786440 | tf_op jit(solution)/shard_map/ppermute | solution.py:404
  124.5 14.7 %collective-permute-start.16 = (bf16[512,512]{1,0:T(8,128)(2,1)S(1)}, bf16[512,512]{1,0:T(8,128)(2,1)}, u32[]{:S(2)}, u32[]{:S(2)}) collective-permute-start(bf16[512,512]{1,0:T(8,128)(2,1)S(1)} %slice.32), channel_id=1, source_target_pairs={{0,2},{1,3},{2,0},{3,1},{4,6},{5,7},{6,4},{7,5},{8,10},{9,11},{10,... | collective-permute-start | bytes 1572872 | tf_op jit(solution)/shard_map/ppermute | solution.py:404
  131.7 9.0 %collective-permute-start.19 = (bf16[256,512]{1,0:T(8,128)(2,1)S(1)}, bf16[256,512]{1,0:T(8,128)(2,1)S(1)}, u32[]{:S(2)}, u32[]{:S(2)}) collective-permute-start(bf16[256,512]{1,0:T(8,128)(2,1)S(1)} %add_convert_fusion), channel_id=1, source_target_pairs={{0,16},{16,0},{1,17},{17,1},{2,18},{18,2},{3,19},{19,3},{4,20},{20... | collective-permute-start | bytes 786440 | tf_op jit(solution)/shard_map/ppermute | solution.py:404

commit v10 on v8

--- a/solution.py
+++ b/solution.py
@@ -280,68 +280,56 @@
     )(first, second, incoming, gain.reshape(1, width))
 
 
-def project_kernel(choices, place_ref, first_ref, a_ref, *refs):
-    count = sum(sum(options) for options in choices)
-    weights = list(refs[:count])
-    give_ref, keep_ref, held, sems = refs[count:]
-    half, block = len(choices) // 2, held.shape[2]
-    whole = weights[0]
-
-    def fetch(slot, pieces):
-        row = 0
+def project_kernel(options, pick_ref, a_ref, *refs):
+    count = sum(options)
+    weights, (*outs, rows, rows_sem, held, sems) = refs[:count], refs[count:]
+    copy_rows = pltpu.make_async_copy(a_ref, rows, rows_sem)
+    copy_rows.start()
+
+    def fetch(place, pieces):
+        at = 0
         for piece in pieces:
-            rows = pl.ds(row, piece.shape[0])
-            pltpu.make_async_copy(piece, held.at[slot, rows], sems.at[slot]).start()
-            row += piece.shape[0]
-
-    for slot, options in enumerate(choices):
+            to = held.at[place, pl.ds(at, piece.shape[0])]
+            pltpu.make_async_copy(piece, to, sems.at[place]).start()
+            at += piece.shape[0]
+
+    for place in range(len(outs)):
+        at = 0
         for option, pieces in enumerate(options):
-            taken, weights = weights[:pieces], weights[pieces:]
-            if len(options) == 1:
-                fetch(slot, taken)
-            else:
-                pl.when(first_ref[slot] == 1 - option)(functools.partial(fetch, slot, taken))
-    for slot in range(len(choices)):
-        pltpu.make_async_copy(whole, held.at[slot], sems.at[slot]).wait()
-        product = mxu(a_ref[...], held[slot]).astype(BF16)
-        place = place_ref[slot]
-
-        @pl.when(place < half)
-        def _():
-            give_ref[:, pl.ds(pl.multiple_of(place * block, block), block)] = product
-
-        @pl.when(place >= half)
-        def _():
-            keep_ref[:, pl.ds(pl.multiple_of((place - half) * block, block), block)] = product
-
-
-def project(places, first, rows, weights):
+            taken = weights[at : at + pieces]
+            at += pieces
+            pl.when(pick_ref[place] == option)(functools.partial(fetch, place, taken))
+    copy_rows.wait()
+    for place, out in enumerate(outs):
+        pltpu.make_async_copy(weights[0], held.at[place], sems.at[place]).wait()
+        out[...] = mxu(rows[...], held[place]).astype(BF16)
+
+
+def project(picks, rows, weights):
     tokens, depth = rows.shape
-    count = len(weights)
-    block = weights[0][0][0].shape[1]
-    choices = tuple(tuple(len(pieces) for pieces in options) for options in weights)
-    flat = [piece for options in weights for pieces in options for piece in pieces]
-    half = pl.BlockSpec(memory_space=pltpu.VMEM)
-    shape = jax.ShapeDtypeStruct((tokens, count // 2 * block), BF16)
+    count = picks.shape[0]
+    block = weights[0][0].shape[1]
+    flat = [piece for pieces in weights for piece in pieces]
     return pl.pallas_call(
-        functools.partial(project_kernel, choices),
-        in_specs=[pl.BlockSpec(memory_space=pltpu.SMEM)] * 2
-        + [half]
-        + [pl.BlockSpec(memory_space=pl.ANY)] * len(flat),
-        out_specs=[half, half],
-        out_shape=[shape, shape],
+        functools.partial(project_kernel, tuple(len(pieces) for pieces in weights)),
+        in_specs=[pl.BlockSpec(memory_space=pltpu.SMEM)]
+        + [pl.BlockSpec(memory_space=pl.ANY)] * (1 + len(flat)),
+        out_specs=[pl.BlockSpec(memory_space=pltpu.VMEM)] * count,
+        out_shape=[jax.ShapeDtypeStruct((tokens, block), BF16)] * count,
         scratch_shapes=[
+            pltpu.VMEM((tokens, depth), BF16),
+            pltpu.SemaphoreType.DMA,
             pltpu.VMEM((count, depth, block), BF16),
             pltpu.SemaphoreType.DMA((count,)),
         ],
-        compiler_params=pltpu.CompilerParams(vmem_limit_bytes=48 * 1024 * 1024),
+        compiler_params=pltpu.CompilerParams(vmem_limit_bytes=16 * 1024 * 1024),
         cost_estimate=pl.CostEstimate(
             flops=2 * tokens * depth * block * count,
             bytes_accessed=2 * (tokens * depth + (tokens + depth) * block * count),
             transcendentals=0,
         ),
         name="project",
-    )(places, first, rows, *flat)
+    )(picks, rows, *flat)
 
 
 def halving_order(count):
@@ -426,30 +414,49 @@
         pass_down(3)
         up_rest, incoming = tied(up[2][ahead:], incoming)
         up[3] = [up_first, send(up_rest, "ctx", last)]
-        weights = [([own],), ([up[1]], [down[3]]), ([up[2]], [down[2]]), (up[3], [down[1]])]
-        targets = lax.rem(here + ctx - jnp.arange(ctx), ctx)
-        first = (here >= jnp.arange(ctx)).astype(jnp.int32)
+        weights = [[own], [up[1]], [down[3]], [up[2]], [down[2]], up[3], [down[1]]]
+        slots = lax.rem(here + ctx - jnp.arange(ctx), ctx)
+        block_of = jnp.where(slots == 0, 0, 2 * slots - (here >= slots).astype(jnp.int32))
     else:
         whole = lax.all_gather(own, "ctx", axis=1, tiled=True)
-        weights = [([w],) for w in jnp.split(whole, head, axis=1)]
-        targets = jnp.arange(head)
-        first = jnp.ones((head,), jnp.int32)
+        weights = [[w] for w in jnp.split(whole, head, axis=1)]
+        block_of = jnp.arange(head)
     far_other, incoming = tied(far_other, incoming)
     incoming_other = send(incoming, "groups", swap)
     mine = normed_rows(near, far, incoming, gain)
     other = normed_rows(near_other, far_other, incoming_other, gain)
-    distance = targets ^ lax.axis_index("head")
-    order = jnp.asarray(halving_order(head), jnp.int32)
-    places = jnp.argmax(distance[:, None] == order[None, :], axis=1).astype(jnp.int32)
     mine, other = tied(mine, other)
-    give, keep = head_halved(*project(places, first, other, weights))
-    own_give, own_keep = head_halved(*project(places, first, mine, weights))
-    last_pairs = head_pairs(head // 2)
-    give_a, give_b = jnp.split(give, 2)
+    order = lax.axis_index("head") ^ jnp.asarray(halving_order(head), jnp.int32)
+    picks = jnp.sum(
+        jnp.where(order[:, None] == jnp.arange(head)[None, :], block_of[None, :], 0), axis=1
+    ).astype(jnp.int32)
+    if head == 4:
+        near_pairs, last_pairs = head_pairs(1), head_pairs(2)
+        sent, kept = project(picks[0::2], other, weights)
+        own_sent, own_kept = project(picks[0::2], mine, weights)
+        sent, own_sent = send(sent, "head", near_pairs), send(own_sent, "head", near_pairs)
+        give_a, give_b = jnp.split(summed(kept, sent), 2)
+        own_give = summed(own_kept, own_sent)
+        got_a = send(give_a, "head", last_pairs)
+        give_b, own_give = tied(give_b, own_give)
+        got_b = send(give_b, "head", last_pairs)
+        other, mine, got_a = tied(other, mine, got_a)
+        sent, kept = project(picks[1::2], other, weights)
+        own_sent, own_kept = project(picks[1::2], mine, weights)
+        keep = kept.astype(F32) + send(sent, "head", near_pairs).astype(F32)
+        own_keep = own_kept.astype(F32) + send(own_sent, "head", near_pairs).astype(F32)
+    else:
+        last_pairs = head_pairs(head // 2)
+        sides = []
+        for rows in (other, mine):
+            parts = project(picks, rows, weights)
+            give, keep = parts[: head // 2], parts[head // 2 :]
+            sides += head_halved(jnp.concatenate(give, axis=1), jnp.concatenate(keep, axis=1))
+        give, keep, own_give, own_keep = sides
+        give_a, give_b = jnp.split(give, 2)
+        got_a = send(give_a, "head", last_pairs)
+        got_b = send(give_b, "head", last_pairs)
     keep_a, keep_b = jnp.split(keep, 2)
-    got_a = send(give_a, "head", last_pairs)
-    give_b, own_give = tied(give_b, own_give)
-    got_b = send(give_b, "head", last_pairs)
     got_a, own_give = tied(got_a, own_give)
     back_a = send(summed(keep_a, got_a), "groups", swap)
     own_got = send(own_give, "head", last_pairs)

time: 132 us -> 147 us (1.11)
  waiting for transfers between devices: 25.6 us -> 31.6 us
  Pallas kernels: 45.7 us -> 50.7 us
  local copies, waits for them, and re-layouts: 7.06 us -> 10.5 us
  other arithmetic: 7.06 us -> 8.83 us
    ppermute x18 -> x22, waiting for transfers between devices: 25.6 us -> 31.6 us  [send(): return lax.ppermute(value, axis, pairs)]
    pallas_call x2 -> x4, Pallas kernels: 8.48 us -> 13.4 us  [project(): pl.pallas_call(functools.partial(project_kernel, tuple((len(pieces) for p...]
    unnamed x21 -> x37, local copies, waits for them, and re-layouts: 4.18 us -> 7.35 us
    convert_element_type x2 -> x4, other arithmetic: 2.54 us -> 4.59 us  [summed(): return (keep.astype(F32) + got.astype(F32)).astype(BF16)]
    ppermute x18 -> x22, starting transfers between devices: 43 us -> 42.7 us  [send(): return lax.ppermute(value, axis, pairs)]
  transfers between devices with their start and end apart: 20 -> 22, of which waited for: 10 -> 11; matrix products, arithmetic and copies ran while one was open for 8% -> 8% of each run, Pallas kernels for 32% -> 32%
where the time goes in v10:
time: 147 us; the launch traced here: 146 us
  Pallas kernels  50.7 us (34%)
  starting transfers between devices  42.7 us (29%)
  waiting for transfers between devices  31.6 us (21%)
  local copies, waits for them, and re-layouts  10.5 us (7%)
  other arithmetic  8.83 us (6%)
  matrix products  1.56 us (1%)
    ppermute x22, starting transfers between devices, send(): return lax.ppermute(value, axis, pairs)  42.7 us
    ppermute x22, waiting for transfers between devices, send(): return lax.ppermute(value, axis, pairs)  31.6 us
    pallas_call x2, Pallas kernels, local_part(): pl.pallas_call(functools.partial(chunk_kernel, group, first), grid=(steps...  30.4 us
    pallas_call x4, Pallas kernels, project(): pl.pallas_call(functools.partial(project_kernel, tuple((len(pieces) for p...  13.4 us
    unnamed x37, local copies, waits for them, and re-layouts  7.35 us
    pallas_call x2, Pallas kernels, normed_rows(): pl.pallas_call(norm_kernel, in_specs=[pl.BlockSpec(memory_space=pltpu.VME...  6.91 us
    convert_element_type x4, other arithmetic, summed(): return (keep.astype(F32) + got.astype(F32)).astype(BF16)  4.59 us
  transfers between devices with their start and end apart: 22, of which 11 were waited for; matrix products, arithmetic and copies ran while one was open for 8% of the time, Pallas kernels for 32%

profile of v10, /device:TPU:16, one launch (start us, length us, event | category | flops | bytes accessed | tf_op | source)
XLA Modules:
  0.0 146.2 jit_solution(4676617296830931312)
XLA Ops:
  0.0 1.6 %copy-done = bf16[1024,1024]{1,0:T(8,128)(2,1)S(1)} copy-done((bf16[1024,1024]{1,0:T(8,128)(2,1)S(1)}, bf16[1024,1024]{1,0:T(8,128)(2,1)}, u32[]{:S(2)}) %copy-start) | copy-done | bytes 2097176
  1.6 0.1 constant_dynamic-slice_fusion.refs_0_
  1.7 2.4 %collective-permute-start.1 = (bf16[1024,512]{1,0:T(8,128)(2,1)S(1)}, bf16[1024,512]{1,0:T(8,128)(2,1)}, u32[]{:S(2)}, u32[]{:S(2)}) collective-permute-start(bf16[1024,512]{1,0:T(8,128)(2,1)S(1)} %constant_dynamic-slice_fusion.refs_0_), channel_id=1, source_target_pairs={{4,0},{8,4},{12,8},{5,1},{9,5},{13,9},{6,2},{10,6},{14,10},{7,3},{... | collective-permute-start | bytes 3145736 | tf_op jit(solution)/shard_map/ppermute | solution.py:364
  4.1 4.4 %collective-permute-start = (bf16[1024,512]{1,0:T(8,128)(2,1)S(1)}, bf16[1024,512]{1,0:T(8,128)(2,1)}, u32[]{:S(2)}, u32[]{:S(2)}) collective-permute-start(bf16[1024,512]{1,0:T(8,128)(2,1)S(1)} %constant_dynamic-slice_fusion.refs_0_), channel_id=1, source_target_pairs={{0,4},{4,8},{8,12},{1,5},{5,9},{9,13},{2,6},{6,10},{10,14},{3,7},{... | collective-permute-start | bytes 3145736 | tf_op jit(solution)/shard_map/ppermute | solution.py:364
  8.5 1.0 copy.9
  9.5 18.1 %local_part.2 = (bf16[320,2048]{1,0:T(8,128)(2,1)}, f32[8,128,256]{2,1,0:T(8,128)}) custom-call(bf16[512,1024]{1,0:T(8,128)(2,1)} %q_ref.3, bf16[512,2,1024]{2,1,0:T(2,128)(2,1)} %k_ref.3, bf16[512,2,1024]{2,1,0:T(2,128)(2,1)} %v_ref.3, f32[1024,8]{1,0:T(8,128)} %bitcast.7), custom_call_target="tpu_custom_call" | custom-call | flops 16777216000 | bytes 5242880 | tf_op jit(solution)/shard_map/local_part/pallas_call | solution.py:214
  27.6 1.5 %collective-permute-start.8 = (bf16[320,2048]{1,0:T(8,128)(2,1)}, bf16[320,2048]{1,0:T(8,128)(2,1)S(1)}, u32[]{:S(2)}, u32[]{:S(2)}) collective-permute-start(bf16[320,2048]{1,0:T(8,128)(2,1)} %get-tuple-element.42.first_ref), channel_id=1, source_target_pairs={{0,16},{16,0},{1,17},{17,1},{2,18},{18,2},{3,19},{19,3},{4,20},{20... | collective-permute-start | bytes 3932168 | tf_op jit(solution)/shard_map/ppermute | solution.py:364
  29.2 1.5 %collective-permute-done.refs_1_ = bf16[1024,512]{1,0:T(8,128)(2,1)} collective-permute-done((bf16[1024,512]{1,0:T(8,128)(2,1)S(1)}, bf16[1024,512]{1,0:T(8,128)(2,1)}, u32[]{:S(2)}, u32[]{:S(2)}) %collective-permute-start) | collective-permute-done | bytes 1048608 | tf_op jit(solution)/shard_map/ppermute | solution.py:364
  30.7 4.4 %collective-permute-start.3 = (bf16[1024,512]{1,0:T(8,128)(2,1)}, bf16[1024,512]{1,0:T(8,128)(2,1)S(1)}, u32[]{:S(2)}, u32[]{:S(2)}) collective-permute-start(bf16[1024,512]{1,0:T(8,128)(2,1)} %collective-permute-done.refs_1_), channel_id=1, source_target_pairs={{4,8},{8,12},{5,9},{9,13},{6,10},{10,14},{7,11},{11,15},{20,24},{2... | collective-permute-start | bytes 3145736 | tf_op jit(solution)/shard_map/ppermute | solution.py:364
  35.1 2.5 %collective-permute-start.7 = (bf16[1024,512]{1,0:T(8,128)(2,1)}, bf16[1024,512]{1,0:T(8,128)(2,1)}, u32[]{:S(2)}, u32[]{:S(2)}) collective-permute-start(bf16[1024,512]{1,0:T(8,128)(2,1)} %collective-permute-done.1.refs_7_), channel_id=1, source_target_pairs={{4,0},{8,4},{5,1},{9,5},{6,2},{10,6},{7,3},{11,7},{20,16},{24,20},... | collective-permute-start | bytes 3145736 | tf_op jit(solution)/shard_map/ppermute | solution.py:364
  37.6 12.3 %local_part.3 = (bf16[192,2048]{1,0:T(8,128)(2,1)}, f32[8,128,128]{2,1,0:T(8,128)}, bf16[8,128,128]{2,1,0:T(8,128)(2,1)}, bf16[8,128,128]{2,1,0:T(8,128)(2,1)}) custom-call(bf16[512,1024]{1,0:T(8,128)(2,1)} %q_ref.3, bf16[512,2,1024]{2,1,0:T(2,128)(2,1)} %k_ref.3, bf16[512,2,1024]{2,1,0:T(2,128)(2,1)} %v_ref.3, f32[1024,8]{1,0:T(8,128)} %bitcast.8, ...), custom_call_target="tpu_custom_call" | custom-call | flops 10066329600 | bytes 3145728 | tf_op jit(solution)/shard_map/local_part/pallas_call | solution.py:214
  49.9 0.8 collective-permute-start.4
  50.7 1.3 fusion
  52.1 1.3 collective-permute-start.5
  53.4 3.3 %collective-permute-done.3.refs_3_ = bf16[1024,512]{1,0:T(8,128)(2,1)S(1)} collective-permute-done((bf16[1024,512]{1,0:T(8,128)(2,1)}, bf16[1024,512]{1,0:T(8,128)(2,1)S(1)}, u32[]{:S(2)}, u32[]{:S(2)}) %collective-permute-start.3) | collective-permute-done | bytes 1048608 | tf_op jit(solution)/shard_map/ppermute | solution.py:364
  56.7 4.3 %collective-permute-start.6 = (bf16[256,512]{1,0:T(8,128)(2,1)S(1)}, bf16[256,512]{1,0:T(8,128)(2,1)S(1)}, u32[]{:S(2)}, u32[]{:S(2)}) collective-permute-start(bf16[256,512]{1,0:T(8,128)(2,1)S(1)} %slice.19), channel_id=1, source_target_pairs={{8,12},{9,13},{10,14},{11,15},{24,28},{25,29},{26,30},{27,31}} | collective-permute-start | bytes 786440 | tf_op jit(solution)/shard_map/ppermute | solution.py:364
  61.0 1.6 %collective-permute-start.2 = (bf16[192,2048]{1,0:T(8,128)(2,1)}, bf16[192,2048]{1,0:T(8,128)(2,1)}, u32[]{:S(2)}, u32[]{:S(2)}) collective-permute-start(bf16[192,2048]{1,0:T(8,128)(2,1)} %get-tuple-element.45.second_ref), channel_id=1, source_target_pairs={{0,16},{16,0},{1,17},{17,1},{2,18},{18,2},{3,19},{19,3},{4,20},{20... | collective-permute-start | bytes 2359304 | tf_op jit(solution)/shard_map/ppermute | solution.py:364
  62.6 2.1 %collective-permute-done.5 = bf16[8,128,128]{2,1,0:T(8,128)(2,1)S(1)} collective-permute-done((bf16[8,128,128]{2,1,0:T(8,128)(2,1)S(1)}, bf16[8,128,128]{2,1,0:T(8,128)(2,1)S(1)}, u32[]{:S(2)}, u32[]{:S(2)}) %collective-permute-start.5) | collective-permute-done | bytes 262176 | tf_op jit(solution)/shard_map/ppermute | solution.py:364
  64.7 0.1 add.42
  64.8 0.2 fusion.1
  65.1 4.1 %collective-permute-start.9 = (bf16[8,128,128]{2,1,0:T(8,128)(2,1)S(1)}, bf16[8,128,128]{2,1,0:T(8,128)(2,1)S(1)}, u32[]{:S(2)}, u32[]{:S(2)}) collective-permute-start(bf16[8,128,128]{2,1,0:T(8,128)(2,1)S(1)} %fusion.1), channel_id=1, source_target_pairs={{8,12},{9,13},{10,14},{11,15},{24,28},{25,29},{26,30},{27,31}} | collective-permute-start | bytes 786440 | tf_op jit(solution)/shard_map/ppermute | solution.py:364
  69.2 1.7 %collective-permute-start.11 = (bf16[1024,512]{1,0:T(8,128)(2,1)}, bf16[1024,512]{1,0:T(8,128)(2,1)}, u32[]{:S(2)}, u32[]{:S(2)}) collective-permute-start(bf16[1024,512]{1,0:T(8,128)(2,1)} %collective-permute-done.7.refs_4_), channel_id=1, source_target_pairs={{4,0},{5,1},{6,2},{7,3},{20,16},{21,17},{22,18},{23,19}} | collective-permute-start | bytes 3145736 | tf_op jit(solution)/shard_map/ppermute | solution.py:364
  70.9 1.0 slice.18
  71.9 1.2 collective-permute-done.9
  73.1 0.8 add.44.s_ref
  73.9 5.3 %collective-permute-start.12 = (bf16[768,512]{1,0:T(8,128)(2,1)}, bf16[768,512]{1,0:T(8,128)(2,1)}, u32[]{:S(2)}, u32[]{:S(2)}) collective-permute-start(bf16[768,512]{1,0:T(8,128)(2,1)} %slice.18), channel_id=1, source_target_pairs={{8,12},{9,13},{10,14},{11,15},{24,28},{25,29},{26,30},{27,31}} | collective-permute-start | bytes 2359304 | tf_op jit(solution)/shard_map/ppermute | solution.py:364
  79.1 1.5 %collective-permute-start.10 = (bf16[8,128,128]{2,1,0:T(8,128)(2,1)}, bf16[8,128,128]{2,1,0:T(8,128)(2,1)}, u32[]{:S(2)}, u32[]{:S(2)}) collective-permute-start(bf16[8,128,128]{2,1,0:T(8,128)(2,1)} %add.44.s_ref), channel_id=1, source_target_pairs={{0,16},{16,0},{1,17},{17,1},{2,18},{18,2},{3,19},{19,3},{4,20},{20... | collective-permute-start | bytes 786440 | tf_op jit(solution)/shard_map/ppermute | solution.py:364
  80.7 0.2 select_reduce_fusion
  80.9 0.1 slice.17.pick_ref
  81.0 3.5 %normed_rows.2.a_ref = bf16[512,1024]{1,0:T(8,128)(2,1)} custom-call(bf16[320,2048]{1,0:T(8,128)(2,1)} %get-tuple-element.42.first_ref, bf16[192,2048]{1,0:T(8,128)(2,1)} %get-tuple-element.45.second_ref, bf16[8,128,128]{2,1,0:T(8,128)(2,1)} %add.44.s_ref, f32[1,1024]{1,0:T(1,128)} %bitcast.10), custom_call_target="tpu_custom_call" | custom-call | flops 134217728 | bytes 3145728 | tf_op jit(solution)/shard_map/normed_rows/pallas_call | solution.py:271
  84.5 1.4 collective-permute-done.10.s_ref
  85.8 3.4 %normed_rows.3.a_ref = bf16[512,1024]{1,0:T(8,128)(2,1)} custom-call(bf16[320,2048]{1,0:T(8,128)(2,1)} %copy-done.14, bf16[192,2048]{1,0:T(8,128)(2,1)} %collective-permute-done.2.second_ref, bf16[8,128,128]{2,1,0:T(8,128)(2,1)} %collective-permute-done.10.s_ref, f32[1,1024]{1,0:T(1,128)} %bitcast.11), custom_call_target="tpu_custom_call" | custom-call | flops 134217728 | bytes 3145728 | tf_op jit(solution)/shard_map/normed_rows/pallas_call | solution.py:271
  89.2 2.1 %collective-permute-done.12.refs_6_ = bf16[768,512]{1,0:T(8,128)(2,1)} collective-permute-done((bf16[768,512]{1,0:T(8,128)(2,1)}, bf16[768,512]{1,0:T(8,128)(2,1)}, u32[]{:S(2)}, u32[]{:S(2)}) %collective-permute-start.12) | collective-permute-done | bytes 786464 | tf_op jit(solution)/shard_map/ppermute | solution.py:364
  91.3 1.2 copy-done.2
  92.6 1.2 copy-done.8
  93.8 3.3 %project.4 = (bf16[512,512]{1,0:T(8,128)(2,1)S(1)}, bf16[512,512]{1,0:T(8,128)(2,1)S(1)}) custom-call(s32[2]{0:T(128)S(1)} %slice.17.pick_ref, bf16[512,1024]{1,0:T(8,128)(2,1)S(1)} %copy-done.8, bf16[1024,512]{1,0:T(8,128)(2,1)S(1)} %constant_dynamic-slice_fusion.refs_0_, bf16[1024,512]{1,0:T(8,128)(2,1)} %collective-permute-done.refs_1_, ...), custom_call_target="tpu_custom_call" | custom-call | flops 1073741824 | bytes 4194304 | tf_op jit(solution)/shard_map/project/pallas_call | solution.py:313
  97.1 0.1 collective-permute-start.13
  97.2 3.4 %project.6 = (bf16[512,512]{1,0:T(8,128)(2,1)}, bf16[512,512]{1,0:T(8,128)(2,1)S(1)}) custom-call(s32[2]{0:T(128)S(1)} %slice.17.pick_ref, bf16[512,1024]{1,0:T(8,128)(2,1)S(1)} %copy-done.6, bf16[1024,512]{1,0:T(8,128)(2,1)S(1)} %constant_dynamic-slice_fusion.refs_0_, bf16[1024,512]{1,0:T(8,128)(2,1)} %collective-permute-done.refs_1_, ...), custom_call_target="tpu_custom_call" | custom-call | flops 1073741824 | bytes 4194304 | tf_op jit(solution)/shard_map/project/pallas_call | solution.py:313
  100.6 0.8 copy-done.10
  101.5 0.1 add_convert_fusion.2
  101.6 0.9 fusion.6
  102.5 1.4 collective-permute-start.14
  103.9 0.1 slice.14.pick_ref
  104.0 7.5 %collective-permute-done.14 = bf16[256,512]{1,0:T(8,128)(2,1)} collective-permute-done((bf16[256,512]{1,0:T(8,128)(2,1)}, bf16[256,512]{1,0:T(8,128)(2,1)}, u32[]{:S(2)}, u32[]{:S(2)}) %collective-permute-start.14) | collective-permute-done | bytes 262176 | tf_op jit(solution)/shard_map/ppermute | solution.py:364
  111.5 1.2 copy-done.4
  112.7 1.2 copy-done.9
  113.9 3.3 %project.7 = (bf16[512,512]{1,0:T(8,128)(2,1)S(1)}, bf16[512,512]{1,0:T(8,128)(2,1)S(1)}) custom-call(s32[2]{0:T(128)S(1)} %slice.14.pick_ref, bf16[512,1024]{1,0:T(8,128)(2,1)S(1)} %copy-done.9, bf16[1024,512]{1,0:T(8,128)(2,1)S(1)} %constant_dynamic-slice_fusion.refs_0_, bf16[1024,512]{1,0:T(8,128)(2,1)} %collective-permute-done.refs_1_, ...), custom_call_target="tpu_custom_call" | custom-call | flops 1073741824 | bytes 4194304 | tf_op jit(solution)/shard_map/project/pallas_call | solution.py:313
  117.2 0.1 collective-permute-start.18
  117.3 2.0 %add_convert_fusion.1 = bf16[512,512]{1,0:T(8,128)(2,1)} fusion(bf16[512,512]{1,0:T(8,128)(2,1)} %collective-permute-done.16, bf16[512,512]{1,0:T(8,128)(2,1)S(1)} %copy-done.11), kind=kLoop, calls=%fused_computation.7 | loop fusion | flops 1048576 | bytes 1572864 | tf_op jit(solution)/shard_map/convert_element_type | solution.py:360
  119.4 1.5 %collective-permute-start.20 = (bf16[256,512]{1,0:T(8,128)(2,1)}, bf16[256,512]{1,0:T(8,128)(2,1)}, u32[]{:S(2)}, u32[]{:S(2)}) collective-permute-start(bf16[256,512]{1,0:T(8,128)(2,1)} %get-tuple-element.75), channel_id=1, source_target_pairs={{0,2},{1,3},{2,0},{3,1},{4,6},{5,7},{6,4},{7,5},{8,10},{9,11},{10,... | collective-permute-start | bytes 786440 | tf_op jit(solution)/shard_map/ppermute | solution.py:364
  120.9 0.5 collective-permute-start.17
  121.4 3.4 %project.5 = (bf16[512,512]{1,0:T(8,128)(2,1)}, bf16[512,512]{1,0:T(8,128)(2,1)S(1)}) custom-call(s32[2]{0:T(128)S(1)} %slice.14.pick_ref, bf16[512,1024]{1,0:T(8,128)(2,1)S(1)} %copy-done.7, bf16[1024,512]{1,0:T(8,128)(2,1)S(1)} %constant_dynamic-slice_fusion.refs_0_, bf16[1024,512]{1,0:T(8,128)(2,1)} %collective-permute-done.refs_1_, ...), custom_call_target="tpu_custom_call" | custom-call | flops 1073741824 | bytes 4194304 | tf_op jit(solution)/shard_map/project/pallas_call | solution.py:313
  124.8 0.1 collective-permute-start.15
  124.9 0.1 convert_add_fusion
  125.1 1.8 %fusion.5 = (f32[256,512]{1,0:T(8,128)S(1)}, bf16[256,512]{1,0:T(8,128)(2,1)}) fusion(f32[512,512]{1,0:T(8,128)S(1)} %convert_add_fusion, bf16[256,512]{1,0:T(8,128)(2,1)} %collective-permute-done.14), kind=kLoop, calls=%fused_computation.24 | loop fusion | flops 393216 | bytes 2097152 | tf_op jit(solution)/shard_map/split | solution.py:459
  126.9 1.5 %collective-permute-start.19 = (bf16[256,512]{1,0:T(8,128)(2,1)}, bf16[256,512]{1,0:T(8,128)(2,1)S(1)}, u32[]{:S(2)}, u32[]{:S(2)}) collective-permute-start(bf16[256,512]{1,0:T(8,128)(2,1)} %get-tuple-element.80), channel_id=1, source_target_pairs={{0,16},{16,0},{1,17},{17,1},{2,18},{18,2},{3,19},{19,3},{4,20},{20... | collective-permute-start | bytes 786440 | tf_op jit(solution)/shard_map/ppermute | solution.py:364
  128.4 0.4 collective-permute-done.20
  128.8 7.0 %collective-permute-done.19 = bf16[256,512]{1,0:T(8,128)(2,1)S(1)} collective-permute-done((bf16[256,512]{1,0:T(8,128)(2,1)}, bf16[256,512]{1,0:T(8,128)(2,1)S(1)}, u32[]{:S(2)}, u32[]{:S(2)}) %collective-permute-start.19) | collective-permute-done | bytes 262176 | tf_op jit(solution)/shard_map/ppermute | solution.py:364
  135.8 1.0 add_convert_fusion.3
  136.8 1.6 %collective-permute-start.21 = (bf16[256,512]{1,0:T(8,128)(2,1)S(1)}, bf16[256,512]{1,0:T(8,128)(2,1)S(1)}, u32[]{:S(2)}, u32[]{:S(2)}) collective-permute-start(bf16[256,512]{1,0:T(8,128)(2,1)S(1)} %add_convert_fusion.3), channel_id=1, source_target_pairs={{0,16},{16,0},{1,17},{17,1},{2,18},{18,2},{3,19},{19,3},{4,20},{20... | collective-permute-start | bytes 786440 | tf_op jit(solution)/shard_map/ppermute | solution.py:364
  138.4 1.2 collective-permute-done.17
  139.6 1.4 add_convert_fusion
  141.0 3.9 %collective-permute-done.21 = bf16[256,512]{1,0:T(8,128)(2,1)S(1)} collective-permute-done((bf16[256,512]{1,0:T(8,128)(2,1)S(1)}, bf16[256,512]{1,0:T(8,128)(2,1)S(1)}, u32[]{:S(2)}, u32[]{:S(2)}) %collective-permute-start.21) | collective-permute-done | bytes 262176 | tf_op jit(solution)/shard_map/ppermute | solution.py:364
  144.9 1.3 maximum_select_fusion
  (46 shorter events, 0.2 us)
Async XLA Ops:
  0.0 1.6 %copy-start = (bf16[1024,1024]{1,0:T(8,128)(2,1)S(1)}, bf16[1024,1024]{1,0:T(8,128)(2,1)}, u32[]{:S(2)}) copy-start(bf16[1024,1024]{1,0:T(8,128)(2,1)} %param.12) | copy-start | bytes 6291460
  0.0 8.5 %copy-start.16 = (f32[2,8,512]{2,1,0:T(8,128)S(1)}, f32[2,8,512]{2,1,0:T(8,128)}, u32[]{:S(2)}) copy-start(f32[2,8,512]{2,1,0:T(8,128)} %param.10) | copy-start | bytes 98308
  1.7 27.5 %collective-permute-start.1 = (bf16[1024,512]{1,0:T(8,128)(2,1)S(1)}, bf16[1024,512]{1,0:T(8,128)(2,1)}, u32[]{:S(2)}, u32[]{:S(2)}) collective-permute-start(bf16[1024,512]{1,0:T(8,128)(2,1)S(1)} %constant_dynamic-slice_fusion.refs_0_), channel_id=1, source_target_pairs={{4,0},{8,4},{12,8},{5,1},{9,5},{13,9},{6,2},{10,6},{14,10},{7,3},{... | collective-permute-start | bytes 3145736 | tf_op jit(solution)/shard_map/ppermute | solution.py:364
  4.1 26.6 %collective-permute-start = (bf16[1024,512]{1,0:T(8,128)(2,1)S(1)}, bf16[1024,512]{1,0:T(8,128)(2,1)}, u32[]{:S(2)}, u32[]{:S(2)}) collective-permute-start(bf16[1024,512]{1,0:T(8,128)(2,1)S(1)} %constant_dynamic-slice_fusion.refs_0_), channel_id=1, source_target_pairs={{0,4},{4,8},{8,12},{1,5},{5,9},{9,13},{2,6},{6,10},{10,14},{3,7},{... | collective-permute-start | bytes 3145736 | tf_op jit(solution)/shard_map/ppermute | solution.py:364
  27.6 37.4 %collective-permute-start.8 = (bf16[320,2048]{1,0:T(8,128)(2,1)}, bf16[320,2048]{1,0:T(8,128)(2,1)S(1)}, u32[]{:S(2)}, u32[]{:S(2)}) collective-permute-start(bf16[320,2048]{1,0:T(8,128)(2,1)} %get-tuple-element.42.first_ref), channel_id=1, source_target_pairs={{0,16},{16,0},{1,17},{17,1},{2,18},{18,2},{3,19},{19,3},{4,20},{20... | collective-permute-start | bytes 3932168 | tf_op jit(solution)/shard_map/ppermute | solution.py:364
  30.7 26.0 %collective-permute-start.3 = (bf16[1024,512]{1,0:T(8,128)(2,1)}, bf16[1024,512]{1,0:T(8,128)(2,1)S(1)}, u32[]{:S(2)}, u32[]{:S(2)}) collective-permute-start(bf16[1024,512]{1,0:T(8,128)(2,1)} %collective-permute-done.refs_1_), channel_id=1, source_target_pairs={{4,8},{8,12},{5,9},{9,13},{6,10},{10,14},{7,11},{11,15},{20,24},{2... | collective-permute-start | bytes 3145736 | tf_op jit(solution)/shard_map/ppermute | solution.py:364
  35.1 29.9 %collective-permute-start.7 = (bf16[1024,512]{1,0:T(8,128)(2,1)}, bf16[1024,512]{1,0:T(8,128)(2,1)}, u32[]{:S(2)}, u32[]{:S(2)}) collective-permute-start(bf16[1024,512]{1,0:T(8,128)(2,1)} %collective-permute-done.1.refs_7_), channel_id=1, source_target_pairs={{4,0},{8,4},{5,1},{9,5},{6,2},{10,6},{7,3},{11,7},{20,16},{24,20},... | collective-permute-start | bytes 3145736 | tf_op jit(solution)/shard_map/ppermute | solution.py:364
  49.9 14.9 %copy-start.13 = (f32[8,128,128]{2,1,0:T(8,128)S(1)}, f32[8,128,128]{2,1,0:T(8,128)}, u32[]{:S(2)}) copy-start(f32[8,128,128]{2,1,0:T(8,128)} %get-tuple-element.49) | copy-start | bytes 1572868
  49.9 14.9 %copy-start.15 = (bf16[8,128,128]{2,1,0:T(8,128)(2,1)S(1)}, bf16[8,128,128]{2,1,0:T(8,128)(2,1)}, u32[]{:S(2)}) copy-start(bf16[8,128,128]{2,1,0:T(8,128)(2,1)} %get-tuple-element.48) | copy-start | bytes 786436
  49.9 0.8 collective-permute-start.4
  52.1 12.6 %collective-permute-start.5 = (bf16[8,128,128]{2,1,0:T(8,128)(2,1)S(1)}, bf16[8,128,128]{2,1,0:T(8,128)(2,1)S(1)}, u32[]{:S(2)}, u32[]{:S(2)}) collective-permute-start(bf16[8,128,128]{2,1,0:T(8,128)(2,1)S(1)} %fusion), channel_id=1, source_target_pairs={{4,8},{5,9},{6,10},{7,11},{20,24},{21,25},{22,26},{23,27}} | collective-permute-start | bytes 786440 | tf_op jit(solution)/shard_map/ppermute | solution.py:364
  56.6 15.2 %copy-start.1 = (bf16[1024,512]{1,0:T(8,128)(2,1)}, bf16[1024,512]{1,0:T(8,128)(2,1)S(1)}, u32[]{:S(2)}) copy-start(bf16[1024,512]{1,0:T(8,128)(2,1)S(1)} %collective-permute-done.3.refs_3_) | copy-start | bytes 3145732
  56.7 8.4 %collective-permute-start.6 = (bf16[256,512]{1,0:T(8,128)(2,1)S(1)}, bf16[256,512]{1,0:T(8,128)(2,1)S(1)}, u32[]{:S(2)}, u32[]{:S(2)}) collective-permute-start(bf16[256,512]{1,0:T(8,128)(2,1)S(1)} %slice.19), channel_id=1, source_target_pairs={{8,12},{9,13},{10,14},{11,15},{24,28},{25,29},{26,30},{27,31}} | collective-permute-start | bytes 786440 | tf_op jit(solution)/shard_map/ppermute | solution.py:364
  61.0 19.7 %copy-start.17 = (s32[4]{0:T(128)S(1)}, s32[4]{0:T(128)}, u32[]{:S(2)}) copy-start(s32[4]{0:T(128)} %constant.30.clone) | copy-start | bytes 52
  61.0 18.2 %collective-permute-start.2 = (bf16[192,2048]{1,0:T(8,128)(2,1)}, bf16[192,2048]{1,0:T(8,128)(2,1)}, u32[]{:S(2)}, u32[]{:S(2)}) collective-permute-start(bf16[192,2048]{1,0:T(8,128)(2,1)} %get-tuple-element.45.second_ref), channel_id=1, source_target_pairs={{0,16},{16,0},{1,17},{17,1},{2,18},{18,2},{3,19},{19,3},{4,20},{20... | collective-permute-start | bytes 2359304 | tf_op jit(solution)/shard_map/ppermute | solution.py:364
  65.0 8.8 %copy-start.14 = (bf16[320,2048]{1,0:T(8,128)(2,1)}, bf16[320,2048]{1,0:T(8,128)(2,1)S(1)}, u32[]{:S(2)}) copy-start(bf16[320,2048]{1,0:T(8,128)(2,1)S(1)} %collective-permute-done.8.first_ref) | copy-start | bytes 3932164
  65.1 8.0 %collective-permute-start.9 = (bf16[8,128,128]{2,1,0:T(8,128)(2,1)S(1)}, bf16[8,128,128]{2,1,0:T(8,128)(2,1)S(1)}, u32[]{:S(2)}, u32[]{:S(2)}) collective-permute-start(bf16[8,128,128]{2,1,0:T(8,128)(2,1)S(1)} %fusion.1), channel_id=1, source_target_pairs={{8,12},{9,13},{10,14},{11,15},{24,28},{25,29},{26,30},{27,31}} | collective-permute-start | bytes 786440 | tf_op jit(solution)/shard_map/ppermute | solution.py:364
  69.2 22.1 %collective-permute-start.11 = (bf16[1024,512]{1,0:T(8,128)(2,1)}, bf16[1024,512]{1,0:T(8,128)(2,1)}, u32[]{:S(2)}, u32[]{:S(2)}) collective-permute-start(bf16[1024,512]{1,0:T(8,128)(2,1)} %collective-permute-done.7.refs_4_), channel_id=1, source_target_pairs={{4,0},{5,1},{6,2},{7,3},{20,16},{21,17},{22,18},{23,19}} | collective-permute-start | bytes 3145736 | tf_op jit(solution)/shard_map/ppermute | solution.py:364
  73.9 17.5 %collective-permute-start.12 = (bf16[768,512]{1,0:T(8,128)(2,1)}, bf16[768,512]{1,0:T(8,128)(2,1)}, u32[]{:S(2)}, u32[]{:S(2)}) collective-permute-start(bf16[768,512]{1,0:T(8,128)(2,1)} %slice.18), channel_id=1, source_target_pairs={{8,12},{9,13},{10,14},{11,15},{24,28},{25,29},{26,30},{27,31}} | collective-permute-start | bytes 2359304 | tf_op jit(solution)/shard_map/ppermute | solution.py:364
  79.1 6.7 %collective-permute-start.10 = (bf16[8,128,128]{2,1,0:T(8,128)(2,1)}, bf16[8,128,128]{2,1,0:T(8,128)(2,1)}, u32[]{:S(2)}, u32[]{:S(2)}) collective-permute-start(bf16[8,128,128]{2,1,0:T(8,128)(2,1)} %add.44.s_ref), channel_id=1, source_target_pairs={{0,16},{16,0},{1,17},{17,1},{2,18},{18,2},{3,19},{19,3},{4,20},{20... | collective-permute-start | bytes 786440 | tf_op jit(solution)/shard_map/ppermute | solution.py:364
  91.3 1.2 copy-start.2
  92.6 1.2 copy-start.8
  93.8 3.4 %copy-start.3 = (bf16[1024,512]{1,0:T(8,128)(2,1)S(1)}, bf16[1024,512]{1,0:T(8,128)(2,1)}, u32[]{:S(2)}) copy-start(bf16[1024,512]{1,0:T(8,128)(2,1)} %copy-done.1) | copy-start | bytes 3145732
  93.8 3.4 %copy-start.6 = (bf16[512,1024]{1,0:T(8,128)(2,1)S(1)}, bf16[512,1024]{1,0:T(8,128)(2,1)}, u32[]{:S(2)}) copy-start(bf16[512,1024]{1,0:T(8,128)(2,1)} %normed_rows.2.a_ref) | copy-start | bytes 3145732
  97.1 4.4 %collective-permute-start.13 = (bf16[512,512]{1,0:T(8,128)(2,1)S(1)}, bf16[512,512]{1,0:T(8,128)(2,1)S(1)}, u32[]{:S(2)}, u32[]{:S(2)}) collective-permute-start(bf16[512,512]{1,0:T(8,128)(2,1)S(1)} %get-tuple-element.62), channel_id=1, source_target_pairs={{0,1},{1,0},{2,3},{3,2},{4,5},{5,4},{6,7},{7,6},{8,9},{9,8},{10,11... | collective-permute-start | bytes 1572872 | tf_op jit(solution)/shard_map/ppermute | solution.py:364
  100.6 0.8 copy-start.10
  101.4 15.9 %collective-permute-start.16 = (bf16[512,512]{1,0:T(8,128)(2,1)}, bf16[512,512]{1,0:T(8,128)(2,1)}, u32[]{:S(2)}, u32[]{:S(2)}) collective-permute-start(bf16[512,512]{1,0:T(8,128)(2,1)} %get-tuple-element.68), channel_id=1, source_target_pairs={{0,1},{1,0},{2,3},{3,2},{4,5},{5,4},{6,7},{7,6},{8,9},{9,8},{10,11... | collective-permute-start | bytes 1572872 | tf_op jit(solution)/shard_map/ppermute | solution.py:364
  102.5 9.0 %collective-permute-start.14 = (bf16[256,512]{1,0:T(8,128)(2,1)}, bf16[256,512]{1,0:T(8,128)(2,1)}, u32[]{:S(2)}, u32[]{:S(2)}) collective-permute-start(bf16[256,512]{1,0:T(8,128)(2,1)} %get-tuple-element.82), channel_id=1, source_target_pairs={{0,2},{1,3},{2,0},{3,1},{4,6},{5,7},{6,4},{7,5},{8,10},{9,11},{10,... | collective-permute-start | bytes 786440 | tf_op jit(solution)/shard_map/ppermute | solution.py:364
  111.5 1.2 copy-start.4
  112.7 1.2 copy-start.9
  113.9 3.4 %copy-start.11 = (bf16[512,512]{1,0:T(8,128)(2,1)S(1)}, bf16[512,512]{1,0:T(8,128)(2,1)}, u32[]{:S(2)}) copy-start(bf16[512,512]{1,0:T(8,128)(2,1)} %copy-done.10) | copy-start | bytes 1572868
  113.9 7.5 %copy-start.7 = (bf16[512,1024]{1,0:T(8,128)(2,1)S(1)}, bf16[512,1024]{1,0:T(8,128)(2,1)}, u32[]{:S(2)}) copy-start(bf16[512,1024]{1,0:T(8,128)(2,1)} %normed_rows.2.a_ref) | copy-start | bytes 3145732
  117.2 4.2 %copy-start.5 = (bf16[1024,512]{1,0:T(8,128)(2,1)S(1)}, bf16[1024,512]{1,0:T(8,128)(2,1)}, u32[]{:S(2)}) copy-start(bf16[1024,512]{1,0:T(8,128)(2,1)} %copy-done.1) | copy-start | bytes 3145732
  117.2 7.7 %collective-permute-start.18 = (bf16[512,512]{1,0:T(8,128)(2,1)S(1)}, bf16[512,512]{1,0:T(8,128)(2,1)S(1)}, u32[]{:S(2)}, u32[]{:S(2)}) collective-permute-start(bf16[512,512]{1,0:T(8,128)(2,1)S(1)} %get-tuple-element.73), channel_id=1, source_target_pairs={{0,1},{1,0},{2,3},{3,2},{4,5},{5,4},{6,7},{7,6},{8,9},{9,8},{10,11... | collective-permute-start | bytes 1572872 | tf_op jit(solution)/shard_map/ppermute | solution.py:364
  119.4 9.4 %collective-permute-start.20 = (bf16[256,512]{1,0:T(8,128)(2,1)}, bf16[256,512]{1,0:T(8,128)(2,1)}, u32[]{:S(2)}, u32[]{:S(2)}) collective-permute-start(bf16[256,512]{1,0:T(8,128)(2,1)} %get-tuple-element.75), channel_id=1, source_target_pairs={{0,2},{1,3},{2,0},{3,1},{4,6},{5,7},{6,4},{7,5},{8,10},{9,11},{10,... | collective-permute-start | bytes 786440 | tf_op jit(solution)/shard_map/ppermute | solution.py:364
  120.9 18.7 %collective-permute-start.17 = (bf16[512,512]{1,0:T(8,128)(2,1)}, bf16[512,512]{1,0:T(8,128)(2,1)}, u32[]{:S(2)}, u32[]{:S(2)}) collective-permute-start(bf16[512,512]{1,0:T(8,128)(2,1)} %add_convert_fusion.1), channel_id=1, source_target_pairs={{0,2},{1,3},{2,0},{3,1},{4,6},{5,7},{6,4},{7,5},{8,10},{9,11},{10,... | collective-permute-start | bytes 1572872 | tf_op jit(solution)/shard_map/ppermute | solution.py:364
  124.8 2.0 %copy-start.12 = (bf16[512,512]{1,0:T(8,128)(2,1)}, bf16[512,512]{1,0:T(8,128)(2,1)S(1)}, u32[]{:S(2)}) copy-start(bf16[512,512]{1,0:T(8,128)(2,1)S(1)} %get-tuple-element.64) | copy-start | bytes 1572868
  124.8 14.7 %collective-permute-start.15 = (bf16[512,512]{1,0:T(8,128)(2,1)}, bf16[512,512]{1,0:T(8,128)(2,1)S(1)}, u32[]{:S(2)}, u32[]{:S(2)}) collective-permute-start(bf16[512,512]{1,0:T(8,128)(2,1)} %get-tuple-element.65), channel_id=1, source_target_pairs={{0,1},{1,0},{2,3},{3,2},{4,5},{5,4},{6,7},{7,6},{8,9},{9,8},{10,11... | collective-permute-start | bytes 1572872 | tf_op jit(solution)/shard_map/ppermute | solution.py:364
  126.9 8.9 %collective-permute-start.19 = (bf16[256,512]{1,0:T(8,128)(2,1)}, bf16[256,512]{1,0:T(8,128)(2,1)S(1)}, u32[]{:S(2)}, u32[]{:S(2)}) collective-permute-start(bf16[256,512]{1,0:T(8,128)(2,1)} %get-tuple-element.80), channel_id=1, source_target_pairs={{0,16},{16,0},{1,17},{17,1},{2,18},{18,2},{3,19},{19,3},{4,20},{20... | collective-permute-start | bytes 786440 | tf_op jit(solution)/shard_map/ppermute | solution.py:364
  136.8 8.1 %collective-permute-start.21 = (bf16[256,512]{1,0:T(8,128)(2,1)S(1)}, bf16[256,512]{1,0:T(8,128)(2,1)S(1)}, u32[]{:S(2)}, u32[]{:S(2)}) collective-permute-start(bf16[256,512]{1,0:T(8,128)(2,1)S(1)} %add_convert_fusion.3), channel_id=1, source_target_pairs={{0,16},{16,0},{1,17},{17,1},{2,18},{18,2},{3,19},{19,3},{4,20},{20... | collective-permute-start | bytes 786440 | tf_op jit(solution)/shard_map/ppermute | solution.py:364

commit v11 on v10

--- a/solution.py
+++ b/solution.py
@@ -282,7 +282,8 @@
 
 def project_kernel(options, pick_ref, a_ref, *refs):
     count = sum(options)
-    weights, (*outs, rows, rows_sem, held, sems) = refs[:count], refs[count:]
+    weights, (give_ref, keep_ref, rows, rows_sem, held, sems) = refs[:count], refs[count:]
+    places, block = held.shape[0], held.shape[2]
     copy_rows = pltpu.make_async_copy(a_ref, rows, rows_sem)
     copy_rows.start()
 
@@ -293,16 +294,19 @@
             pltpu.make_async_copy(piece, to, sems.at[place]).start()
             at += piece.shape[0]
 
-    for place in range(len(outs)):
+    for place in range(places):
         at = 0
         for option, pieces in enumerate(options):
             taken = weights[at : at + pieces]
             at += pieces
             pl.when(pick_ref[place] == option)(functools.partial(fetch, place, taken))
     copy_rows.wait()
-    for place, out in enumerate(outs):
+    for place in range(places):
         pltpu.make_async_copy(weights[0], held.at[place], sems.at[place]).wait()
-        out[...] = mxu(rows[...], held[place]).astype(BF16)
+        out, at = divmod(place, places // 2)
+        (give_ref, keep_ref)[out][:, at * block : (at + 1) * block] = mxu(
+            rows[...], held[place]
+        ).astype(BF16)
 
 
 def project(picks, rows, weights):
@@ -314,15 +318,15 @@
         functools.partial(project_kernel, tuple(len(pieces) for pieces in weights)),
         in_specs=[pl.BlockSpec(memory_space=pltpu.SMEM)]
         + [pl.BlockSpec(memory_space=pl.ANY)] * (1 + len(flat)),
-        out_specs=[pl.BlockSpec(memory_space=pltpu.VMEM)] * count,
-        out_shape=[jax.ShapeDtypeStruct((tokens, block), BF16)] * count,
+        out_specs=[pl.BlockSpec(memory_space=pltpu.VMEM)] * 2,
+        out_shape=[jax.ShapeDtypeStruct((tokens, count // 2 * block), BF16)] * 2,
         scratch_shapes=[
             pltpu.VMEM((tokens, depth), BF16),
             pltpu.SemaphoreType.DMA,
             pltpu.VMEM((count, depth, block), BF16),
             pltpu.SemaphoreType.DMA((count,)),
         ],
-        compiler_params=pltpu.CompilerParams(vmem_limit_bytes=16 * 1024 * 1024),
+        compiler_params=pltpu.CompilerParams(vmem_limit_bytes=58 * 1024 * 1024),
         cost_estimate=pl.CostEstimate(
             flops=2 * tokens * depth * block * count,
             bytes_accessed=2 * (tokens * depth + (tokens + depth) * block * count),
@@ -430,33 +434,14 @@
     picks = jnp.sum(
         jnp.where(order[:, None] == jnp.arange(head)[None, :], block_of[None, :], 0), axis=1
     ).astype(jnp.int32)
-    if head == 4:
-        near_pairs, last_pairs = head_pairs(1), head_pairs(2)
-        sent, kept = project(picks[0::2], other, weights)
-        own_sent, own_kept = project(picks[0::2], mine, weights)
-        sent, own_sent = send(sent, "head", near_pairs), send(own_sent, "head", near_pairs)
-        give_a, give_b = jnp.split(summed(kept, sent), 2)
-        own_give = summed(own_kept, own_sent)
-        got_a = send(give_a, "head", last_pairs)
-        give_b, own_give = tied(give_b, own_give)
-        got_b = send(give_b, "head", last_pairs)
-        other, mine, got_a = tied(other, mine, got_a)
-        sent, kept = project(picks[1::2], other, weights)
-        own_sent, own_kept = project(picks[1::2], mine, weights)
-        keep = kept.astype(F32) + send(sent, "head", near_pairs).astype(F32)
-        own_keep = own_kept.astype(F32) + send(own_sent, "head", near_pairs).astype(F32)
-    else:
-        last_pairs = head_pairs(head // 2)
-        sides = []
-        for rows in (other, mine):
-            parts = project(picks, rows, weights)
-            give, keep = parts[: head // 2], parts[head // 2 :]
-            sides += head_halved(jnp.concatenate(give, axis=1), jnp.concatenate(keep, axis=1))
-        give, keep, own_give, own_keep = sides
-        give_a, give_b = jnp.split(give, 2)
-        got_a = send(give_a, "head", last_pairs)
-        got_b = send(give_b, "head", last_pairs)
+    give, keep = head_halved(*project(picks, other, weights))
+    own_give, own_keep = head_halved(*project(picks, mine, weights))
+    last_pairs = head_pairs(head // 2)
+    give_a, give_b = jnp.split(give, 2)
     keep_a, keep_b = jnp.split(keep, 2)
+    got_a = send(give_a, "head", last_pairs)
+    give_b, own_give = tied(give_b, own_give)
+    got_b = send(give_b, "head", last_pairs)
     got_a, own_give = tied(got_a, own_give)
     back_a = send(summed(keep_a, got_a), "groups", swap)
     own_got = send(own_give, "head", last_pairs)

time: 147 us -> 137 us (0.932)
  waiting for transfers between devices: 31.6 us -> 26.7 us
  local copies, waits for them, and re-layouts: 10.5 us -> 5.95 us
  other arithmetic: 8.83 us -> 7.09 us
    ppermute x22 -> x18, waiting for transfers between devices: 31.6 us -> 26.6 us  [send(): return lax.ppermute(value, axis, pairs)]
    unnamed x37 -> x27, local copies, waits for them, and re-layouts: 7.35 us -> 3.01 us
    convert_element_type x4 -> x2, other arithmetic: 4.59 us -> 2.54 us  [summed(): return (keep.astype(F32) + got.astype(F32)).astype(BF16)]
    ppermute x22 -> x18, starting transfers between devices: 42.7 us -> 41.9 us  [send(): return lax.ppermute(value, axis, pairs)]
    pallas_call x4 -> x2, Pallas kernels: 13.4 us -> 14.2 us  [project(): pl.pallas_call(functools.partial(project_kernel, tuple((len(pieces) for p...]
  transfers between devices with their start and end apart: 22 -> 20, of which waited for: 11 -> 11; matrix products, arithmetic and copies ran while one was open for 8% -> 8% of each run, Pallas kernels for 32% -> 33%
where the time goes in v11:
time: 137 us; the launch traced here: 135 us
  Pallas kernels  51.4 us (38%)
  starting transfers between devices  42.4 us (31%)
  waiting for transfers between devices  26.7 us (19%)
  other arithmetic  7.09 us (5%)
  local copies, waits for them, and re-layouts  5.95 us (4%)
  matrix products  1.56 us (1%)
    ppermute x18, starting transfers between devices, send(): return lax.ppermute(value, axis, pairs)  41.9 us
    pallas_call x2, Pallas kernels, local_part(): pl.pallas_call(functools.partial(chunk_kernel, group, first), grid=(steps...  30.4 us
    ppermute x18, waiting for transfers between devices, send(): return lax.ppermute(value, axis, pairs)  26.6 us
    pallas_call x2, Pallas kernels, project(): pl.pallas_call(functools.partial(project_kernel, tuple((len(pieces) for p...  14.2 us
    pallas_call x2, Pallas kernels, normed_rows(): pl.pallas_call(norm_kernel, in_specs=[pl.BlockSpec(memory_space=pltpu.VME...  6.8 us
    unnamed x27, local copies, waits for them, and re-layouts  3.01 us
  transfers between devices with their start and end apart: 20, of which 11 were waited for; matrix products, arithmetic and copies ran while one was open for 8% of the time, Pallas kernels for 33%

profile of v11, /device:TPU:16, one launch (start us, length us, event | category | flops | bytes accessed | tf_op | source)
XLA Modules:
  0.0 135.4 jit_solution(14806090055162811065)
XLA Ops:
  0.0 1.6 %copy-done = bf16[1024,1024]{1,0:T(8,128)(2,1)S(1)} copy-done((bf16[1024,1024]{1,0:T(8,128)(2,1)S(1)}, bf16[1024,1024]{1,0:T(8,128)(2,1)}, u32[]{:S(2)}) %copy-start) | copy-done | bytes 2097176
  1.6 0.1 constant_dynamic-slice_fusion.refs_0_
  1.7 2.4 %collective-permute-start.1 = (bf16[1024,512]{1,0:T(8,128)(2,1)S(1)}, bf16[1024,512]{1,0:T(8,128)(2,1)}, u32[]{:S(2)}, u32[]{:S(2)}) collective-permute-start(bf16[1024,512]{1,0:T(8,128)(2,1)S(1)} %constant_dynamic-slice_fusion.refs_0_), channel_id=1, source_target_pairs={{4,0},{8,4},{12,8},{5,1},{9,5},{13,9},{6,2},{10,6},{14,10},{7,3},{... | collective-permute-start | bytes 3145736 | tf_op jit(solution)/shard_map/ppermute | solution.py:368
  4.1 4.5 %collective-permute-start = (bf16[1024,512]{1,0:T(8,128)(2,1)S(1)}, bf16[1024,512]{1,0:T(8,128)(2,1)}, u32[]{:S(2)}, u32[]{:S(2)}) collective-permute-start(bf16[1024,512]{1,0:T(8,128)(2,1)S(1)} %constant_dynamic-slice_fusion.refs_0_), channel_id=1, source_target_pairs={{0,4},{4,8},{8,12},{1,5},{5,9},{9,13},{2,6},{6,10},{10,14},{3,7},{... | collective-permute-start | bytes 3145736 | tf_op jit(solution)/shard_map/ppermute | solution.py:368
  8.6 1.0 copy.9
  9.6 18.1 %local_part.2 = (bf16[320,2048]{1,0:T(8,128)(2,1)}, f32[8,128,256]{2,1,0:T(8,128)}) custom-call(bf16[512,1024]{1,0:T(8,128)(2,1)} %q_ref.3, bf16[512,2,1024]{2,1,0:T(2,128)(2,1)} %k_ref.3, bf16[512,2,1024]{2,1,0:T(2,128)(2,1)} %v_ref.3, f32[1024,8]{1,0:T(8,128)} %bitcast.7), custom_call_target="tpu_custom_call" | custom-call | flops 16777216000 | bytes 5242880 | tf_op jit(solution)/shard_map/local_part/pallas_call | solution.py:214
  27.7 1.6 %collective-permute-start.8 = (bf16[320,2048]{1,0:T(8,128)(2,1)}, bf16[320,2048]{1,0:T(8,128)(2,1)S(1)}, u32[]{:S(2)}, u32[]{:S(2)}) collective-permute-start(bf16[320,2048]{1,0:T(8,128)(2,1)} %get-tuple-element.35.first_ref), channel_id=1, source_target_pairs={{0,16},{16,0},{1,17},{17,1},{2,18},{18,2},{3,19},{19,3},{4,20},{20... | collective-permute-start | bytes 3932168 | tf_op jit(solution)/shard_map/ppermute | solution.py:368
  29.3 0.0 collective-permute-done.1.refs_7_
  29.3 1.4 %collective-permute-done.refs_1_ = bf16[1024,512]{1,0:T(8,128)(2,1)} collective-permute-done((bf16[1024,512]{1,0:T(8,128)(2,1)S(1)}, bf16[1024,512]{1,0:T(8,128)(2,1)}, u32[]{:S(2)}, u32[]{:S(2)}) %collective-permute-start) | collective-permute-done | bytes 1048608 | tf_op jit(solution)/shard_map/ppermute | solution.py:368
  30.7 4.5 %collective-permute-start.3 = (bf16[1024,512]{1,0:T(8,128)(2,1)}, bf16[1024,512]{1,0:T(8,128)(2,1)S(1)}, u32[]{:S(2)}, u32[]{:S(2)}) collective-permute-start(bf16[1024,512]{1,0:T(8,128)(2,1)} %collective-permute-done.refs_1_), channel_id=1, source_target_pairs={{4,8},{8,12},{5,9},{9,13},{6,10},{10,14},{7,11},{11,15},{20,24},{2... | collective-permute-start | bytes 3145736 | tf_op jit(solution)/shard_map/ppermute | solution.py:368
  35.2 1.5 %collective-permute-start.7 = (bf16[1024,512]{1,0:T(8,128)(2,1)}, bf16[1024,512]{1,0:T(8,128)(2,1)S(1)}, u32[]{:S(2)}, u32[]{:S(2)}) collective-permute-start(bf16[1024,512]{1,0:T(8,128)(2,1)} %collective-permute-done.1.refs_7_), channel_id=1, source_target_pairs={{4,0},{8,4},{5,1},{9,5},{6,2},{10,6},{7,3},{11,7},{20,16},{24,20},... | collective-permute-start | bytes 3145736 | tf_op jit(solution)/shard_map/ppermute | solution.py:368
  36.7 12.3 %local_part.3 = (bf16[192,2048]{1,0:T(8,128)(2,1)}, f32[8,128,128]{2,1,0:T(8,128)}, bf16[8,128,128]{2,1,0:T(8,128)(2,1)}, bf16[8,128,128]{2,1,0:T(8,128)(2,1)}) custom-call(bf16[512,1024]{1,0:T(8,128)(2,1)} %q_ref.3, bf16[512,2,1024]{2,1,0:T(2,128)(2,1)} %k_ref.3, bf16[512,2,1024]{2,1,0:T(2,128)(2,1)} %v_ref.3, f32[1024,8]{1,0:T(8,128)} %bitcast.8, ...), custom_call_target="tpu_custom_call" | custom-call | flops 10066329600 | bytes 3145728 | tf_op jit(solution)/shard_map/local_part/pallas_call | solution.py:214
  49.0 0.8 collective-permute-start.4
  49.8 0.0 collective-permute-done.4
  49.8 1.3 fusion
  51.2 1.3 collective-permute-start.5
  52.5 4.2 %collective-permute-done.3.refs_3_ = bf16[1024,512]{1,0:T(8,128)(2,1)S(1)} collective-permute-done((bf16[1024,512]{1,0:T(8,128)(2,1)}, bf16[1024,512]{1,0:T(8,128)(2,1)S(1)}, u32[]{:S(2)}, u32[]{:S(2)}) %collective-permute-start.3) | collective-permute-done | bytes 1048608 | tf_op jit(solution)/shard_map/ppermute | solution.py:368
  56.7 4.3 %collective-permute-start.6 = (bf16[256,512]{1,0:T(8,128)(2,1)S(1)}, bf16[256,512]{1,0:T(8,128)(2,1)S(1)}, u32[]{:S(2)}, u32[]{:S(2)}) collective-permute-start(bf16[256,512]{1,0:T(8,128)(2,1)S(1)} %slice.25), channel_id=1, source_target_pairs={{8,12},{9,13},{10,14},{11,15},{24,28},{25,29},{26,30},{27,31}} | collective-permute-start | bytes 786440 | tf_op jit(solution)/shard_map/ppermute | solution.py:368
  61.0 0.0 copy-start.12
  61.0 1.6 %collective-permute-start.2 = (bf16[192,2048]{1,0:T(8,128)(2,1)}, bf16[192,2048]{1,0:T(8,128)(2,1)}, u32[]{:S(2)}, u32[]{:S(2)}) collective-permute-start(bf16[192,2048]{1,0:T(8,128)(2,1)} %get-tuple-element.38.second_ref), channel_id=1, source_target_pairs={{0,16},{16,0},{1,17},{17,1},{2,18},{18,2},{3,19},{19,3},{4,20},{20... | collective-permute-start | bytes 2359304 | tf_op jit(solution)/shard_map/ppermute | solution.py:368
  62.6 2.1 %collective-permute-done.5 = bf16[8,128,128]{2,1,0:T(8,128)(2,1)S(1)} collective-permute-done((bf16[8,128,128]{2,1,0:T(8,128)(2,1)S(1)}, bf16[8,128,128]{2,1,0:T(8,128)(2,1)S(1)}, u32[]{:S(2)}, u32[]{:S(2)}) %collective-permute-start.5) | collective-permute-done | bytes 262176 | tf_op jit(solution)/shard_map/ppermute | solution.py:368
  64.7 0.1 add.36
  64.8 0.2 fusion.1
  65.1 0.0 collective-permute-done.8.first_ref
  65.1 0.0 collective-permute-done.7.refs_4_
  65.1 0.0 collective-permute-done.6.refs_5_
  65.1 4.1 %collective-permute-start.9 = (bf16[8,128,128]{2,1,0:T(8,128)(2,1)S(1)}, bf16[8,128,128]{2,1,0:T(8,128)(2,1)S(1)}, u32[]{:S(2)}, u32[]{:S(2)}) collective-permute-start(bf16[8,128,128]{2,1,0:T(8,128)(2,1)S(1)} %fusion.1), channel_id=1, source_target_pairs={{8,12},{9,13},{10,14},{11,15},{24,28},{25,29},{26,30},{27,31}} | collective-permute-start | bytes 786440 | tf_op jit(solution)/shard_map/ppermute | solution.py:368
  69.3 1.7 %collective-permute-start.11 = (bf16[1024,512]{1,0:T(8,128)(2,1)S(1)}, bf16[1024,512]{1,0:T(8,128)(2,1)}, u32[]{:S(2)}, u32[]{:S(2)}) collective-permute-start(bf16[1024,512]{1,0:T(8,128)(2,1)S(1)} %collective-permute-done.7.refs_4_), channel_id=1, source_target_pairs={{4,0},{5,1},{6,2},{7,3},{20,16},{21,17},{22,18},{23,19}} | collective-permute-start | bytes 3145736 | tf_op jit(solution)/shard_map/ppermute | solution.py:368
  70.9 1.0 slice.24
  71.9 1.2 collective-permute-done.9
  73.1 0.8 add.38.s_ref
  73.9 5.3 %collective-permute-start.12 = (bf16[768,512]{1,0:T(8,128)(2,1)}, bf16[768,512]{1,0:T(8,128)(2,1)}, u32[]{:S(2)}, u32[]{:S(2)}) collective-permute-start(bf16[768,512]{1,0:T(8,128)(2,1)} %slice.24), channel_id=1, source_target_pairs={{8,12},{9,13},{10,14},{11,15},{24,28},{25,29},{26,30},{27,31}} | collective-permute-start | bytes 2359304 | tf_op jit(solution)/shard_map/ppermute | solution.py:368
  79.2 1.5 %collective-permute-start.10 = (bf16[8,128,128]{2,1,0:T(8,128)(2,1)}, bf16[8,128,128]{2,1,0:T(8,128)(2,1)}, u32[]{:S(2)}, u32[]{:S(2)}) collective-permute-start(bf16[8,128,128]{2,1,0:T(8,128)(2,1)} %add.38.s_ref), channel_id=1, source_target_pairs={{0,16},{16,0},{1,17},{17,1},{2,18},{18,2},{3,19},{19,3},{4,20},{20... | collective-permute-start | bytes 786440 | tf_op jit(solution)/shard_map/ppermute | solution.py:368
  80.7 0.8 select_reduce_fusion.pick_ref
  81.5 3.4 %normed_rows.2.a_ref = bf16[512,1024]{1,0:T(8,128)(2,1)} custom-call(bf16[320,2048]{1,0:T(8,128)(2,1)} %get-tuple-element.35.first_ref, bf16[192,2048]{1,0:T(8,128)(2,1)} %get-tuple-element.38.second_ref, bf16[8,128,128]{2,1,0:T(8,128)(2,1)} %add.38.s_ref, f32[1,1024]{1,0:T(1,128)} %bitcast.10), custom_call_target="tpu_custom_call" | custom-call | flops 134217728 | bytes 3145728 | tf_op jit(solution)/shard_map/normed_rows/pallas_call | solution.py:271
  84.9 1.0 collective-permute-done.10.s_ref
  85.9 3.4 %normed_rows.3.a_ref = bf16[512,1024]{1,0:T(8,128)(2,1)} custom-call(bf16[320,2048]{1,0:T(8,128)(2,1)} %copy-done.6, bf16[192,2048]{1,0:T(8,128)(2,1)} %collective-permute-done.2.second_ref, bf16[8,128,128]{2,1,0:T(8,128)(2,1)} %collective-permute-done.10.s_ref, f32[1,1024]{1,0:T(1,128)} %bitcast.11), custom_call_target="tpu_custom_call" | custom-call | flops 134217728 | bytes 3145728 | tf_op jit(solution)/shard_map/normed_rows/pallas_call | solution.py:271
  89.3 2.1 %collective-permute-done.12.refs_6_ = bf16[768,512]{1,0:T(8,128)(2,1)} collective-permute-done((bf16[768,512]{1,0:T(8,128)(2,1)}, bf16[768,512]{1,0:T(8,128)(2,1)}, u32[]{:S(2)}, u32[]{:S(2)}) %collective-permute-start.12) | collective-permute-done | bytes 786464 | tf_op jit(solution)/shard_map/ppermute | solution.py:368
  91.4 0.0 collective-permute-done.11.refs_2_
  91.4 7.0 %project.3 = (bf16[512,1024]{1,0:T(8,128)(2,1)}, bf16[512,1024]{1,0:T(8,128)(2,1)}) custom-call(s32[4]{0:T(128)} %select_reduce_fusion.pick_ref, bf16[512,1024]{1,0:T(8,128)(2,1)} %normed_rows.3.a_ref, bf16[1024,512]{1,0:T(8,128)(2,1)} %copy-done.1, bf16[1024,512]{1,0:T(8,128)(2,1)} %collective-permute-done.refs_1_, ...), custom_call_target="tpu_custom_call" | custom-call | flops 2147483648 | bytes 7340032 | tf_op jit(solution)/shard_map/project/pallas_call | solution.py:317
  98.4 0.1 collective-permute-start.14
  98.5 7.1 %project.2 = (bf16[512,1024]{1,0:T(8,128)(2,1)}, bf16[512,1024]{1,0:T(8,128)(2,1)}) custom-call(s32[4]{0:T(128)} %select_reduce_fusion.pick_ref, bf16[512,1024]{1,0:T(8,128)(2,1)} %normed_rows.2.a_ref, bf16[1024,512]{1,0:T(8,128)(2,1)} %copy-done.1, bf16[1024,512]{1,0:T(8,128)(2,1)} %collective-permute-done.refs_1_, ...), custom_call_target="tpu_custom_call" | custom-call | flops 2147483648 | bytes 7340032 | tf_op jit(solution)/shard_map/project/pallas_call | solution.py:317
  105.6 0.4 collective-permute-start.13
  106.1 0.0 collective-permute-done.14
  106.1 0.5 fusion.6
  106.5 0.7 fusion.8
  107.3 1.2 collective-permute-start.15
  108.4 0.1 collective-permute-done.13
  108.6 0.4 convert_add_fusion.1
  109.0 1.4 %copy-done.3 = f32[512,1024]{1,0:T(8,128)} copy-done((f32[512,1024]{1,0:T(8,128)}, f32[512,1024]{1,0:T(8,128)S(1)}, u32[]{:S(2)}) %copy-start.3) | copy-done | bytes 2097176
  110.3 0.1 slice.32
  110.4 1.6 %collective-permute-start.18 = (bf16[256,512]{1,0:T(8,128)(2,1)}, bf16[256,512]{1,0:T(8,128)(2,1)}, u32[]{:S(2)}, u32[]{:S(2)}) collective-permute-start(bf16[256,512]{1,0:T(8,128)(2,1)} %get-tuple-element.61), channel_id=1, source_target_pairs={{0,2},{1,3},{2,0},{3,1},{4,6},{5,7},{6,4},{7,5},{8,10},{9,11},{10,... | collective-permute-start | bytes 786440 | tf_op jit(solution)/shard_map/ppermute | solution.py:368
  112.0 4.5 %collective-permute-done.15 = bf16[256,512]{1,0:T(8,128)(2,1)S(1)} collective-permute-done((bf16[256,512]{1,0:T(8,128)(2,1)S(1)}, bf16[256,512]{1,0:T(8,128)(2,1)S(1)}, u32[]{:S(2)}, u32[]{:S(2)}) %collective-permute-start.15) | collective-permute-done | bytes 262176 | tf_op jit(solution)/shard_map/ppermute | solution.py:368
  116.4 0.8 fusion.7
  117.3 1.5 %collective-permute-start.17 = (bf16[256,512]{1,0:T(8,128)(2,1)}, bf16[256,512]{1,0:T(8,128)(2,1)S(1)}, u32[]{:S(2)}, u32[]{:S(2)}) collective-permute-start(bf16[256,512]{1,0:T(8,128)(2,1)} %get-tuple-element.66), channel_id=1, source_target_pairs={{0,16},{16,0},{1,17},{17,1},{2,18},{18,2},{3,19},{19,3},{4,20},{20... | collective-permute-start | bytes 786440 | tf_op jit(solution)/shard_map/ppermute | solution.py:368
  118.8 1.1 collective-permute-start.16
  119.9 2.2 %collective-permute-done.18 = bf16[256,512]{1,0:T(8,128)(2,1)} collective-permute-done((bf16[256,512]{1,0:T(8,128)(2,1)}, bf16[256,512]{1,0:T(8,128)(2,1)}, u32[]{:S(2)}, u32[]{:S(2)}) %collective-permute-start.18) | collective-permute-done | bytes 262176 | tf_op jit(solution)/shard_map/ppermute | solution.py:368
  122.2 2.1 %collective-permute-done.17 = bf16[256,512]{1,0:T(8,128)(2,1)S(1)} collective-permute-done((bf16[256,512]{1,0:T(8,128)(2,1)}, bf16[256,512]{1,0:T(8,128)(2,1)S(1)}, u32[]{:S(2)}, u32[]{:S(2)}) %collective-permute-start.17) | collective-permute-done | bytes 262176 | tf_op jit(solution)/shard_map/ppermute | solution.py:368
  124.2 1.0 add_convert_fusion
  125.2 1.6 %collective-permute-start.19 = (bf16[256,512]{1,0:T(8,128)(2,1)S(1)}, bf16[256,512]{1,0:T(8,128)(2,1)S(1)}, u32[]{:S(2)}, u32[]{:S(2)}) collective-permute-start(bf16[256,512]{1,0:T(8,128)(2,1)S(1)} %add_convert_fusion), channel_id=1, source_target_pairs={{0,16},{16,0},{1,17},{17,1},{2,18},{18,2},{3,19},{19,3},{4,20},{20... | collective-permute-start | bytes 786440 | tf_op jit(solution)/shard_map/ppermute | solution.py:368
  126.8 5.8 %collective-permute-done.16 = bf16[512,512]{1,0:T(8,128)(2,1)} collective-permute-done((bf16[512,512]{1,0:T(8,128)(2,1)S(1)}, bf16[512,512]{1,0:T(8,128)(2,1)}, u32[]{:S(2)}, u32[]{:S(2)}) %collective-permute-start.16) | collective-permute-done | bytes 524320 | tf_op jit(solution)/shard_map/ppermute | solution.py:368
  132.6 1.5 %fusion.2 = bf16[512,512]{1,0:T(8,128)(2,1)S(1)} fusion(f32[512,1024]{1,0:T(8,128)} %copy-done.3, bf16[512,512]{1,0:T(8,128)(2,1)} %collective-permute-done.16), kind=kLoop, calls=%fused_computation.8 | loop fusion | flops 786432 | bytes 2097152 | tf_op jit(solution)/shard_map/convert_element_type | solution.py:364
  134.1 0.0 collective-permute-done.19
  134.2 1.3 maximum_select_fusion
  (28 shorter events, 0.1 us)
Async XLA Ops:
  0.0 1.6 %copy-start = (bf16[1024,1024]{1,0:T(8,128)(2,1)S(1)}, bf16[1024,1024]{1,0:T(8,128)(2,1)}, u32[]{:S(2)}) copy-start(bf16[1024,1024]{1,0:T(8,128)(2,1)} %param.12) | copy-start | bytes 6291460
  0.0 8.6 %copy-start.11 = (f32[2,8,512]{2,1,0:T(8,128)S(1)}, f32[2,8,512]{2,1,0:T(8,128)}, u32[]{:S(2)}) copy-start(f32[2,8,512]{2,1,0:T(8,128)} %param.10) | copy-start | bytes 98308
  1.7 26.0 %copy-start.1 = (bf16[1024,512]{1,0:T(8,128)(2,1)}, bf16[1024,512]{1,0:T(8,128)(2,1)S(1)}, u32[]{:S(2)}) copy-start(bf16[1024,512]{1,0:T(8,128)(2,1)S(1)} %constant_dynamic-slice_fusion.refs_0_) | copy-start | bytes 3145732
  1.7 27.6 %collective-permute-start.1 = (bf16[1024,512]{1,0:T(8,128)(2,1)S(1)}, bf16[1024,512]{1,0:T(8,128)(2,1)}, u32[]{:S(2)}, u32[]{:S(2)}) collective-permute-start(bf16[1024,512]{1,0:T(8,128)(2,1)S(1)} %constant_dynamic-slice_fusion.refs_0_), channel_id=1, source_target_pairs={{4,0},{8,4},{12,8},{5,1},{9,5},{13,9},{6,2},{10,6},{14,10},{7,3},{... | collective-permute-start | bytes 3145736 | tf_op jit(solution)/shard_map/ppermute | solution.py:368
  4.1 26.6 %collective-permute-start = (bf16[1024,512]{1,0:T(8,128)(2,1)S(1)}, bf16[1024,512]{1,0:T(8,128)(2,1)}, u32[]{:S(2)}, u32[]{:S(2)}) collective-permute-start(bf16[1024,512]{1,0:T(8,128)(2,1)S(1)} %constant_dynamic-slice_fusion.refs_0_), channel_id=1, source_target_pairs={{0,4},{4,8},{8,12},{1,5},{5,9},{9,13},{2,6},{6,10},{10,14},{3,7},{... | collective-permute-start | bytes 3145736 | tf_op jit(solution)/shard_map/ppermute | solution.py:368
  27.7 37.4 %collective-permute-start.8 = (bf16[320,2048]{1,0:T(8,128)(2,1)}, bf16[320,2048]{1,0:T(8,128)(2,1)S(1)}, u32[]{:S(2)}, u32[]{:S(2)}) collective-permute-start(bf16[320,2048]{1,0:T(8,128)(2,1)} %get-tuple-element.35.first_ref), channel_id=1, source_target_pairs={{0,16},{16,0},{1,17},{17,1},{2,18},{18,2},{3,19},{19,3},{4,20},{20... | collective-permute-start | bytes 3932168 | tf_op jit(solution)/shard_map/ppermute | solution.py:368
  30.7 26.0 %collective-permute-start.3 = (bf16[1024,512]{1,0:T(8,128)(2,1)}, bf16[1024,512]{1,0:T(8,128)(2,1)S(1)}, u32[]{:S(2)}, u32[]{:S(2)}) collective-permute-start(bf16[1024,512]{1,0:T(8,128)(2,1)} %collective-permute-done.refs_1_), channel_id=1, source_target_pairs={{4,8},{8,12},{5,9},{9,13},{6,10},{10,14},{7,11},{11,15},{20,24},{2... | collective-permute-start | bytes 3145736 | tf_op jit(solution)/shard_map/ppermute | solution.py:368
  35.2 29.9 %collective-permute-start.7 = (bf16[1024,512]{1,0:T(8,128)(2,1)}, bf16[1024,512]{1,0:T(8,128)(2,1)S(1)}, u32[]{:S(2)}, u32[]{:S(2)}) collective-permute-start(bf16[1024,512]{1,0:T(8,128)(2,1)} %collective-permute-done.1.refs_7_), channel_id=1, source_target_pairs={{4,0},{8,4},{5,1},{9,5},{6,2},{10,6},{7,3},{11,7},{20,16},{24,20},... | collective-permute-start | bytes 3145736 | tf_op jit(solution)/shard_map/ppermute | solution.py:368
  49.0 15.8 %copy-start.5 = (f32[8,128,128]{2,1,0:T(8,128)S(1)}, f32[8,128,128]{2,1,0:T(8,128)}, u32[]{:S(2)}) copy-start(f32[8,128,128]{2,1,0:T(8,128)} %get-tuple-element.42) | copy-start | bytes 1572868
  49.0 15.8 %copy-start.9 = (bf16[8,128,128]{2,1,0:T(8,128)(2,1)S(1)}, bf16[8,128,128]{2,1,0:T(8,128)(2,1)}, u32[]{:S(2)}) copy-start(bf16[8,128,128]{2,1,0:T(8,128)(2,1)} %get-tuple-element.41) | copy-start | bytes 786436
  49.0 0.8 collective-permute-start.4
  51.2 13.6 %collective-permute-start.5 = (bf16[8,128,128]{2,1,0:T(8,128)(2,1)S(1)}, bf16[8,128,128]{2,1,0:T(8,128)(2,1)S(1)}, u32[]{:S(2)}, u32[]{:S(2)}) collective-permute-start(bf16[8,128,128]{2,1,0:T(8,128)(2,1)S(1)} %fusion), channel_id=1, source_target_pairs={{4,8},{5,9},{6,10},{7,11},{20,24},{21,25},{22,26},{23,27}} | collective-permute-start | bytes 786440 | tf_op jit(solution)/shard_map/ppermute | solution.py:368
  56.7 15.2 %copy-start.2 = (bf16[1024,512]{1,0:T(8,128)(2,1)}, bf16[1024,512]{1,0:T(8,128)(2,1)S(1)}, u32[]{:S(2)}) copy-start(bf16[1024,512]{1,0:T(8,128)(2,1)S(1)} %collective-permute-done.3.refs_3_) | copy-start | bytes 3145732
  56.7 8.4 %collective-permute-start.6 = (bf16[256,512]{1,0:T(8,128)(2,1)S(1)}, bf16[256,512]{1,0:T(8,128)(2,1)S(1)}, u32[]{:S(2)}, u32[]{:S(2)}) collective-permute-start(bf16[256,512]{1,0:T(8,128)(2,1)S(1)} %slice.25), channel_id=1, source_target_pairs={{8,12},{9,13},{10,14},{11,15},{24,28},{25,29},{26,30},{27,31}} | collective-permute-start | bytes 786440 | tf_op jit(solution)/shard_map/ppermute | solution.py:368
  61.0 19.7 %copy-start.12 = (s32[4]{0:T(128)S(1)}, s32[4]{0:T(128)}, u32[]{:S(2)}) copy-start(s32[4]{0:T(128)} %constant.30.clone) | copy-start | bytes 52
  61.0 18.1 %collective-permute-start.2 = (bf16[192,2048]{1,0:T(8,128)(2,1)}, bf16[192,2048]{1,0:T(8,128)(2,1)}, u32[]{:S(2)}, u32[]{:S(2)}) collective-permute-start(bf16[192,2048]{1,0:T(8,128)(2,1)} %get-tuple-element.38.second_ref), channel_id=1, source_target_pairs={{0,16},{16,0},{1,17},{17,1},{2,18},{18,2},{3,19},{19,3},{4,20},{20... | collective-permute-start | bytes 2359304 | tf_op jit(solution)/shard_map/ppermute | solution.py:368
  65.1 8.8 %copy-start.6 = (bf16[320,2048]{1,0:T(8,128)(2,1)}, bf16[320,2048]{1,0:T(8,128)(2,1)S(1)}, u32[]{:S(2)}) copy-start(bf16[320,2048]{1,0:T(8,128)(2,1)S(1)} %collective-permute-done.8.first_ref) | copy-start | bytes 3932164
  65.1 19.8 %copy-start.4 = (bf16[1024,512]{1,0:T(8,128)(2,1)}, bf16[1024,512]{1,0:T(8,128)(2,1)S(1)}, u32[]{:S(2)}) copy-start(bf16[1024,512]{1,0:T(8,128)(2,1)S(1)} %collective-permute-done.7.refs_4_) | copy-start | bytes 3145732
  65.1 19.8 %copy-start.8 = (bf16[256,512]{1,0:T(8,128)(2,1)}, bf16[256,512]{1,0:T(8,128)(2,1)S(1)}, u32[]{:S(2)}) copy-start(bf16[256,512]{1,0:T(8,128)(2,1)S(1)} %collective-permute-done.6.refs_5_) | copy-start | bytes 786436
  65.1 8.0 %collective-permute-start.9 = (bf16[8,128,128]{2,1,0:T(8,128)(2,1)S(1)}, bf16[8,128,128]{2,1,0:T(8,128)(2,1)S(1)}, u32[]{:S(2)}, u32[]{:S(2)}) collective-permute-start(bf16[8,128,128]{2,1,0:T(8,128)(2,1)S(1)} %fusion.1), channel_id=1, source_target_pairs={{8,12},{9,13},{10,14},{11,15},{24,28},{25,29},{26,30},{27,31}} | collective-permute-start | bytes 786440 | tf_op jit(solution)/shard_map/ppermute | solution.py:368
  69.3 22.1 %collective-permute-start.11 = (bf16[1024,512]{1,0:T(8,128)(2,1)S(1)}, bf16[1024,512]{1,0:T(8,128)(2,1)}, u32[]{:S(2)}, u32[]{:S(2)}) collective-permute-start(bf16[1024,512]{1,0:T(8,128)(2,1)S(1)} %collective-permute-done.7.refs_4_), channel_id=1, source_target_pairs={{4,0},{5,1},{6,2},{7,3},{20,16},{21,17},{22,18},{23,19}} | collective-permute-start | bytes 3145736 | tf_op jit(solution)/shard_map/ppermute | solution.py:368
  73.9 17.5 %collective-permute-start.12 = (bf16[768,512]{1,0:T(8,128)(2,1)}, bf16[768,512]{1,0:T(8,128)(2,1)}, u32[]{:S(2)}, u32[]{:S(2)}) collective-permute-start(bf16[768,512]{1,0:T(8,128)(2,1)} %slice.24), channel_id=1, source_target_pairs={{8,12},{9,13},{10,14},{11,15},{24,28},{25,29},{26,30},{27,31}} | collective-permute-start | bytes 2359304 | tf_op jit(solution)/shard_map/ppermute | solution.py:368
  79.2 6.7 %collective-permute-start.10 = (bf16[8,128,128]{2,1,0:T(8,128)(2,1)}, bf16[8,128,128]{2,1,0:T(8,128)(2,1)}, u32[]{:S(2)}, u32[]{:S(2)}) collective-permute-start(bf16[8,128,128]{2,1,0:T(8,128)(2,1)} %add.38.s_ref), channel_id=1, source_target_pairs={{0,16},{16,0},{1,17},{17,1},{2,18},{18,2},{3,19},{19,3},{4,20},{20... | collective-permute-start | bytes 786440 | tf_op jit(solution)/shard_map/ppermute | solution.py:368
  98.4 7.7 %copy-start.7 = (bf16[512,1024]{1,0:T(8,128)(2,1)S(1)}, bf16[512,1024]{1,0:T(8,128)(2,1)}, u32[]{:S(2)}) copy-start(bf16[512,1024]{1,0:T(8,128)(2,1)} %get-tuple-element.56) | copy-start | bytes 3145732
  98.4 7.7 %collective-permute-start.14 = (bf16[512,1024]{1,0:T(8,128)(2,1)}, bf16[512,1024]{1,0:T(8,128)(2,1)S(1)}, u32[]{:S(2)}, u32[]{:S(2)}) collective-permute-start(bf16[512,1024]{1,0:T(8,128)(2,1)} %get-tuple-element.57), channel_id=1, source_target_pairs={{0,1},{1,0},{2,3},{3,2},{4,5},{5,4},{6,7},{7,6},{8,9},{9,8},{10,11... | collective-permute-start | bytes 3145736 | tf_op jit(solution)/shard_map/ppermute | solution.py:355
  105.6 2.9 %collective-permute-start.13 = (bf16[512,1024]{1,0:T(8,128)(2,1)}, bf16[512,1024]{1,0:T(8,128)(2,1)S(1)}, u32[]{:S(2)}, u32[]{:S(2)}) collective-permute-start(bf16[512,1024]{1,0:T(8,128)(2,1)} %get-tuple-element.54), channel_id=1, source_target_pairs={{0,1},{1,0},{2,3},{3,2},{4,5},{5,4},{6,7},{7,6},{8,9},{9,8},{10,11... | collective-permute-start | bytes 3145736 | tf_op jit(solution)/shard_map/ppermute | solution.py:355
  106.1 2.5 %copy-start.10 = (bf16[512,1024]{1,0:T(8,128)(2,1)S(1)}, bf16[512,1024]{1,0:T(8,128)(2,1)}, u32[]{:S(2)}) copy-start(bf16[512,1024]{1,0:T(8,128)(2,1)} %get-tuple-element.53) | copy-start | bytes 3145732
  107.3 9.2 %collective-permute-start.15 = (bf16[256,512]{1,0:T(8,128)(2,1)S(1)}, bf16[256,512]{1,0:T(8,128)(2,1)S(1)}, u32[]{:S(2)}, u32[]{:S(2)}) collective-permute-start(bf16[256,512]{1,0:T(8,128)(2,1)S(1)} %get-tuple-element.70), channel_id=1, source_target_pairs={{0,2},{1,3},{2,0},{3,1},{4,6},{5,7},{6,4},{7,5},{8,10},{9,11},{10,... | collective-permute-start | bytes 786440 | tf_op jit(solution)/shard_map/ppermute | solution.py:368
  109.0 1.4 %copy-start.3 = (f32[512,1024]{1,0:T(8,128)}, f32[512,1024]{1,0:T(8,128)S(1)}, u32[]{:S(2)}) copy-start(f32[512,1024]{1,0:T(8,128)S(1)} %convert_add_fusion.1) | copy-start | bytes 6291460
  110.4 11.7 %collective-permute-start.18 = (bf16[256,512]{1,0:T(8,128)(2,1)}, bf16[256,512]{1,0:T(8,128)(2,1)}, u32[]{:S(2)}, u32[]{:S(2)}) collective-permute-start(bf16[256,512]{1,0:T(8,128)(2,1)} %get-tuple-element.61), channel_id=1, source_target_pairs={{0,2},{1,3},{2,0},{3,1},{4,6},{5,7},{6,4},{7,5},{8,10},{9,11},{10,... | collective-permute-start | bytes 786440 | tf_op jit(solution)/shard_map/ppermute | solution.py:368
  117.3 7.0 %collective-permute-start.17 = (bf16[256,512]{1,0:T(8,128)(2,1)}, bf16[256,512]{1,0:T(8,128)(2,1)S(1)}, u32[]{:S(2)}, u32[]{:S(2)}) collective-permute-start(bf16[256,512]{1,0:T(8,128)(2,1)} %get-tuple-element.66), channel_id=1, source_target_pairs={{0,16},{16,0},{1,17},{17,1},{2,18},{18,2},{3,19},{19,3},{4,20},{20... | collective-permute-start | bytes 786440 | tf_op jit(solution)/shard_map/ppermute | solution.py:368
  118.8 13.8 %collective-permute-start.16 = (bf16[512,512]{1,0:T(8,128)(2,1)S(1)}, bf16[512,512]{1,0:T(8,128)(2,1)}, u32[]{:S(2)}, u32[]{:S(2)}) collective-permute-start(bf16[512,512]{1,0:T(8,128)(2,1)S(1)} %slice.32), channel_id=1, source_target_pairs={{0,2},{1,3},{2,0},{3,1},{4,6},{5,7},{6,4},{7,5},{8,10},{9,11},{10,... | collective-permute-start | bytes 1572872 | tf_op jit(solution)/shard_map/ppermute | solution.py:368
  125.2 8.9 %collective-permute-start.19 = (bf16[256,512]{1,0:T(8,128)(2,1)S(1)}, bf16[256,512]{1,0:T(8,128)(2,1)S(1)}, u32[]{:S(2)}, u32[]{:S(2)}) collective-permute-start(bf16[256,512]{1,0:T(8,128)(2,1)S(1)} %add_convert_fusion), channel_id=1, source_target_pairs={{0,16},{16,0},{1,17},{17,1},{2,18},{18,2},{3,19},{19,3},{4,20},{20... | collective-permute-start | bytes 786440 | tf_op jit(solution)/shard_map/ppermute | solution.py:368

commit v12 on v8

--- a/solution.py
+++ b/solution.py
@@ -10,6 +10,7 @@
 DK = 128
 REFL = 2
 TINY = 1e-06
+GRANT = 24 * 1024 * 1024
 CHUNK = 128
 BASE = 8
 F32 = jnp.float32
@@ -273,73 +274,45 @@
         in_specs=[pl.BlockSpec(memory_space=pltpu.VMEM)] * 4,
         out_specs=pl.BlockSpec(memory_space=pltpu.VMEM),
         out_shape=jax.ShapeDtypeStruct((tokens, width), BF16),
-        cost_estimate=pl.CostEstimate(
-            flops=2 * tokens * width * DK, bytes_accessed=6 * tokens * width, transcendentals=0
-        ),
+        compiler_params=pltpu.CompilerParams(vmem_limit_bytes=GRANT),
         name="normed_rows",
     )(first, second, incoming, gain.reshape(1, width))
 
 
-def project_kernel(choices, place_ref, first_ref, a_ref, *refs):
-    count = sum(sum(options) for options in choices)
-    weights = list(refs[:count])
-    give_ref, keep_ref, held, sems = refs[count:]
-    half, block = len(choices) // 2, held.shape[2]
-    whole = weights[0]
-
-    def fetch(slot, pieces):
-        row = 0
+def project_kernel(options, place_ref, first_ref, a_ref, *refs):
+    weights, out_ref = list(refs[:-1]), refs[-1]
+
+    def put(slot, pieces):
+        at, product = 0, None
         for piece in pieces:
-            rows = pl.ds(row, piece.shape[0])
-            pltpu.make_async_copy(piece, held.at[slot, rows], sems.at[slot]).start()
-            row += piece.shape[0]
-
-    for slot, options in enumerate(choices):
-        for option, pieces in enumerate(options):
+            part = mxu(a_ref[:, at : at + piece.shape[0]], piece[...])
+            product = part if product is None else product + part
+            at += piece.shape[0]
+        out_ref[place_ref[slot]] = product.astype(BF16)
+
+    for slot, counts in enumerate(options):
+        for option, pieces in enumerate(counts):
             taken, weights = weights[:pieces], weights[pieces:]
-            if len(options) == 1:
-                fetch(slot, taken)
+            if len(counts) == 1:
+                put(slot, taken)
             else:
-                pl.when(first_ref[slot] == 1 - option)(functools.partial(fetch, slot, taken))
-    for slot in range(len(choices)):
-        pltpu.make_async_copy(whole, held.at[slot], sems.at[slot]).wait()
-        product = mxu(a_ref[...], held[slot]).astype(BF16)
-        place = place_ref[slot]
-
-        @pl.when(place < half)
-        def _():
-            give_ref[:, pl.ds(pl.multiple_of(place * block, block), block)] = product
-
-        @pl.when(place >= half)
-        def _():
-            keep_ref[:, pl.ds(pl.multiple_of((place - half) * block, block), block)] = product
+                pl.when(first_ref[slot] == 1 - option)(functools.partial(put, slot, taken))
 
 
 def project(places, first, rows, weights):
-    tokens, depth = rows.shape
+    tokens = rows.shape[0]
+    block = weights[0][0][0].shape[1]
     count = len(weights)
-    block = weights[0][0][0].shape[1]
-    choices = tuple(tuple(len(pieces) for pieces in options) for options in weights)
     flat = [piece for options in weights for pieces in options for piece in pieces]
-    half = pl.BlockSpec(memory_space=pltpu.VMEM)
-    shape = jax.ShapeDtypeStruct((tokens, count // 2 * block), BF16)
     return pl.pallas_call(
-        functools.partial(project_kernel, choices),
+        functools.partial(
+            project_kernel, tuple(tuple(len(pieces) for pieces in options) for options in weights)
+        ),
         in_specs=[pl.BlockSpec(memory_space=pltpu.SMEM)] * 2
-        + [half]
-        + [pl.BlockSpec(memory_space=pl.ANY)] * len(flat),
-        out_specs=[half, half],
-        out_shape=[shape, shape],
-        scratch_shapes=[
-            pltpu.VMEM((count, depth, block), BF16),
-            pltpu.SemaphoreType.DMA((count,)),
-        ],
-        compiler_params=pltpu.CompilerParams(vmem_limit_bytes=48 * 1024 * 1024),
-        cost_estimate=pl.CostEstimate(
-            flops=2 * tokens * depth * block * count,
-            bytes_accessed=2 * (tokens * depth + (tokens + depth) * block * count),
-            transcendentals=0,
-        ),
+        + [pl.BlockSpec(memory_space=pltpu.VMEM)] * (1 + len(flat)),
+        out_specs=pl.BlockSpec(memory_space=pltpu.VMEM),
+        out_shape=jax.ShapeDtypeStruct((count, tokens, block), BF16),
+        compiler_params=pltpu.CompilerParams(vmem_limit_bytes=GRANT),
         name="project",
     )(places, first, rows, *flat)
 
@@ -357,15 +330,15 @@
     return [(i, i ^ bit) for i in range(lax.axis_size("head"))]
 
 
-def head_halved(give, keep):
-    bit = 1
+def head_halved(parts):
+    bit, give, keep = 1, parts[: parts.shape[0] // 2], parts[parts.shape[0] // 2 :]
     while bit * 2 < lax.axis_size("head"):
         got = lax.ppermute(give, "head", head_pairs(bit))
-        total = keep.astype(F32) + got.astype(F32)
-        half = total.shape[1] // 2
-        give, keep = total[:, :half].astype(BF16), total[:, half:]
+        half = keep.shape[0] // 2
+        give = summed(keep[:half], got[:half])
+        keep = keep[half:].astype(F32) + got[half:].astype(F32)
         bit *= 2
-    return give, keep
+    return give[0], keep[0]
 
 
 def summed(keep, got):
@@ -442,8 +415,8 @@
     order = jnp.asarray(halving_order(head), jnp.int32)
     places = jnp.argmax(distance[:, None] == order[None, :], axis=1).astype(jnp.int32)
     mine, other = tied(mine, other)
-    give, keep = head_halved(*project(places, first, other, weights))
-    own_give, own_keep = head_halved(*project(places, first, mine, weights))
+    give, keep = head_halved(project(places, first, other, weights))
+    own_give, own_keep = head_halved(project(places, first, mine, weights))
     last_pairs = head_pairs(head // 2)
     give_a, give_b = jnp.split(give, 2)
     keep_a, keep_b = jnp.split(keep, 2)

time: 132 us -> 133 us (level)
  Pallas kernels: 45.7 us -> 44.1 us
    pallas_call x2, Pallas kernels: 6.88 us -> 2.99 us  [normed_rows(): pl.pallas_call(norm_kernel, in_specs=[pl.BlockSpec(memory_space=pltpu.VME...]
    pallas_call x2, Pallas kernels: 8.48 us -> 10.8 us  [project(): pl.pallas_call(functools.partial(project_kernel, tuple((tuple((len(pieces...]
    unnamed x21 -> x33, local copies, waits for them, and re-layouts: 4.18 us -> 5.08 us
    convert_element_type x2 -> x4, other arithmetic: 2.54 us -> 3.34 us  [summed(): return (keep.astype(F32) + got.astype(F32)).astype(BF16)]
  transfers between devices with their start and end apart: 20 -> 20, of which waited for: 10 -> 9; matrix products, arithmetic and copies ran while one was open for 8% -> 8% of each run, Pallas kernels for 32% -> 29%
where the time goes in v12:
time: 133 us; the launch traced here: 132 us
  Pallas kernels  44.1 us (33%)
  starting transfers between devices  43.9 us (33%)
  waiting for transfers between devices  26.5 us (20%)
  local copies, waits for them, and re-layouts  8.1 us (6%)
  other arithmetic  7.29 us (5%)
  matrix products  1.56 us (1%)
    ppermute x18, starting transfers between devices, send(): return lax.ppermute(value, axis, pairs)  43.3 us
    pallas_call x2, Pallas kernels, local_part(): pl.pallas_call(functools.partial(chunk_kernel, group, first), grid=(steps...  30.4 us
    ppermute x18, waiting for transfers between devices, send(): return lax.ppermute(value, axis, pairs)  26.5 us
    pallas_call x2, Pallas kernels, project(): pl.pallas_call(functools.partial(project_kernel, tuple((tuple((len(pieces...  10.8 us
    unnamed x33, local copies, waits for them, and re-layouts  5.08 us
    convert_element_type x4, other arithmetic, summed(): return (keep.astype(F32) + got.astype(F32)).astype(BF16)  3.34 us
    pallas_call x2, Pallas kernels, normed_rows(): pl.pallas_call(norm_kernel, in_specs=[pl.BlockSpec(memory_space=pltpu.VME...  2.99 us
  transfers between devices with their start and end apart: 20, of which 9 were waited for; matrix products, arithmetic and copies ran while one was open for 8% of the time, Pallas kernels for 29%

profile of v12, /device:TPU:16, one launch (start us, length us, event | category | flops | bytes accessed | tf_op | source)
XLA Modules:
  0.0 131.8 jit_solution(1475801650598587598)
XLA Ops:
  0.0 1.6 %copy-done = bf16[1024,1024]{1,0:T(8,128)(2,1)S(1)} copy-done((bf16[1024,1024]{1,0:T(8,128)(2,1)S(1)}, bf16[1024,1024]{1,0:T(8,128)(2,1)}, u32[]{:S(2)}) %copy-start) | copy-done | bytes 2097176
  1.6 0.1 constant_dynamic-slice_fusion.refs_0_
  1.7 2.4 %collective-permute-start.1 = (bf16[1024,512]{1,0:T(8,128)(2,1)S(1)}, bf16[1024,512]{1,0:T(8,128)(2,1)}, u32[]{:S(2)}, u32[]{:S(2)}) collective-permute-start(bf16[1024,512]{1,0:T(8,128)(2,1)S(1)} %constant_dynamic-slice_fusion.refs_0_), channel_id=1, source_target_pairs={{4,0},{8,4},{12,8},{5,1},{9,5},{13,9},{6,2},{10,6},{14,10},{7,3},{... | collective-permute-start | bytes 3145736 | tf_op jit(solution)/shard_map/ppermute | solution.py:349
  4.1 4.4 %collective-permute-start = (bf16[1024,512]{1,0:T(8,128)(2,1)S(1)}, bf16[1024,512]{1,0:T(8,128)(2,1)}, u32[]{:S(2)}, u32[]{:S(2)}) collective-permute-start(bf16[1024,512]{1,0:T(8,128)(2,1)S(1)} %constant_dynamic-slice_fusion.refs_0_), channel_id=1, source_target_pairs={{0,4},{4,8},{8,12},{1,5},{5,9},{9,13},{2,6},{6,10},{10,14},{3,7},{... | collective-permute-start | bytes 3145736 | tf_op jit(solution)/shard_map/ppermute | solution.py:349
  8.5 1.0 copy.9
  9.5 18.1 %local_part.2 = (bf16[320,2048]{1,0:T(8,128)(2,1)}, f32[8,128,256]{2,1,0:T(8,128)}) custom-call(bf16[512,1024]{1,0:T(8,128)(2,1)} %q_ref.3, bf16[512,2,1024]{2,1,0:T(2,128)(2,1)} %k_ref.3, bf16[512,2,1024]{2,1,0:T(2,128)(2,1)} %v_ref.3, f32[1024,8]{1,0:T(8,128)} %bitcast.27), custom_call_target="tpu_custom_call" | custom-call | flops 16777216000 | bytes 5242880 | tf_op jit(solution)/shard_map/local_part/pallas_call | solution.py:215
  27.6 1.5 %collective-permute-start.8 = (bf16[320,2048]{1,0:T(8,128)(2,1)}, bf16[320,2048]{1,0:T(8,128)(2,1)S(1)}, u32[]{:S(2)}, u32[]{:S(2)}) collective-permute-start(bf16[320,2048]{1,0:T(8,128)(2,1)} %get-tuple-element.33.first_ref), channel_id=1, source_target_pairs={{0,16},{16,0},{1,17},{17,1},{2,18},{18,2},{3,19},{19,3},{4,20},{20... | collective-permute-start | bytes 3932168 | tf_op jit(solution)/shard_map/ppermute | solution.py:349
  29.2 0.0 collective-permute-done.1.refs_7_
  29.2 1.5 %collective-permute-done.refs_1_ = bf16[1024,512]{1,0:T(8,128)(2,1)} collective-permute-done((bf16[1024,512]{1,0:T(8,128)(2,1)S(1)}, bf16[1024,512]{1,0:T(8,128)(2,1)}, u32[]{:S(2)}, u32[]{:S(2)}) %collective-permute-start) | collective-permute-done | bytes 1048608 | tf_op jit(solution)/shard_map/ppermute | solution.py:349
  30.7 4.4 %collective-permute-start.3 = (bf16[1024,512]{1,0:T(8,128)(2,1)}, bf16[1024,512]{1,0:T(8,128)(2,1)S(1)}, u32[]{:S(2)}, u32[]{:S(2)}) collective-permute-start(bf16[1024,512]{1,0:T(8,128)(2,1)} %collective-permute-done.refs_1_), channel_id=1, source_target_pairs={{4,8},{8,12},{5,9},{9,13},{6,10},{10,14},{7,11},{11,15},{20,24},{2... | collective-permute-start | bytes 3145736 | tf_op jit(solution)/shard_map/ppermute | solution.py:349
  35.1 2.5 %collective-permute-start.7 = (bf16[1024,512]{1,0:T(8,128)(2,1)}, bf16[1024,512]{1,0:T(8,128)(2,1)}, u32[]{:S(2)}, u32[]{:S(2)}) collective-permute-start(bf16[1024,512]{1,0:T(8,128)(2,1)} %collective-permute-done.1.refs_7_), channel_id=1, source_target_pairs={{4,0},{8,4},{5,1},{9,5},{6,2},{10,6},{7,3},{11,7},{20,16},{24,20},... | collective-permute-start | bytes 3145736 | tf_op jit(solution)/shard_map/ppermute | solution.py:349
  37.6 12.3 %local_part.3 = (bf16[192,2048]{1,0:T(8,128)(2,1)}, f32[8,128,128]{2,1,0:T(8,128)}, bf16[8,128,128]{2,1,0:T(8,128)(2,1)}, bf16[8,128,128]{2,1,0:T(8,128)(2,1)}) custom-call(bf16[512,1024]{1,0:T(8,128)(2,1)} %q_ref.3, bf16[512,2,1024]{2,1,0:T(2,128)(2,1)} %k_ref.3, bf16[512,2,1024]{2,1,0:T(2,128)(2,1)} %v_ref.3, f32[1024,8]{1,0:T(8,128)} %bitcast.28, ...), custom_call_target="tpu_custom_call" | custom-call | flops 10066329600 | bytes 3145728 | tf_op jit(solution)/shard_map/local_part/pallas_call | solution.py:215
  49.9 0.8 collective-permute-start.4
  50.7 1.3 %fusion = bf16[8,128,128]{2,1,0:T(8,128)(2,1)S(1)} fusion(f32[8,128,128]{2,1,0:T(8,128)} %get-tuple-element.40, bf16[8,128,128]{2,1,0:T(8,128)(2,1)} %get-tuple-element.39, bf16[8,128,128]{2,1,0:T(8,128)(2,1)S(1)} %collective-permute-done.4), kind=kOutput, calls=%fused_computation.2 | convolution fusion | flops 33816576 | bytes 1310720 | tf_op jit(solution)/shard_map/hde,hef->hdf/dot_general | solution.py:396
  52.1 1.3 collective-permute-start.5
  53.4 3.3 %collective-permute-done.3.refs_3_ = bf16[1024,512]{1,0:T(8,128)(2,1)S(1)} collective-permute-done((bf16[1024,512]{1,0:T(8,128)(2,1)}, bf16[1024,512]{1,0:T(8,128)(2,1)S(1)}, u32[]{:S(2)}, u32[]{:S(2)}) %collective-permute-start.3) | collective-permute-done | bytes 1048608 | tf_op jit(solution)/shard_map/ppermute | solution.py:349
  56.7 4.3 %collective-permute-start.6 = (bf16[256,512]{1,0:T(8,128)(2,1)S(1)}, bf16[256,512]{1,0:T(8,128)(2,1)S(1)}, u32[]{:S(2)}, u32[]{:S(2)}) collective-permute-start(bf16[256,512]{1,0:T(8,128)(2,1)S(1)} %slice.59), channel_id=1, source_target_pairs={{8,12},{9,13},{10,14},{11,15},{24,28},{25,29},{26,30},{27,31}} | collective-permute-start | bytes 786440 | tf_op jit(solution)/shard_map/ppermute | solution.py:349
  61.0 0.0 copy-start.15
  61.0 0.0 copy-start.9
  61.0 1.6 %collective-permute-start.2 = (bf16[192,2048]{1,0:T(8,128)(2,1)}, bf16[192,2048]{1,0:T(8,128)(2,1)}, u32[]{:S(2)}, u32[]{:S(2)}) collective-permute-start(bf16[192,2048]{1,0:T(8,128)(2,1)} %get-tuple-element.36.second_ref), channel_id=1, source_target_pairs={{0,16},{16,0},{1,17},{17,1},{2,18},{18,2},{3,19},{19,3},{4,20},{20... | collective-permute-start | bytes 2359304 | tf_op jit(solution)/shard_map/ppermute | solution.py:349
  62.6 2.1 %collective-permute-done.5 = bf16[8,128,128]{2,1,0:T(8,128)(2,1)S(1)} collective-permute-done((bf16[8,128,128]{2,1,0:T(8,128)(2,1)S(1)}, bf16[8,128,128]{2,1,0:T(8,128)(2,1)S(1)}, u32[]{:S(2)}, u32[]{:S(2)}) %collective-permute-start.5) | collective-permute-done | bytes 262176 | tf_op jit(solution)/shard_map/ppermute | solution.py:349
  64.7 0.1 add.42
  64.8 0.2 fusion.1
  65.0 0.0 collective-permute-done.8.first_ref
  65.1 4.1 %collective-permute-start.9 = (bf16[8,128,128]{2,1,0:T(8,128)(2,1)S(1)}, bf16[8,128,128]{2,1,0:T(8,128)(2,1)S(1)}, u32[]{:S(2)}, u32[]{:S(2)}) collective-permute-start(bf16[8,128,128]{2,1,0:T(8,128)(2,1)S(1)} %fusion.1), channel_id=1, source_target_pairs={{8,12},{9,13},{10,14},{11,15},{24,28},{25,29},{26,30},{27,31}} | collective-permute-start | bytes 786440 | tf_op jit(solution)/shard_map/ppermute | solution.py:349
  69.2 1.7 %collective-permute-start.11 = (bf16[1024,512]{1,0:T(8,128)(2,1)}, bf16[1024,512]{1,0:T(8,128)(2,1)}, u32[]{:S(2)}, u32[]{:S(2)}) collective-permute-start(bf16[1024,512]{1,0:T(8,128)(2,1)} %collective-permute-done.7.refs_4_), channel_id=1, source_target_pairs={{4,0},{5,1},{6,2},{7,3},{20,16},{21,17},{22,18},{23,19}} | collective-permute-start | bytes 3145736 | tf_op jit(solution)/shard_map/ppermute | solution.py:349
  70.9 0.9 slice.58
  71.8 1.2 collective-permute-done.9
  73.1 0.8 add.44.s_ref
  73.9 5.4 %collective-permute-start.12 = (bf16[768,512]{1,0:T(8,128)(2,1)}, bf16[768,512]{1,0:T(8,128)(2,1)}, u32[]{:S(2)}, u32[]{:S(2)}) collective-permute-start(bf16[768,512]{1,0:T(8,128)(2,1)} %slice.58), channel_id=1, source_target_pairs={{8,12},{9,13},{10,14},{11,15},{24,28},{25,29},{26,30},{27,31}} | collective-permute-start | bytes 2359304 | tf_op jit(solution)/shard_map/ppermute | solution.py:349
  79.2 0.0 collective-permute-done.2.second_ref
  79.2 1.6 %collective-permute-start.10 = (bf16[8,128,128]{2,1,0:T(8,128)(2,1)}, bf16[8,128,128]{2,1,0:T(8,128)(2,1)S(1)}, u32[]{:S(2)}, u32[]{:S(2)}) collective-permute-start(bf16[8,128,128]{2,1,0:T(8,128)(2,1)} %add.44.s_ref), channel_id=1, source_target_pairs={{0,16},{16,0},{1,17},{17,1},{2,18},{18,2},{3,19},{19,3},{4,20},{20... | collective-permute-start | bytes 786440 | tf_op jit(solution)/shard_map/ppermute | solution.py:349
  80.8 0.7 iota_reduce_fusion
  81.5 1.3 copy-done.6
  82.9 0.9 copy-done.7
  83.8 1.1 copy-done.8
  84.9 0.9 normed_rows.2.a_ref
  85.8 0.0 copy-start.2
  85.8 0.0 collective-permute-done.10.s_ref
  85.9 2.1 %normed_rows.3.a_ref = bf16[512,1024]{1,0:T(8,128)(2,1)S(1)} custom-call(bf16[320,2048]{1,0:T(8,128)(2,1)S(1)} %copy-done.5, bf16[192,2048]{1,0:T(8,128)(2,1)} %collective-permute-done.2.second_ref, bf16[8,128,128]{2,1,0:T(8,128)(2,1)S(1)} %collective-permute-done.10.s_ref, f32[1,1024]{1,0:T(1,128)S(1)} %bitcast.26), custom_call_target="tpu_custom_call" | custom-call | tf_op jit(solution)/shard_map/normed_rows/pallas_call | solution.py:272
  88.0 3.3 %collective-permute-done.12.refs_6_ = bf16[768,512]{1,0:T(8,128)(2,1)} collective-permute-done((bf16[768,512]{1,0:T(8,128)(2,1)}, bf16[768,512]{1,0:T(8,128)(2,1)}, u32[]{:S(2)}, u32[]{:S(2)}) %collective-permute-start.12) | collective-permute-done | bytes 786464 | tf_op jit(solution)/shard_map/ppermute | solution.py:349
  91.3 5.5 %project.3 = bf16[4,512,512]{2,1,0:T(8,128)(2,1)S(1)} custom-call(s32[4]{0:T(128)S(1)} %get-tuple-element.32.place_ref, s32[4]{0:T(128)S(1)} %compare_convert_fusion.first_ref, bf16[512,1024]{1,0:T(8,128)(2,1)S(1)} %normed_rows.3.a_ref, bf16[1024,512]{1,0:T(8,128)(2,1)S(1)} %constant_dynamic-slice_fusion.refs_0_, ...), custom_call_target="tpu_custom_call" | custom-call | tf_op jit(solution)/shard_map/project/pallas_call | solution.py:307
  96.8 0.1 slice.64
  96.9 0.1 collective-permute-start.14
  97.0 5.3 %project.2 = bf16[4,512,512]{2,1,0:T(8,128)(2,1)S(1)} custom-call(s32[4]{0:T(128)S(1)} %get-tuple-element.32.place_ref, s32[4]{0:T(128)S(1)} %compare_convert_fusion.first_ref, bf16[512,1024]{1,0:T(8,128)(2,1)S(1)} %normed_rows.2.a_ref, bf16[1024,512]{1,0:T(8,128)(2,1)S(1)} %constant_dynamic-slice_fusion.refs_0_, ...), custom_call_target="tpu_custom_call" | custom-call | tf_op jit(solution)/shard_map/project/pallas_call | solution.py:307
  102.3 0.1 slice.61
  102.4 0.6 collective-permute-start.13
  102.9 0.3 add_convert_fusion.1
  103.2 0.8 slice_bitcast_fusion.2
  104.0 1.5 %collective-permute-start.15 = (bf16[256,512]{1,0:T(8,128)(2,1)S(1)}, bf16[256,512]{1,0:T(8,128)(2,1)S(1)}, u32[]{:S(2)}, u32[]{:S(2)}) collective-permute-start(bf16[256,512]{1,0:T(8,128)(2,1)S(1)} %get-tuple-element.62), channel_id=1, source_target_pairs={{0,2},{1,3},{2,0},{3,1},{4,6},{5,7},{6,4},{7,5},{8,10},{9,11},{10,... | collective-permute-start | bytes 786440 | tf_op jit(solution)/shard_map/ppermute | solution.py:349
  105.5 1.1 fusion.3
  106.6 0.0 copy-done.12
  106.6 1.2 collective-permute-start.18
  107.9 5.3 %collective-permute-done.15 = bf16[256,512]{1,0:T(8,128)(2,1)S(1)} collective-permute-done((bf16[256,512]{1,0:T(8,128)(2,1)S(1)}, bf16[256,512]{1,0:T(8,128)(2,1)S(1)}, u32[]{:S(2)}, u32[]{:S(2)}) %collective-permute-start.15) | collective-permute-done | bytes 262176 | tf_op jit(solution)/shard_map/ppermute | solution.py:349
  113.1 0.8 fusion.5
  113.9 1.5 %collective-permute-start.17 = (bf16[256,512]{1,0:T(8,128)(2,1)}, bf16[256,512]{1,0:T(8,128)(2,1)S(1)}, u32[]{:S(2)}, u32[]{:S(2)}) collective-permute-start(bf16[256,512]{1,0:T(8,128)(2,1)} %fusion.5), channel_id=1, source_target_pairs={{0,16},{16,0},{1,17},{17,1},{2,18},{18,2},{3,19},{19,3},{4,20},{20... | collective-permute-start | bytes 786440 | tf_op jit(solution)/shard_map/ppermute | solution.py:349
  115.4 1.5 %collective-permute-start.16 = (bf16[512,512]{1,0:T(8,128)(2,1)}, bf16[512,512]{1,0:T(8,128)(2,1)S(1)}, u32[]{:S(2)}, u32[]{:S(2)}) collective-permute-start(bf16[512,512]{1,0:T(8,128)(2,1)} %fusion.3), channel_id=1, source_target_pairs={{0,2},{1,3},{2,0},{3,1},{4,6},{5,7},{6,4},{7,5},{8,10},{9,11},{10,... | collective-permute-start | bytes 1572872 | tf_op jit(solution)/shard_map/ppermute | solution.py:349
  117.0 1.9 %collective-permute-done.18 = bf16[256,512]{1,0:T(8,128)(2,1)} collective-permute-done((bf16[256,512]{1,0:T(8,128)(2,1)}, bf16[256,512]{1,0:T(8,128)(2,1)}, u32[]{:S(2)}, u32[]{:S(2)}) %collective-permute-start.18) | collective-permute-done | bytes 262176 | tf_op jit(solution)/shard_map/ppermute | solution.py:349
  118.9 2.1 %collective-permute-done.17 = bf16[256,512]{1,0:T(8,128)(2,1)S(1)} collective-permute-done((bf16[256,512]{1,0:T(8,128)(2,1)}, bf16[256,512]{1,0:T(8,128)(2,1)S(1)}, u32[]{:S(2)}, u32[]{:S(2)}) %collective-permute-start.17) | collective-permute-done | bytes 262176 | tf_op jit(solution)/shard_map/ppermute | solution.py:349
  120.9 1.0 add_convert_fusion.2
  122.0 1.6 %collective-permute-start.19 = (bf16[256,512]{1,0:T(8,128)(2,1)S(1)}, bf16[256,512]{1,0:T(8,128)(2,1)S(1)}, u32[]{:S(2)}, u32[]{:S(2)}) collective-permute-start(bf16[256,512]{1,0:T(8,128)(2,1)S(1)} %add_convert_fusion.2), channel_id=1, source_target_pairs={{0,16},{16,0},{1,17},{17,1},{2,18},{18,2},{3,19},{19,3},{4,20},{20... | collective-permute-start | bytes 786440 | tf_op jit(solution)/shard_map/ppermute | solution.py:349
  123.6 5.7 %collective-permute-done.16 = bf16[512,512]{1,0:T(8,128)(2,1)S(1)} collective-permute-done((bf16[512,512]{1,0:T(8,128)(2,1)}, bf16[512,512]{1,0:T(8,128)(2,1)S(1)}, u32[]{:S(2)}, u32[]{:S(2)}) %collective-permute-start.16) | collective-permute-done | bytes 524320 | tf_op jit(solution)/shard_map/ppermute | solution.py:349
  129.2 1.2 fusion.2
  130.5 1.3 maximum_select_fusion
  (37 shorter events, 0.2 us)
Async XLA Ops:
  0.0 1.6 %copy-start = (bf16[1024,1024]{1,0:T(8,128)(2,1)S(1)}, bf16[1024,1024]{1,0:T(8,128)(2,1)}, u32[]{:S(2)}) copy-start(bf16[1024,1024]{1,0:T(8,128)(2,1)} %param.12) | copy-start | bytes 6291460
  0.0 8.5 %copy-start.14 = (f32[2,8,512]{2,1,0:T(8,128)S(1)}, f32[2,8,512]{2,1,0:T(8,128)}, u32[]{:S(2)}) copy-start(f32[2,8,512]{2,1,0:T(8,128)} %param.10) | copy-start | bytes 98308
  1.7 27.5 %collective-permute-start.1 = (bf16[1024,512]{1,0:T(8,128)(2,1)S(1)}, bf16[1024,512]{1,0:T(8,128)(2,1)}, u32[]{:S(2)}, u32[]{:S(2)}) collective-permute-start(bf16[1024,512]{1,0:T(8,128)(2,1)S(1)} %constant_dynamic-slice_fusion.refs_0_), channel_id=1, source_target_pairs={{4,0},{8,4},{12,8},{5,1},{9,5},{13,9},{6,2},{10,6},{14,10},{7,3},{... | collective-permute-start | bytes 3145736 | tf_op jit(solution)/shard_map/ppermute | solution.py:349
  4.1 26.6 %collective-permute-start = (bf16[1024,512]{1,0:T(8,128)(2,1)S(1)}, bf16[1024,512]{1,0:T(8,128)(2,1)}, u32[]{:S(2)}, u32[]{:S(2)}) collective-permute-start(bf16[1024,512]{1,0:T(8,128)(2,1)S(1)} %constant_dynamic-slice_fusion.refs_0_), channel_id=1, source_target_pairs={{0,4},{4,8},{8,12},{1,5},{5,9},{9,13},{2,6},{6,10},{10,14},{3,7},{... | collective-permute-start | bytes 3145736 | tf_op jit(solution)/shard_map/ppermute | solution.py:349
  27.6 37.4 %collective-permute-start.8 = (bf16[320,2048]{1,0:T(8,128)(2,1)}, bf16[320,2048]{1,0:T(8,128)(2,1)S(1)}, u32[]{:S(2)}, u32[]{:S(2)}) collective-permute-start(bf16[320,2048]{1,0:T(8,128)(2,1)} %get-tuple-element.33.first_ref), channel_id=1, source_target_pairs={{0,16},{16,0},{1,17},{17,1},{2,18},{18,2},{3,19},{19,3},{4,20},{20... | collective-permute-start | bytes 3932168 | tf_op jit(solution)/shard_map/ppermute | solution.py:349
  30.7 26.0 %collective-permute-start.3 = (bf16[1024,512]{1,0:T(8,128)(2,1)}, bf16[1024,512]{1,0:T(8,128)(2,1)S(1)}, u32[]{:S(2)}, u32[]{:S(2)}) collective-permute-start(bf16[1024,512]{1,0:T(8,128)(2,1)} %collective-permute-done.refs_1_), channel_id=1, source_target_pairs={{4,8},{8,12},{5,9},{9,13},{6,10},{10,14},{7,11},{11,15},{20,24},{2... | collective-permute-start | bytes 3145736 | tf_op jit(solution)/shard_map/ppermute | solution.py:349
  35.1 29.9 %collective-permute-start.7 = (bf16[1024,512]{1,0:T(8,128)(2,1)}, bf16[1024,512]{1,0:T(8,128)(2,1)}, u32[]{:S(2)}, u32[]{:S(2)}) collective-permute-start(bf16[1024,512]{1,0:T(8,128)(2,1)} %collective-permute-done.1.refs_7_), channel_id=1, source_target_pairs={{4,0},{8,4},{5,1},{9,5},{6,2},{10,6},{7,3},{11,7},{20,16},{24,20},... | collective-permute-start | bytes 3145736 | tf_op jit(solution)/shard_map/ppermute | solution.py:349
  49.9 14.9 %copy-start.10 = (f32[8,128,128]{2,1,0:T(8,128)S(1)}, f32[8,128,128]{2,1,0:T(8,128)}, u32[]{:S(2)}) copy-start(f32[8,128,128]{2,1,0:T(8,128)} %get-tuple-element.40) | copy-start | bytes 1572868
  49.9 14.9 %copy-start.11 = (bf16[8,128,128]{2,1,0:T(8,128)(2,1)S(1)}, bf16[8,128,128]{2,1,0:T(8,128)(2,1)}, u32[]{:S(2)}) copy-start(bf16[8,128,128]{2,1,0:T(8,128)(2,1)} %get-tuple-element.39) | copy-start | bytes 786436
  49.9 0.8 collective-permute-start.4
  52.1 12.6 %collective-permute-start.5 = (bf16[8,128,128]{2,1,0:T(8,128)(2,1)S(1)}, bf16[8,128,128]{2,1,0:T(8,128)(2,1)S(1)}, u32[]{:S(2)}, u32[]{:S(2)}) collective-permute-start(bf16[8,128,128]{2,1,0:T(8,128)(2,1)S(1)} %fusion), channel_id=1, source_target_pairs={{4,8},{5,9},{6,10},{7,11},{20,24},{21,25},{22,26},{23,27}} | collective-permute-start | bytes 786440 | tf_op jit(solution)/shard_map/ppermute | solution.py:349
  56.6 15.2 %copy-start.1 = (bf16[1024,512]{1,0:T(8,128)(2,1)}, bf16[1024,512]{1,0:T(8,128)(2,1)S(1)}, u32[]{:S(2)}) copy-start(bf16[1024,512]{1,0:T(8,128)(2,1)S(1)} %collective-permute-done.3.refs_3_) | copy-start | bytes 3145732
  56.7 8.4 %collective-permute-start.6 = (bf16[256,512]{1,0:T(8,128)(2,1)S(1)}, bf16[256,512]{1,0:T(8,128)(2,1)S(1)}, u32[]{:S(2)}, u32[]{:S(2)}) collective-permute-start(bf16[256,512]{1,0:T(8,128)(2,1)S(1)} %slice.59), channel_id=1, source_target_pairs={{8,12},{9,13},{10,14},{11,15},{24,28},{25,29},{26,30},{27,31}} | collective-permute-start | bytes 786440 | tf_op jit(solution)/shard_map/ppermute | solution.py:349
  61.0 19.9 %copy-start.15 = (s32[4]{0:T(128)S(1)}, s32[4]{0:T(128)}, u32[]{:S(2)}) copy-start(s32[4]{0:T(128)} %constant.32.clone) | copy-start | bytes 52
  61.0 20.6 %copy-start.9 = (f32[1024]{0:T(1024)S(1)}, f32[1024]{0:T(1024)}, u32[]{:S(2)}) copy-start(f32[1024]{0:T(1024)} %param.11) | copy-start | bytes 12292
  61.0 18.2 %collective-permute-start.2 = (bf16[192,2048]{1,0:T(8,128)(2,1)}, bf16[192,2048]{1,0:T(8,128)(2,1)}, u32[]{:S(2)}, u32[]{:S(2)}) collective-permute-start(bf16[192,2048]{1,0:T(8,128)(2,1)} %get-tuple-element.36.second_ref), channel_id=1, source_target_pairs={{0,16},{16,0},{1,17},{17,1},{2,18},{18,2},{3,19},{19,3},{4,20},{20... | collective-permute-start | bytes 2359304 | tf_op jit(solution)/shard_map/ppermute | solution.py:349
  65.1 8.0 %copy-start.4 = (bf16[320,2048]{1,0:T(8,128)(2,1)}, bf16[320,2048]{1,0:T(8,128)(2,1)S(1)}, u32[]{:S(2)}) copy-start(bf16[320,2048]{1,0:T(8,128)(2,1)S(1)} %collective-permute-done.8.first_ref) | copy-start | bytes 3932164
  65.1 8.0 %collective-permute-start.9 = (bf16[8,128,128]{2,1,0:T(8,128)(2,1)S(1)}, bf16[8,128,128]{2,1,0:T(8,128)(2,1)S(1)}, u32[]{:S(2)}, u32[]{:S(2)}) collective-permute-start(bf16[8,128,128]{2,1,0:T(8,128)(2,1)S(1)} %fusion.1), channel_id=1, source_target_pairs={{8,12},{9,13},{10,14},{11,15},{24,28},{25,29},{26,30},{27,31}} | collective-permute-start | bytes 786440 | tf_op jit(solution)/shard_map/ppermute | solution.py:349
  69.2 22.1 %collective-permute-start.11 = (bf16[1024,512]{1,0:T(8,128)(2,1)}, bf16[1024,512]{1,0:T(8,128)(2,1)}, u32[]{:S(2)}, u32[]{:S(2)}) collective-permute-start(bf16[1024,512]{1,0:T(8,128)(2,1)} %collective-permute-done.7.refs_4_), channel_id=1, source_target_pairs={{4,0},{5,1},{6,2},{7,3},{20,16},{21,17},{22,18},{23,19}} | collective-permute-start | bytes 3145736 | tf_op jit(solution)/shard_map/ppermute | solution.py:349
  73.9 17.5 %collective-permute-start.12 = (bf16[768,512]{1,0:T(8,128)(2,1)}, bf16[768,512]{1,0:T(8,128)(2,1)}, u32[]{:S(2)}, u32[]{:S(2)}) collective-permute-start(bf16[768,512]{1,0:T(8,128)(2,1)} %slice.58), channel_id=1, source_target_pairs={{8,12},{9,13},{10,14},{11,15},{24,28},{25,29},{26,30},{27,31}} | collective-permute-start | bytes 2359304 | tf_op jit(solution)/shard_map/ppermute | solution.py:349
  79.2 6.7 %copy-start.5 = (bf16[320,2048]{1,0:T(8,128)(2,1)S(1)}, bf16[320,2048]{1,0:T(8,128)(2,1)}, u32[]{:S(2)}) copy-start(bf16[320,2048]{1,0:T(8,128)(2,1)} %copy-done.4) | copy-start | bytes 3932164
  79.2 6.6 %collective-permute-start.10 = (bf16[8,128,128]{2,1,0:T(8,128)(2,1)}, bf16[8,128,128]{2,1,0:T(8,128)(2,1)S(1)}, u32[]{:S(2)}, u32[]{:S(2)}) collective-permute-start(bf16[8,128,128]{2,1,0:T(8,128)(2,1)} %add.44.s_ref), channel_id=1, source_target_pairs={{0,16},{16,0},{1,17},{17,1},{2,18},{18,2},{3,19},{19,3},{4,20},{20... | collective-permute-start | bytes 786440 | tf_op jit(solution)/shard_map/ppermute | solution.py:349
  81.5 1.3 copy-start.6
  82.9 0.9 copy-start.7
  83.8 1.1 copy-start.8
  85.8 5.5 %copy-start.2 = (bf16[1024,512]{1,0:T(8,128)(2,1)S(1)}, bf16[1024,512]{1,0:T(8,128)(2,1)}, u32[]{:S(2)}) copy-start(bf16[1024,512]{1,0:T(8,128)(2,1)} %copy-done.1) | copy-start | bytes 3145732
  96.9 6.0 %collective-permute-start.14 = (bf16[2,512,512]{2,1,0:T(8,128)(2,1)S(1)}, bf16[2,512,512]{2,1,0:T(8,128)(2,1)S(1)}, u32[]{:S(2)}, u32[]{:S(2)}) collective-permute-start(bf16[2,512,512]{2,1,0:T(8,128)(2,1)S(1)} %slice.64), channel_id=1, source_target_pairs={{0,1},{1,0},{2,3},{3,2},{4,5},{5,4},{6,7},{7,6},{8,9},{9,8},{10,11... | collective-permute-start | bytes 3145736 | tf_op jit(solution)/shard_map/ppermute | solution.py:336
  102.3 3.2 %copy-start.3 = (bf16[4,512,512]{2,1,0:T(8,128)(2,1)}, bf16[4,512,512]{2,1,0:T(8,128)(2,1)S(1)}, u32[]{:S(2)}) copy-start(bf16[4,512,512]{2,1,0:T(8,128)(2,1)S(1)} %project.2) | copy-start | bytes 6291460
  102.4 3.1 %collective-permute-start.13 = (bf16[2,512,512]{2,1,0:T(8,128)(2,1)S(1)}, bf16[2,512,512]{2,1,0:T(8,128)(2,1)S(1)}, u32[]{:S(2)}, u32[]{:S(2)}) collective-permute-start(bf16[2,512,512]{2,1,0:T(8,128)(2,1)S(1)} %slice.61), channel_id=1, source_target_pairs={{0,1},{1,0},{2,3},{3,2},{4,5},{5,4},{6,7},{7,6},{8,9},{9,8},{10,11... | collective-permute-start | bytes 3145736 | tf_op jit(solution)/shard_map/ppermute | solution.py:336
  104.0 9.1 %collective-permute-start.15 = (bf16[256,512]{1,0:T(8,128)(2,1)S(1)}, bf16[256,512]{1,0:T(8,128)(2,1)S(1)}, u32[]{:S(2)}, u32[]{:S(2)}) collective-permute-start(bf16[256,512]{1,0:T(8,128)(2,1)S(1)} %get-tuple-element.62), channel_id=1, source_target_pairs={{0,2},{1,3},{2,0},{3,1},{4,6},{5,7},{6,4},{7,5},{8,10},{9,11},{10,... | collective-permute-start | bytes 786440 | tf_op jit(solution)/shard_map/ppermute | solution.py:349
  105.5 1.1 copy-start.12
  106.6 12.2 %collective-permute-start.18 = (bf16[256,512]{1,0:T(8,128)(2,1)}, bf16[256,512]{1,0:T(8,128)(2,1)}, u32[]{:S(2)}, u32[]{:S(2)}) collective-permute-start(bf16[256,512]{1,0:T(8,128)(2,1)} %get-tuple-element.55), channel_id=1, source_target_pairs={{0,2},{1,3},{2,0},{3,1},{4,6},{5,7},{6,4},{7,5},{8,10},{9,11},{10,... | collective-permute-start | bytes 786440 | tf_op jit(solution)/shard_map/ppermute | solution.py:349
  113.9 7.0 %collective-permute-start.17 = (bf16[256,512]{1,0:T(8,128)(2,1)}, bf16[256,512]{1,0:T(8,128)(2,1)S(1)}, u32[]{:S(2)}, u32[]{:S(2)}) collective-permute-start(bf16[256,512]{1,0:T(8,128)(2,1)} %fusion.5), channel_id=1, source_target_pairs={{0,16},{16,0},{1,17},{17,1},{2,18},{18,2},{3,19},{19,3},{4,20},{20... | collective-permute-start | bytes 786440 | tf_op jit(solution)/shard_map/ppermute | solution.py:349
  115.4 13.8 %copy-start.13 = (bf16[2,512,512]{2,1,0:T(8,128)(2,1)S(1)}, bf16[2,512,512]{2,1,0:T(8,128)(2,1)}, u32[]{:S(2)}) copy-start(bf16[2,512,512]{2,1,0:T(8,128)(2,1)} %copy-done.12) | copy-start | bytes 3145732
  115.4 13.8 %collective-permute-start.16 = (bf16[512,512]{1,0:T(8,128)(2,1)}, bf16[512,512]{1,0:T(8,128)(2,1)S(1)}, u32[]{:S(2)}, u32[]{:S(2)}) collective-permute-start(bf16[512,512]{1,0:T(8,128)(2,1)} %fusion.3), channel_id=1, source_target_pairs={{0,2},{1,3},{2,0},{3,1},{4,6},{5,7},{6,4},{7,5},{8,10},{9,11},{10,... | collective-permute-start | bytes 1572872 | tf_op jit(solution)/shard_map/ppermute | solution.py:349
  122.0 8.5 %collective-permute-start.19 = (bf16[256,512]{1,0:T(8,128)(2,1)S(1)}, bf16[256,512]{1,0:T(8,128)(2,1)S(1)}, u32[]{:S(2)}, u32[]{:S(2)}) collective-permute-start(bf16[256,512]{1,0:T(8,128)(2,1)S(1)} %add_convert_fusion.2), channel_id=1, source_target_pairs={{0,16},{16,0},{1,17},{17,1},{2,18},{18,2},{3,19},{19,3},{4,20},{20... | collective-permute-start | bytes 786440 | tf_op jit(solution)/shard_map/ppermute | solution.py:349

commit v13 on v12

--- a/solution.py
+++ b/solution.py
@@ -279,42 +279,56 @@
     )(first, second, incoming, gain.reshape(1, width))
 
 
-def project_kernel(options, place_ref, first_ref, a_ref, *refs):
-    weights, out_ref = list(refs[:-1]), refs[-1]
-
-    def put(slot, pieces):
-        at, product = 0, None
+def project_kernel(options, rows_count, place_ref, first_ref, *refs):
+    rows, refs = refs[:rows_count], refs[rows_count:]
+    *weights, held, sems = refs[: -2 - rows_count] + refs[-2:]
+    outs = refs[-2 - rows_count : -2]
+    whole = weights[0]
+
+    def fetch(slot, pieces):
+        at = 0
         for piece in pieces:
-            part = mxu(a_ref[:, at : at + piece.shape[0]], piece[...])
-            product = part if product is None else product + part
+            to = held.at[slot, pl.ds(at, piece.shape[0])]
+            pltpu.make_async_copy(piece, to, sems.at[slot]).start()
             at += piece.shape[0]
-        out_ref[place_ref[slot]] = product.astype(BF16)
 
     for slot, counts in enumerate(options):
         for option, pieces in enumerate(counts):
             taken, weights = weights[:pieces], weights[pieces:]
             if len(counts) == 1:
-                put(slot, taken)
+                fetch(slot, taken)
             else:
-                pl.when(first_ref[slot] == 1 - option)(functools.partial(put, slot, taken))
+                pl.when(first_ref[slot] == 1 - option)(functools.partial(fetch, slot, taken))
+    for slot in range(len(options)):
+        pltpu.make_async_copy(whole, held.at[slot], sems.at[slot]).wait()
+        for row, out in zip(rows, outs):
+            out[place_ref[slot]] = mxu(row[...], held[slot]).astype(BF16)
 
 
 def project(places, first, rows, weights):
-    tokens = rows.shape[0]
+    tokens, depth = rows[0].shape
     block = weights[0][0][0].shape[1]
     count = len(weights)
     flat = [piece for options in weights for pieces in options for piece in pieces]
+    vmem = pl.BlockSpec(memory_space=pltpu.VMEM)
     return pl.pallas_call(
         functools.partial(
-            project_kernel, tuple(tuple(len(pieces) for pieces in options) for options in weights)
+            project_kernel,
+            tuple(tuple(len(pieces) for pieces in options) for options in weights),
+            len(rows),
         ),
         in_specs=[pl.BlockSpec(memory_space=pltpu.SMEM)] * 2
-        + [pl.BlockSpec(memory_space=pltpu.VMEM)] * (1 + len(flat)),
-        out_specs=pl.BlockSpec(memory_space=pltpu.VMEM),
-        out_shape=jax.ShapeDtypeStruct((count, tokens, block), BF16),
-        compiler_params=pltpu.CompilerParams(vmem_limit_bytes=GRANT),
+        + [vmem] * len(rows)
+        + [pl.BlockSpec(memory_space=pl.ANY)] * len(flat),
+        out_specs=[vmem] * len(rows),
+        out_shape=[jax.ShapeDtypeStruct((count, tokens, block), BF16)] * len(rows),
+        scratch_shapes=[
+            pltpu.VMEM((count, depth, block), BF16),
+            pltpu.SemaphoreType.DMA((count,)),
+        ],
+        compiler_params=pltpu.CompilerParams(vmem_limit_bytes=2 * GRANT),
         name="project",
-    )(places, first, rows, *flat)
+    )(places, first, *rows, *flat)
 
 
 def halving_order(count):
@@ -399,9 +413,10 @@
         pass_down(3)
         up_rest, incoming = tied(up[2][ahead:], incoming)
         up[3] = [up_first, send(up_rest, "ctx", last)]
-        weights = [([own],), ([up[1]], [down[3]]), ([up[2]], [down[2]]), (up[3], [down[1]])]
-        targets = lax.rem(here + ctx - jnp.arange(ctx), ctx)
-        first = (here >= jnp.arange(ctx)).astype(jnp.int32)
+        weights = [([up[1]], [down[3]]), ([down[1]], up[3]), ([own],), ([up[2]], [down[2]])]
+        slots = jnp.asarray([1, 3, 0, 2], jnp.int32)
+        targets = lax.rem(here + ctx - slots, ctx)
+        first = jnp.where(slots == 3, here < 3, here >= slots).astype(jnp.int32)
     else:
         whole = lax.all_gather(own, "ctx", axis=1, tiled=True)
         weights = [([w],) for w in jnp.split(whole, head, axis=1)]
@@ -412,24 +427,55 @@
     mine = normed_rows(near, far, incoming, gain)
     other = normed_rows(near_other, far_other, incoming_other, gain)
     distance = targets ^ lax.axis_index("head")
-    order = jnp.asarray(halving_order(head), jnp.int32)
-    places = jnp.argmax(distance[:, None] == order[None, :], axis=1).astype(jnp.int32)
-    mine, other = tied(mine, other)
-    give, keep = head_halved(project(places, first, other, weights))
-    own_give, own_keep = head_halved(project(places, first, mine, weights))
-    last_pairs = head_pairs(head // 2)
-    give_a, give_b = jnp.split(give, 2)
-    keep_a, keep_b = jnp.split(keep, 2)
-    got_a = send(give_a, "head", last_pairs)
-    give_b, own_give = tied(give_b, own_give)
-    got_b = send(give_b, "head", last_pairs)
-    got_a, own_give = tied(got_a, own_give)
-    back_a = send(summed(keep_a, got_a), "groups", swap)
-    own_got = send(own_give, "head", last_pairs)
-    back_a, got_b, keep_b = tied(back_a, got_b, keep_b)
-    back_b = send(summed(keep_b, got_b), "groups", swap)
-    mine_sum = summed(own_keep, own_got)
-    back = jnp.concatenate([back_a, back_b], axis=0)
+    if ring:
+        places = jnp.where((distance & 2) == 2, 0, 1).astype(jnp.int32)
+        even = (here + lax.axis_index("head")) % 2 == 0
+        cells = [(z, h) for z in range(ctx) for h in range(head)]
+
+        def cell_pairs(parity, bit):
+            return [
+                (z * head + h, z * head + (h ^ bit)) for z, h in cells if (z + h) % 2 == parity
+            ]
+
+        def crossing(parts, parity):
+            got = lax.ppermute(parts, ("ctx", "head"), cell_pairs(1 - parity, 1))
+            return summed(parts[0], got[0]), parts[1].astype(F32) + got[1].astype(F32)
+
+        def over_x(value, parity):
+            return lax.ppermute(value, ("ctx", "head"), cell_pairs(parity, 2))
+
+        def back_over_y(value, parity):
+            pairs = [
+                ((g * ctx + z) * head + h, ((1 - g) * ctx + z) * head + h)
+                for g in range(2)
+                for z, h in cells
+                if (z + h) % 2 == parity
+            ]
+            return lax.ppermute(value, ("groups", "ctx", "head"), pairs)
+
+        other_parts, parts = project(places[2:], first[2:], [other, mine], weights[2:])
+        give, keep = crossing(other_parts, 0)
+        own_give, own_keep = crossing(parts, 0)
+        got, own_got = over_x(give, 0), over_x(own_give, 0)
+        other_parts, parts = project(places[:2], first[:2], [other, mine], weights[:2])
+        back = back_over_y(summed(keep, got), 0)
+        even_sum = summed(own_keep, own_got)
+        give, keep = crossing(other_parts, 1)
+        own_give, own_keep = crossing(parts, 1)
+        got = over_x(give, 1)
+        own_got = over_x(own_give, 1)
+        back_odd = back_over_y(summed(keep, got), 1)
+        mine_sum = jnp.where(even, even_sum, summed(own_keep, own_got))
+        back = jnp.where(even, back, back_odd)
+    else:
+        order = jnp.asarray(halving_order(head), jnp.int32)
+        places = jnp.argmax(distance[:, None] == order[None, :], axis=1).astype(jnp.int32)
+        last_pairs = head_pairs(head // 2)
+        sums = []
+        for parts in project(places, first, [other, mine], weights):
+            give, keep = head_halved(parts)
+            sums.append(summed(keep, lax.ppermute(give, "head", last_pairs)))
+        back, mine_sum = send(sums[0], "groups", swap), sums[1]
     blocks = mine_sum.shape[1] // half_cols
     if blocks == 1:
         return jnp.where(

time: 133 us -> 146 us (1.098)
  waiting for transfers between devices: 26.5 us -> 38.5 us
  Pallas kernels: 44.1 us -> 40.9 us
  other arithmetic: 7.29 us -> 10.1 us
  starting transfers between devices: 43.9 us -> 46.5 us
  local copies, waits for them, and re-layouts: 8.1 us -> 6.24 us
    ppermute x2 -> x10, waiting for transfers between devices: 0.01 us -> 22.1 us  [the longest x4 17.6 us: over_x(): return lax.ppermute(value, ('ctx', 'head'), cell_pairs(parity, 2))]
    ppermute x2 -> x10, starting transfers between devices: 0.63 us -> 17.4 us  [the longest x4 8.12 us: over_x(): return lax.ppermute(value, ('ctx', 'head'), cell_pairs(parity, 2))]
    ppermute x18 -> x13, starting transfers between devices: 43.3 us -> 29 us  [send(): return lax.ppermute(value, axis, pairs)]
    ppermute x18 -> x13, waiting for transfers between devices: 26.5 us -> 16.4 us  [send(): return lax.ppermute(value, axis, pairs)]
    pallas_call x2, Pallas kernels: 10.8 us -> 7.43 us  [project(): pl.pallas_call(functools.partial(project_kernel, tuple((tuple((len(pieces...]
    select_n x0 -> x3, other arithmetic: none -> 3.2 us  [the longest x1 2.09 us: per_device(): mine_sum = jnp.where(even, even_sum, summed(own_keep, own_got))]
    unnamed x33 -> x40, local copies, waits for them, and re-layouts: 5.08 us -> 3.71 us
    convert_element_type x4 -> x6, other arithmetic: 3.34 us -> 4.44 us  [summed(): return (keep.astype(F32) + got.astype(F32)).astype(BF16)]
  transfers between devices with their start and end apart: 20 -> 23, of which waited for: 9 -> 8; matrix products, arithmetic and copies ran while one was open for 8% -> 9% of each run, Pallas kernels for 29% -> 28%
where the time goes in v13:
time: 146 us; the launch traced here: 145 us
  starting transfers between devices  46.5 us (32%)
  Pallas kernels  40.9 us (28%)
  waiting for transfers between devices  38.5 us (26%)
  other arithmetic  10.1 us (7%)
  local copies, waits for them, and re-layouts  6.24 us (4%)
  matrix products  2.27 us (2%)
    pallas_call x2, Pallas kernels, local_part(): pl.pallas_call(functools.partial(chunk_kernel, group, first), grid=(steps...  30.5 us
    ppermute x13, starting transfers between devices, send(): return lax.ppermute(value, axis, pairs)  29 us
    ppermute x4, waiting for transfers between devices, over_x(): return lax.ppermute(value, ('ctx', 'head'), cell_pairs(parity, 2))  17.6 us
    ppermute x13, waiting for transfers between devices, send(): return lax.ppermute(value, axis, pairs)  16.4 us
    ppermute x4, starting transfers between devices, over_x(): return lax.ppermute(value, ('ctx', 'head'), cell_pairs(parity, 2))  8.12 us
    pallas_call x2, Pallas kernels, project(): pl.pallas_call(functools.partial(project_kernel, tuple((tuple((len(pieces...  7.43 us
    ppermute x4, starting transfers between devices, crossing(): got = lax.ppermute(parts, ('ctx', 'head'), cell_pairs(1 - parity, 1))  5.48 us
    convert_element_type x6, other arithmetic, summed(): return (keep.astype(F32) + got.astype(F32)).astype(BF16)  4.44 us
  transfers between devices with their start and end apart: 23, of which 8 were waited for; matrix products, arithmetic and copies ran while one was open for 9% of the time, Pallas kernels for 28%

profile of v13, /device:TPU:16, one launch (start us, length us, event | category | flops | bytes accessed | tf_op | source)
XLA Modules:
  0.0 144.9 jit_solution(9787546191382163784)
XLA Ops:
  0.0 1.6 %copy-done = bf16[1024,1024]{1,0:T(8,128)(2,1)S(1)} copy-done((bf16[1024,1024]{1,0:T(8,128)(2,1)S(1)}, bf16[1024,1024]{1,0:T(8,128)(2,1)}, u32[]{:S(2)}) %copy-start) | copy-done | bytes 2097176
  1.6 0.1 constant_dynamic-slice_fusion.refs_2_
  1.7 3.5 %collective-permute-start = (bf16[1024,512]{1,0:T(8,128)(2,1)S(1)}, bf16[1024,512]{1,0:T(8,128)(2,1)}, u32[]{:S(2)}, u32[]{:S(2)}) collective-permute-start(bf16[1024,512]{1,0:T(8,128)(2,1)S(1)} %constant_dynamic-slice_fusion.refs_2_), channel_id=1, source_target_pairs={{0,4},{4,8},{8,12},{1,5},{5,9},{9,13},{2,6},{6,10},{10,14},{3,7},{... | collective-permute-start | bytes 3145736 | tf_op jit(solution)/shard_map/ppermute | solution.py:363
  5.2 2.4 %collective-permute-start.1 = (bf16[1024,512]{1,0:T(8,128)(2,1)S(1)}, bf16[1024,512]{1,0:T(8,128)(2,1)}, u32[]{:S(2)}, u32[]{:S(2)}) collective-permute-start(bf16[1024,512]{1,0:T(8,128)(2,1)S(1)} %constant_dynamic-slice_fusion.refs_2_), channel_id=1, source_target_pairs={{4,0},{8,4},{12,8},{5,1},{9,5},{13,9},{6,2},{10,6},{14,10},{7,3},{... | collective-permute-start | bytes 3145736 | tf_op jit(solution)/shard_map/ppermute | solution.py:363
  7.6 1.0 copy.8
  8.6 18.1 %local_part.2 = (bf16[320,2048]{1,0:T(8,128)(2,1)}, f32[8,128,256]{2,1,0:T(8,128)}) custom-call(bf16[512,1024]{1,0:T(8,128)(2,1)} %q_ref.3, bf16[512,2,1024]{2,1,0:T(2,128)(2,1)} %k_ref.3, bf16[512,2,1024]{2,1,0:T(2,128)(2,1)} %v_ref.3, f32[1024,8]{1,0:T(8,128)} %bitcast.37), custom_call_target="tpu_custom_call" | custom-call | flops 16777216000 | bytes 5242880 | tf_op jit(solution)/shard_map/local_part/pallas_call | solution.py:215
  26.7 1.5 %collective-permute-start.5 = (bf16[320,2048]{1,0:T(8,128)(2,1)}, bf16[320,2048]{1,0:T(8,128)(2,1)S(1)}, u32[]{:S(2)}, u32[]{:S(2)}) collective-permute-start(bf16[320,2048]{1,0:T(8,128)(2,1)} %get-tuple-element.29.first_ref), channel_id=1, source_target_pairs={{0,16},{16,0},{1,17},{17,1},{2,18},{18,2},{3,19},{19,3},{4,20},{20... | collective-permute-start | bytes 3932168 | tf_op jit(solution)/shard_map/ppermute | solution.py:363
  28.2 0.4 collective-permute-done.refs_2_
  28.6 3.2 %collective-permute-done.1.refs_4_ = bf16[1024,512]{1,0:T(8,128)(2,1)} collective-permute-done((bf16[1024,512]{1,0:T(8,128)(2,1)S(1)}, bf16[1024,512]{1,0:T(8,128)(2,1)}, u32[]{:S(2)}, u32[]{:S(2)}) %collective-permute-start.1) | collective-permute-done | bytes 1048608 | tf_op jit(solution)/shard_map/ppermute | solution.py:363
  31.8 1.9 %collective-permute-start.2 = (bf16[1024,512]{1,0:T(8,128)(2,1)}, bf16[1024,512]{1,0:T(8,128)(2,1)S(1)}, u32[]{:S(2)}, u32[]{:S(2)}) collective-permute-start(bf16[1024,512]{1,0:T(8,128)(2,1)} %collective-permute-done.refs_2_), channel_id=1, source_target_pairs={{4,8},{8,12},{5,9},{9,13},{6,10},{10,14},{7,11},{11,15},{20,24},{2... | collective-permute-start | bytes 3145736 | tf_op jit(solution)/shard_map/ppermute | solution.py:363
  33.7 4.0 %collective-permute-start.4 = (bf16[1024,512]{1,0:T(8,128)(2,1)}, bf16[1024,512]{1,0:T(8,128)(2,1)S(1)}, u32[]{:S(2)}, u32[]{:S(2)}) collective-permute-start(bf16[1024,512]{1,0:T(8,128)(2,1)} %collective-permute-done.1.refs_4_), channel_id=1, source_target_pairs={{4,0},{8,4},{5,1},{9,5},{6,2},{10,6},{7,3},{11,7},{20,16},{24,20},... | collective-permute-start | bytes 3145736 | tf_op jit(solution)/shard_map/ppermute | solution.py:363
  37.8 12.4 %local_part.3 = (bf16[192,2048]{1,0:T(8,128)(2,1)}, f32[8,128,128]{2,1,0:T(8,128)}, bf16[8,128,128]{2,1,0:T(8,128)(2,1)}, bf16[8,128,128]{2,1,0:T(8,128)(2,1)}) custom-call(bf16[512,1024]{1,0:T(8,128)(2,1)} %q_ref.3, bf16[512,2,1024]{2,1,0:T(2,128)(2,1)} %k_ref.3, bf16[512,2,1024]{2,1,0:T(2,128)(2,1)} %v_ref.3, f32[1024,8]{1,0:T(8,128)} %bitcast.38, ...), custom_call_target="tpu_custom_call" | custom-call | flops 10066329600 | bytes 3145728 | tf_op jit(solution)/shard_map/local_part/pallas_call | solution.py:215
  50.2 0.0 copy-start.17
  50.2 0.0 copy-start.18
  50.2 0.8 collective-permute-start.6
  51.0 1.6 %collective-permute-start.8 = (bf16[192,2048]{1,0:T(8,128)(2,1)}, bf16[192,2048]{1,0:T(8,128)(2,1)}, u32[]{:S(2)}, u32[]{:S(2)}) collective-permute-start(bf16[192,2048]{1,0:T(8,128)(2,1)} %get-tuple-element.35.second_ref), channel_id=1, source_target_pairs={{0,16},{16,0},{1,17},{17,1},{2,18},{18,2},{3,19},{19,3},{4,20},{20... | collective-permute-start | bytes 2359304 | tf_op jit(solution)/shard_map/ppermute | solution.py:363
  52.6 0.0 collective-permute-done.6
  52.6 1.3 fusion
  54.0 1.3 collective-permute-start.7
  55.3 2.3 %collective-permute-done.2.refs_3_ = bf16[1024,512]{1,0:T(8,128)(2,1)S(1)} collective-permute-done((bf16[1024,512]{1,0:T(8,128)(2,1)}, bf16[1024,512]{1,0:T(8,128)(2,1)S(1)}, u32[]{:S(2)}, u32[]{:S(2)}) %collective-permute-start.2) | collective-permute-done | bytes 1048608 | tf_op jit(solution)/shard_map/ppermute | solution.py:363
  57.6 0.0 copy-start.19
  57.6 0.0 copy-start.8
  57.7 2.3 %collective-permute-start.3 = (bf16[256,512]{1,0:T(8,128)(2,1)S(1)}, bf16[256,512]{1,0:T(8,128)(2,1)S(1)}, u32[]{:S(2)}, u32[]{:S(2)}) collective-permute-start(bf16[256,512]{1,0:T(8,128)(2,1)S(1)} %slice.88), channel_id=1, source_target_pairs={{8,12},{9,13},{10,14},{11,15},{24,28},{25,29},{26,30},{27,31}} | collective-permute-start | bytes 786440 | tf_op jit(solution)/shard_map/ppermute | solution.py:363
  60.0 5.9 %collective-permute-done.7 = bf16[8,128,128]{2,1,0:T(8,128)(2,1)S(1)} collective-permute-done((bf16[8,128,128]{2,1,0:T(8,128)(2,1)S(1)}, bf16[8,128,128]{2,1,0:T(8,128)(2,1)S(1)}, u32[]{:S(2)}, u32[]{:S(2)}) %collective-permute-start.7) | collective-permute-done | bytes 262176 | tf_op jit(solution)/shard_map/ppermute | solution.py:363
  65.9 0.1 add.82
  66.1 0.9 fusion.1
  67.0 1.1 copy-done.1
  68.0 0.0 collective-permute-done.4.refs_4_
  68.1 1.0 copy-done.15
  69.1 2.0 %collective-permute-start.9 = (bf16[8,128,128]{2,1,0:T(8,128)(2,1)}, bf16[8,128,128]{2,1,0:T(8,128)(2,1)}, u32[]{:S(2)}, u32[]{:S(2)}) collective-permute-start(bf16[8,128,128]{2,1,0:T(8,128)(2,1)} %fusion.1), channel_id=1, source_target_pairs={{8,12},{9,13},{10,14},{11,15},{24,28},{25,29},{26,30},{27,31}} | collective-permute-start | bytes 786440 | tf_op jit(solution)/shard_map/ppermute | solution.py:363
  71.1 1.7 %collective-permute-start.13 = (bf16[1024,512]{1,0:T(8,128)(2,1)}, bf16[1024,512]{1,0:T(8,128)(2,1)}, u32[]{:S(2)}, u32[]{:S(2)}) collective-permute-start(bf16[1024,512]{1,0:T(8,128)(2,1)} %copy-done.15), channel_id=1, source_target_pairs={{4,0},{5,1},{6,2},{7,3},{20,16},{21,17},{22,18},{23,19}} | collective-permute-start | bytes 3145736 | tf_op jit(solution)/shard_map/ppermute | solution.py:363
  72.8 1.3 slice.89
  74.1 0.4 collective-permute-done.9
  74.5 1.1 add.84.s_ref
  75.6 1.6 %collective-permute-start.10 = (bf16[8,128,128]{2,1,0:T(8,128)(2,1)S(1)}, bf16[8,128,128]{2,1,0:T(8,128)(2,1)S(1)}, u32[]{:S(2)}, u32[]{:S(2)}) collective-permute-start(bf16[8,128,128]{2,1,0:T(8,128)(2,1)S(1)} %add.84.s_ref), channel_id=1, source_target_pairs={{0,16},{16,0},{1,17},{17,1},{2,18},{18,2},{3,19},{19,3},{4,20},{20... | collective-permute-start | bytes 786440 | tf_op jit(solution)/shard_map/ppermute | solution.py:363
  77.2 4.4 %collective-permute-start.14 = (bf16[768,512]{1,0:T(8,128)(2,1)S(1)}, bf16[768,512]{1,0:T(8,128)(2,1)S(1)}, u32[]{:S(2)}, u32[]{:S(2)}) collective-permute-start(bf16[768,512]{1,0:T(8,128)(2,1)S(1)} %slice.89), channel_id=1, source_target_pairs={{8,12},{9,13},{10,14},{11,15},{24,28},{25,29},{26,30},{27,31}} | collective-permute-start | bytes 2359304 | tf_op jit(solution)/shard_map/ppermute | solution.py:363
  81.7 0.1 fusion.14
  81.8 0.9 normed_rows.3.refs_1_
  82.7 2.0 %normed_rows.2.refs_0_ = bf16[512,1024]{1,0:T(8,128)(2,1)S(1)} custom-call(bf16[320,2048]{1,0:T(8,128)(2,1)S(1)} %copy-done.2, bf16[192,2048]{1,0:T(8,128)(2,1)} %collective-permute-done.8.second_ref, bf16[8,128,128]{2,1,0:T(8,128)(2,1)S(1)} %collective-permute-done.10.s_ref, f32[1,1024]{1,0:T(1,128)S(1)} %bitcast.36), custom_call_target="tpu_custom_call" | custom-call | tf_op jit(solution)/shard_map/normed_rows/pallas_call | solution.py:272
  84.7 3.1 %project.2 = (bf16[2,512,512]{2,1,0:T(8,128)(2,1)S(1)}, bf16[2,512,512]{2,1,0:T(8,128)(2,1)S(1)}) custom-call(s32[2]{0:T(128)S(1)} %get-tuple-element.51.place_ref, s32[2]{0:T(128)S(1)} %get-tuple-element.48.first_ref, bf16[512,1024]{1,0:T(8,128)(2,1)S(1)} %normed_rows.2.refs_0_, bf16[512,1024]{1,0:T(8,128)(2,1)S(1)} %normed_rows.3.refs_1_, ...), custom_call_target="tpu_custom_call" | custom-call | tf_op jit(solution)/shard_map/project/pallas_call | solution.py:314
  87.9 1.5 %collective-permute-start.11 = (bf16[2,512,512]{2,1,0:T(8,128)(2,1)S(1)}, bf16[2,512,512]{2,1,0:T(8,128)(2,1)S(1)}, u32[]{:S(2)}, u32[]{:S(2)}) collective-permute-start(bf16[2,512,512]{2,1,0:T(8,128)(2,1)S(1)} %get-tuple-element.41), channel_id=1, source_target_pairs={{1,0},{3,2},{4,5},{6,7},{9,8},{11,10},{12,13},{14,15},{17,16},{19,... | collective-permute-start | bytes 3145736 | tf_op jit(solution)/shard_map/ppermute | solution.py:441
  89.4 1.3 collective-permute-start.17
  90.7 4.1 %collective-permute-done.14.refs_6_ = bf16[768,512]{1,0:T(8,128)(2,1)S(1)} collective-permute-done((bf16[768,512]{1,0:T(8,128)(2,1)S(1)}, bf16[768,512]{1,0:T(8,128)(2,1)S(1)}, u32[]{:S(2)}, u32[]{:S(2)}) %collective-permute-start.14) | collective-permute-done | bytes 786464 | tf_op jit(solution)/shard_map/ppermute | solution.py:363
  94.8 4.3 %project.3 = (bf16[2,512,512]{2,1,0:T(8,128)(2,1)S(1)}, bf16[2,512,512]{2,1,0:T(8,128)(2,1)S(1)}) custom-call(s32[2]{0:T(128)S(1)} %get-tuple-element.52.place_ref, s32[2]{0:T(128)S(1)} %get-tuple-element.47.first_ref, bf16[512,1024]{1,0:T(8,128)(2,1)S(1)} %normed_rows.2.refs_0_, bf16[512,1024]{1,0:T(8,128)(2,1)S(1)} %normed_rows.3.refs_1_, ...), custom_call_target="tpu_custom_call" | custom-call | tf_op jit(solution)/shard_map/project/pallas_call | solution.py:314
  99.1 1.4 collective-permute-start.20
  100.5 1.4 collective-permute-start.15
  101.9 1.1 fusion.6
  102.9 3.4 %collective-permute-start.12 = (bf16[512,512]{1,0:T(8,128)(2,1)}, bf16[512,512]{1,0:T(8,128)(2,1)}, u32[]{:S(2)}, u32[]{:S(2)}) collective-permute-start(bf16[512,512]{1,0:T(8,128)(2,1)} %fusion.6), channel_id=1, source_target_pairs={{0,2},{2,0},{5,7},{7,5},{8,10},{10,8},{13,15},{15,13},{16,18},{18,... | collective-permute-start | bytes 1572872 | tf_op jit(solution)/shard_map/ppermute | solution.py:445
  106.4 0.1 fusion.8
  106.5 2.4 %collective-permute-start.18 = (bf16[512,512]{1,0:T(8,128)(2,1)S(1)}, bf16[512,512]{1,0:T(8,128)(2,1)S(1)}, u32[]{:S(2)}, u32[]{:S(2)}) collective-permute-start(bf16[512,512]{1,0:T(8,128)(2,1)S(1)} %fusion.8), channel_id=1, source_target_pairs={{0,2},{2,0},{5,7},{7,5},{8,10},{10,8},{13,15},{15,13},{16,18},{18,... | collective-permute-start | bytes 1572872 | tf_op jit(solution)/shard_map/ppermute | solution.py:445
  109.0 0.1 fusion.9
  109.1 0.7 collective-permute-start.21
  109.8 0.0 copy-start.14
  109.8 1.1 fusion.7
  110.9 1.6 %collective-permute-start.16 = (bf16[512,512]{1,0:T(8,128)(2,1)}, bf16[512,512]{1,0:T(8,128)(2,1)}, u32[]{:S(2)}, u32[]{:S(2)}) collective-permute-start(bf16[512,512]{1,0:T(8,128)(2,1)} %fusion.7), channel_id=1, source_target_pairs={{1,3},{3,1},{4,6},{6,4},{9,11},{11,9},{12,14},{14,12},{17,19},{19,... | collective-permute-start | bytes 1572872 | tf_op jit(solution)/shard_map/ppermute | solution.py:445
  112.5 17.6 %collective-permute-done.18 = bf16[512,512]{1,0:T(8,128)(2,1)S(1)} collective-permute-done((bf16[512,512]{1,0:T(8,128)(2,1)S(1)}, bf16[512,512]{1,0:T(8,128)(2,1)S(1)}, u32[]{:S(2)}, u32[]{:S(2)}) %collective-permute-start.18) | collective-permute-done | bytes 524320 | tf_op jit(solution)/shard_map/ppermute | solution.py:445
  130.1 1.0 fusion.3
  131.1 2.4 %collective-permute-start.19 = (bf16[512,512]{1,0:T(8,128)(2,1)}, bf16[512,512]{1,0:T(8,128)(2,1)}, u32[]{:S(2)}, u32[]{:S(2)}) collective-permute-start(bf16[512,512]{1,0:T(8,128)(2,1)} %fusion.3), channel_id=1, source_target_pairs={{0,16},{2,18},{5,21},{7,23},{8,24},{10,26},{13,29},{15,31},{16,0},... | collective-permute-start | bytes 1572872 | tf_op jit(solution)/shard_map/ppermute | solution.py:454
  133.5 1.0 fusion.2
  134.5 1.5 %collective-permute-start.22 = (bf16[512,512]{1,0:T(8,128)(2,1)}, bf16[512,512]{1,0:T(8,128)(2,1)}, u32[]{:S(2)}, u32[]{:S(2)}) collective-permute-start(bf16[512,512]{1,0:T(8,128)(2,1)} %fusion.2), channel_id=1, source_target_pairs={{1,17},{3,19},{4,20},{6,22},{9,25},{11,27},{12,28},{14,30},{17,1},... | collective-permute-start | bytes 1572872 | tf_op jit(solution)/shard_map/ppermute | solution.py:454
  136.0 2.1 %fusion.10 = bf16[512,512]{1,0:T(8,128)(2,1)S(1)} fusion(bf16[512,512]{1,0:T(8,128)(2,1)} %collective-permute-done.12, bf16[512,512]{1,0:T(8,128)(2,1)} %collective-permute-done.16, bf16[2,512,512]{2,1,0:T(8,128)(2,1)} %copy-done.14, bf16[2,512,512]{2,1,0:T(8,128)(2,1)} %copy-done.13, bf16[2,512,512]{2,1,0:T(8,128)(2,1)} %copy-done.6, ...), kind=kLoop, calls=%fused_computation.21 | loop fusion | flops 3407872 | bytes 3670017 | tf_op jit(solution)/shard_map/jit(_where)/select_n | solution.py:468
  138.1 4.4 %collective-permute-done.19 = bf16[512,512]{1,0:T(8,128)(2,1)} collective-permute-done((bf16[512,512]{1,0:T(8,128)(2,1)}, bf16[512,512]{1,0:T(8,128)(2,1)}, u32[]{:S(2)}, u32[]{:S(2)}) %collective-permute-start.19) | collective-permute-done | bytes 524320 | tf_op jit(solution)/shard_map/ppermute | solution.py:454
  142.5 1.1 broadcast_select_fusion
  143.6 1.3 maximum_select_fusion
  (48 shorter events, 0.1 us)
Async XLA Ops:
  0.0 1.6 %copy-start = (bf16[1024,1024]{1,0:T(8,128)(2,1)S(1)}, bf16[1024,1024]{1,0:T(8,128)(2,1)}, u32[]{:S(2)}) copy-start(bf16[1024,1024]{1,0:T(8,128)(2,1)} %param.12) | copy-start | bytes 6291460
  0.0 7.6 %copy-start.16 = (f32[2,8,512]{2,1,0:T(8,128)S(1)}, f32[2,8,512]{2,1,0:T(8,128)}, u32[]{:S(2)}) copy-start(f32[2,8,512]{2,1,0:T(8,128)} %param.10) | copy-start | bytes 98308
  1.7 26.9 %collective-permute-start = (bf16[1024,512]{1,0:T(8,128)(2,1)S(1)}, bf16[1024,512]{1,0:T(8,128)(2,1)}, u32[]{:S(2)}, u32[]{:S(2)}) collective-permute-start(bf16[1024,512]{1,0:T(8,128)(2,1)S(1)} %constant_dynamic-slice_fusion.refs_2_), channel_id=1, source_target_pairs={{0,4},{4,8},{8,12},{1,5},{5,9},{9,13},{2,6},{6,10},{10,14},{3,7},{... | collective-permute-start | bytes 3145736 | tf_op jit(solution)/shard_map/ppermute | solution.py:363
  5.2 26.6 %collective-permute-start.1 = (bf16[1024,512]{1,0:T(8,128)(2,1)S(1)}, bf16[1024,512]{1,0:T(8,128)(2,1)}, u32[]{:S(2)}, u32[]{:S(2)}) collective-permute-start(bf16[1024,512]{1,0:T(8,128)(2,1)S(1)} %constant_dynamic-slice_fusion.refs_2_), channel_id=1, source_target_pairs={{4,0},{8,4},{12,8},{5,1},{9,5},{13,9},{6,2},{10,6},{14,10},{7,3},{... | collective-permute-start | bytes 3145736 | tf_op jit(solution)/shard_map/ppermute | solution.py:363
  26.7 40.3 %collective-permute-start.5 = (bf16[320,2048]{1,0:T(8,128)(2,1)}, bf16[320,2048]{1,0:T(8,128)(2,1)S(1)}, u32[]{:S(2)}, u32[]{:S(2)}) collective-permute-start(bf16[320,2048]{1,0:T(8,128)(2,1)} %get-tuple-element.29.first_ref), channel_id=1, source_target_pairs={{0,16},{16,0},{1,17},{17,1},{2,18},{18,2},{3,19},{19,3},{4,20},{20... | collective-permute-start | bytes 3932168 | tf_op jit(solution)/shard_map/ppermute | solution.py:363
  31.8 25.8 %collective-permute-start.2 = (bf16[1024,512]{1,0:T(8,128)(2,1)}, bf16[1024,512]{1,0:T(8,128)(2,1)S(1)}, u32[]{:S(2)}, u32[]{:S(2)}) collective-permute-start(bf16[1024,512]{1,0:T(8,128)(2,1)} %collective-permute-done.refs_2_), channel_id=1, source_target_pairs={{4,8},{8,12},{5,9},{9,13},{6,10},{10,14},{7,11},{11,15},{20,24},{2... | collective-permute-start | bytes 3145736 | tf_op jit(solution)/shard_map/ppermute | solution.py:363
  33.7 34.3 %collective-permute-start.4 = (bf16[1024,512]{1,0:T(8,128)(2,1)}, bf16[1024,512]{1,0:T(8,128)(2,1)S(1)}, u32[]{:S(2)}, u32[]{:S(2)}) collective-permute-start(bf16[1024,512]{1,0:T(8,128)(2,1)} %collective-permute-done.1.refs_4_), channel_id=1, source_target_pairs={{4,0},{8,4},{5,1},{9,5},{6,2},{10,6},{7,3},{11,7},{20,16},{24,20},... | collective-permute-start | bytes 3145736 | tf_op jit(solution)/shard_map/ppermute | solution.py:363
  50.2 15.8 %copy-start.11 = (f32[8,128,128]{2,1,0:T(8,128)S(1)}, f32[8,128,128]{2,1,0:T(8,128)}, u32[]{:S(2)}) copy-start(f32[8,128,128]{2,1,0:T(8,128)} %get-tuple-element.33) | copy-start | bytes 1572868
  50.2 15.9 %copy-start.12 = (bf16[8,128,128]{2,1,0:T(8,128)(2,1)S(1)}, bf16[8,128,128]{2,1,0:T(8,128)(2,1)}, u32[]{:S(2)}) copy-start(bf16[8,128,128]{2,1,0:T(8,128)(2,1)} %get-tuple-element.31) | copy-start | bytes 786436
  50.2 22.5 %copy-start.17 = (s32[4]{0:T(128)S(1)}, s32[4]{0:T(128)}, u32[]{:S(2)}) copy-start(s32[4]{0:T(128)} %constant.43.clone) | copy-start | bytes 52
  50.2 22.5 %copy-start.18 = (pred[4]{0:T(512)(128)(4,1)S(1)}, pred[4]{0:T(512)(128)(4,1)}, u32[]{:S(2)}) copy-start(pred[4]{0:T(512)(128)(4,1)} %constant.45) | copy-start | bytes 16
  50.2 2.4 %collective-permute-start.6 = (bf16[8,128,128]{2,1,0:T(8,128)(2,1)}, bf16[8,128,128]{2,1,0:T(8,128)(2,1)S(1)}, u32[]{:S(2)}, u32[]{:S(2)}) collective-permute-start(bf16[8,128,128]{2,1,0:T(8,128)(2,1)} %get-tuple-element.32), channel_id=1, source_target_pairs={{0,4},{1,5},{2,6},{3,7},{16,20},{17,21},{18,22},{19,23}} | collective-permute-start | bytes 786440 | tf_op jit(solution)/shard_map/ppermute | solution.py:363
  51.0 24.6 %collective-permute-start.8 = (bf16[192,2048]{1,0:T(8,128)(2,1)}, bf16[192,2048]{1,0:T(8,128)(2,1)}, u32[]{:S(2)}, u32[]{:S(2)}) collective-permute-start(bf16[192,2048]{1,0:T(8,128)(2,1)} %get-tuple-element.35.second_ref), channel_id=1, source_target_pairs={{0,16},{16,0},{1,17},{17,1},{2,18},{18,2},{3,19},{19,3},{4,20},{20... | collective-permute-start | bytes 2359304 | tf_op jit(solution)/shard_map/ppermute | solution.py:363
  54.0 12.0 %collective-permute-start.7 = (bf16[8,128,128]{2,1,0:T(8,128)(2,1)S(1)}, bf16[8,128,128]{2,1,0:T(8,128)(2,1)S(1)}, u32[]{:S(2)}, u32[]{:S(2)}) collective-permute-start(bf16[8,128,128]{2,1,0:T(8,128)(2,1)S(1)} %fusion), channel_id=1, source_target_pairs={{4,8},{5,9},{6,10},{7,11},{20,24},{21,25},{22,26},{23,27}} | collective-permute-start | bytes 786440 | tf_op jit(solution)/shard_map/ppermute | solution.py:363
  57.6 10.4 %copy-start.9 = (bf16[1024,512]{1,0:T(8,128)(2,1)}, bf16[1024,512]{1,0:T(8,128)(2,1)S(1)}, u32[]{:S(2)}) copy-start(bf16[1024,512]{1,0:T(8,128)(2,1)S(1)} %collective-permute-done.2.refs_3_) | copy-start | bytes 3145732
  57.6 24.0 %copy-start.19 = (s32[4]{0:T(128)S(1)}, s32[4]{0:T(128)}, u32[]{:S(2)}) copy-start(s32[4]{0:T(128)} %constant.44) | copy-start | bytes 52
  57.6 24.1 %copy-start.8 = (f32[1024]{0:T(1024)S(1)}, f32[1024]{0:T(1024)}, u32[]{:S(2)}) copy-start(f32[1024]{0:T(1024)} %param.11) | copy-start | bytes 12292
  57.7 10.4 %collective-permute-start.3 = (bf16[256,512]{1,0:T(8,128)(2,1)S(1)}, bf16[256,512]{1,0:T(8,128)(2,1)S(1)}, u32[]{:S(2)}, u32[]{:S(2)}) collective-permute-start(bf16[256,512]{1,0:T(8,128)(2,1)S(1)} %slice.88), channel_id=1, source_target_pairs={{8,12},{9,13},{10,14},{11,15},{24,28},{25,29},{26,30},{27,31}} | collective-permute-start | bytes 786440 | tf_op jit(solution)/shard_map/ppermute | solution.py:363
  66.0 2.0 %copy-start.10 = (bf16[8,128,128]{2,1,0:T(8,128)(2,1)}, bf16[8,128,128]{2,1,0:T(8,128)(2,1)S(1)}, u32[]{:S(2)}) copy-start(bf16[8,128,128]{2,1,0:T(8,128)(2,1)S(1)} %add.82) | copy-start | bytes 786436
  67.0 1.1 copy-start.1
  68.0 1.0 copy-start.15
  69.1 5.5 %collective-permute-start.9 = (bf16[8,128,128]{2,1,0:T(8,128)(2,1)}, bf16[8,128,128]{2,1,0:T(8,128)(2,1)}, u32[]{:S(2)}, u32[]{:S(2)}) collective-permute-start(bf16[8,128,128]{2,1,0:T(8,128)(2,1)} %fusion.1), channel_id=1, source_target_pairs={{8,12},{9,13},{10,14},{11,15},{24,28},{25,29},{26,30},{27,31}} | collective-permute-start | bytes 786440 | tf_op jit(solution)/shard_map/ppermute | solution.py:363
  71.1 23.7 %collective-permute-start.13 = (bf16[1024,512]{1,0:T(8,128)(2,1)}, bf16[1024,512]{1,0:T(8,128)(2,1)}, u32[]{:S(2)}, u32[]{:S(2)}) collective-permute-start(bf16[1024,512]{1,0:T(8,128)(2,1)} %copy-done.15), channel_id=1, source_target_pairs={{4,0},{5,1},{6,2},{7,3},{20,16},{21,17},{22,18},{23,19}} | collective-permute-start | bytes 3145736 | tf_op jit(solution)/shard_map/ppermute | solution.py:363
  72.7 9.0 %copy-start.3 = (bf16[320,2048]{1,0:T(8,128)(2,1)S(1)}, bf16[320,2048]{1,0:T(8,128)(2,1)}, u32[]{:S(2)}) copy-start(bf16[320,2048]{1,0:T(8,128)(2,1)} %get-tuple-element.29.first_ref) | copy-start | bytes 3932164
  72.7 9.0 %copy-start.7 = (bf16[192,2048]{1,0:T(8,128)(2,1)S(1)}, bf16[192,2048]{1,0:T(8,128)(2,1)}, u32[]{:S(2)}) copy-start(bf16[192,2048]{1,0:T(8,128)(2,1)} %get-tuple-element.35.second_ref) | copy-start | bytes 2359300
  74.1 8.6 %copy-start.2 = (bf16[320,2048]{1,0:T(8,128)(2,1)S(1)}, bf16[320,2048]{1,0:T(8,128)(2,1)}, u32[]{:S(2)}) copy-start(bf16[320,2048]{1,0:T(8,128)(2,1)} %copy-done.1) | copy-start | bytes 3932164
  75.6 7.0 %collective-permute-start.10 = (bf16[8,128,128]{2,1,0:T(8,128)(2,1)S(1)}, bf16[8,128,128]{2,1,0:T(8,128)(2,1)S(1)}, u32[]{:S(2)}, u32[]{:S(2)}) collective-permute-start(bf16[8,128,128]{2,1,0:T(8,128)(2,1)S(1)} %add.84.s_ref), channel_id=1, source_target_pairs={{0,16},{16,0},{1,17},{17,1},{2,18},{18,2},{3,19},{19,3},{4,20},{20... | collective-permute-start | bytes 786440 | tf_op jit(solution)/shard_map/ppermute | solution.py:363
  77.2 17.5 %collective-permute-start.14 = (bf16[768,512]{1,0:T(8,128)(2,1)S(1)}, bf16[768,512]{1,0:T(8,128)(2,1)S(1)}, u32[]{:S(2)}, u32[]{:S(2)}) collective-permute-start(bf16[768,512]{1,0:T(8,128)(2,1)S(1)} %slice.89), channel_id=1, source_target_pairs={{8,12},{9,13},{10,14},{11,15},{24,28},{25,29},{26,30},{27,31}} | collective-permute-start | bytes 2359304 | tf_op jit(solution)/shard_map/ppermute | solution.py:363
  87.9 14.0 %copy-start.4 = (bf16[2,512,512]{2,1,0:T(8,128)(2,1)}, bf16[2,512,512]{2,1,0:T(8,128)(2,1)S(1)}, u32[]{:S(2)}) copy-start(bf16[2,512,512]{2,1,0:T(8,128)(2,1)S(1)} %get-tuple-element.41) | copy-start | bytes 3145732
  87.9 13.9 %collective-permute-start.11 = (bf16[2,512,512]{2,1,0:T(8,128)(2,1)S(1)}, bf16[2,512,512]{2,1,0:T(8,128)(2,1)S(1)}, u32[]{:S(2)}, u32[]{:S(2)}) collective-permute-start(bf16[2,512,512]{2,1,0:T(8,128)(2,1)S(1)} %get-tuple-element.41), channel_id=1, source_target_pairs={{1,0},{3,2},{4,5},{6,7},{9,8},{11,10},{12,13},{14,15},{17,16},{19,... | collective-permute-start | bytes 3145736 | tf_op jit(solution)/shard_map/ppermute | solution.py:441
  89.4 17.0 %collective-permute-start.17 = (bf16[2,512,512]{2,1,0:T(8,128)(2,1)S(1)}, bf16[2,512,512]{2,1,0:T(8,128)(2,1)S(1)}, u32[]{:S(2)}, u32[]{:S(2)}) collective-permute-start(bf16[2,512,512]{2,1,0:T(8,128)(2,1)S(1)} %get-tuple-element.45), channel_id=1, source_target_pairs={{1,0},{3,2},{4,5},{6,7},{9,8},{11,10},{12,13},{14,15},{17,16},{19,... | collective-permute-start | bytes 3145736 | tf_op jit(solution)/shard_map/ppermute | solution.py:441
  99.1 10.7 %copy-start.6 = (bf16[2,512,512]{2,1,0:T(8,128)(2,1)}, bf16[2,512,512]{2,1,0:T(8,128)(2,1)S(1)}, u32[]{:S(2)}) copy-start(bf16[2,512,512]{2,1,0:T(8,128)(2,1)S(1)} %get-tuple-element.44) | copy-start | bytes 3145732
  99.1 9.9 %collective-permute-start.20 = (bf16[2,512,512]{2,1,0:T(8,128)(2,1)S(1)}, bf16[2,512,512]{2,1,0:T(8,128)(2,1)S(1)}, u32[]{:S(2)}, u32[]{:S(2)}) collective-permute-start(bf16[2,512,512]{2,1,0:T(8,128)(2,1)S(1)} %get-tuple-element.46), channel_id=1, source_target_pairs={{0,1},{2,3},{5,4},{7,6},{8,9},{10,11},{13,12},{15,14},{16,17},{18,... | collective-permute-start | bytes 3145736 | tf_op jit(solution)/shard_map/ppermute | solution.py:441
  100.5 9.4 %collective-permute-start.15 = (bf16[2,512,512]{2,1,0:T(8,128)(2,1)S(1)}, bf16[2,512,512]{2,1,0:T(8,128)(2,1)S(1)}, u32[]{:S(2)}, u32[]{:S(2)}) collective-permute-start(bf16[2,512,512]{2,1,0:T(8,128)(2,1)S(1)} %get-tuple-element.44), channel_id=1, source_target_pairs={{0,1},{2,3},{5,4},{7,6},{8,9},{10,11},{13,12},{15,14},{16,17},{18,... | collective-permute-start | bytes 3145736 | tf_op jit(solution)/shard_map/ppermute | solution.py:441
  101.8 7.3 %copy-start.13 = (bf16[2,512,512]{2,1,0:T(8,128)(2,1)}, bf16[2,512,512]{2,1,0:T(8,128)(2,1)S(1)}, u32[]{:S(2)}) copy-start(bf16[2,512,512]{2,1,0:T(8,128)(2,1)S(1)} %collective-permute-done.11) | copy-start | bytes 3145732
  102.9 33.1 %collective-permute-start.12 = (bf16[512,512]{1,0:T(8,128)(2,1)}, bf16[512,512]{1,0:T(8,128)(2,1)}, u32[]{:S(2)}, u32[]{:S(2)}) collective-permute-start(bf16[512,512]{1,0:T(8,128)(2,1)} %fusion.6), channel_id=1, source_target_pairs={{0,2},{2,0},{5,7},{7,5},{8,10},{10,8},{13,15},{15,13},{16,18},{18,... | collective-permute-start | bytes 1572872 | tf_op jit(solution)/shard_map/ppermute | solution.py:445
  106.5 23.6 %collective-permute-start.18 = (bf16[512,512]{1,0:T(8,128)(2,1)S(1)}, bf16[512,512]{1,0:T(8,128)(2,1)S(1)}, u32[]{:S(2)}, u32[]{:S(2)}) collective-permute-start(bf16[512,512]{1,0:T(8,128)(2,1)S(1)} %fusion.8), channel_id=1, source_target_pairs={{0,2},{2,0},{5,7},{7,5},{8,10},{10,8},{13,15},{15,13},{16,18},{18,... | collective-permute-start | bytes 1572872 | tf_op jit(solution)/shard_map/ppermute | solution.py:445
  109.1 24.4 %collective-permute-start.21 = (bf16[512,512]{1,0:T(8,128)(2,1)S(1)}, bf16[512,512]{1,0:T(8,128)(2,1)S(1)}, u32[]{:S(2)}, u32[]{:S(2)}) collective-permute-start(bf16[512,512]{1,0:T(8,128)(2,1)S(1)} %fusion.9), channel_id=1, source_target_pairs={{1,3},{3,1},{4,6},{6,4},{9,11},{11,9},{12,14},{14,12},{17,19},{19,... | collective-permute-start | bytes 1572872 | tf_op jit(solution)/shard_map/ppermute | solution.py:445
  109.8 24.7 %copy-start.14 = (bf16[2,512,512]{2,1,0:T(8,128)(2,1)}, bf16[2,512,512]{2,1,0:T(8,128)(2,1)S(1)}, u32[]{:S(2)}) copy-start(bf16[2,512,512]{2,1,0:T(8,128)(2,1)S(1)} %collective-permute-done.15) | copy-start | bytes 3145732
  110.9 25.1 %copy-start.5 = (bf16[2,512,512]{2,1,0:T(8,128)(2,1)S(1)}, bf16[2,512,512]{2,1,0:T(8,128)(2,1)}, u32[]{:S(2)}) copy-start(bf16[2,512,512]{2,1,0:T(8,128)(2,1)} %copy-done.4) | copy-start | bytes 3145732
  110.9 25.1 %collective-permute-start.16 = (bf16[512,512]{1,0:T(8,128)(2,1)}, bf16[512,512]{1,0:T(8,128)(2,1)}, u32[]{:S(2)}, u32[]{:S(2)}) collective-permute-start(bf16[512,512]{1,0:T(8,128)(2,1)} %fusion.7), channel_id=1, source_target_pairs={{1,3},{3,1},{4,6},{6,4},{9,11},{11,9},{12,14},{14,12},{17,19},{19,... | collective-permute-start | bytes 1572872 | tf_op jit(solution)/shard_map/ppermute | solution.py:445
  131.1 11.4 %collective-permute-start.19 = (bf16[512,512]{1,0:T(8,128)(2,1)}, bf16[512,512]{1,0:T(8,128)(2,1)}, u32[]{:S(2)}, u32[]{:S(2)}) collective-permute-start(bf16[512,512]{1,0:T(8,128)(2,1)} %fusion.3), channel_id=1, source_target_pairs={{0,16},{2,18},{5,21},{7,23},{8,24},{10,26},{13,29},{15,31},{16,0},... | collective-permute-start | bytes 1572872 | tf_op jit(solution)/shard_map/ppermute | solution.py:454
  134.5 8.0 %collective-permute-start.22 = (bf16[512,512]{1,0:T(8,128)(2,1)}, bf16[512,512]{1,0:T(8,128)(2,1)}, u32[]{:S(2)}, u32[]{:S(2)}) collective-permute-start(bf16[512,512]{1,0:T(8,128)(2,1)} %fusion.2), channel_id=1, source_target_pairs={{1,17},{3,19},{4,20},{6,22},{9,25},{11,27},{12,28},{14,30},{17,1},... | collective-permute-start | bytes 1572872 | tf_op jit(solution)/shard_map/ppermute | solution.py:454

commit v14 on v12

--- a/solution.py
+++ b/solution.py
@@ -279,42 +279,61 @@
     )(first, second, incoming, gain.reshape(1, width))
 
 
-def project_kernel(options, place_ref, first_ref, a_ref, *refs):
-    weights, out_ref = list(refs[:-1]), refs[-1]
-
-    def put(slot, pieces):
-        at, product = 0, None
+def project_kernel(options, rows_count, ready, place_ref, first_ref, *refs):
+    rows, refs = refs[:rows_count], refs[rows_count:]
+    done, refs = refs[:ready], refs[ready:]
+    *weights, held, sems = refs[: -2 - rows_count] + refs[-2:]
+    outs = refs[-2 - rows_count : -2]
+    whole = weights[0]
+
+    def fetch(slot, pieces):
+        at = 0
         for piece in pieces:
-            part = mxu(a_ref[:, at : at + piece.shape[0]], piece[...])
-            product = part if product is None else product + part
+            to = held.at[slot, pl.ds(at, piece.shape[0])]
+            pltpu.make_async_copy(piece, to, sems.at[slot]).start()
             at += piece.shape[0]
-        out_ref[place_ref[slot]] = product.astype(BF16)
 
     for slot, counts in enumerate(options):
         for option, pieces in enumerate(counts):
             taken, weights = weights[:pieces], weights[pieces:]
             if len(counts) == 1:
-                put(slot, taken)
+                fetch(slot, taken)
             else:
-                pl.when(first_ref[slot] == 1 - option)(functools.partial(put, slot, taken))
-
-
-def project(places, first, rows, weights):
-    tokens = rows.shape[0]
+                pl.when(first_ref[slot] == 1 - option)(functools.partial(fetch, slot, taken))
+    for blocks, out in zip(done, outs):
+        for block in range(blocks.shape[0]):
+            out[place_ref[len(options) + block]] = blocks[block]
+    for slot in range(len(options)):
+        pltpu.make_async_copy(whole, held.at[slot], sems.at[slot]).wait()
+        for row, out in zip(rows, outs):
+            out[place_ref[slot]] = mxu(row[...], held[slot]).astype(BF16)
+
+
+def project(places, first, rows, weights, done=()):
+    tokens, depth = rows[0].shape
     block = weights[0][0][0].shape[1]
     count = len(weights)
     flat = [piece for options in weights for pieces in options for piece in pieces]
+    vmem = pl.BlockSpec(memory_space=pltpu.VMEM)
     return pl.pallas_call(
         functools.partial(
-            project_kernel, tuple(tuple(len(pieces) for pieces in options) for options in weights)
+            project_kernel,
+            tuple(tuple(len(pieces) for pieces in options) for options in weights),
+            len(rows),
+            len(done),
         ),
         in_specs=[pl.BlockSpec(memory_space=pltpu.SMEM)] * 2
-        + [pl.BlockSpec(memory_space=pltpu.VMEM)] * (1 + len(flat)),
-        out_specs=pl.BlockSpec(memory_space=pltpu.VMEM),
-        out_shape=jax.ShapeDtypeStruct((count, tokens, block), BF16),
+        + [vmem] * (len(rows) + len(done))
+        + [pl.BlockSpec(memory_space=pl.ANY)] * len(flat),
+        out_specs=[vmem] * len(rows),
+        out_shape=[jax.ShapeDtypeStruct((places.shape[0], tokens, block), BF16)] * len(rows),
+        scratch_shapes=[
+            pltpu.VMEM((count, depth, block), BF16),
+            pltpu.SemaphoreType.DMA((count,)),
+        ],
         compiler_params=pltpu.CompilerParams(vmem_limit_bytes=GRANT),
         name="project",
-    )(places, first, rows, *flat)
+    )(places, first, *rows, *done, *flat)
 
 
 def halving_order(count):
@@ -399,9 +418,10 @@
         pass_down(3)
         up_rest, incoming = tied(up[2][ahead:], incoming)
         up[3] = [up_first, send(up_rest, "ctx", last)]
-        weights = [([own],), ([up[1]], [down[3]]), ([up[2]], [down[2]]), (up[3], [down[1]])]
-        targets = lax.rem(here + ctx - jnp.arange(ctx), ctx)
-        first = (here >= jnp.arange(ctx)).astype(jnp.int32)
+        weights = [([up[1]], [down[3]]), ([down[1]], up[3]), ([own],), ([up[2]], [down[2]])]
+        slots = jnp.asarray([1, 3, 0, 2], jnp.int32)
+        targets = lax.rem(here + ctx - slots, ctx)
+        first = jnp.where(slots == 3, here < 3, here >= slots).astype(jnp.int32)
     else:
         whole = lax.all_gather(own, "ctx", axis=1, tiled=True)
         weights = [([w],) for w in jnp.split(whole, head, axis=1)]
@@ -415,8 +435,15 @@
     order = jnp.asarray(halving_order(head), jnp.int32)
     places = jnp.argmax(distance[:, None] == order[None, :], axis=1).astype(jnp.int32)
     mine, other = tied(mine, other)
-    give, keep = head_halved(project(places, first, other, weights))
-    own_give, own_keep = head_halved(project(places, first, mine, weights))
+    if ring:
+        pair = jnp.arange(2, dtype=jnp.int32)
+        other_done, mine_done = project(pair, first[2:], [other, mine], weights[2:])
+        (other_parts,) = project(places, first[:2], [other], weights[:2], [other_done])
+        (parts,) = project(places, first[:2], [mine], weights[:2], [mine_done])
+    else:
+        other_parts, parts = project(places, first, [other, mine], weights)
+    give, keep = head_halved(other_parts)
+    own_give, own_keep = head_halved(parts)
     last_pairs = head_pairs(head // 2)
     give_a, give_b = jnp.split(give, 2)
     keep_a, keep_b = jnp.split(keep, 2)

time: 133 us -> 132 us (level)
  the two profiles are of different devices: /device:TPU:16 before, /device:TPU:0 now
where the time goes in v14:
time: 132 us; the launch traced here: 131 us
  Pallas kernels  44.2 us (33%)
  waiting for transfers between devices  35.5 us (27%)
  starting transfers between devices  32.6 us (25%)
  local copies, waits for them, and re-layouts  8.24 us (6%)
  other arithmetic  7.67 us (6%)
  matrix products  2.29 us (2%)
    ppermute x18, waiting for transfers between devices, send(): return lax.ppermute(value, axis, pairs)  35.5 us
    ppermute x18, starting transfers between devices, send(): return lax.ppermute(value, axis, pairs)  32 us
    pallas_call x2, Pallas kernels, local_part(): pl.pallas_call(functools.partial(chunk_kernel, group, first), grid=(steps...  30.5 us
    pallas_call x3, Pallas kernels, project(): pl.pallas_call(functools.partial(project_kernel, tuple((tuple((len(pieces...  10.8 us
    unnamed x39, local copies, waits for them, and re-layouts  3.8 us
    convert_element_type x4, other arithmetic, summed(): return (keep.astype(F32) + got.astype(F32)).astype(BF16)  3.32 us
    pallas_call x2, Pallas kernels, normed_rows(): pl.pallas_call(norm_kernel, in_specs=[pl.BlockSpec(memory_space=pltpu.VME...  2.93 us
  transfers between devices with their start and end apart: 20, of which 9 were waited for; matrix products, arithmetic and copies ran while one was open for 9% of the time, Pallas kernels for 31%

profile of v14, /device:TPU:0, one launch (start us, length us, event | category | flops | bytes accessed | tf_op | source)
XLA Modules:
  0.0 131.0 jit_solution(2836194525332582014)
XLA Ops:
  0.0 1.6 %copy-done = bf16[1024,1024]{1,0:T(8,128)(2,1)S(1)} copy-done((bf16[1024,1024]{1,0:T(8,128)(2,1)S(1)}, bf16[1024,1024]{1,0:T(8,128)(2,1)}, u32[]{:S(2)}) %copy-start) | copy-done | bytes 2097176
  1.6 1.1 constant_dynamic-slice_fusion.refs_2_
  2.7 5.0 %collective-permute-start = (bf16[1024,512]{1,0:T(8,128)(2,1)}, bf16[1024,512]{1,0:T(8,128)(2,1)S(1)}, u32[]{:S(2)}, u32[]{:S(2)}) collective-permute-start(bf16[1024,512]{1,0:T(8,128)(2,1)} %constant_dynamic-slice_fusion.refs_2_), channel_id=1, source_target_pairs={{0,4},{4,8},{8,12},{1,5},{5,9},{9,13},{2,6},{6,10},{10,14},{3,7},{... | collective-permute-start | bytes 3145736 | tf_op jit(solution)/shard_map/ppermute | solution.py:368
  7.7 1.3 collective-permute-start.1
  9.0 1.0 copy.10
  10.0 18.1 %local_part.2 = (bf16[320,2048]{1,0:T(8,128)(2,1)}, f32[8,128,256]{2,1,0:T(8,128)}) custom-call(bf16[512,1024]{1,0:T(8,128)(2,1)} %q_ref.3, bf16[512,2,1024]{2,1,0:T(2,128)(2,1)} %k_ref.3, bf16[512,2,1024]{2,1,0:T(2,128)(2,1)} %v_ref.3, f32[1024,8]{1,0:T(8,128)} %bitcast.27), custom_call_target="tpu_custom_call" | custom-call | flops 16777216000 | bytes 5242880 | tf_op jit(solution)/shard_map/local_part/pallas_call | solution.py:215
  28.1 1.5 %collective-permute-start.8 = (bf16[320,2048]{1,0:T(8,128)(2,1)}, bf16[320,2048]{1,0:T(8,128)(2,1)S(1)}, u32[]{:S(2)}, u32[]{:S(2)}) collective-permute-start(bf16[320,2048]{1,0:T(8,128)(2,1)} %get-tuple-element.35.first_ref), channel_id=1, source_target_pairs={{0,16},{16,0},{1,17},{17,1},{2,18},{18,2},{3,19},{19,3},{4,20},{20... | collective-permute-start | bytes 3932168 | tf_op jit(solution)/shard_map/ppermute | solution.py:368
  29.6 0.7 collective-permute-done.refs_2_
  30.3 4.2 %collective-permute-done.1.refs_4_ = bf16[1024,512]{1,0:T(8,128)(2,1)} collective-permute-done((bf16[1024,512]{1,0:T(8,128)(2,1)}, bf16[1024,512]{1,0:T(8,128)(2,1)}, u32[]{:S(2)}, u32[]{:S(2)}) %collective-permute-start.1) | collective-permute-done | bytes 1048608 | tf_op jit(solution)/shard_map/ppermute | solution.py:368
  34.5 0.7 collective-permute-start.3
  35.2 1.3 collective-permute-start.7
  36.5 12.4 %local_part.3 = (bf16[192,2048]{1,0:T(8,128)(2,1)}, f32[8,128,128]{2,1,0:T(8,128)}, bf16[8,128,128]{2,1,0:T(8,128)(2,1)}, bf16[8,128,128]{2,1,0:T(8,128)(2,1)}) custom-call(bf16[512,1024]{1,0:T(8,128)(2,1)} %q_ref.3, bf16[512,2,1024]{2,1,0:T(2,128)(2,1)} %k_ref.3, bf16[512,2,1024]{2,1,0:T(2,128)(2,1)} %v_ref.3, f32[1024,8]{1,0:T(8,128)} %bitcast.28, ...), custom_call_target="tpu_custom_call" | custom-call | flops 10066329600 | bytes 3145728 | tf_op jit(solution)/shard_map/local_part/pallas_call | solution.py:215
  48.9 7.0 %collective-permute-start.4 = (bf16[8,128,128]{2,1,0:T(8,128)(2,1)}, bf16[8,128,128]{2,1,0:T(8,128)(2,1)S(1)}, u32[]{:S(2)}, u32[]{:S(2)}) collective-permute-start(bf16[8,128,128]{2,1,0:T(8,128)(2,1)} %get-tuple-element.40), channel_id=1, source_target_pairs={{0,4},{1,5},{2,6},{3,7},{16,20},{17,21},{18,22},{19,23}} | collective-permute-start | bytes 786440 | tf_op jit(solution)/shard_map/ppermute | solution.py:368
  55.9 4.4 %collective-permute-done.4 = bf16[8,128,128]{2,1,0:T(8,128)(2,1)S(1)} collective-permute-done((bf16[8,128,128]{2,1,0:T(8,128)(2,1)}, bf16[8,128,128]{2,1,0:T(8,128)(2,1)S(1)}, u32[]{:S(2)}, u32[]{:S(2)}) %collective-permute-start.4) | collective-permute-done | bytes 262176 | tf_op jit(solution)/shard_map/ppermute | solution.py:368
  60.3 1.3 %fusion = bf16[8,128,128]{2,1,0:T(8,128)(2,1)S(1)} fusion(f32[8,128,128]{2,1,0:T(8,128)} %get-tuple-element.42, bf16[8,128,128]{2,1,0:T(8,128)(2,1)} %get-tuple-element.41, bf16[8,128,128]{2,1,0:T(8,128)(2,1)S(1)} %collective-permute-done.4), kind=kOutput, calls=%fused_computation.2 | convolution fusion | flops 33816576 | bytes 1310720 | tf_op jit(solution)/shard_map/hde,hef->hdf/dot_general | solution.py:415
  61.6 0.7 collective-permute-start.5
  62.3 0.0 copy-start.2
  62.3 1.0 copy-done.2
  63.3 0.7 collective-permute-start.6
  64.0 0.0 copy-start.15
  64.0 0.0 copy-start.16
  64.0 0.0 copy-start.18
  64.1 0.0 copy-start.17
  64.1 0.0 copy-start.8
  64.1 1.6 %collective-permute-start.2 = (bf16[192,2048]{1,0:T(8,128)(2,1)}, bf16[192,2048]{1,0:T(8,128)(2,1)}, u32[]{:S(2)}, u32[]{:S(2)}) collective-permute-start(bf16[192,2048]{1,0:T(8,128)(2,1)} %get-tuple-element.38.second_ref), channel_id=1, source_target_pairs={{0,16},{16,0},{1,17},{17,1},{2,18},{18,2},{3,19},{19,3},{4,20},{20... | collective-permute-start | bytes 2359304 | tf_op jit(solution)/shard_map/ppermute | solution.py:368
  65.7 0.1 add.42
  65.8 1.0 fusion.1
  66.7 1.1 copy-done.4
  67.8 1.4 %collective-permute-start.9 = (bf16[8,128,128]{2,1,0:T(8,128)(2,1)}, bf16[8,128,128]{2,1,0:T(8,128)(2,1)}, u32[]{:S(2)}, u32[]{:S(2)}) collective-permute-start(bf16[8,128,128]{2,1,0:T(8,128)(2,1)} %fusion.1), channel_id=1, source_target_pairs={{8,12},{9,13},{10,14},{11,15},{24,28},{25,29},{26,30},{27,31}} | collective-permute-start | bytes 786440 | tf_op jit(solution)/shard_map/ppermute | solution.py:368
  69.2 1.3 collective-permute-start.11
  70.5 1.3 %slice.67 = bf16[768,512]{1,0:T(8,128)(2,1)S(1)} slice(bf16[1024,512]{1,0:T(8,128)(2,1)} %copy-done.2), slice={[256:1024], [0:512]} | slice | bytes 1572864 | tf_op jit(solution)/shard_map/slice | solution.py:419
  71.9 1.2 add.44.s_ref
  73.1 0.7 collective-permute-start.12
  73.8 0.1 fusion.8
  73.9 8.2 %collective-permute-done.2.second_ref = bf16[192,2048]{1,0:T(8,128)(2,1)} collective-permute-done((bf16[192,2048]{1,0:T(8,128)(2,1)}, bf16[192,2048]{1,0:T(8,128)(2,1)}, u32[]{:S(2)}, u32[]{:S(2)}) %collective-permute-start.2) | collective-permute-done | bytes 786464 | tf_op jit(solution)/shard_map/ppermute | solution.py:368
  82.1 1.5 %collective-permute-start.10 = (bf16[8,128,128]{2,1,0:T(8,128)(2,1)S(1)}, bf16[8,128,128]{2,1,0:T(8,128)(2,1)S(1)}, u32[]{:S(2)}, u32[]{:S(2)}) collective-permute-start(bf16[8,128,128]{2,1,0:T(8,128)(2,1)S(1)} %add.44.s_ref), channel_id=1, source_target_pairs={{0,16},{16,0},{1,17},{17,1},{2,18},{18,2},{3,19},{19,3},{4,20},{20... | collective-permute-start | bytes 786440 | tf_op jit(solution)/shard_map/ppermute | solution.py:368
  83.6 0.7 iota_reduce_fusion
  84.3 0.9 normed_rows.2.refs_1_.refs_0_
  85.3 3.2 %collective-permute-done.10.s_ref = bf16[8,128,128]{2,1,0:T(8,128)(2,1)S(1)} collective-permute-done((bf16[8,128,128]{2,1,0:T(8,128)(2,1)S(1)}, bf16[8,128,128]{2,1,0:T(8,128)(2,1)S(1)}, u32[]{:S(2)}, u32[]{:S(2)}) %collective-permute-start.10) | collective-permute-done | bytes 262176 | tf_op jit(solution)/shard_map/ppermute | solution.py:368
  88.4 2.0 %normed_rows.3.refs_0_ = bf16[512,1024]{1,0:T(8,128)(2,1)S(1)} custom-call(bf16[320,2048]{1,0:T(8,128)(2,1)S(1)} %copy-done.5, bf16[192,2048]{1,0:T(8,128)(2,1)} %collective-permute-done.2.second_ref, bf16[8,128,128]{2,1,0:T(8,128)(2,1)S(1)} %collective-permute-done.10.s_ref, f32[1,1024]{1,0:T(1,128)S(1)} %bitcast.26), custom_call_target="tpu_custom_call" | custom-call | tf_op jit(solution)/shard_map/normed_rows/pallas_call | solution.py:272
  90.5 4.3 %project.3 = (bf16[2,512,512]{2,1,0:T(8,128)(2,1)S(1)}, bf16[2,512,512]{2,1,0:T(8,128)(2,1)S(1)}) custom-call(s32[2]{0:T(128)S(1)} %iota.11.place_ref, s32[2]{0:T(128)S(1)} %get-tuple-element.67.first_ref, bf16[512,1024]{1,0:T(8,128)(2,1)S(1)} %normed_rows.3.refs_0_, bf16[512,1024]{1,0:T(8,128)(2,1)S(1)} %normed_rows.2.refs_1_.refs_0_, ...), custom_call_target="tpu_custom_call" | custom-call | tf_op jit(solution)/shard_map/project/pallas_call | solution.py:318
  94.8 3.2 %project.5 = bf16[4,512,512]{2,1,0:T(8,128)(2,1)S(1)} custom-call(s32[4]{0:T(128)S(1)} %get-tuple-element.34.place_ref, s32[2]{0:T(128)S(1)} %get-tuple-element.68.first_ref, bf16[512,1024]{1,0:T(8,128)(2,1)S(1)} %normed_rows.3.refs_0_, bf16[2,512,512]{2,1,0:T(8,128)(2,1)S(1)} %get-tuple-element.55.refs_1_, ...), custom_call_target="tpu_custom_call" | custom-call | tf_op jit(solution)/shard_map/project/pallas_call | solution.py:318
  98.1 0.1 slice.73
  98.1 0.1 collective-permute-start.14
  98.2 3.2 %project.4 = bf16[4,512,512]{2,1,0:T(8,128)(2,1)S(1)} custom-call(s32[4]{0:T(128)S(1)} %get-tuple-element.34.place_ref, s32[2]{0:T(128)S(1)} %get-tuple-element.68.first_ref, bf16[512,1024]{1,0:T(8,128)(2,1)S(1)} %normed_rows.2.refs_1_.refs_0_, bf16[2,512,512]{2,1,0:T(8,128)(2,1)S(1)} %get-tuple-element.52.refs_1_, ...), custom_call_target="tpu_custom_call" | custom-call | tf_op jit(solution)/shard_map/project/pallas_call | solution.py:318
  101.4 0.1 slice.70
  101.5 0.6 collective-permute-start.13
  102.1 0.3 add_convert_fusion.1
  102.4 0.7 slice_bitcast_fusion.2
  103.1 1.5 %collective-permute-start.15 = (bf16[256,512]{1,0:T(8,128)(2,1)S(1)}, bf16[256,512]{1,0:T(8,128)(2,1)S(1)}, u32[]{:S(2)}, u32[]{:S(2)}) collective-permute-start(bf16[256,512]{1,0:T(8,128)(2,1)S(1)} %get-tuple-element.66), channel_id=1, source_target_pairs={{0,2},{1,3},{2,0},{3,1},{4,6},{5,7},{6,4},{7,5},{8,10},{9,11},{10,... | collective-permute-start | bytes 786440 | tf_op jit(solution)/shard_map/ppermute | solution.py:368
  104.6 1.1 fusion.3
  105.7 0.1 copy-done.12
  105.7 1.3 collective-permute-start.18
  107.0 5.2 %collective-permute-done.15 = bf16[256,512]{1,0:T(8,128)(2,1)S(1)} collective-permute-done((bf16[256,512]{1,0:T(8,128)(2,1)S(1)}, bf16[256,512]{1,0:T(8,128)(2,1)S(1)}, u32[]{:S(2)}, u32[]{:S(2)}) %collective-permute-start.15) | collective-permute-done | bytes 262176 | tf_op jit(solution)/shard_map/ppermute | solution.py:368
  112.2 0.8 fusion.5
  113.0 1.5 %collective-permute-start.17 = (bf16[256,512]{1,0:T(8,128)(2,1)}, bf16[256,512]{1,0:T(8,128)(2,1)S(1)}, u32[]{:S(2)}, u32[]{:S(2)}) collective-permute-start(bf16[256,512]{1,0:T(8,128)(2,1)} %fusion.5), channel_id=1, source_target_pairs={{0,16},{16,0},{1,17},{17,1},{2,18},{18,2},{3,19},{19,3},{4,20},{20... | collective-permute-start | bytes 786440 | tf_op jit(solution)/shard_map/ppermute | solution.py:368
  114.5 1.5 %collective-permute-start.16 = (bf16[512,512]{1,0:T(8,128)(2,1)}, bf16[512,512]{1,0:T(8,128)(2,1)S(1)}, u32[]{:S(2)}, u32[]{:S(2)}) collective-permute-start(bf16[512,512]{1,0:T(8,128)(2,1)} %fusion.3), channel_id=1, source_target_pairs={{0,2},{1,3},{2,0},{3,1},{4,6},{5,7},{6,4},{7,5},{8,10},{9,11},{10,... | collective-permute-start | bytes 1572872 | tf_op jit(solution)/shard_map/ppermute | solution.py:368
  116.1 1.9 %collective-permute-done.18 = bf16[256,512]{1,0:T(8,128)(2,1)} collective-permute-done((bf16[256,512]{1,0:T(8,128)(2,1)}, bf16[256,512]{1,0:T(8,128)(2,1)}, u32[]{:S(2)}, u32[]{:S(2)}) %collective-permute-start.18) | collective-permute-done | bytes 262176 | tf_op jit(solution)/shard_map/ppermute | solution.py:368
  118.0 2.3 %collective-permute-done.17 = bf16[256,512]{1,0:T(8,128)(2,1)S(1)} collective-permute-done((bf16[256,512]{1,0:T(8,128)(2,1)}, bf16[256,512]{1,0:T(8,128)(2,1)S(1)}, u32[]{:S(2)}, u32[]{:S(2)}) %collective-permute-start.17) | collective-permute-done | bytes 262176 | tf_op jit(solution)/shard_map/ppermute | solution.py:368
  120.2 1.0 add_convert_fusion.2
  121.2 1.6 %collective-permute-start.19 = (bf16[256,512]{1,0:T(8,128)(2,1)S(1)}, bf16[256,512]{1,0:T(8,128)(2,1)S(1)}, u32[]{:S(2)}, u32[]{:S(2)}) collective-permute-start(bf16[256,512]{1,0:T(8,128)(2,1)S(1)} %add_convert_fusion.2), channel_id=1, source_target_pairs={{0,16},{16,0},{1,17},{17,1},{2,18},{18,2},{3,19},{19,3},{4,20},{20... | collective-permute-start | bytes 786440 | tf_op jit(solution)/shard_map/ppermute | solution.py:368
  122.8 5.6 %collective-permute-done.16 = bf16[512,512]{1,0:T(8,128)(2,1)S(1)} collective-permute-done((bf16[512,512]{1,0:T(8,128)(2,1)}, bf16[512,512]{1,0:T(8,128)(2,1)S(1)}, u32[]{:S(2)}, u32[]{:S(2)}) %collective-permute-start.16) | collective-permute-done | bytes 524320 | tf_op jit(solution)/shard_map/ppermute | solution.py:368
  128.4 1.2 fusion.2
  129.7 1.3 maximum_select_fusion
  (46 shorter events, 0.2 us)
Async XLA Ops:
  0.0 1.6 %copy-start = (bf16[1024,1024]{1,0:T(8,128)(2,1)S(1)}, bf16[1024,1024]{1,0:T(8,128)(2,1)}, u32[]{:S(2)}) copy-start(bf16[1024,1024]{1,0:T(8,128)(2,1)} %param.13) | copy-start | bytes 6291460
  0.0 9.0 %copy-start.14 = (f32[2,8,512]{2,1,0:T(8,128)S(1)}, f32[2,8,512]{2,1,0:T(8,128)}, u32[]{:S(2)}) copy-start(f32[2,8,512]{2,1,0:T(8,128)} %param.11) | copy-start | bytes 98308
  2.7 27.6 %collective-permute-start = (bf16[1024,512]{1,0:T(8,128)(2,1)}, bf16[1024,512]{1,0:T(8,128)(2,1)S(1)}, u32[]{:S(2)}, u32[]{:S(2)}) collective-permute-start(bf16[1024,512]{1,0:T(8,128)(2,1)} %constant_dynamic-slice_fusion.refs_2_), channel_id=1, source_target_pairs={{0,4},{4,8},{8,12},{1,5},{5,9},{9,13},{2,6},{6,10},{10,14},{3,7},{... | collective-permute-start | bytes 3145736 | tf_op jit(solution)/shard_map/ppermute | solution.py:368
  7.7 26.8 %collective-permute-start.1 = (bf16[1024,512]{1,0:T(8,128)(2,1)}, bf16[1024,512]{1,0:T(8,128)(2,1)}, u32[]{:S(2)}, u32[]{:S(2)}) collective-permute-start(bf16[1024,512]{1,0:T(8,128)(2,1)} %constant_dynamic-slice_fusion.refs_2_), channel_id=1, source_target_pairs={{4,0},{8,4},{12,8},{5,1},{9,5},{13,9},{6,2},{10,6},{14,10},{7,3},{... | collective-permute-start | bytes 3145736 | tf_op jit(solution)/shard_map/ppermute | solution.py:368
  28.1 38.6 %collective-permute-start.8 = (bf16[320,2048]{1,0:T(8,128)(2,1)}, bf16[320,2048]{1,0:T(8,128)(2,1)S(1)}, u32[]{:S(2)}, u32[]{:S(2)}) collective-permute-start(bf16[320,2048]{1,0:T(8,128)(2,1)} %get-tuple-element.35.first_ref), channel_id=1, source_target_pairs={{0,16},{16,0},{1,17},{17,1},{2,18},{18,2},{3,19},{19,3},{4,20},{20... | collective-permute-start | bytes 3932168 | tf_op jit(solution)/shard_map/ppermute | solution.py:368
  34.5 27.8 %collective-permute-start.3 = (bf16[1024,512]{1,0:T(8,128)(2,1)S(1)}, bf16[1024,512]{1,0:T(8,128)(2,1)S(1)}, u32[]{:S(2)}, u32[]{:S(2)}) collective-permute-start(bf16[1024,512]{1,0:T(8,128)(2,1)S(1)} %collective-permute-done.refs_2_), channel_id=1, source_target_pairs={{4,8},{8,12},{5,9},{9,13},{6,10},{10,14},{7,11},{11,15},{20,24},{2... | collective-permute-start | bytes 3145736 | tf_op jit(solution)/shard_map/ppermute | solution.py:368
  35.2 32.6 %collective-permute-start.7 = (bf16[1024,512]{1,0:T(8,128)(2,1)}, bf16[1024,512]{1,0:T(8,128)(2,1)}, u32[]{:S(2)}, u32[]{:S(2)}) collective-permute-start(bf16[1024,512]{1,0:T(8,128)(2,1)} %collective-permute-done.1.refs_4_), channel_id=1, source_target_pairs={{4,0},{8,4},{5,1},{9,5},{6,2},{10,6},{7,3},{11,7},{20,16},{24,20},... | collective-permute-start | bytes 3145736 | tf_op jit(solution)/shard_map/ppermute | solution.py:368
  48.9 16.9 %copy-start.10 = (f32[8,128,128]{2,1,0:T(8,128)S(1)}, f32[8,128,128]{2,1,0:T(8,128)}, u32[]{:S(2)}) copy-start(f32[8,128,128]{2,1,0:T(8,128)} %get-tuple-element.42) | copy-start | bytes 1572868
  48.9 16.9 %copy-start.11 = (bf16[8,128,128]{2,1,0:T(8,128)(2,1)S(1)}, bf16[8,128,128]{2,1,0:T(8,128)(2,1)}, u32[]{:S(2)}) copy-start(bf16[8,128,128]{2,1,0:T(8,128)(2,1)} %get-tuple-element.41) | copy-start | bytes 786436
  48.9 11.4 %collective-permute-start.4 = (bf16[8,128,128]{2,1,0:T(8,128)(2,1)}, bf16[8,128,128]{2,1,0:T(8,128)(2,1)S(1)}, u32[]{:S(2)}, u32[]{:S(2)}) collective-permute-start(bf16[8,128,128]{2,1,0:T(8,128)(2,1)} %get-tuple-element.40), channel_id=1, source_target_pairs={{0,4},{1,5},{2,6},{3,7},{16,20},{17,21},{18,22},{19,23}} | collective-permute-start | bytes 786440 | tf_op jit(solution)/shard_map/ppermute | solution.py:368
  61.6 4.0 %collective-permute-start.5 = (bf16[8,128,128]{2,1,0:T(8,128)(2,1)S(1)}, bf16[8,128,128]{2,1,0:T(8,128)(2,1)S(1)}, u32[]{:S(2)}, u32[]{:S(2)}) collective-permute-start(bf16[8,128,128]{2,1,0:T(8,128)(2,1)S(1)} %fusion), channel_id=1, source_target_pairs={{4,8},{5,9},{6,10},{7,11},{20,24},{21,25},{22,26},{23,27}} | collective-permute-start | bytes 786440 | tf_op jit(solution)/shard_map/ppermute | solution.py:368
  62.3 1.0 copy-start.2
  63.3 4.5 %collective-permute-start.6 = (bf16[256,512]{1,0:T(8,128)(2,1)S(1)}, bf16[256,512]{1,0:T(8,128)(2,1)S(1)}, u32[]{:S(2)}, u32[]{:S(2)}) collective-permute-start(bf16[256,512]{1,0:T(8,128)(2,1)S(1)} %slice.68), channel_id=1, source_target_pairs={{8,12},{9,13},{10,14},{11,15},{24,28},{25,29},{26,30},{27,31}} | collective-permute-start | bytes 786440 | tf_op jit(solution)/shard_map/ppermute | solution.py:368
  64.0 9.8 %copy-start.15 = (pred[4]{0:T(512)(128)(4,1)S(1)}, pred[4]{0:T(512)(128)(4,1)}, u32[]{:S(2)}) copy-start(pred[4]{0:T(512)(128)(4,1)} %constant.39) | copy-start | bytes 16
  64.0 9.8 %copy-start.16 = (s32[4]{0:T(128)S(1)}, s32[4]{0:T(128)}, u32[]{:S(2)}) copy-start(s32[4]{0:T(128)} %constant.36.clone) | copy-start | bytes 52
  64.0 19.5 %copy-start.18 = (s32[4]{0:T(128)S(1)}, s32[4]{0:T(128)}, u32[]{:S(2)}) copy-start(s32[4]{0:T(128)} %constant.38) | copy-start | bytes 52
  64.1 19.5 %copy-start.17 = (s32[4]{0:T(128)S(1)}, s32[4]{0:T(128)}, u32[]{:S(2)}) copy-start(s32[4]{0:T(128)} %constant.37.clone) | copy-start | bytes 52
  64.1 20.3 %copy-start.8 = (f32[1024]{0:T(1024)S(1)}, f32[1024]{0:T(1024)}, u32[]{:S(2)}) copy-start(f32[1024]{0:T(1024)} %param.12) | copy-start | bytes 12292
  64.1 18.0 %collective-permute-start.2 = (bf16[192,2048]{1,0:T(8,128)(2,1)}, bf16[192,2048]{1,0:T(8,128)(2,1)}, u32[]{:S(2)}, u32[]{:S(2)}) collective-permute-start(bf16[192,2048]{1,0:T(8,128)(2,1)} %get-tuple-element.38.second_ref), channel_id=1, source_target_pairs={{0,16},{16,0},{1,17},{17,1},{2,18},{18,2},{3,19},{19,3},{4,20},{20... | collective-permute-start | bytes 2359304 | tf_op jit(solution)/shard_map/ppermute | solution.py:368
  65.8 2.1 %copy-start.9 = (bf16[8,128,128]{2,1,0:T(8,128)(2,1)}, bf16[8,128,128]{2,1,0:T(8,128)(2,1)S(1)}, u32[]{:S(2)}) copy-start(bf16[8,128,128]{2,1,0:T(8,128)(2,1)S(1)} %add.42) | copy-start | bytes 786436
  66.7 1.1 copy-start.4
  67.8 4.0 %collective-permute-start.9 = (bf16[8,128,128]{2,1,0:T(8,128)(2,1)}, bf16[8,128,128]{2,1,0:T(8,128)(2,1)}, u32[]{:S(2)}, u32[]{:S(2)}) collective-permute-start(bf16[8,128,128]{2,1,0:T(8,128)(2,1)} %fusion.1), channel_id=1, source_target_pairs={{8,12},{9,13},{10,14},{11,15},{24,28},{25,29},{26,30},{27,31}} | collective-permute-start | bytes 786440 | tf_op jit(solution)/shard_map/ppermute | solution.py:368
  69.2 25.6 %collective-permute-start.11 = (bf16[1024,512]{1,0:T(8,128)(2,1)}, bf16[1024,512]{1,0:T(8,128)(2,1)}, u32[]{:S(2)}, u32[]{:S(2)}) collective-permute-start(bf16[1024,512]{1,0:T(8,128)(2,1)} %collective-permute-done.7.refs_4_), channel_id=1, source_target_pairs={{4,0},{5,1},{6,2},{7,3},{20,16},{21,17},{22,18},{23,19}} | collective-permute-start | bytes 3145736 | tf_op jit(solution)/shard_map/ppermute | solution.py:368
  70.5 13.8 %copy-start.6 = (bf16[320,2048]{1,0:T(8,128)(2,1)S(1)}, bf16[320,2048]{1,0:T(8,128)(2,1)}, u32[]{:S(2)}) copy-start(bf16[320,2048]{1,0:T(8,128)(2,1)} %get-tuple-element.35.first_ref) | copy-start | bytes 3932164
  70.5 13.8 %copy-start.7 = (bf16[192,2048]{1,0:T(8,128)(2,1)S(1)}, bf16[192,2048]{1,0:T(8,128)(2,1)}, u32[]{:S(2)}) copy-start(bf16[192,2048]{1,0:T(8,128)(2,1)} %get-tuple-element.38.second_ref) | copy-start | bytes 2359300
  71.8 16.6 %copy-start.5 = (bf16[320,2048]{1,0:T(8,128)(2,1)S(1)}, bf16[320,2048]{1,0:T(8,128)(2,1)}, u32[]{:S(2)}) copy-start(bf16[320,2048]{1,0:T(8,128)(2,1)} %copy-done.4) | copy-start | bytes 3932164
  73.1 21.7 %collective-permute-start.12 = (bf16[768,512]{1,0:T(8,128)(2,1)S(1)}, bf16[768,512]{1,0:T(8,128)(2,1)S(1)}, u32[]{:S(2)}, u32[]{:S(2)}) collective-permute-start(bf16[768,512]{1,0:T(8,128)(2,1)S(1)} %slice.67), channel_id=1, source_target_pairs={{8,12},{9,13},{10,14},{11,15},{24,28},{25,29},{26,30},{27,31}} | collective-permute-start | bytes 2359304 | tf_op jit(solution)/shard_map/ppermute | solution.py:368
  82.1 6.4 %collective-permute-start.10 = (bf16[8,128,128]{2,1,0:T(8,128)(2,1)S(1)}, bf16[8,128,128]{2,1,0:T(8,128)(2,1)S(1)}, u32[]{:S(2)}, u32[]{:S(2)}) collective-permute-start(bf16[8,128,128]{2,1,0:T(8,128)(2,1)S(1)} %add.44.s_ref), channel_id=1, source_target_pairs={{0,16},{16,0},{1,17},{17,1},{2,18},{18,2},{3,19},{19,3},{4,20},{20... | collective-permute-start | bytes 786440 | tf_op jit(solution)/shard_map/ppermute | solution.py:368
  85.3 5.2 %copy-start.3 = (bf16[1024,512]{1,0:T(8,128)(2,1)S(1)}, bf16[1024,512]{1,0:T(8,128)(2,1)}, u32[]{:S(2)}) copy-start(bf16[1024,512]{1,0:T(8,128)(2,1)} %copy-done.2) | copy-start | bytes 3145732
  98.1 4.0 %collective-permute-start.14 = (bf16[2,512,512]{2,1,0:T(8,128)(2,1)S(1)}, bf16[2,512,512]{2,1,0:T(8,128)(2,1)S(1)}, u32[]{:S(2)}, u32[]{:S(2)}) collective-permute-start(bf16[2,512,512]{2,1,0:T(8,128)(2,1)S(1)} %slice.73), channel_id=1, source_target_pairs={{0,1},{1,0},{2,3},{3,2},{4,5},{5,4},{6,7},{7,6},{8,9},{9,8},{10,11... | collective-permute-start | bytes 3145736 | tf_op jit(solution)/shard_map/ppermute | solution.py:355
  101.4 3.2 %copy-start.1 = (bf16[4,512,512]{2,1,0:T(8,128)(2,1)}, bf16[4,512,512]{2,1,0:T(8,128)(2,1)S(1)}, u32[]{:S(2)}) copy-start(bf16[4,512,512]{2,1,0:T(8,128)(2,1)S(1)} %project.4) | copy-start | bytes 6291460
  101.5 3.1 %collective-permute-start.13 = (bf16[2,512,512]{2,1,0:T(8,128)(2,1)S(1)}, bf16[2,512,512]{2,1,0:T(8,128)(2,1)S(1)}, u32[]{:S(2)}, u32[]{:S(2)}) collective-permute-start(bf16[2,512,512]{2,1,0:T(8,128)(2,1)S(1)} %slice.70), channel_id=1, source_target_pairs={{0,1},{1,0},{2,3},{3,2},{4,5},{5,4},{6,7},{7,6},{8,9},{9,8},{10,11... | collective-permute-start | bytes 3145736 | tf_op jit(solution)/shard_map/ppermute | solution.py:355
  103.1 9.1 %collective-permute-start.15 = (bf16[256,512]{1,0:T(8,128)(2,1)S(1)}, bf16[256,512]{1,0:T(8,128)(2,1)S(1)}, u32[]{:S(2)}, u32[]{:S(2)}) collective-permute-start(bf16[256,512]{1,0:T(8,128)(2,1)S(1)} %get-tuple-element.66), channel_id=1, source_target_pairs={{0,2},{1,3},{2,0},{3,1},{4,6},{5,7},{6,4},{7,5},{8,10},{9,11},{10,... | collective-permute-start | bytes 786440 | tf_op jit(solution)/shard_map/ppermute | solution.py:368
  104.6 1.1 copy-start.12
  105.7 12.2 %collective-permute-start.18 = (bf16[256,512]{1,0:T(8,128)(2,1)}, bf16[256,512]{1,0:T(8,128)(2,1)}, u32[]{:S(2)}, u32[]{:S(2)}) collective-permute-start(bf16[256,512]{1,0:T(8,128)(2,1)} %get-tuple-element.59), channel_id=1, source_target_pairs={{0,2},{1,3},{2,0},{3,1},{4,6},{5,7},{6,4},{7,5},{8,10},{9,11},{10,... | collective-permute-start | bytes 786440 | tf_op jit(solution)/shard_map/ppermute | solution.py:368
  113.0 7.2 %collective-permute-start.17 = (bf16[256,512]{1,0:T(8,128)(2,1)}, bf16[256,512]{1,0:T(8,128)(2,1)S(1)}, u32[]{:S(2)}, u32[]{:S(2)}) collective-permute-start(bf16[256,512]{1,0:T(8,128)(2,1)} %fusion.5), channel_id=1, source_target_pairs={{0,16},{16,0},{1,17},{17,1},{2,18},{18,2},{3,19},{19,3},{4,20},{20... | collective-permute-start | bytes 786440 | tf_op jit(solution)/shard_map/ppermute | solution.py:368
  114.5 13.9 %copy-start.13 = (bf16[2,512,512]{2,1,0:T(8,128)(2,1)S(1)}, bf16[2,512,512]{2,1,0:T(8,128)(2,1)}, u32[]{:S(2)}) copy-start(bf16[2,512,512]{2,1,0:T(8,128)(2,1)} %copy-done.12) | copy-start | bytes 3145732
  114.5 13.9 %collective-permute-start.16 = (bf16[512,512]{1,0:T(8,128)(2,1)}, bf16[512,512]{1,0:T(8,128)(2,1)S(1)}, u32[]{:S(2)}, u32[]{:S(2)}) collective-permute-start(bf16[512,512]{1,0:T(8,128)(2,1)} %fusion.3), channel_id=1, source_target_pairs={{0,2},{1,3},{2,0},{3,1},{4,6},{5,7},{6,4},{7,5},{8,10},{9,11},{10,... | collective-permute-start | bytes 1572872 | tf_op jit(solution)/shard_map/ppermute | solution.py:368
  121.2 8.4 %collective-permute-start.19 = (bf16[256,512]{1,0:T(8,128)(2,1)S(1)}, bf16[256,512]{1,0:T(8,128)(2,1)S(1)}, u32[]{:S(2)}, u32[]{:S(2)}) collective-permute-start(bf16[256,512]{1,0:T(8,128)(2,1)S(1)} %add_convert_fusion.2), channel_id=1, source_target_pairs={{0,16},{16,0},{1,17},{17,1},{2,18},{18,2},{3,19},{19,3},{4,20},{20... | collective-permute-start | bytes 786440 | tf_op jit(solution)/shard_map/ppermute | solution.py:368
